TPU v7x, 32 devices: a whole 2x2x4 slice. The times are simulated.
32 devices in a mesh: geo: 8 (over z, x), bins: 4 (over y, core).
Axes of the slice: x: 2, y: 2, z: 4, core: 2. Of those that a mesh axis runs over, the one named last changes fastest.
Arguments:
- spectrum: float32 [1152, 64, 256], P('bins', 'geo'), may hold values from 0.1 to 2
- sea_mask: int32 [64, 256], P('geo'), may hold values 0 or 1
- kernel_linear: bfloat16 [1152, 1152], replicated, may hold values from -0.1875 to 0.1875
- kernel_square: bfloat16 [1152, 1152], replicated, may hold values from -0.1875 to 0.1875
- drift_kernel: bfloat16 [128, 1152], replicated, may hold values from -0.1875 to 0.1875
- ocean: float32 [2, 64, 64, 256], P(None, 'bins', 'geo'), may hold values from -3 to 3
Outputs:
- spectrum_out: float32 [1152, 64, 256], P('bins', 'geo')
- ocean_out: float32 [2, 64, 64, 256], P(None, 'bins', 'geo')
Inputs may be any that keep to these rules, and one draw needn't show every extreme that they name: `sea_mask`: 1 marks a sea column, 0 a land column.
All inputs are finite; a program needn't handle non-finite values. No bound on the sum of `sea_mask` on one device may be relied on, other than what follows from the above.
Results may differ from a plain program's by a relative error of at most 0.0018.
Values sent between devices are 32-bit elements; how exact they have to be, the bound alone decides.
No kernel may reach another device: no remote copies, remote signals or barrier semaphores. Data moves between devices by JAX's collectives and lax.ppermute only.
A program may use at most 128 MiB of HBM per device.

v0:
```python
import jax
import jax.numpy as jnp
from jax import lax
from jax.sharding import PartitionSpec as P

NDIR = 36
NFREQ = 32
NB = 1152
STEPS = 3
SUB = 2


DT_SOURCE = 0.5
DT_OCEAN = 0.2
CORIOLIS = 1.0
VISCOSITY = 1.0
DOPPLER = 0.1


def spread(block, axis, holder):
    block = jnp.where(lax.axis_index(axis) == holder, block, jnp.zeros_like(block))
    return lax.psum(block, axis)


def extended_2(shard, sides, width):
    for axis, dim in sides:
        size, length = (lax.axis_size(axis), shard.shape[dim])
        up = [(i, (i + 1) % size) for i in range(size)]
        down = [(j, i) for i, j in up]
        last = lax.slice_in_dim(shard, length - width, length, axis=dim)
        first = lax.slice_in_dim(shard, 0, width, axis=dim)
        before = lax.ppermute(last, axis, up)
        after = lax.ppermute(first, axis, down)
        shard = jnp.concatenate([before, shard, after], axis=dim)
    return shard


def speeds(first_bin, bin_count):
    bin_index = first_bin + jnp.arange(bin_count, dtype=jnp.int32)
    direction = (bin_index // NFREQ).astype(jnp.float32)
    frequency = (bin_index % NFREQ).astype(jnp.float32)
    group_speed = 0.4 / (1.0 + frequency / 16.0)
    bin_angle = 2.0 * jnp.pi / NDIR * direction
    return (group_speed * jnp.cos(bin_angle), group_speed * jnp.sin(bin_angle))


def along_y(energy, speed_y):
    flux_plus = jnp.maximum(speed_y, 0.0) * energy
    flux_minus = jnp.minimum(speed_y, 0.0) * energy
    zeros_edge = jnp.zeros_like(flux_plus[..., :1])
    plus_before = jnp.concatenate([zeros_edge, flux_plus[..., :-1]], axis=-1)
    minus_after = jnp.concatenate([flux_minus[..., 1:], zeros_edge], axis=-1)
    return flux_plus - plus_before + (minus_after - flux_minus)


def step_cells(energy, plus_left, flux_plus, flux_minus, minus_right, speed_y, sea_float):
    moved = energy - (flux_plus - plus_left + (minus_right - flux_minus)) - along_y(energy, speed_y)
    return moved * sea_float


def renew_source(energy, interaction, squares_sum, sea_float):
    return energy + DT_SOURCE * (sea_float * (interaction * energy / (1.0 + squares_sum / NB)))


def laplace(centre, west_side, east_side):
    zeros_edge = jnp.zeros_like(centre[..., :1])
    north_side = jnp.concatenate([centre[..., 1:], zeros_edge], axis=-1)
    south_side = jnp.concatenate([zeros_edge, centre[..., :-1]], axis=-1)
    return east_side + west_side + (north_side + south_side) - 4.0 * centre


def ocean_step(ocean_state, west_side, east_side, stokes_u, stokes_v, sea_float):
    laplacian = laplace(ocean_state, west_side, east_side)
    new_u = (
        ocean_state[0]
        + DT_OCEAN * (CORIOLIS * (ocean_state[1] + stokes_v) + VISCOSITY * laplacian[0])
    ) * sea_float
    new_v = (
        ocean_state[1]
        + DT_OCEAN * (-(CORIOLIS * (ocean_state[0] + stokes_u)) + VISCOSITY * laplacian[1])
    ) * sea_float
    return jnp.stack([new_u, new_v])


def per_device(spectrum, sea_mask, kernel_linear, kernel_square, drift_kernel, ocean):
    bin_count = spectrum.shape[0]
    width_x = spectrum.shape[1]
    width_y = spectrum.shape[2]
    columns = width_x * width_y
    levels = ocean.shape[1]
    bin_parts = lax.axis_size("bins")
    bin_rank = lax.axis_index("bins")
    first_bin = bin_rank * bin_count
    speed_cx, speed_cy = speeds(first_bin, bin_count)
    sea_float = sea_mask.astype(jnp.float32)
    energy = spectrum
    ocean_state = ocean
    for step_index in range(STEPS):
        current = spread(ocean_state[:, 0], "bins", 0)
        tanh_cur = jnp.tanh(current)
        stacked = jnp.concatenate([energy, tanh_cur, sea_float[None]], axis=0)
        widened = extended_2(stacked, (("geo", 1),), SUB)
        energy_wide = widened[:bin_count]
        tanh_east = widened[bin_count]
        tanh_north = widened[bin_count + 1]
        sea_wide = widened[bin_count + 2]
        for substep in range(SUB):
            speed_x = speed_cx[:, None, None] + DOPPLER * tanh_east[None]
            speed_y = speed_cy[:, None, None] + DOPPLER * tanh_north[None]
            flux_plus = jnp.maximum(speed_x, 0.0) * energy_wide
            flux_minus = jnp.minimum(speed_x, 0.0) * energy_wide
            energy_wide = step_cells(
                energy_wide[:, 1:-1],
                flux_plus[:, :-2],
                flux_plus[:, 1:-1],
                flux_minus[:, 1:-1],
                flux_minus[:, 2:],
                speed_y[:, 1:-1],
                sea_wide[1:-1],
            )
            tanh_east = tanh_east[1:-1]
            tanh_north = tanh_north[1:-1]
            sea_wide = sea_wide[1:-1]
        energy = energy_wide
        energy_flat = energy.reshape(bin_count, columns)
        gathered = lax.all_to_all(energy_flat, "bins", split_axis=1, concat_axis=0, tiled=True)
        col_share = columns // bin_parts
        sea_share = lax.dynamic_slice_in_dim(
            sea_float.reshape(columns), bin_rank * col_share, col_share
        )
        rounded = gathered.astype(jnp.bfloat16)
        squared = (gathered * gathered).astype(jnp.bfloat16)
        interaction = jnp.dot(kernel_linear, rounded, preferred_element_type=jnp.float32) + jnp.dot(
            kernel_square, squared, preferred_element_type=jnp.float32
        )
        updated = renew_source(
            gathered, interaction, jnp.sum(gathered * gathered, axis=0), sea_share
        )
        stokes_cols = jnp.dot(
            drift_kernel, updated.astype(jnp.bfloat16), preferred_element_type=jnp.float32
        )
        energy_flat, stokes_drift = (
            lax.all_to_all(updated, "bins", split_axis=0, concat_axis=1, tiled=True),
            lax.all_to_all(stokes_cols, "bins", split_axis=0, concat_axis=1, tiled=True),
        )
        energy = energy_flat.reshape(bin_count, width_x, width_y)
        stokes_drift = stokes_drift.reshape(levels, 2, width_x, width_y)
        extended = extended_2(ocean_state, (("geo", 2),), 1)
        ocean_state = ocean_step(
            ocean_state,
            extended[:, :, :-2],
            extended[:, :, 2:],
            stokes_drift[:, 0],
            stokes_drift[:, 1],
            sea_float,
        )
    return (energy, ocean_state)


def solution(mesh):
    return jax.shard_map(
        per_device,
        mesh=mesh,
        in_specs=(
            P("bins", "geo", None),
            P("geo", None),
            P(),
            P(),
            P(),
            P(None, "bins", "geo", None),
        ),
        out_specs=(P("bins", "geo", None), P(None, "bins", "geo", None)),
        check_vma=False,
    )
```

profile of v0, /device:TPU:0, one launch (start us, length us, event | category | flops | bytes accessed | tf_op | source)
XLA Modules:
  0.0 560.9 jit_solution(10839193764957474302)
XLA Ops:
  2.2 12.7 %psum.21 = f32[2,8,256]{2,1,0:T(8,128)S(1)} all-reduce(f32[2,8,256]{2,1,0:T(8,128)S(1)} %fusion.147), channel_id=1, replica_groups=mesh['geo'=8,'bins'=4] {'bins'}, use_global_device_ids=true, to_apply=%region_0.1 | all-reduce | flops 4096 | bytes 32768 | tf_op jit(solution)/shard_map/psum | solution.py:22
  22.7 21.0 %collective-permute-done = f32[291,2,256]{2,1,0:T(2,128)} collective-permute-done((f32[291,2,256]{2,1,0:T(2,128)}, f32[291,2,256]{2,1,0:T(2,128)}, u32[]{:S(2)}, u32[]{:S(2)}) %collective-permute-start) | collective-permute-done | bytes 596000 | tf_op jit(solution)/shard_map/ppermute | solution.py:32
  55.4 4.2 fusion.6
  59.5 20.4 %fusion.10 = (f32[288,10,256]{2,1,0:T(8,128)}, f32[288,10,256]{2,1,0:T(8,128)}) fusion(f32[10,256]{1,0:T(8,128)S(1)} %get-tuple-element.35, f32[288]{0:T(512)S(1)} %get-tuple-element.73, f32[10,256]{1,0:T(8,128)S(1)} %get-tuple-element.36, f32[288,10,256]{2,1,0:T(8,128)} %copy-done.4, f32[288,10,255]{2,1,0:T(8,128)} %slice.488, ...), kind=kLoop, calls=%fused_computation.31 | loop fusion | flops 8847360 | bytes 32438912 | tf_op jit(solution)/shard_map/mul | solution.py:110
  86.3 4.1 fusion.71
  98.0 4.7 all-to-all-start
  102.8 28.5 %all-to-all-done = f32[288,4,512]{2,0,1:T(8,128)} async-done(((f32[288,4,512]{2,0,1:T(8,128)}), f32[288,4,512]{2,0,1:T(8,128)}, u32[]{:S(2)}, u32[]{:S(2)}) %all-to-all-start) | async-done | bytes 2359328 | tf_op jit(solution)/shard_map/all_to_all | solution.py:126
  139.9 4.1 fusion.53
  156.1 4.5 all-to-all-start.1
  165.9 5.0 collective-permute-done.3
  174.9 20.1 %psum.22 = f32[2,8,256]{2,1,0:T(8,128)S(1)} all-reduce(f32[2,8,256]{2,1,0:T(8,128)S(1)} %select_bitcast_fusion.1), channel_id=1, replica_groups=mesh['geo'=8,'bins'=4] {'bins'}, use_global_device_ids=true, to_apply=%region_2.3 | all-reduce | flops 4096 | bytes 32768 | tf_op jit(solution)/shard_map/psum | solution.py:22
  195.0 4.6 copy.71
  206.1 4.6 collective-permute-start.5
  210.7 20.6 %collective-permute-done.4 = f32[291,2,256]{2,1,0:T(2,128)S(1)} collective-permute-done((f32[291,2,256]{2,1,0:T(2,128)S(1)}, f32[291,2,256]{2,1,0:T(2,128)S(1)}, u32[]{:S(2)}, u32[]{:S(2)}) %collective-permute-start.4) | collective-permute-done | bytes 596000 | tf_op jit(solution)/shard_map/ppermute | solution.py:32
  235.8 4.6 fusion.12
  247.4 20.4 %fusion.16 = (f32[288,10,256]{2,1,0:T(8,128)}, f32[288,10,256]{2,1,0:T(8,128)}) fusion(f32[10,256]{1,0:T(8,128)S(1)} %get-tuple-element.30, f32[288]{0:T(512)S(1)} %get-tuple-element.73, f32[10,256]{1,0:T(8,128)S(1)} %get-tuple-element.31, f32[288,10,256]{2,1,0:T(8,128)} %copy-done.5, f32[288,10,255]{2,1,0:T(8,128)} %slice.524, ...), kind=kLoop, calls=%fused_computation.37 | loop fusion | flops 8847360 | bytes 32438912 | tf_op jit(solution)/shard_map/mul | solution.py:110
  274.2 4.1 fusion.67
  284.4 32.0 %all_to_all.153 = f32[288,4,512]{2,0,1:T(8,128)} all-to-all(f32[288,4,512]{2,0,1:T(8,128)S(1)} %copy.84), channel_id=1, replica_groups=mesh['geo'=8,'bins'=4] {'bins'}, dimensions={1} | all-to-all | bytes 4718592 | tf_op jit(solution)/shard_map/all_to_all | solution.py:126
  337.8 4.5 all-to-all-start.4
  346.4 4.9 collective-permute-done.7
  356.0 20.7 %psum.23 = f32[2,8,256]{2,1,0:T(8,128)S(1)} all-reduce(f32[2,8,256]{2,1,0:T(8,128)S(1)} %select_bitcast_fusion), channel_id=1, replica_groups=mesh['geo'=8,'bins'=4] {'bins'}, use_global_device_ids=true, to_apply=%region_4.5 | all-reduce | flops 4096 | bytes 32768 | tf_op jit(solution)/shard_map/psum | solution.py:22
  376.7 4.6 copy.88
  387.3 4.9 collective-permute-start.9
  392.2 20.5 %collective-permute-done.8 = f32[291,2,256]{2,1,0:T(2,128)S(1)} collective-permute-done((f32[291,2,256]{2,1,0:T(2,128)S(1)}, f32[291,2,256]{2,1,0:T(2,128)S(1)}, u32[]{:S(2)}, u32[]{:S(2)}) %collective-permute-start.8) | collective-permute-done | bytes 596000 | tf_op jit(solution)/shard_map/ppermute | solution.py:32
  417.0 4.6 fusion.18
  428.5 20.4 %fusion.22 = (f32[288,10,256]{2,1,0:T(8,128)}, f32[288,10,256]{2,1,0:T(8,128)}) fusion(f32[10,256]{1,0:T(8,128)S(1)} %get-tuple-element.25, f32[288]{0:T(512)S(1)} %get-tuple-element.73, f32[10,256]{1,0:T(8,128)S(1)} %get-tuple-element.26, f32[288,10,256]{2,1,0:T(8,128)} %copy-done.6, f32[288,10,255]{2,1,0:T(8,128)} %slice.562, ...), kind=kLoop, calls=%fused_computation.43 | loop fusion | flops 8847360 | bytes 32438912 | tf_op jit(solution)/shard_map/mul | solution.py:110
  455.3 4.1 fusion.63
  465.5 32.0 %all_to_all.154 = f32[288,4,512]{2,0,1:T(8,128)} all-to-all(f32[288,4,512]{2,0,1:T(8,128)S(1)} %copy.92), channel_id=1, replica_groups=mesh['geo'=8,'bins'=4] {'bins'}, dimensions={1} | all-to-all | bytes 4718592 | tf_op jit(solution)/shard_map/all_to_all | solution.py:126
  519.1 4.5 all-to-all-start.7
  527.7 4.6 collective-permute-done.11
  535.2 17.0 %all-to-all-done.7 = f32[4,288,512]{2,1,0:T(8,128)} async-done(((f32[4,288,512]{2,1,0:T(8,128)}), f32[4,288,512]{2,1,0:T(8,128)}, u32[]{:S(2)}, u32[]{:S(2)}) %all-to-all-start.7) | async-done | bytes 2359328 | tf_op jit(solution)/shard_map/all_to_all | solution.py:143
  552.2 4.6 copy.96
  (187 shorter events, 187.3 us)
Async XLA Ops:
  0.6 133.7 %copy-start = (bf16[1152,1152]{1,0:T(8,128)(2,1)S(1)}, bf16[1152,1152]{1,0:T(8,128)(2,1)}, u32[]{:S(2)}) copy-start(bf16[1152,1152]{1,0:T(8,128)(2,1)} %param.8) | copy-start | bytes 7962628
  17.9 25.8 %collective-permute-start = (f32[291,2,256]{2,1,0:T(2,128)}, f32[291,2,256]{2,1,0:T(2,128)}, u32[]{:S(2)}, u32[]{:S(2)}) collective-permute-start(f32[291,2,256]{2,1,0:T(2,128)} %get-tuple-element.49), channel_id=1, source_target_pairs={{0,4},{4,8},{8,12},{12,16},{16,20},{20,24},{24,28},{28,0},{1,5},{5... | collective-permute-start | bytes 1787912 | tf_op jit(solution)/shard_map/ppermute | solution.py:32
  19.4 26.3 %collective-permute-start.1 = (f32[291,2,256]{2,1,0:T(2,128)S(1)}, f32[291,2,256]{2,1,0:T(2,128)}, u32[]{:S(2)}, u32[]{:S(2)}) collective-permute-start(f32[291,2,256]{2,1,0:T(2,128)S(1)} %get-tuple-element.50), channel_id=1, source_target_pairs={{4,0},{8,4},{12,8},{16,12},{20,16},{24,20},{28,24},{0,28},{5,1},{9... | collective-permute-start | bytes 1787912 | tf_op jit(solution)/shard_map/ppermute | solution.py:33
  48.3 7.1 %copy-start.2 = (f32[291,12,256]{2,1,0:T(8,128)}, f32[291,12,256]{2,1,0:T(8,128)S(1)}, u32[]{:S(2)}) copy-start(f32[291,12,256]{2,1,0:T(8,128)S(1)} %fusion.1) | copy-start | bytes 10727428
  79.9 6.4 %slice-start.2 = ((s8[4718592]{0:T(1024)(128)(4,1)}), s8[4194304]{0:T(1024)(128)(4,1)S(1)}, s32[]{:S(2)}) async-start(s8[4718592]{0:T(1024)(128)(4,1)} %bitcast.196), calls=%async_computation.11 | async-start | bytes 8388608
  98.0 33.3 %all-to-all-start = ((f32[288,4,512]{2,0,1:T(8,128)}), f32[288,4,512]{2,0,1:T(8,128)}, u32[]{:S(2)}, u32[]{:S(2)}) async-start(f32[288,4,512]{2,0,1:T(8,128)} %copy.67), calls=%async_computation | async-start | bytes 4718592 | tf_op jit(solution)/shard_map/all_to_all | solution.py:126
  134.3 5.6 %copy-start.20 = (f32[1152,512]{0,1:T(8,128)S(1)}, f32[1152,512]{0,1:T(8,128)}, u32[]{:S(2)}) copy-start(f32[1152,512]{0,1:T(8,128)} %copy.69) | copy-start | bytes 7077892
  134.3 5.6 %copy-start.23 = (bf16[1152,1152]{1,0:T(8,128)(2,1)S(1)}, bf16[1152,1152]{1,0:T(8,128)(2,1)}, u32[]{:S(2)}) copy-start(bf16[1152,1152]{1,0:T(8,128)(2,1)} %param.9) | copy-start | bytes 7962628
  139.9 5.5 copy-start.18
  146.7 9.4 %all-to-all-start.2 = ((f32[4,32,512]{2,1,0:T(8,128)}), f32[4,32,512]{2,1,0:T(8,128)S(1)}, u32[]{:S(2)}, u32[]{:S(2)}) async-start(f32[4,32,512]{2,1,0:T(8,128)} %bitcast.14), calls=%async_computation.2 | async-start | bytes 524288 | tf_op jit(solution)/shard_map/all_to_all | solution.py:144
  153.2 7.4 %copy-start.17 = (f32[2,16,8,256]{3,2,1,0:T(8,128)S(1)}, f32[2,16,8,256]{3,2,1,0:T(8,128)}, u32[]{:S(2)}) copy-start(f32[2,16,8,256]{3,2,1,0:T(8,128)} %param.11) | copy-start | bytes 786436
  156.1 8.2 %copy-start.22 = (f32[4,32,512]{2,1,0:T(8,128)}, f32[4,32,512]{2,1,0:T(8,128)S(1)}, u32[]{:S(2)}) copy-start(f32[4,32,512]{2,1,0:T(8,128)S(1)} %all-to-all-done.2) | copy-start | bytes 786436
  156.1 38.9 %all-to-all-start.1 = ((f32[4,288,512]{2,1,0:T(8,128)}), f32[4,288,512]{2,1,0:T(8,128)}, u32[]{:S(2)}, u32[]{:S(2)}) async-start(f32[4,288,512]{2,1,0:T(8,128)} %bitcast.202), calls=%async_computation.1 | async-start | bytes 4718592 | tf_op jit(solution)/shard_map/all_to_all | solution.py:143
  160.7 5.2 collective-permute-start.2
  164.3 6.6 %collective-permute-start.3 = (f32[2,16,1,256]{3,2,0,1:T(1,128)S(1)}, f32[2,16,1,256]{3,2,0,1:T(1,128)S(1)}, u32[]{:S(2)}, u32[]{:S(2)}) collective-permute-start(f32[2,16,1,256]{3,2,0,1:T(1,128)S(1)} %get-tuple-element.68), channel_id=1, source_target_pairs={{0,4},{4,8},{8,12},{12,16},{16,20},{20,24},{24,28},{28,0},{1,5},{5... | collective-permute-start | bytes 98312 | tf_op jit(solution)/shard_map/ppermute | solution.py:32
  203.2 31.3 %copy-start.13 = (f32[288,8,256]{2,1,0:T(8,128)S(1)}, f32[288,8,256]{2,1,0:T(8,128)}, u32[]{:S(2)}) copy-start(f32[288,8,256]{2,1,0:T(8,128)} %reshape.189) | copy-start | bytes 7077892
  205.5 25.7 %collective-permute-start.4 = (f32[291,2,256]{2,1,0:T(2,128)S(1)}, f32[291,2,256]{2,1,0:T(2,128)S(1)}, u32[]{:S(2)}, u32[]{:S(2)}) collective-permute-start(f32[291,2,256]{2,1,0:T(2,128)S(1)} %get-tuple-element.47), channel_id=1, source_target_pairs={{0,4},{4,8},{8,12},{12,16},{16,20},{20,24},{24,28},{28,0},{1,5},{5... | collective-permute-start | bytes 1787912 | tf_op jit(solution)/shard_map/ppermute | solution.py:32
  206.1 28.4 %collective-permute-start.5 = (f32[291,2,256]{2,1,0:T(2,128)S(1)}, f32[291,2,256]{2,1,0:T(2,128)S(1)}, u32[]{:S(2)}, u32[]{:S(2)}) collective-permute-start(f32[291,2,256]{2,1,0:T(2,128)S(1)} %get-tuple-element.48), channel_id=1, source_target_pairs={{4,0},{8,4},{12,8},{16,12},{20,16},{24,20},{28,24},{0,28},{5,1},{9... | collective-permute-start | bytes 1787912 | tf_op jit(solution)/shard_map/ppermute | solution.py:33
  235.8 5.1 copy-start.3
  267.7 6.4 %slice-start.4 = ((s8[4718592]{0:T(1024)(128)(4,1)}), s8[4194304]{0:T(1024)(128)(4,1)S(1)}, s32[]{:S(2)}) async-start(s8[4718592]{0:T(1024)(128)(4,1)} %bitcast.198), calls=%async_computation.13 | async-start | bytes 8388608
  328.4 9.4 %all-to-all-start.5 = ((f32[4,32,512]{2,1,0:T(8,128)}), f32[4,32,512]{2,1,0:T(8,128)S(1)}, u32[]{:S(2)}, u32[]{:S(2)}) async-start(f32[4,32,512]{2,1,0:T(8,128)} %bitcast.31), calls=%async_computation.5 | async-start | bytes 524288 | tf_op jit(solution)/shard_map/all_to_all | solution.py:144
  337.8 38.9 %all-to-all-start.4 = ((f32[4,288,512]{2,1,0:T(8,128)}), f32[4,288,512]{2,1,0:T(8,128)}, u32[]{:S(2)}, u32[]{:S(2)}) async-start(f32[4,288,512]{2,1,0:T(8,128)} %bitcast.200), calls=%async_computation.4 | async-start | bytes 4718592 | tf_op jit(solution)/shard_map/all_to_all | solution.py:143
  342.4 4.0 collective-permute-start.6
  344.7 6.6 %collective-permute-start.7 = (f32[2,16,1,256]{3,2,0,1:T(1,128)S(1)}, f32[2,16,1,256]{3,2,0,1:T(1,128)S(1)}, u32[]{:S(2)}, u32[]{:S(2)}) collective-permute-start(f32[2,16,1,256]{3,2,0,1:T(1,128)S(1)} %get-tuple-element.64), channel_id=1, source_target_pairs={{0,4},{4,8},{8,12},{12,16},{16,20},{20,24},{24,28},{28,0},{1,5},{5... | collective-permute-start | bytes 98312 | tf_op jit(solution)/shard_map/ppermute | solution.py:32
  384.9 30.7 %copy-start.12 = (f32[288,8,256]{2,1,0:T(8,128)S(1)}, f32[288,8,256]{2,1,0:T(8,128)}, u32[]{:S(2)}) copy-start(f32[288,8,256]{2,1,0:T(8,128)} %reshape.191) | copy-start | bytes 7077892
  387.3 25.5 %collective-permute-start.8 = (f32[291,2,256]{2,1,0:T(2,128)S(1)}, f32[291,2,256]{2,1,0:T(2,128)S(1)}, u32[]{:S(2)}, u32[]{:S(2)}) collective-permute-start(f32[291,2,256]{2,1,0:T(2,128)S(1)} %get-tuple-element.45), channel_id=1, source_target_pairs={{0,4},{4,8},{8,12},{12,16},{16,20},{20,24},{24,28},{28,0},{1,5},{5... | collective-permute-start | bytes 1787912 | tf_op jit(solution)/shard_map/ppermute | solution.py:32
  387.3 28.3 %collective-permute-start.9 = (f32[291,2,256]{2,1,0:T(2,128)S(1)}, f32[291,2,256]{2,1,0:T(2,128)S(1)}, u32[]{:S(2)}, u32[]{:S(2)}) collective-permute-start(f32[291,2,256]{2,1,0:T(2,128)S(1)} %get-tuple-element.46), channel_id=1, source_target_pairs={{4,0},{8,4},{12,8},{16,12},{20,16},{24,20},{28,24},{0,28},{5,1},{9... | collective-permute-start | bytes 1787912 | tf_op jit(solution)/shard_map/ppermute | solution.py:33
  448.9 6.4 %slice-start = ((s8[4718592]{0:T(1024)(128)(4,1)}), s8[4194304]{0:T(1024)(128)(4,1)S(1)}, s32[]{:S(2)}) async-start(s8[4718592]{0:T(1024)(128)(4,1)} %bitcast.194), calls=%async_computation.9 | async-start | bytes 8388608
  509.7 9.4 %all-to-all-start.8 = ((f32[4,32,512]{2,1,0:T(8,128)}), f32[4,32,512]{2,1,0:T(8,128)S(1)}, u32[]{:S(2)}, u32[]{:S(2)}) async-start(f32[4,32,512]{2,1,0:T(8,128)} %bitcast.48), calls=%async_computation.8 | async-start | bytes 524288 | tf_op jit(solution)/shard_map/all_to_all | solution.py:144
  519.1 33.1 %all-to-all-start.7 = ((f32[4,288,512]{2,1,0:T(8,128)}), f32[4,288,512]{2,1,0:T(8,128)}, u32[]{:S(2)}, u32[]{:S(2)}) async-start(f32[4,288,512]{2,1,0:T(8,128)} %bitcast.201), calls=%async_computation.7 | async-start | bytes 4718592 | tf_op jit(solution)/shard_map/all_to_all | solution.py:143
  523.7 4.0 collective-permute-start.10
  525.7 6.6 %collective-permute-start.11 = (f32[2,16,1,256]{3,2,0,1:T(1,128)S(1)}, f32[2,16,1,256]{3,2,0,1:T(1,128)S(1)}, u32[]{:S(2)}, u32[]{:S(2)}) collective-permute-start(f32[2,16,1,256]{3,2,0,1:T(1,128)S(1)} %get-tuple-element.60), channel_id=1, source_target_pairs={{0,4},{4,8},{8,12},{12,16},{16,20},{20,24},{24,28},{28,0},{1,5},{5... | collective-permute-start | bytes 98312 | tf_op jit(solution)/shard_map/ppermute | solution.py:32
  (19 other events, 62.8 us)
where the time goes:
time: 571 us; the launch traced here: 561 us
  waiting for transfers between devices  144 us (25%)
  other arithmetic  126 us (22%)
  blocking collectives  117 us (20%)
  local copies, waits for them, and re-layouts  96.8 us (17%)
  starting transfers between devices  51.4 us (9%)
  matrix products  23.7 us (4%)
    ppermute x6, waiting for transfers between devices, extended_2(): before = lax.ppermute(last, axis, up)  76.7 us
    mul x6, other arithmetic, per_device(): flux_plus = jnp.maximum(speed_x, 0.0) * energy_wide  74.4 us
    all_to_all x2, blocking collectives, per_device(): lax.all_to_all(energy_flat, 'bins', split_axis=1, concat_axis=0, tiled=True)  64 us
    psum x3, blocking collectives, spread(): return lax.psum(block, axis)  53.4 us
    all_to_all x9, local copies, waits for them, and re-layouts, per_device(): lax.all_to_all(energy_flat, 'bins', split_axis=1, concat_axis=0, tiled=True)  28.9 us
    all_to_all x1, waiting for transfers between devices, per_device(): lax.all_to_all(energy_flat, 'bins', split_axis=1, concat_axis=0, tiled=True)  28.5 us
    ppermute x6, starting transfers between devices, extended_2(): after = lax.ppermute(first, axis, down)  20.6 us
    all_to_all x3, waiting for transfers between devices, per_device(): lax.all_to_all(updated, 'bins', split_axis=0, concat_axis=1, tiled=True)  17 us
  transfers between devices with their start and end apart: 19, of which 17 were waited for; matrix products, arithmetic and copies ran while one was open for 4% of the time, Pallas kernels for 0%

commit v1 on v0

v1 whole, which is shorter than its diff:
```python
import functools

import jax
import jax.numpy as jnp
from jax import lax
from jax.experimental import pallas as pl
from jax.experimental.pallas import tpu as pltpu
from jax.sharding import PartitionSpec as P

NDIR = 36
NFREQ = 32
STEPS = 3
SUB = 2
DT_SOURCE = 0.5
DT_OCEAN = 0.2
CORIOLIS = 1.0
VISCOSITY = 1.0
DOPPLER = 0.1

LANES = 128
PAD = 8
VMEM = pl.BlockSpec(memory_space=pltpu.VMEM)
SMEM = pl.BlockSpec(memory_space=pltpu.SMEM)


def params(mib):
    return pltpu.CompilerParams(vmem_limit_bytes=mib * 1024 * 1024)


def sizes_of(parts, bins_here, levels_here, rows, width):
    z = dict(B=parts, nb=bins_here, L=levels_here, R=rows, W=width, C=width // parts)
    z["mt"] = bins_here // LANES
    z["main"] = z["mt"] * LANES
    z["nr"] = bins_here - z["main"]
    z["no"] = 2 * levels_here
    z["Fr"] = LANES // z["nr"]
    z["Fo"] = LANES // z["no"]
    z["Rr"] = rows // z["Fr"]
    z["Ro"] = rows // z["Fo"]
    z["slabs"] = rows * z["mt"] + z["Rr"] + z["Ro"]
    z["NB"] = parts * bins_here
    z["CH"] = z["NB"] + LANES
    assert z["nr"] * parts == LANES and z["no"] * parts == LANES
    assert z["Rr"] * z["Fr"] == rows and z["Ro"] * z["Fo"] == rows
    return z


def lane_group(width):
    return lax.broadcasted_iota(jnp.int32, (1, LANES), 1) // width


def pack_kernel(z, who, spec_in, ocean_in, out, spec, ocean):
    B, R, C, mt = z["B"], z["R"], z["C"], z["mt"]
    for half in range(z["W"] // LANES):
        spec[half] = spec_in[:, half * LANES : (half + 1) * LANES]
        ocean[half] = ocean_in[:, half * LANES : (half + 1) * LANES]
    mine = who[0]
    slots = [lax.rem(c - mine + B, B) for c in range(B)]

    def put(slab, half, block):
        turned = block.T
        for i in range(LANES // C):
            c = half * (LANES // C) + i
            out[slots[c], slab] = turned[i * C : (i + 1) * C]

    for half in range(z["W"] // LANES):
        for r in range(R):
            for t in range(mt):
                put(r * mt + t, half, spec[half, pl.ds(t * LANES * R + r, LANES, stride=R), :])
        for src, first, count, fold, base in (
            (spec, z["main"], z["nr"], z["Fr"], R * mt),
            (ocean, 0, z["no"], z["Fo"], R * mt + z["Rr"]),
        ):
            for rr in range(R // fold):
                pieces = [
                    src[half, pl.ds(first * R + rr + i * (R // fold), count, stride=R), :]
                    for i in range(fold)
                ]
                put(base + rr, half, jnp.concatenate(pieces, axis=0))


def unpack_kernel(z, who, *refs):
    B, R, C, mt = z["B"], z["R"], z["C"], z["mt"]
    got, (out, left, right) = refs[:B], refs[B:]
    share = who[0]
    src = [lax.rem(share - k + B, B) for k in range(B)]
    for k in range(B):
        for t in range(mt):
            lanes = pl.ds(pl.multiple_of(src[k] * z["main"] + t * LANES, LANES), LANES)
            for r in range(R):
                out[r, :, lanes] = got[k][r * mt + t]
    for count, fold, base, first in (
        (z["nr"], z["Fr"], R * mt, B * z["main"]),
        (z["no"], z["Fo"], R * mt + z["Rr"], z["NB"]),
    ):
        group = lane_group(count)
        deep = R // fold
        for r in range(R):
            tile = jnp.zeros((C, LANES), jnp.float32)
            for k in range(B):
                shift = lax.rem((src[k] - r // deep) * count + LANES, LANES)
                moved = pltpu.roll(got[k][base + r % deep], shift, axis=1)
                tile = jnp.where(group == src[k], moved, tile)
            out[r, :, first : first + LANES] = tile
    for r in range(R):
        left[2 * r : 2 * r + 2] = out[r, 0:2]
        right[2 * r : 2 * r + 2] = out[r, C - 2 : C]


def send_back_kernel(z, who, state, out):
    B, R, C, mt = z["B"], z["R"], z["C"], z["mt"]
    share = who[0]
    for k in range(B):
        src = lax.rem(share - k + B, B)
        for t in range(mt):
            lanes = pl.ds(pl.multiple_of(src * z["main"] + t * LANES, LANES), LANES)
            for r in range(R):
                out[k, r * mt + t] = state[r, :, lanes]
        for count, fold, base, first in (
            (z["nr"], z["Fr"], R * mt, B * z["main"]),
            (z["no"], z["Fo"], R * mt + z["Rr"], z["NB"]),
        ):
            group = lane_group(count)
            deep = R // fold
            for rr in range(deep):
                tile = jnp.zeros((C, LANES), jnp.float32)
                for i in range(fold):
                    shift = lax.rem((i - src) * count + LANES, LANES)
                    moved = pltpu.roll(
                        state[rr + i * deep, :, first : first + LANES], shift, axis=1
                    )
                    tile = jnp.where(group == i, moved, tile)
                out[k, base + rr] = tile


def restore_kernel(z, who, *refs):
    B, R, C, mt = z["B"], z["R"], z["C"], z["mt"]
    got, (spec_out, ocean_out, wide, spec, ocean) = refs[:B], refs[B:]
    mine = who[0]
    for k in range(B):
        c = lax.rem(mine + k, B)
        wide[:, pl.ds(pl.multiple_of(c * C, C), C), :] = got[k][...]
    for half in range(z["W"] // LANES):
        cols = pl.ds(half * LANES, LANES)
        for r in range(R):
            for t in range(mt):
                at = pl.ds(t * LANES * R + r, LANES, stride=R)
                spec[half, at, :] = wide[r * mt + t, cols].T
        for dst, first, count, fold, base in (
            (spec, z["main"], z["nr"], z["Fr"], R * mt),
            (ocean, 0, z["no"], z["Fo"], R * mt + z["Rr"]),
        ):
            for rr in range(R // fold):
                turned = wide[base + rr, cols].T
                for i in range(fold):
                    at = pl.ds(first * R + rr + i * (R // fold), count, stride=R)
                    dst[half, at, :] = turned[i * count : (i + 1) * count]
        spec_out[:, cols] = spec[half]
        ocean_out[:, cols] = ocean[half]


def step_kernel(
    z, state, up, down, left, right, up_corner, down_corner, sea, speed, weights, drift_weights,
    new, new_left, new_right, ext, moved, moved_twice, east, north,
):
    R, C, NB, CH, L = z["R"], z["C"], z["NB"], z["CH"], z["L"]
    E = C + 2 * PAD
    own = slice(PAD, PAD + C)

    for r in range(R):
        ext[r + 2, own] = state[r]
        ext[r + 2, PAD - 2 : PAD] = left[2 * r : 2 * r + 2]
        ext[r + 2, PAD + C : PAD + C + 2] = right[2 * r : 2 * r + 2]
    for rows, corner, at in ((up, up_corner, 0), (down, down_corner, R + 2)):
        for i in range(2):
            ext[at + i, own] = rows[i]
            ext[at + i, PAD - 2 : PAD] = corner[2 * i : 2 * i + 2]
            ext[at + i, PAD + C : PAD + C + 2] = corner[4 + 2 * i : 6 + 2 * i]

    for r in range(R + 4):
        top = ext[r, :, NB:CH]
        east[r] = DOPPLER * jnp.tanh(jnp.broadcast_to(top[:, 0:1], (E, LANES)))
        north[r] = DOPPLER * jnp.tanh(jnp.broadcast_to(top[:, L : L + 1], (E, LANES)))

    def advect(read, write, first, last, speed_cx, speed_cy):
        def along_x(r):
            energy = read(r)
            speed_x = speed_cx + east[r]
            return (
                energy,
                jnp.maximum(speed_x, 0.0) * energy,
                jnp.minimum(speed_x, 0.0) * energy,
            )

        _, plus_before, _ = along_x(first - 1)
        energy, plus, minus = along_x(first)
        for r in range(first, last):
            energy_next, plus_next, minus_next = along_x(r + 1)
            speed_y = speed_cy + north[r]
            plus_y = jnp.maximum(speed_y, 0.0) * energy
            minus_y = jnp.minimum(speed_y, 0.0) * energy
            result = (
                energy
                - ((plus - plus_before) + (minus_next - minus))
                - (
                    (plus_y - pltpu.roll(plus_y, 1, axis=0))
                    + (pltpu.roll(minus_y, E - 1, axis=0) - minus_y)
                )
            )
            write(r, result * sea[r])
            plus_before, energy, plus, minus = plus, energy_next, plus_next, minus_next

    def one_tile(j, carry):
        lanes = pl.ds(pl.multiple_of(j * LANES, LANES), LANES)
        speed_cx = speed[0:1, lanes]
        speed_cy = speed[1:2, lanes]

        def write_first(r, value):
            moved[r] = value

        def write_second(r, value):
            moved_twice[r - 2, :, lanes] = value[own]

        advect(lambda r: ext[r, :, lanes], write_first, 1, R + 3, speed_cx, speed_cy)
        advect(lambda r: moved[r], write_second, 2, R + 2, speed_cx, speed_cy)
        return carry

    lax.fori_loop(0, NB // LANES, one_tile, 0)

    chunk_rows = max(1, 256 // C)
    comp = (lax.broadcasted_iota(jnp.int32, (1, LANES), 1) // L) % 2
    sign = jnp.where(comp == 0, 1.0, -1.0).astype(jnp.float32)

    def one_chunk(m, carry):
        at = m * chunk_rows
        rows = pl.ds(at, chunk_rows)
        energy = moved_twice[rows].reshape(chunk_rows * C, NB)
        squares = energy * energy
        interaction = jnp.dot(
            energy.astype(jnp.bfloat16), weights[:NB], preferred_element_type=jnp.float32
        ) + jnp.dot(
            squares.astype(jnp.bfloat16), weights[NB:], preferred_element_type=jnp.float32
        )
        total = jnp.sum(squares, axis=1, keepdims=True)
        sea_here = sea[pl.ds(at + 2, chunk_rows), own].reshape(chunk_rows * C, LANES)
        scale = (DT_SOURCE * sea_here[:, 0:1]) / (1.0 + total / NB)
        fresh = energy + scale * (interaction * energy)
        new[rows, :, 0:NB] = fresh.reshape(chunk_rows, C, NB)
        drift = jnp.dot(
            fresh.astype(jnp.bfloat16), drift_weights[...], preferred_element_type=jnp.float32
        )
        for i in range(chunk_rows):
            r = at + i + 2
            here = ext[r, :, NB:CH]
            lap = (
                (ext[r + 1, own, NB:CH] + ext[r - 1, own, NB:CH])
                + (pltpu.roll(here, E - 1, axis=0) + pltpu.roll(here, 1, axis=0))[own]
                - 4.0 * here[own]
            )
            centre = here[own]
            other = jnp.where(
                comp == 0, pltpu.roll(centre, LANES - L, axis=1), pltpu.roll(centre, L, axis=1)
            )
            turn = sign * (CORIOLIS * (other + drift[i * C : (i + 1) * C]))
            new[at + i, :, NB:CH] = (centre + DT_OCEAN * (turn + VISCOSITY * lap)) * sea[r, own]
        return carry

    lax.fori_loop(0, R // chunk_rows, one_chunk, 0)

    for r in range(R):
        new_left[2 * r : 2 * r + 2] = new[r, 0:2]
        new_right[2 * r : 2 * r + 2] = new[r, C - 2 : C]


def speeds(bin_count):
    bin_index = jnp.arange(bin_count, dtype=jnp.int32)
    direction = (bin_index // NFREQ).astype(jnp.float32)
    frequency = (bin_index % NFREQ).astype(jnp.float32)
    group_speed = 0.4 / (1.0 + frequency / 16.0)
    bin_angle = (2.0 * jnp.pi / NDIR) * direction
    return group_speed * jnp.cos(bin_angle), group_speed * jnp.sin(bin_angle)


def per_device(G, B, spectrum, sea_mask, kernel_linear, kernel_square, drift_kernel, ocean):
    nb, R, W = spectrum.shape
    L = ocean.shape[1]
    z = sizes_of(B, nb, L, R, W)
    C, NB, CH, slabs = z["C"], z["NB"], z["CH"], z["slabs"]
    half = B // 2
    axes = ("geo", "bins")
    geo, part = lax.axis_index("geo"), lax.axis_index("bins")

    def tile_of(g, b):
        return (g // 2) * 2 + b % 2

    def share_of(g, b):
        along = b // 2
        return along + half * (g % 2) + (half - 1 - 2 * along) * (g % 2)

    def device_at(q, c):
        m, along = c // half, c % half
        along = along if m == 0 else half - 1 - along
        return ((q // 2) * 2 + m) * B + 2 * along + q % 2

    tile, share = tile_of(geo, part), share_of(geo, part)
    forward = [
        [(g * B + b, device_at(g, (b + k) % B)) for g in range(G) for b in range(B)]
        for k in range(B)
    ]
    pairs = [(q, c) for q in range(G) for c in range(B)]
    to_next_row = [(device_at(q, c), device_at((q + 1) % G, c)) for q, c in pairs]
    to_prev_row = [(t, s) for s, t in to_next_row]
    to_next_col = [(device_at(q, c), device_at(q, c + 1)) for q, c in pairs if c + 1 < B]
    to_prev_col = [(t, s) for s, t in to_next_col]

    part_id = part.astype(jnp.int32).reshape(1)
    share_id = share.astype(jnp.int32).reshape(1)

    def reordered(array, axis):
        shape = array.shape
        split = array.reshape(shape[:axis] + (B, nb) + shape[axis + 1 :])
        head = lax.slice_in_dim(split, 0, z["main"], axis=axis + 1)
        tail = lax.slice_in_dim(split, z["main"], nb, axis=axis + 1)
        pieces = [p.reshape(shape[:axis] + (-1,) + shape[axis + 1 :]) for p in (head, tail)]
        return jnp.concatenate(pieces, axis=axis)

    weights = jnp.concatenate(
        [reordered(reordered(k, 0), 1).T for k in (kernel_linear, kernel_square)], axis=0
    )
    drift_rows = drift_kernel.reshape(B, L, 2, NB)[:, :, ::-1].transpose(0, 2, 1, 3)
    drift_weights = reordered(drift_rows.reshape(2 * B * L, NB), 1).T
    speed = reordered(jnp.stack(speeds(NB)), 1)
    speed = jnp.concatenate([speed, jnp.zeros((6, NB), jnp.float32)], axis=0)

    columns_scratch = [
        pltpu.VMEM((W // LANES, nb * R, LANES), jnp.float32),
        pltpu.VMEM((W // LANES, 2 * L * R, LANES), jnp.float32),
    ]

    packed = pl.pallas_call(
        functools.partial(pack_kernel, z),
        out_shape=jax.ShapeDtypeStruct((B, slabs, C, LANES), jnp.float32),
        in_specs=[SMEM, VMEM, VMEM],
        out_specs=VMEM,
        scratch_shapes=columns_scratch,
        compiler_params=params(32),
        name="pack",
    )(part_id, spectrum.reshape(nb * R, W), ocean.reshape(2 * L * R, W))
    got = [lax.ppermute(packed[k], axes, forward[k]) for k in range(B)]

    mask = lax.all_gather(sea_mask, "geo", axis=0, tiled=True)
    mask = jnp.concatenate([mask[-2:], mask, mask[:2]], axis=0)
    mask = jnp.pad(mask, ((0, 0), (PAD, PAD)))
    mask = lax.dynamic_slice(mask, (tile * R, share * C), (R + 4, C + 2 * PAD))
    sea = jnp.broadcast_to(mask.astype(jnp.float32)[..., None], mask.shape + (LANES,))

    state_shape = jax.ShapeDtypeStruct((R, C, CH), jnp.float32)
    edge_shape = jax.ShapeDtypeStruct((2 * R, CH), jnp.float32)
    state, left, right = pl.pallas_call(
        functools.partial(unpack_kernel, z),
        out_shape=(state_shape, edge_shape, edge_shape),
        in_specs=[SMEM] + [VMEM] * B,
        out_specs=(VMEM,) * 3,
        compiler_params=params(32),
        name="unpack",
    )(share_id, *got)

    E = C + 2 * PAD
    step = pl.pallas_call(
        functools.partial(step_kernel, z),
        out_shape=(state_shape, edge_shape, edge_shape),
        in_specs=[VMEM] * 11,
        out_specs=(VMEM,) * 3,
        scratch_shapes=[
            pltpu.VMEM((R + 4, E, CH), jnp.float32),
            pltpu.VMEM((R + 4, E, LANES), jnp.float32),
            pltpu.VMEM((R, C, NB), jnp.float32),
            pltpu.VMEM((R + 4, E, LANES), jnp.float32),
            pltpu.VMEM((R + 4, E, LANES), jnp.float32),
        ],
        compiler_params=params(48),
        name="coupled_step",
    )
    for _ in range(STEPS):
        from_left = lax.ppermute(right, axes, to_next_col)
        from_right = lax.ppermute(left, axes, to_prev_col)
        up = lax.ppermute(state[R - 2 :], axes, to_next_row)
        down = lax.ppermute(state[:2], axes, to_prev_row)
        bottom = jnp.concatenate([from_left[-4:], from_right[-4:]], axis=0)
        top = jnp.concatenate([from_left[:4], from_right[:4]], axis=0)
        up_corner = lax.ppermute(bottom, axes, to_next_row)
        down_corner = lax.ppermute(top, axes, to_prev_row)
        state, left, right = step(
            state, up, down, from_left, from_right, up_corner, down_corner,
            sea, speed, weights, drift_weights,
        )

    packed = pl.pallas_call(
        functools.partial(send_back_kernel, z),
        out_shape=jax.ShapeDtypeStruct((B, slabs, C, LANES), jnp.float32),
        in_specs=[SMEM, VMEM],
        out_specs=VMEM,
        compiler_params=params(32),
        name="send_back",
    )(share_id, state)
    back = [lax.ppermute(packed[k], axes, [(t, s) for s, t in forward[k]]) for k in range(B)]
    spectrum_out, ocean_out = pl.pallas_call(
        functools.partial(restore_kernel, z),
        out_shape=(
            jax.ShapeDtypeStruct((nb * R, W), jnp.float32),
            jax.ShapeDtypeStruct((2 * L * R, W), jnp.float32),
        ),
        in_specs=[SMEM] + [VMEM] * B,
        out_specs=(VMEM,) * 2,
        scratch_shapes=[pltpu.VMEM((slabs, W, LANES), jnp.float32)] + columns_scratch,
        compiler_params=params(32),
        name="restore",
    )(part_id, *back)
    return spectrum_out.reshape(nb, R, W), ocean_out.reshape(2, L, R, W)


def solution(mesh):
    return jax.shard_map(
        functools.partial(per_device, mesh.shape["geo"], mesh.shape["bins"]),
        mesh=mesh,
        in_specs=(
            P("bins", "geo", None),
            P("geo", None),
            P(),
            P(),
            P(),
            P(None, "bins", "geo", None),
        ),
        out_specs=(P("bins", "geo", None), P(None, "bins", "geo", None)),
        check_vma=False,
    )
```

time: 571 us -> 246 us (0.43)
  the two profiles are of different devices: /device:TPU:0 before, /device:TPU:1 now
where the time goes in v1:
time: 246 us; the launch traced here: 245 us
  starting transfers between devices  66.9 us (27%)
  waiting for transfers between devices  55.6 us (23%)
  Pallas kernels  45.5 us (18%)
  local copies, waits for them, and re-layouts  37 us (15%)
  blocking collectives  24.9 us (10%)
  other arithmetic  14.2 us (6%)
    pallas_call x3, Pallas kernels, per_device(): step(state, up, down, from_left, from_right, up_corner, down_corner, sea,...  40.4 us
    ppermute x3, waiting for transfers between devices, per_device(): up_corner = lax.ppermute(bottom, axes, to_next_row)  28.5 us
    ppermute x4, waiting for transfers between devices, per_device(): lax.ppermute(packed[k], axes, [(t, s) for s, t in forward[k]])  26 us
    all_gather x1, blocking collectives, per_device(): mask = lax.all_gather(sea_mask, 'geo', axis=0, tiled=True)  24.9 us
    slice x7, local copies, waits for them, and re-layouts, reordered(): head = lax.slice_in_dim(split, 0, z['main'], axis=axis + 1)  15.4 us
    ppermute x4, starting transfers between devices, per_device(): lax.ppermute(packed[k], axes, [(t, s) for s, t in forward[k]])  14.1 us
    concatenate x6, local copies, waits for them, and re-layouts, reordered(): return jnp.concatenate(pieces, axis=axis)  13.8 us
    ppermute x3, starting transfers between devices, per_device(): from_left = lax.ppermute(right, axes, to_next_col)  12.4 us
  transfers between devices with their start and end apart: 26, of which 8 were waited for; matrix products, arithmetic and copies ran while one was open for 19% of the time, Pallas kernels for 0%

profile of v1, /device:TPU:1, one launch (start us, length us, event | category | flops | bytes accessed | tf_op | source)
XLA Modules:
  0.0 245.2 jit_solution(4139282452297695707)
XLA Ops:
  5.7 2.0 collective-permute-start.3
  7.7 4.5 %collective-permute-start.2 = (f32[20,64,128]{2,1,0:T(8,128)}, f32[20,64,128]{2,1,0:T(8,128)S(1)}, u32[]{:S(2)}, u32[]{:S(2)}) collective-permute-start(f32[20,64,128]{2,1,0:T(8,128)} %get-tuple-element.37), channel_id=1, source_target_pairs={{0,6},{1,4},{2,0},{3,2},{4,7},{5,5},{6,1},{7,3},{8,14},{9,12},{10,... | collective-permute-start | bytes 1966088 | tf_op jit(solution)/shard_map/ppermute | solution.py:349
  13.1 3.2 %collective-permute-start = (f32[20,64,128]{2,1,0:T(8,128)}, f32[20,64,128]{2,1,0:T(8,128)S(1)}, u32[]{:S(2)}, u32[]{:S(2)}) collective-permute-start(f32[20,64,128]{2,1,0:T(8,128)} %get-tuple-element.39), channel_id=1, source_target_pairs={{0,0},{1,2},{2,6},{3,4},{4,1},{5,3},{6,7},{7,5},{8,8},{9,10},{10,1... | collective-permute-start | bytes 1966088 | tf_op jit(solution)/shard_map/ppermute | solution.py:349
  18.2 3.3 %slice.172 = bf16[4,256,1152]{2,1,0:T(8,128)(2,1)} slice(bf16[4,288,1152]{2,1,0:T(8,128)(2,1)} %bitcast.52), slice={[0:4], [0:256], [0:1152]} | slice | bytes 4718592 | tf_op jit(solution)/shard_map/slice | solution.py:322
  23.8 5.1 %copy.20 = bf16[4,256,1152]{1,0,2:T(4,128)(2,1)} copy(bf16[4,256,1152]{2,1,0:T(8,128)(2,1)} %slice.172) | data formatting | bytes 4718592 | tf_op jit(solution)/shard_map/slice | solution.py:322
  28.9 5.4 %concatenate.61 = bf16[1024,4,288]{0,2,1:T(8,128)(2,1)} reshape(bf16[4,256,1152]{1,0,2:T(4,128)(2,1)} %copy.20) | data formatting | bytes 4718592 | tf_op jit(solution)/shard_map/concatenate | solution.py:325
  41.1 5.1 %copy.22 = bf16[4,256,1152]{1,0,2:T(4,128)(2,1)} copy(bf16[4,256,1152]{2,1,0:T(8,128)(2,1)} %slice.176) | data formatting | bytes 4718592 | tf_op jit(solution)/shard_map/slice | solution.py:322
  46.2 5.4 %concatenate.65 = bf16[1024,4,288]{0,2,1:T(8,128)(2,1)} reshape(bf16[4,256,1152]{1,0,2:T(4,128)(2,1)} %copy.22) | data formatting | bytes 4718592 | tf_op jit(solution)/shard_map/concatenate | solution.py:325
  55.3 24.9 %all_gather.3 = s32[64,256]{1,0:T(8,128)S(1)} all-gather(s32[8,256]{1,0:T(8,128)S(1)} %copy-done.10), channel_id=1, replica_groups=mesh['geo'=8,'bins'=4] {'geo'}, dimensions={0}, use_global_device_ids=true | all-gather | bytes 73728 | tf_op jit(solution)/shard_map/all_gather | solution.py:351
  80.7 4.1 %maximum_bitcast_fusion = (bf16[1152,1152]{1,0:T(8,128)(2,1)S(1)}, bf16[1152,1152]{1,0:T(8,128)(2,1)S(1)}) fusion(bf16[1152,128]{0,1:T(8,128)(2,1)} %bitcast.55, bf16[1152,1024]{0,1:T(8,128)(2,1)} %bitcast.49, bf16[1152,128]{0,1:T(8,128)(2,1)} %bitcast.56, bf16[1152,1024]{0,1:T(8,128)(2,1)} %bitcast.50), kind=kLoop, calls=%fused_computation.3 | loop fusion | flops 10616832 | bytes 10616832 | tf_op jit(solution)/shard_map/transpose | solution.py:328
  84.8 2.8 %pad_maximum_fusion.weights = bf16[2304,1152]{1,0:T(8,128)(2,1)} fusion(bf16[1152,1152]{1,0:T(8,128)(2,1)S(1)} %get-tuple-element.57, bf16[1152,1152]{1,0:T(8,128)(2,1)S(1)} %get-tuple-element.56), kind=kLoop, calls=%fused_computation | loop fusion | flops 10616832 | bytes 10616832 | tf_op jit(solution)/shard_map/concatenate | solution.py:327
  88.3 3.5 %collective-permute-start.6 = (f32[16,1280]{1,0:T(8,128)S(1)}, f32[16,1280]{1,0:T(8,128)S(1)}, u32[]{:S(2)}, u32[]{:S(2)}) collective-permute-start(f32[16,1280]{1,0:T(8,128)S(1)} %get-tuple-element.15), channel_id=1, source_target_pairs={{0,2},{2,6},{6,4},{1,3},{3,7},{7,5},{8,10},{10,14},{14,12},{9,11},... | collective-permute-start | bytes 245768 | tf_op jit(solution)/shard_map/ppermute | solution.py:385
  93.2 4.8 %collective-permute-start.5 = (f32[2,64,1280]{2,1,0:T(8,128)S(1)}, f32[2,64,1280]{2,1,0:T(8,128)S(1)}, u32[]{:S(2)}, u32[]{:S(2)}) collective-permute-start(f32[2,64,1280]{2,1,0:T(8,128)S(1)} %get-tuple-element.34), channel_id=1, source_target_pairs={{1,0},{3,2},{7,6},{5,4},{8,1},{10,3},{14,7},{12,5},{9,8},{11,10},{... | collective-permute-start | bytes 1966088 | tf_op jit(solution)/shard_map/ppermute | solution.py:388
  98.1 3.3 %collective-permute-start.8 = (f32[8,1280]{1,0:T(8,128)S(1)}, f32[8,1280]{1,0:T(8,128)S(1)}, u32[]{:S(2)}, u32[]{:S(2)}) collective-permute-start(f32[8,1280]{1,0:T(8,128)S(1)} %pad_maximum_fusion.3), channel_id=1, source_target_pairs={{0,1},{2,3},{6,7},{4,5},{1,8},{3,10},{7,14},{5,12},{8,9},{10,11},{... | collective-permute-start | bytes 122888 | tf_op jit(solution)/shard_map/ppermute | solution.py:391
  103.3 9.9 %collective-permute-done.8.up_corner = f32[8,1280]{1,0:T(8,128)S(1)} collective-permute-done((f32[8,1280]{1,0:T(8,128)S(1)}, f32[8,1280]{1,0:T(8,128)S(1)}, u32[]{:S(2)}, u32[]{:S(2)}) %collective-permute-start.8) | collective-permute-done | bytes 40992 | tf_op jit(solution)/shard_map/ppermute | solution.py:391
  113.4 13.3 %coupled_step.3 = (f32[8,64,1280]{2,1,0:T(8,128)S(1)}, f32[16,1280]{1,0:T(8,128)S(1)}, f32[16,1280]{1,0:T(8,128)S(1)}) custom-call(f32[8,64,1280]{2,1,0:T(8,128)} %copy-done.1, f32[2,64,1280]{2,1,0:T(8,128)S(1)} %collective-permute-done.4.up, f32[2,64,1280]{2,1,0:T(8,128)S(1)} %collective-permute-done.5.down, f32[16,1280]{1,0:T(8,128)S(1)} %collective-permute-done.6.left, ...), custom_call_target="tpu_custom_call" | custom-call | tf_op jit(solution)/shard_map/coupled_step/pallas_call | solution.py:393
  126.7 4.3 %collective-permute-start.12 = (f32[16,1280]{1,0:T(8,128)S(1)}, f32[16,1280]{1,0:T(8,128)S(1)}, u32[]{:S(2)}, u32[]{:S(2)}) collective-permute-start(f32[16,1280]{1,0:T(8,128)S(1)} %get-tuple-element.18), channel_id=1, source_target_pairs={{0,2},{2,6},{6,4},{1,3},{3,7},{7,5},{8,10},{10,14},{14,12},{9,11},... | collective-permute-start | bytes 245768 | tf_op jit(solution)/shard_map/ppermute | solution.py:385
  132.4 4.0 %collective-permute-start.11 = (f32[2,64,1280]{2,1,0:T(8,128)S(1)}, f32[2,64,1280]{2,1,0:T(8,128)S(1)}, u32[]{:S(2)}, u32[]{:S(2)}) collective-permute-start(f32[2,64,1280]{2,1,0:T(8,128)S(1)} %get-tuple-element.32), channel_id=1, source_target_pairs={{1,0},{3,2},{7,6},{5,4},{8,1},{10,3},{14,7},{12,5},{9,8},{11,10},{... | collective-permute-start | bytes 1966088 | tf_op jit(solution)/shard_map/ppermute | solution.py:388
  136.4 3.8 %collective-permute-start.14 = (f32[8,1280]{1,0:T(8,128)S(1)}, f32[8,1280]{1,0:T(8,128)S(1)}, u32[]{:S(2)}, u32[]{:S(2)}) collective-permute-start(f32[8,1280]{1,0:T(8,128)S(1)} %pad_maximum_fusion.5), channel_id=1, source_target_pairs={{0,1},{2,3},{6,7},{4,5},{1,8},{3,10},{7,14},{5,12},{8,9},{10,11},{... | collective-permute-start | bytes 122888 | tf_op jit(solution)/shard_map/ppermute | solution.py:391
  141.4 9.8 %collective-permute-done.14.up_corner = f32[8,1280]{1,0:T(8,128)S(1)} collective-permute-done((f32[8,1280]{1,0:T(8,128)S(1)}, f32[8,1280]{1,0:T(8,128)S(1)}, u32[]{:S(2)}, u32[]{:S(2)}) %collective-permute-start.14) | collective-permute-done | bytes 40992 | tf_op jit(solution)/shard_map/ppermute | solution.py:391
  151.2 13.3 %coupled_step.4 = (f32[8,64,1280]{2,1,0:T(8,128)S(1)}, f32[16,1280]{1,0:T(8,128)S(1)}, f32[16,1280]{1,0:T(8,128)S(1)}) custom-call(f32[8,64,1280]{2,1,0:T(8,128)} %copy-done.2, f32[2,64,1280]{2,1,0:T(8,128)S(1)} %collective-permute-done.10.up, f32[2,64,1280]{2,1,0:T(8,128)S(1)} %collective-permute-done.11.down, f32[16,1280]{1,0:T(8,128)S(1)} %collective-permute-done.12.left, ...), custom_call_target="tpu_custom_call" | custom-call | tf_op jit(solution)/shard_map/coupled_step/pallas_call | solution.py:393
  164.5 4.6 %collective-permute-start.18 = (f32[16,1280]{1,0:T(8,128)S(1)}, f32[16,1280]{1,0:T(8,128)S(1)}, u32[]{:S(2)}, u32[]{:S(2)}) collective-permute-start(f32[16,1280]{1,0:T(8,128)S(1)} %get-tuple-element.21), channel_id=1, source_target_pairs={{0,2},{2,6},{6,4},{1,3},{3,7},{7,5},{8,10},{10,14},{14,12},{9,11},... | collective-permute-start | bytes 245768 | tf_op jit(solution)/shard_map/ppermute | solution.py:385
  170.5 3.1 %collective-permute-start.17 = (f32[2,64,1280]{2,1,0:T(8,128)S(1)}, f32[2,64,1280]{2,1,0:T(8,128)S(1)}, u32[]{:S(2)}, u32[]{:S(2)}) collective-permute-start(f32[2,64,1280]{2,1,0:T(8,128)S(1)} %get-tuple-element.30), channel_id=1, source_target_pairs={{1,0},{3,2},{7,6},{5,4},{8,1},{10,3},{14,7},{12,5},{9,8},{11,10},{... | collective-permute-start | bytes 1966088 | tf_op jit(solution)/shard_map/ppermute | solution.py:388
  174.7 3.7 %collective-permute-start.20 = (f32[8,1280]{1,0:T(8,128)S(1)}, f32[8,1280]{1,0:T(8,128)S(1)}, u32[]{:S(2)}, u32[]{:S(2)}) collective-permute-start(f32[8,1280]{1,0:T(8,128)S(1)} %pad_maximum_fusion.7), channel_id=1, source_target_pairs={{0,1},{2,3},{6,7},{4,5},{1,8},{3,10},{7,14},{5,12},{8,9},{10,11},{... | collective-permute-start | bytes 122888 | tf_op jit(solution)/shard_map/ppermute | solution.py:391
  178.7 8.8 %collective-permute-done.20.up_corner = f32[8,1280]{1,0:T(8,128)S(1)} collective-permute-done((f32[8,1280]{1,0:T(8,128)S(1)}, f32[8,1280]{1,0:T(8,128)S(1)}, u32[]{:S(2)}, u32[]{:S(2)}) %collective-permute-start.20) | collective-permute-done | bytes 40992 | tf_op jit(solution)/shard_map/ppermute | solution.py:391
  187.5 13.9 %coupled_step.5 = (f32[8,64,1280]{2,1,0:T(8,128)S(1)}, f32[16,1280]{1,0:T(8,128)}, f32[16,1280]{1,0:T(8,128)}) custom-call(f32[8,64,1280]{2,1,0:T(8,128)} %copy-done, f32[2,64,1280]{2,1,0:T(8,128)S(1)} %collective-permute-done.16.up, f32[2,64,1280]{2,1,0:T(8,128)S(1)} %collective-permute-done.17.down, f32[16,1280]{1,0:T(8,128)S(1)} %collective-permute-done.18.left, ...), custom_call_target="tpu_custom_call" | custom-call | tf_op jit(solution)/shard_map/coupled_step/pallas_call | solution.py:393
  202.2 8.3 %collective-permute-start.25 = (f32[20,64,128]{2,1,0:T(8,128)S(1)}, f32[20,64,128]{2,1,0:T(8,128)S(1)}, u32[]{:S(2)}, u32[]{:S(2)}) collective-permute-start(f32[20,64,128]{2,1,0:T(8,128)S(1)} %get-tuple-element.26), channel_id=1, source_target_pairs={{4,0},{0,1},{2,2},{6,3},{5,4},{1,5},{3,6},{7,7},{12,8},{8,9},{10,1... | collective-permute-start | bytes 1966088 | tf_op jit(solution)/shard_map/ppermute | solution.py:406
  214.0 2.4 collective-permute-start.22
  218.0 8.4 %collective-permute-done.24.refs_2_ = f32[20,64,128]{2,1,0:T(8,128)S(1)} collective-permute-done((f32[20,64,128]{2,1,0:T(8,128)S(1)}, f32[20,64,128]{2,1,0:T(8,128)S(1)}, u32[]{:S(2)}, u32[]{:S(2)}) %collective-permute-start.24) | collective-permute-done | bytes 655392 | tf_op jit(solution)/shard_map/ppermute | solution.py:406
  226.4 6.4 %collective-permute-done.23.refs_1_ = f32[20,64,128]{2,1,0:T(8,128)S(1)} collective-permute-done((f32[20,64,128]{2,1,0:T(8,128)S(1)}, f32[20,64,128]{2,1,0:T(8,128)S(1)}, u32[]{:S(2)}, u32[]{:S(2)}) %collective-permute-start.23) | collective-permute-done | bytes 655392 | tf_op jit(solution)/shard_map/ppermute | solution.py:406
  232.8 9.6 %collective-permute-done.22.refs_0_ = f32[20,64,128]{2,1,0:T(8,128)S(1)} collective-permute-done((f32[20,64,128]{2,1,0:T(8,128)S(1)}, f32[20,64,128]{2,1,0:T(8,128)S(1)}, u32[]{:S(2)}, u32[]{:S(2)}) %collective-permute-start.22) | collective-permute-done | bytes 655392 | tf_op jit(solution)/shard_map/ppermute | solution.py:406
  242.3 2.9 %restore.1 = (f32[2304,256]{1,0:T(8,128)}, f32[256,256]{1,0:T(8,128)}) custom-call(s32[1]{0:T(128)} %bitcast.who, f32[20,64,128]{2,1,0:T(8,128)S(1)} %collective-permute-done.22.refs_0_, f32[20,64,128]{2,1,0:T(8,128)S(1)} %collective-permute-done.23.refs_1_, f32[20,64,128]{2,1,0:T(8,128)S(1)} %collective-permute-done.24.refs_2_, ...), custom_call_target="tpu_custom_call" | custom-call | tf_op jit(solution)/shard_map/restore/pallas_call | solution.py:407
  (106 shorter events, 36.6 us)
Async XLA Ops:
  4.1 12.3 %copy-start.9 = (bf16[128,1152]{1,0:T(8,128)(2,1)S(1)}, bf16[128,1152]{1,0:T(8,128)(2,1)}, u32[]{:S(2)}) copy-start(bf16[128,1152]{1,0:T(8,128)(2,1)} %param.10) | copy-start | bytes 884740
  5.7 81.9 %collective-permute-start.3 = (f32[20,64,128]{2,1,0:T(8,128)}, f32[20,64,128]{2,1,0:T(8,128)S(1)}, u32[]{:S(2)}, u32[]{:S(2)}) collective-permute-start(f32[20,64,128]{2,1,0:T(8,128)} %get-tuple-element.36), channel_id=1, source_target_pairs={{0,4},{1,0},{2,2},{3,6},{4,5},{5,1},{6,3},{7,7},{8,12},{9,8},{10,1... | collective-permute-start | bytes 1966088 | tf_op jit(solution)/shard_map/ppermute | solution.py:349
  7.7 79.9 %collective-permute-start.2 = (f32[20,64,128]{2,1,0:T(8,128)}, f32[20,64,128]{2,1,0:T(8,128)S(1)}, u32[]{:S(2)}, u32[]{:S(2)}) collective-permute-start(f32[20,64,128]{2,1,0:T(8,128)} %get-tuple-element.37), channel_id=1, source_target_pairs={{0,6},{1,4},{2,0},{3,2},{4,7},{5,5},{6,1},{7,3},{8,14},{9,12},{10,... | collective-permute-start | bytes 1966088 | tf_op jit(solution)/shard_map/ppermute | solution.py:349
  12.1 75.5 %collective-permute-start.1 = (f32[20,64,128]{2,1,0:T(8,128)}, f32[20,64,128]{2,1,0:T(8,128)S(1)}, u32[]{:S(2)}, u32[]{:S(2)}) collective-permute-start(f32[20,64,128]{2,1,0:T(8,128)} %get-tuple-element.38), channel_id=1, source_target_pairs={{0,2},{1,6},{2,4},{3,0},{4,3},{5,7},{6,5},{7,1},{8,10},{9,14},{10,... | collective-permute-start | bytes 1966088 | tf_op jit(solution)/shard_map/ppermute | solution.py:349
  13.1 74.5 %collective-permute-start = (f32[20,64,128]{2,1,0:T(8,128)}, f32[20,64,128]{2,1,0:T(8,128)S(1)}, u32[]{:S(2)}, u32[]{:S(2)}) collective-permute-start(f32[20,64,128]{2,1,0:T(8,128)} %get-tuple-element.39), channel_id=1, source_target_pairs={{0,0},{1,2},{2,6},{3,4},{4,1},{5,3},{6,7},{7,5},{8,8},{9,10},{10,1... | collective-permute-start | bytes 1966088 | tf_op jit(solution)/shard_map/ppermute | solution.py:349
  53.5 26.8 %slice-start = ((bf16[128,4,288]{2,1,0:T(4,128)(2,1)}), bf16[128,4,32]{2,1,0:T(4,128)(2,1)S(1)}, s32[]{:S(2)}) async-start(bf16[128,4,288]{2,1,0:T(4,128)(2,1)} %copy-done.8), calls=%async_computation | async-start | bytes 262144 | tf_op jit(solution)/shard_map/slice | solution.py:323
  53.5 26.9 %slice-start.1 = ((bf16[128,4,288]{2,1,0:T(4,128)(2,1)}), bf16[128,4,256]{2,1,0:T(4,128)(2,1)S(1)}, s32[]{:S(2)}) async-start(bf16[128,4,288]{2,1,0:T(4,128)(2,1)} %copy-done.8), calls=%async_computation.1 | async-start | bytes 524288 | tf_op jit(solution)/shard_map/slice | solution.py:322
  88.3 25.1 %copy-start.1 = (f32[8,64,1280]{2,1,0:T(8,128)}, f32[8,64,1280]{2,1,0:T(8,128)S(1)}, u32[]{:S(2)}) copy-start(f32[8,64,1280]{2,1,0:T(8,128)S(1)} %get-tuple-element.14.state) | copy-start | bytes 7864324
  88.3 9.7 %collective-permute-start.6 = (f32[16,1280]{1,0:T(8,128)S(1)}, f32[16,1280]{1,0:T(8,128)S(1)}, u32[]{:S(2)}, u32[]{:S(2)}) collective-permute-start(f32[16,1280]{1,0:T(8,128)S(1)} %get-tuple-element.15), channel_id=1, source_target_pairs={{0,2},{2,6},{6,4},{1,3},{3,7},{7,5},{8,10},{10,14},{14,12},{9,11},... | collective-permute-start | bytes 245768 | tf_op jit(solution)/shard_map/ppermute | solution.py:385
  91.8 6.2 %collective-permute-start.7 = (f32[16,1280]{1,0:T(8,128)S(1)}, f32[16,1280]{1,0:T(8,128)S(1)}, u32[]{:S(2)}, u32[]{:S(2)}) collective-permute-start(f32[16,1280]{1,0:T(8,128)S(1)} %get-tuple-element.16), channel_id=1, source_target_pairs={{2,0},{6,2},{4,6},{3,1},{7,3},{5,7},{10,8},{14,10},{12,14},{11,9},... | collective-permute-start | bytes 245768 | tf_op jit(solution)/shard_map/ppermute | solution.py:386
  93.2 20.0 %collective-permute-start.5 = (f32[2,64,1280]{2,1,0:T(8,128)S(1)}, f32[2,64,1280]{2,1,0:T(8,128)S(1)}, u32[]{:S(2)}, u32[]{:S(2)}) collective-permute-start(f32[2,64,1280]{2,1,0:T(8,128)S(1)} %get-tuple-element.34), channel_id=1, source_target_pairs={{1,0},{3,2},{7,6},{5,4},{8,1},{10,3},{14,7},{12,5},{9,8},{11,10},{... | collective-permute-start | bytes 1966088 | tf_op jit(solution)/shard_map/ppermute | solution.py:388
  98.0 15.3 %collective-permute-start.4 = (f32[2,64,1280]{2,1,0:T(8,128)S(1)}, f32[2,64,1280]{2,1,0:T(8,128)S(1)}, u32[]{:S(2)}, u32[]{:S(2)}) collective-permute-start(f32[2,64,1280]{2,1,0:T(8,128)S(1)} %get-tuple-element.35), channel_id=1, source_target_pairs={{0,1},{2,3},{6,7},{4,5},{1,8},{3,10},{7,14},{5,12},{8,9},{10,11},{... | collective-permute-start | bytes 1966088 | tf_op jit(solution)/shard_map/ppermute | solution.py:387
  98.1 15.2 %collective-permute-start.8 = (f32[8,1280]{1,0:T(8,128)S(1)}, f32[8,1280]{1,0:T(8,128)S(1)}, u32[]{:S(2)}, u32[]{:S(2)}) collective-permute-start(f32[8,1280]{1,0:T(8,128)S(1)} %pad_maximum_fusion.3), channel_id=1, source_target_pairs={{0,1},{2,3},{6,7},{4,5},{1,8},{3,10},{7,14},{5,12},{8,9},{10,11},{... | collective-permute-start | bytes 122888 | tf_op jit(solution)/shard_map/ppermute | solution.py:391
  101.3 11.9 %collective-permute-start.9 = (f32[8,1280]{1,0:T(8,128)S(1)}, f32[8,1280]{1,0:T(8,128)S(1)}, u32[]{:S(2)}, u32[]{:S(2)}) collective-permute-start(f32[8,1280]{1,0:T(8,128)S(1)} %pad_maximum_fusion.4), channel_id=1, source_target_pairs={{1,0},{3,2},{7,6},{5,4},{8,1},{10,3},{14,7},{12,5},{9,8},{11,10},{... | collective-permute-start | bytes 122888 | tf_op jit(solution)/shard_map/ppermute | solution.py:392
  126.7 24.5 %copy-start.2 = (f32[8,64,1280]{2,1,0:T(8,128)}, f32[8,64,1280]{2,1,0:T(8,128)S(1)}, u32[]{:S(2)}) copy-start(f32[8,64,1280]{2,1,0:T(8,128)S(1)} %get-tuple-element.17.state) | copy-start | bytes 7864324
  126.7 9.6 %collective-permute-start.12 = (f32[16,1280]{1,0:T(8,128)S(1)}, f32[16,1280]{1,0:T(8,128)S(1)}, u32[]{:S(2)}, u32[]{:S(2)}) collective-permute-start(f32[16,1280]{1,0:T(8,128)S(1)} %get-tuple-element.18), channel_id=1, source_target_pairs={{0,2},{2,6},{6,4},{1,3},{3,7},{7,5},{8,10},{10,14},{14,12},{9,11},... | collective-permute-start | bytes 245768 | tf_op jit(solution)/shard_map/ppermute | solution.py:385
  131.0 5.4 %collective-permute-start.13 = (f32[16,1280]{1,0:T(8,128)S(1)}, f32[16,1280]{1,0:T(8,128)S(1)}, u32[]{:S(2)}, u32[]{:S(2)}) collective-permute-start(f32[16,1280]{1,0:T(8,128)S(1)} %get-tuple-element.19), channel_id=1, source_target_pairs={{2,0},{6,2},{4,6},{3,1},{7,3},{5,7},{10,8},{14,10},{12,14},{11,9},... | collective-permute-start | bytes 245768 | tf_op jit(solution)/shard_map/ppermute | solution.py:386
  132.4 18.8 %collective-permute-start.11 = (f32[2,64,1280]{2,1,0:T(8,128)S(1)}, f32[2,64,1280]{2,1,0:T(8,128)S(1)}, u32[]{:S(2)}, u32[]{:S(2)}) collective-permute-start(f32[2,64,1280]{2,1,0:T(8,128)S(1)} %get-tuple-element.32), channel_id=1, source_target_pairs={{1,0},{3,2},{7,6},{5,4},{8,1},{10,3},{14,7},{12,5},{9,8},{11,10},{... | collective-permute-start | bytes 1966088 | tf_op jit(solution)/shard_map/ppermute | solution.py:388
  136.4 14.8 %collective-permute-start.10 = (f32[2,64,1280]{2,1,0:T(8,128)S(1)}, f32[2,64,1280]{2,1,0:T(8,128)S(1)}, u32[]{:S(2)}, u32[]{:S(2)}) collective-permute-start(f32[2,64,1280]{2,1,0:T(8,128)S(1)} %get-tuple-element.33), channel_id=1, source_target_pairs={{0,1},{2,3},{6,7},{4,5},{1,8},{3,10},{7,14},{5,12},{8,9},{10,11},{... | collective-permute-start | bytes 1966088 | tf_op jit(solution)/shard_map/ppermute | solution.py:387
  136.4 14.7 %collective-permute-start.14 = (f32[8,1280]{1,0:T(8,128)S(1)}, f32[8,1280]{1,0:T(8,128)S(1)}, u32[]{:S(2)}, u32[]{:S(2)}) collective-permute-start(f32[8,1280]{1,0:T(8,128)S(1)} %pad_maximum_fusion.5), channel_id=1, source_target_pairs={{0,1},{2,3},{6,7},{4,5},{1,8},{3,10},{7,14},{5,12},{8,9},{10,11},{... | collective-permute-start | bytes 122888 | tf_op jit(solution)/shard_map/ppermute | solution.py:391
  140.2 11.0 %collective-permute-start.15 = (f32[8,1280]{1,0:T(8,128)S(1)}, f32[8,1280]{1,0:T(8,128)S(1)}, u32[]{:S(2)}, u32[]{:S(2)}) collective-permute-start(f32[8,1280]{1,0:T(8,128)S(1)} %pad_maximum_fusion.6), channel_id=1, source_target_pairs={{1,0},{3,2},{7,6},{5,4},{8,1},{10,3},{14,7},{12,5},{9,8},{11,10},{... | collective-permute-start | bytes 122888 | tf_op jit(solution)/shard_map/ppermute | solution.py:392
  164.5 23.0 %copy-start = (f32[8,64,1280]{2,1,0:T(8,128)}, f32[8,64,1280]{2,1,0:T(8,128)S(1)}, u32[]{:S(2)}) copy-start(f32[8,64,1280]{2,1,0:T(8,128)S(1)} %get-tuple-element.20.state) | copy-start | bytes 7864324
  164.5 9.1 %collective-permute-start.18 = (f32[16,1280]{1,0:T(8,128)S(1)}, f32[16,1280]{1,0:T(8,128)S(1)}, u32[]{:S(2)}, u32[]{:S(2)}) collective-permute-start(f32[16,1280]{1,0:T(8,128)S(1)} %get-tuple-element.21), channel_id=1, source_target_pairs={{0,2},{2,6},{6,4},{1,3},{3,7},{7,5},{8,10},{10,14},{14,12},{9,11},... | collective-permute-start | bytes 245768 | tf_op jit(solution)/shard_map/ppermute | solution.py:385
  169.1 5.6 %collective-permute-start.19 = (f32[16,1280]{1,0:T(8,128)S(1)}, f32[16,1280]{1,0:T(8,128)S(1)}, u32[]{:S(2)}, u32[]{:S(2)}) collective-permute-start(f32[16,1280]{1,0:T(8,128)S(1)} %get-tuple-element.22), channel_id=1, source_target_pairs={{2,0},{6,2},{4,6},{3,1},{7,3},{5,7},{10,8},{14,10},{12,14},{11,9},... | collective-permute-start | bytes 245768 | tf_op jit(solution)/shard_map/ppermute | solution.py:386
  170.5 17.0 %collective-permute-start.17 = (f32[2,64,1280]{2,1,0:T(8,128)S(1)}, f32[2,64,1280]{2,1,0:T(8,128)S(1)}, u32[]{:S(2)}, u32[]{:S(2)}) collective-permute-start(f32[2,64,1280]{2,1,0:T(8,128)S(1)} %get-tuple-element.30), channel_id=1, source_target_pairs={{1,0},{3,2},{7,6},{5,4},{8,1},{10,3},{14,7},{12,5},{9,8},{11,10},{... | collective-permute-start | bytes 1966088 | tf_op jit(solution)/shard_map/ppermute | solution.py:388
  173.6 13.9 %collective-permute-start.16 = (f32[2,64,1280]{2,1,0:T(8,128)S(1)}, f32[2,64,1280]{2,1,0:T(8,128)S(1)}, u32[]{:S(2)}, u32[]{:S(2)}) collective-permute-start(f32[2,64,1280]{2,1,0:T(8,128)S(1)} %get-tuple-element.31), channel_id=1, source_target_pairs={{0,1},{2,3},{6,7},{4,5},{1,8},{3,10},{7,14},{5,12},{8,9},{10,11},{... | collective-permute-start | bytes 1966088 | tf_op jit(solution)/shard_map/ppermute | solution.py:387
  174.7 12.8 %collective-permute-start.20 = (f32[8,1280]{1,0:T(8,128)S(1)}, f32[8,1280]{1,0:T(8,128)S(1)}, u32[]{:S(2)}, u32[]{:S(2)}) collective-permute-start(f32[8,1280]{1,0:T(8,128)S(1)} %pad_maximum_fusion.7), channel_id=1, source_target_pairs={{0,1},{2,3},{6,7},{4,5},{1,8},{3,10},{7,14},{5,12},{8,9},{10,11},{... | collective-permute-start | bytes 122888 | tf_op jit(solution)/shard_map/ppermute | solution.py:391
  178.4 9.1 %collective-permute-start.21 = (f32[8,1280]{1,0:T(8,128)S(1)}, f32[8,1280]{1,0:T(8,128)S(1)}, u32[]{:S(2)}, u32[]{:S(2)}) collective-permute-start(f32[8,1280]{1,0:T(8,128)S(1)} %pad_maximum_fusion.8), channel_id=1, source_target_pairs={{1,0},{3,2},{7,6},{5,4},{8,1},{10,3},{14,7},{12,5},{9,8},{11,10},{... | collective-permute-start | bytes 122888 | tf_op jit(solution)/shard_map/ppermute | solution.py:392
  202.2 15.8 %collective-permute-start.25 = (f32[20,64,128]{2,1,0:T(8,128)S(1)}, f32[20,64,128]{2,1,0:T(8,128)S(1)}, u32[]{:S(2)}, u32[]{:S(2)}) collective-permute-start(f32[20,64,128]{2,1,0:T(8,128)S(1)} %get-tuple-element.26), channel_id=1, source_target_pairs={{4,0},{0,1},{2,2},{6,3},{5,4},{1,5},{3,6},{7,7},{12,8},{8,9},{10,1... | collective-permute-start | bytes 1966088 | tf_op jit(solution)/shard_map/ppermute | solution.py:406
  210.5 15.9 %collective-permute-start.24 = (f32[20,64,128]{2,1,0:T(8,128)S(1)}, f32[20,64,128]{2,1,0:T(8,128)S(1)}, u32[]{:S(2)}, u32[]{:S(2)}) collective-permute-start(f32[20,64,128]{2,1,0:T(8,128)S(1)} %get-tuple-element.27), channel_id=1, source_target_pairs={{6,0},{4,1},{0,2},{2,3},{7,4},{5,5},{1,6},{3,7},{14,8},{12,9},{8,1... | collective-permute-start | bytes 1966088 | tf_op jit(solution)/shard_map/ppermute | solution.py:406
  212.5 20.3 %collective-permute-start.23 = (f32[20,64,128]{2,1,0:T(8,128)S(1)}, f32[20,64,128]{2,1,0:T(8,128)S(1)}, u32[]{:S(2)}, u32[]{:S(2)}) collective-permute-start(f32[20,64,128]{2,1,0:T(8,128)S(1)} %get-tuple-element.28), channel_id=1, source_target_pairs={{2,0},{6,1},{4,2},{0,3},{3,4},{7,5},{5,6},{1,7},{10,8},{14,9},{12,... | collective-permute-start | bytes 1966088 | tf_op jit(solution)/shard_map/ppermute | solution.py:406
  214.0 28.3 %collective-permute-start.22 = (f32[20,64,128]{2,1,0:T(8,128)S(1)}, f32[20,64,128]{2,1,0:T(8,128)S(1)}, u32[]{:S(2)}, u32[]{:S(2)}) collective-permute-start(f32[20,64,128]{2,1,0:T(8,128)S(1)} %get-tuple-element.29), channel_id=1, source_target_pairs={{0,0},{2,1},{6,2},{4,3},{1,4},{3,5},{7,6},{5,7},{8,8},{10,9},{14,1... | collective-permute-start | bytes 1966088 | tf_op jit(solution)/shard_map/ppermute | solution.py:406
  (7 other events, 15.1 us)

commit v2 on v0

v2 whole, which is shorter than its diff:
```python
import functools

import jax
import jax.numpy as jnp
from jax import lax
from jax.experimental import pallas as pl
from jax.experimental.pallas import tpu as pltpu
from jax.sharding import PartitionSpec as P

NDIR = 36
NFREQ = 32
STEPS = 3
SUB = 2
DT_SOURCE = 0.5
DT_OCEAN = 0.2
CORIOLIS = 1.0
VISCOSITY = 1.0
DOPPLER = 0.1

LANES = 128
PAD = 8
EDGE = 2
VMEM = pl.BlockSpec(memory_space=pltpu.VMEM)
SMEM = pl.BlockSpec(memory_space=pltpu.SMEM)
F32 = jnp.float32
BF16 = jnp.bfloat16


def params(mib):
    return pltpu.CompilerParams(vmem_limit_bytes=mib * 1024 * 1024)


class Sizes:
    def __init__(self, parts, bins_here, levels_here, rows, width):
        self.B, self.nb, self.L, self.R, self.W = parts, bins_here, levels_here, rows, width
        self.C = width // parts
        self.mt = bins_here // LANES
        self.main = self.mt * LANES
        self.nr = bins_here - self.main
        self.no = 2 * levels_here
        self.NB = parts * bins_here
        self.CH = self.NB + LANES
        self.edge_rows = (0, 1, rows - 2, rows - 1)
        self.inner_rows = tuple(range(2, rows - 2))
        assert self.nr * parts == LANES and self.no * parts == LANES

    def folds(self, rows):
        out, base = [], len(rows) * self.mt
        for count, lane in ((self.nr, self.B * self.main), (self.no, self.NB)):
            used = min(LANES // count, len(rows))
            deep = len(rows) // used
            assert deep * used == len(rows)
            out.append((count, used, deep, base, lane))
            base += deep
        return out, base

    def slabs(self, rows):
        return self.folds(rows)[1]


def lane_group(width):
    return lax.broadcasted_iota(jnp.int32, (1, LANES), 1) // width


def pack_kernel(z, who, spec_in, ocean_in, *refs):
    B, R, C, W, mt = z.B, z.R, z.C, z.W, z.mt
    outs, (spec, ocean, wide) = refs[: 2 * B], refs[2 * B :]
    mine = who[0]
    at = 0
    for half in range(W // LANES):
        spec[half] = spec_in[:, half * LANES : (half + 1) * LANES]
        ocean[half] = ocean_in[:, half * LANES : (half + 1) * LANES]
    wide[:, 0:PAD, :] = jnp.zeros((wide.shape[0], PAD, LANES), F32)
    wide[:, PAD + W : W + 2 * PAD, :] = jnp.zeros((wide.shape[0], PAD, LANES), F32)
    for which, rows in enumerate((z.edge_rows, z.inner_rows)):
        folds, slabs = z.folds(rows)
        for half in range(W // LANES):
            cols = slice(PAD + half * LANES, PAD + (half + 1) * LANES)
            for i, r in enumerate(rows):
                for t in range(mt):
                    block = spec[half, pl.ds(t * LANES * R + r, LANES, stride=R), :]
                    wide[at + i * mt + t, cols] = block.T
            for (count, used, deep, base, _), src, first in zip(folds, (spec, ocean), (z.main, 0)):
                for rr in range(deep):
                    pieces = [
                        src[half, pl.ds(first * R + rows[rr + i * deep], count, stride=R), :]
                        for i in range(used)
                    ]
                    if used * count < LANES:
                        pieces.append(jnp.zeros((LANES - used * count, LANES), F32))
                    wide[at + base + rr, cols] = jnp.concatenate(pieces, axis=0).T
        for k in range(B):
            start = pl.multiple_of(lax.rem(mine + k, B) * C, PAD)
            outs[which * B + k][...] = wide[at : at + slabs, pl.ds(start, C + 2 * PAD), :]
        at += slabs


def unpack_kernel(z, rows, who, *refs):
    B, mt = z.B, z.mt
    got, outs = refs[:B], refs[B:]
    share = who[0]
    places = [(ref, i) for ref in outs for i in range(ref.shape[0])]
    src = [lax.rem(share - k + B, B) for k in range(B)]
    for k in range(B):
        for t in range(mt):
            lanes = pl.ds(pl.multiple_of(src[k] * z.main + t * LANES, LANES), LANES)
            for i, (ref, at) in enumerate(places):
                ref[at, :, lanes] = got[k][i * mt + t]
    for count, used, deep, base, lane in z.folds(rows)[0]:
        group = lane_group(count)
        for i, (ref, at) in enumerate(places):
            tile = jnp.zeros(ref.shape[1:2] + (LANES,), F32)
            for k in range(B):
                shift = lax.rem((src[k] - i // deep) * count + LANES, LANES)
                moved = pltpu.roll(got[k][base + i % deep], shift, axis=1)
                tile = jnp.where(group == src[k], moved, tile)
            ref[at, :, lane : lane + LANES] = tile


def send_back_kernel(z, rows, who, *refs):
    B, mt = z.B, z.mt
    states, outs = refs[:-B], refs[-B:]
    share = who[0]
    places = [(ref, i) for ref in states for i in range(ref.shape[0])]
    for k in range(B):
        src = lax.rem(share - k + B, B)
        for t in range(mt):
            lanes = pl.ds(pl.multiple_of(src * z.main + t * LANES, LANES), LANES)
            for i, (ref, at) in enumerate(places):
                outs[k][i * mt + t] = ref[at, :, lanes]
        for count, used, deep, base, lane in z.folds(rows)[0]:
            group = lane_group(count)
            for rr in range(deep):
                tile = jnp.zeros((z.C, LANES), F32)
                for i in range(used):
                    ref, at = places[rr + i * deep]
                    shift = lax.rem((i - src) * count + LANES, LANES)
                    moved = pltpu.roll(ref[at, :, lane : lane + LANES], shift, axis=1)
                    tile = jnp.where(group == i, moved, tile)
                outs[k][base + rr] = tile


def restore_kernel(z, who, *refs):
    B, R, C, mt = z.B, z.R, z.C, z.mt
    got, (spec_out, ocean_out, wide, spec, ocean) = refs[: 2 * B], refs[2 * B :]
    mine = who[0]
    at = 0
    for which, rows in enumerate((z.edge_rows, z.inner_rows)):
        folds, slabs = z.folds(rows)
        for k in range(B):
            c = lax.rem(mine + k, B)
            wide[at : at + slabs, pl.ds(pl.multiple_of(c * C, PAD), C), :] = got[which * B + k][...]
        for half in range(z.W // LANES):
            cols = slice(half * LANES, (half + 1) * LANES)
            for i, r in enumerate(rows):
                for t in range(mt):
                    place = pl.ds(t * LANES * R + r, LANES, stride=R)
                    spec[half, place, :] = wide[at + i * mt + t, cols].T
            for (count, used, deep, base, _), dst, first in zip(folds, (spec, ocean), (z.main, 0)):
                for rr in range(deep):
                    turned = wide[at + base + rr, cols].T
                    for i in range(used):
                        place = pl.ds(first * R + rows[rr + i * deep], count, stride=R)
                        dst[half, place, :] = turned[i * count : (i + 1) * count]
        at += slabs
    for half in range(z.W // LANES):
        cols = slice(half * LANES, (half + 1) * LANES)
        spec_out[:, cols] = spec[half]
        ocean_out[:, cols] = ocean[half]


def weights_kernel(z, linear, square, drift, weights, drift_weights):
    B, nb, main, nr, NB, L = z.B, z.nb, z.main, z.nr, z.NB, z.L

    def put(dst, first, lanes, turned):
        for s in range(B):
            dst[first + s * main : first + (s + 1) * main, lanes] = turned[
                s * nb : s * nb + main
            ]
            tail = first + B * main + s * nr
            dst[tail : tail + nr, lanes] = turned[s * nb + main : (s + 1) * nb]

    for n, source in enumerate((linear, square)):
        for s in range(B):
            for t in range(z.mt):
                block = source[s * nb + t * LANES : s * nb + (t + 1) * LANES, :]
                lane = s * main + t * LANES
                put(weights, n * NB, slice(lane, lane + LANES), block.T)
        tails = [source[s * nb + main : (s + 1) * nb, :] for s in range(B)]
        block = jnp.concatenate(tails, axis=0)
        put(weights, n * NB, slice(B * main, NB), block.T)

    row = lax.broadcasted_iota(jnp.int32, (LANES, LANES), 0)
    lane = lax.broadcasted_iota(jnp.int32, (LANES, LANES), 1)
    part, comp, level = lane // (2 * L), (lane // L) % 2, lane % L
    pick = jnp.where(row == 2 * (part * L + level) + 1 - comp, 1.0, 0.0).astype(BF16)
    turned = jnp.dot(drift[...].T, pick, preferred_element_type=F32).astype(BF16)
    put(drift_weights, 0, slice(0, LANES), turned)


def advance(z, groups, outs, cut, sea_at, sea, speed, weights, drift_weights, moved, moved_twice):
    NB, CH, L = z.NB, z.CH, z.L
    E = groups[0][1][0][0].shape[1]
    N = E - 2 * cut
    keep = slice(cut, cut + N)
    sea_cols = pl.ds(sea_at, E)
    places = [(ref, i) for ref in outs for i in range(ref.shape[0])]

    def sea_row(r):
        return sea[r, sea_cols]

    for g, (sea_first, rows) in enumerate(groups):
        n = len(rows)
        tops = [ref[i, :, NB:CH] for ref, i in rows]
        for r in range(n):
            moved[g, 0, r] = DOPPLER * jnp.tanh(jnp.broadcast_to(tops[r][:, 0:1], (E, LANES)))
            moved[g, 1, r] = DOPPLER * jnp.tanh(jnp.broadcast_to(tops[r][:, L : L + 1], (E, LANES)))

    def advect(g, sea_first, read, write, first, last, speed_cx, speed_cy):
        def along_x(r):
            energy = read(r)
            speed_x = speed_cx + moved[g, 0, r]
            return (
                energy,
                jnp.maximum(speed_x, 0.0) * energy,
                jnp.minimum(speed_x, 0.0) * energy,
            )

        _, plus_before, _ = along_x(first - 1)
        energy, plus, minus = along_x(first)
        for r in range(first, last):
            energy_next, plus_next, minus_next = along_x(r + 1)
            speed_y = speed_cy + moved[g, 1, r]
            plus_y = jnp.maximum(speed_y, 0.0) * energy
            minus_y = jnp.minimum(speed_y, 0.0) * energy
            result = (
                energy
                - ((plus - plus_before) + (minus_next - minus))
                - (
                    (plus_y - pltpu.roll(plus_y, 1, axis=0))
                    + (pltpu.roll(minus_y, E - 1, axis=0) - minus_y)
                )
            )
            write(r, result * sea_row(sea_first + r))
            plus_before, energy, plus, minus = plus, energy_next, plus_next, minus_next

    def one_tile(j, carry):
        lanes = pl.ds(pl.multiple_of(j * LANES, LANES), LANES)
        speed_cx = speed[0:1, lanes]
        speed_cy = speed[1:2, lanes]
        done = 0
        for g, (sea_first, rows) in enumerate(groups):
            n = len(rows)

            def read_state(r):
                ref, i = rows[r]
                return ref[i, :, lanes]

            def write_first(r, value):
                moved[g, 2, r] = value

            def write_second(r, value):
                moved_twice[done + r - 2, :, lanes] = value[keep]

            advect(g, sea_first, read_state, write_first, 1, n - 1, speed_cx, speed_cy)
            advect(
                g, sea_first, lambda r: moved[g, 2, r], write_second, 2, n - 2, speed_cx, speed_cy
            )
            done += n - 4
        return carry

    lax.fori_loop(0, NB // LANES, one_tile, 0)

    count = len(places)
    sea_rows = [f + r for f, rows in groups for r in range(2, len(rows) - 2)]
    energy = moved_twice[...].reshape(count * N, NB)
    squares = energy * energy
    interaction = jnp.dot(
        energy.astype(BF16), weights[:NB], preferred_element_type=F32
    ) + jnp.dot(squares.astype(BF16), weights[NB:], preferred_element_type=F32)
    total = jnp.sum(squares, axis=1, keepdims=True)
    sea_here = jnp.concatenate([sea_row(r)[keep] for r in sea_rows], axis=0)
    scale = (DT_SOURCE * sea_here[:, 0:1]) / (1.0 + total / NB)
    fresh = energy + scale * (interaction * energy)
    for i, (ref, at) in enumerate(places):
        ref[at, :, 0:NB] = fresh[i * N : (i + 1) * N]
    drift = jnp.dot(fresh.astype(BF16), drift_weights[...], preferred_element_type=F32)

    comp = (lax.broadcasted_iota(jnp.int32, (1, LANES), 1) // L) % 2
    sign = jnp.where(comp == 0, 1.0, -1.0).astype(F32)
    i = 0
    for sea_first, rows in groups:
        for r in range(2, len(rows) - 2):
            here, before, after = [
                rows[r + d][0][rows[r + d][1], :, NB:CH] for d in (0, -1, 1)
            ]
            lap = (
                (after + before)
                + (pltpu.roll(here, E - 1, axis=0) + pltpu.roll(here, 1, axis=0))
                - 4.0 * here
            )[keep]
            centre = here[keep]
            other = jnp.where(
                comp == 0, pltpu.roll(centre, LANES - L, axis=1), pltpu.roll(centre, L, axis=1)
            )
            turn = sign * (CORIOLIS * (other + drift[i * N : (i + 1) * N]))
            ref, at = places[i]
            ref[at, :, NB:CH] = (
                centre + DT_OCEAN * (turn + VISCOSITY * lap)
            ) * sea_row(sea_first + r)[keep]
            i += 1


def listed(*refs):
    return [(ref, i) for ref in refs for i in range(ref.shape[0])]


def inner_kernel(z, cut, sea_at, top, inner, bottom, sea, *refs):
    (speed, weights, drift_weights, out, moved, moved_twice) = refs
    groups = [(EDGE, listed(top, inner, bottom))]
    advance(
        z, groups, [out], cut, sea_at, sea, speed, weights, drift_weights, moved, moved_twice
    )


def edge_kernel(z, cut, sea_at, up, top, inner, bottom, down, sea, *refs):
    (speed, weights, drift_weights, new_top, new_bottom, moved, moved_twice) = refs
    inside = listed(inner)
    groups = [
        (0, listed(up, top) + inside[:EDGE]),
        (z.R - EDGE, inside[-EDGE:] + listed(bottom, down)),
    ]
    outs = [new_top, new_bottom]
    advance(
        z, groups, outs, cut, sea_at, sea, speed, weights, drift_weights, moved, moved_twice
    )


def speeds(z):
    lane = jnp.arange(z.NB, dtype=jnp.int32)
    head = (lane // z.main) * z.nb + lane % z.main
    rest = lane - z.B * z.main
    tail = (rest // z.nr) * z.nb + z.main + rest % z.nr
    bin_index = jnp.where(lane < z.B * z.main, head, tail)
    direction = (bin_index // NFREQ).astype(F32)
    frequency = (bin_index % NFREQ).astype(F32)
    group_speed = 0.4 / (1.0 + frequency / 16.0)
    bin_angle = (2.0 * jnp.pi / NDIR) * direction
    zeros = jnp.zeros_like(bin_angle)
    rows = [group_speed * jnp.cos(bin_angle), group_speed * jnp.sin(bin_angle)] + [zeros] * 6
    return jnp.stack(rows)


def cost(flops, moved):
    return pl.CostEstimate(flops=int(flops), bytes_accessed=int(moved), transcendentals=0)


def per_device(G, B, spectrum, sea_mask, kernel_linear, kernel_square, drift_kernel, ocean):
    nb, R, W = spectrum.shape
    L = ocean.shape[1]
    z = Sizes(B, nb, L, R, W)
    C, NB, CH = z.C, z.NB, z.CH
    half = B // 2
    axes = ("geo", "bins")
    geo, part = lax.axis_index("geo"), lax.axis_index("bins")

    def device_at(q, c):
        m, along = c // half, c % half
        along = along if m == 0 else half - 1 - along
        return ((q // 2) * 2 + m) * B + 2 * along + q % 2

    along, odd = part // 2, geo % 2
    tile = geo - odd + part % 2
    share = along + (half + half - 1 - 2 * along) * odd
    forward = [
        [(g * B + b, device_at(g, (b + k) % B)) for g in range(G) for b in range(B)]
        for k in range(B)
    ]
    pairs = [(q, c) for q in range(G) for c in range(B)]
    to_next_row = [(device_at(q, c), device_at((q + 1) % G, c)) for q, c in pairs]
    to_prev_row = [(t, s) for s, t in to_next_row]
    part_id = part.astype(jnp.int32).reshape(1)
    share_id = share.astype(jnp.int32).reshape(1)

    def blocks(width):
        return [
            jax.ShapeDtypeStruct((z.slabs(rows), width, LANES), F32)
            for rows in (z.edge_rows, z.inner_rows)
            for _ in range(B)
        ]

    all_slabs = z.slabs(z.edge_rows) + z.slabs(z.inner_rows)
    columns_scratch = [
        pltpu.VMEM((W // LANES, nb * R, LANES), F32),
        pltpu.VMEM((W // LANES, 2 * L * R, LANES), F32),
    ]
    packed = pl.pallas_call(
        functools.partial(pack_kernel, z),
        out_shape=blocks(C + 2 * PAD),
        in_specs=[SMEM, VMEM, VMEM],
        out_specs=[VMEM] * (2 * B),
        scratch_shapes=columns_scratch + [pltpu.VMEM((all_slabs, W + 2 * PAD, LANES), F32)],
        compiler_params=params(24),
        name="pack",
    )(part_id, spectrum.reshape(nb * R, W), ocean.reshape(2 * L * R, W))
    got = [lax.ppermute(packed[i], axes, forward[i % B]) for i in range(2 * B)]

    def mask_of(offset, block):
        perm = [
            (((q + offset) % G) * B + c, device_at(q, c)) for q in range(G) for c in range(B)
        ]
        return lax.ppermute(block, axes, perm)

    mask = jnp.concatenate(
        [mask_of(-1, sea_mask[R - EDGE :]), mask_of(0, sea_mask), mask_of(1, sea_mask[:EDGE])],
        axis=0,
    )
    mask = jnp.pad(mask, ((0, 0), (PAD, PAD)))
    mask = lax.dynamic_slice_in_dim(mask, share * C, C + 2 * PAD, axis=1)
    sea = jnp.broadcast_to(mask.astype(F32)[..., None], mask.shape + (LANES,))

    weights, drift_weights = pl.pallas_call(
        functools.partial(weights_kernel, z),
        out_shape=(
            jax.ShapeDtypeStruct((2 * NB, NB), BF16),
            jax.ShapeDtypeStruct((NB, LANES), BF16),
        ),
        in_specs=[VMEM] * 3,
        out_specs=(VMEM,) * 2,
        compiler_params=params(24),
        cost_estimate=cost(2e9, 4 * NB * NB * 2),
        name="weights",
    )(kernel_linear, kernel_square, drift_kernel)
    speed = speeds(z)

    def unpack(rows, received, counts):
        return pl.pallas_call(
            functools.partial(unpack_kernel, z, rows),
            out_shape=[jax.ShapeDtypeStruct((n, C + 2 * PAD, CH), F32) for n in counts],
            in_specs=[SMEM] + [VMEM] * B,
            out_specs=[VMEM] * len(counts),
            compiler_params=params(16),
            name="unpack",
        )(share_id, *received)

    top, bottom = unpack(z.edge_rows, got[:B], (EDGE, EDGE))
    (inner,) = unpack(z.inner_rows, got[B:], (R - 2 * EDGE,))

    def step_call(body, width, cut, sea_at, counts, groups, deepest, inputs):
        n = width - 2 * cut
        return pl.pallas_call(
            functools.partial(body, z, cut, sea_at),
            out_shape=[jax.ShapeDtypeStruct((k, n, CH), F32) for k in counts],
            in_specs=[VMEM] * (len(inputs) + 4),
            out_specs=[VMEM] * len(counts),
            scratch_shapes=[
                pltpu.VMEM((groups, 3, deepest, width, LANES), F32),
                pltpu.VMEM((sum(counts), n, NB), F32),
            ],
            compiler_params=params(32),
            cost_estimate=cost(6e9, 8e6),
            name=body.__name__,
        )(*inputs, sea, speed, weights, drift_weights)

    width = C + 2 * PAD
    for step in range(STEPS):
        valid = EDGE * (STEPS - 1 - step)
        margin = (width - C) // 2
        cut = margin - valid if valid == 0 or (margin - valid) % 4 == 0 else 0
        sea_at = PAD - margin
        up = lax.ppermute(bottom, axes, to_next_row)
        down = lax.ppermute(top, axes, to_prev_row)
        (new_inner,) = step_call(
            inner_kernel, width, cut, sea_at, (R - 2 * EDGE,), 1, R, (top, inner, bottom)
        )
        top, bottom = step_call(
            edge_kernel, width, cut, sea_at, (EDGE, EDGE), 2, 3 * EDGE,
            (up, top, inner, bottom, down),
        )
        inner = new_inner
        width -= 2 * cut

    def send_back(rows, states):
        shape = jax.ShapeDtypeStruct((z.slabs(rows), C, LANES), F32)
        return pl.pallas_call(
            functools.partial(send_back_kernel, z, rows),
            out_shape=[shape] * B,
            in_specs=[SMEM] + [VMEM] * len(states),
            out_specs=[VMEM] * B,
            compiler_params=params(16),
            name="send_back",
        )(share_id, *states)

    packed = send_back(z.inner_rows, [inner]), send_back(z.edge_rows, [top, bottom])
    packed = list(packed[1]) + list(packed[0])
    back = [
        lax.ppermute(packed[i], axes, [(t, s) for s, t in forward[i % B]]) for i in range(2 * B)
    ]
    spectrum_out, ocean_out = pl.pallas_call(
        functools.partial(restore_kernel, z),
        out_shape=(
            jax.ShapeDtypeStruct((nb * R, W), F32),
            jax.ShapeDtypeStruct((2 * L * R, W), F32),
        ),
        in_specs=[SMEM] + [VMEM] * (2 * B),
        out_specs=(VMEM,) * 2,
        scratch_shapes=[pltpu.VMEM((all_slabs, W, LANES), F32)] + columns_scratch,
        compiler_params=params(24),
        name="restore",
    )(part_id, *back)
    return spectrum_out.reshape(nb, R, W), ocean_out.reshape(2, L, R, W)


def solution(mesh):
    return jax.shard_map(
        functools.partial(per_device, mesh.shape["geo"], mesh.shape["bins"]),
        mesh=mesh,
        in_specs=(
            P("bins", "geo", None),
            P("geo", None),
            P(),
            P(),
            P(),
            P(None, "bins", "geo", None),
        ),
        out_specs=(P("bins", "geo", None), P(None, "bins", "geo", None)),
        check_vma=False,
    )
```

time: 571 us -> 152 us (0.27); the launches traced: 561 us -> 151 us
  other arithmetic: 126 us -> 0.37 us
  blocking collectives: 117 us -> 0 us
  waiting for transfers between devices: 144 us -> 34.8 us
  local copies, waits for them, and re-layouts: 96.8 us -> 8.9 us
  Pallas kernels: 0 us -> 46.7 us
  matrix products: 23.7 us -> 0 us
  starting transfers between devices: 51.4 us -> 58.9 us
    mul x22 -> x1, other arithmetic: 109 us -> 0.2 us  [speeds(): group_speed * jnp.sin(bin_angle)]
    all_to_all x2 -> x0, blocking collectives: 64 us -> none  [per_device(): lax.all_to_all(energy_flat, 'bins', split_axis=1, concat_axis=0, tiled=True)]
    ppermute x12 -> x25, waiting for transfers between devices: 89.5 us -> 34.8 us  [the longest x8 15.4 us: per_device(): got = [lax.ppermute(packed[i], axes, forward[i % B]) for i in range(2 * B)]]
    all_to_all x7 -> x0, waiting for transfers between devices: 54.1 us -> none  [the longest x1 28.5 us: per_device(): lax.all_to_all(energy_flat, 'bins', split_axis=1, concat_axis=0, tiled=True)]
    psum x3 -> x0, blocking collectives: 53.4 us -> none  [spread(): return lax.psum(block, axis)]
    pallas_call x0 -> x13, Pallas kernels: none -> 46.7 us  [the longest x6 37.8 us: step_call(): pl.pallas_call(functools.partial(body, z, cut, sea_at), out_shape=[jax.Sh...]
    all_to_all x15 -> x0, local copies, waits for them, and re-layouts: 45.5 us -> none  [the longest x9 28.9 us: per_device(): lax.all_to_all(energy_flat, 'bins', split_axis=1, concat_axis=0, tiled=True)]
    ppermute x12 -> x25, starting transfers between devices: 22.8 us -> 58.9 us  [the longest x8 20.7 us: per_device(): got = [lax.ppermute(packed[i], axes, forward[i % B]) for i in range(2 * B)]]
  transfers between devices with their start and end apart: 19 -> 25, of which waited for: 17 -> 6; matrix products, arithmetic and copies ran while one was open for 4% -> 0% of each run, Pallas kernels for 0% -> 18%
where the time goes in v2:
time: 152 us; the launch traced here: 151 us
  starting transfers between devices  58.9 us (39%)
  Pallas kernels  46.7 us (31%)
  waiting for transfers between devices  34.8 us (23%)
  local copies, waits for them, and re-layouts  8.9 us (6%)
    pallas_call x6, Pallas kernels, step_call(): pl.pallas_call(functools.partial(body, z, cut, sea_at), out_shape=[jax.Sh...  37.8 us
    ppermute x8, starting transfers between devices, per_device(): got = [lax.ppermute(packed[i], axes, forward[i % B]) for i in range(2 * B)]  20.7 us
    ppermute x8, starting transfers between devices, per_device(): lax.ppermute(packed[i], axes, [(t, s) for s, t in forward[i % B]])  19.5 us
    ppermute x8, waiting for transfers between devices, per_device(): got = [lax.ppermute(packed[i], axes, forward[i % B]) for i in range(2 * B)]  15.4 us
    ppermute x8, waiting for transfers between devices, per_device(): lax.ppermute(packed[i], axes, [(t, s) for s, t in forward[i % B]])  10.8 us
    ppermute x3, starting transfers between devices, per_device(): down = lax.ppermute(top, axes, to_prev_row)  9 us
    ppermute x3, waiting for transfers between devices, per_device(): up = lax.ppermute(bottom, axes, to_next_row)  8.59 us
    unnamed x16, local copies, waits for them, and re-layouts  8.56 us
  transfers between devices with their start and end apart: 25, of which 6 were waited for; matrix products, arithmetic and copies ran while one was open for 0% of the time, Pallas kernels for 18%

profile of v2, /device:TPU:0, one launch (start us, length us, event | category | flops | bytes accessed | tf_op | source)
XLA Modules:
  0.0 150.8 jit_solution(17071826803590807917)
XLA Ops:
  0.7 1.7 %copy-done = f32[288,8,256]{2,1,0:T(8,128)S(1)} copy-done((f32[288,8,256]{2,1,0:T(8,128)S(1)}, f32[288,8,256]{2,1,0:T(8,128)}, u32[]{:S(2)}) %copy-start) | copy-done | bytes 2359320
  3.3 2.1 %pack.1 = (f32[10,80,128]{2,1,0:T(8,128)}, f32[10,80,128]{2,1,0:T(8,128)S(1)}, f32[10,80,128]{2,1,0:T(8,128)S(1)}, f32[10,80,128]{2,1,0:T(8,128)S(1)}, f32[10,80...) custom-call(s32[1]{0:T(128)} %bitcast.who, ...), custom_call_target="tpu_custom_call" | custom-call | tf_op jit(solution)/shard_map/pack/pallas_call | solution.py:397
  6.8 1.6 %collective-permute-start = (f32[10,80,128]{2,1,0:T(8,128)}, f32[10,80,128]{2,1,0:T(8,128)S(1)}, u32[]{:S(2)}, u32[]{:S(2)}) collective-permute-start(f32[10,80,128]{2,1,0:T(8,128)} %get-tuple-element.30), channel_id=1, source_target_pairs={{0,0},{1,2},{2,6},{3,4},{4,1},{5,3},{6,7},{7,5},{8,8},{9,10},{10,1... | collective-permute-start | bytes 1228808 | tf_op jit(solution)/shard_map/ppermute | solution.py:406
  8.5 4.8 %collective-permute-start.1 = (f32[10,80,128]{2,1,0:T(8,128)S(1)}, f32[10,80,128]{2,1,0:T(8,128)S(1)}, u32[]{:S(2)}, u32[]{:S(2)}) collective-permute-start(f32[10,80,128]{2,1,0:T(8,128)S(1)} %get-tuple-element.31), channel_id=1, source_target_pairs={{0,2},{1,6},{2,4},{3,0},{4,3},{5,7},{6,5},{7,1},{8,10},{9,14},{10,... | collective-permute-start | bytes 1228808 | tf_op jit(solution)/shard_map/ppermute | solution.py:406
  13.3 2.5 %collective-permute-start.2 = (f32[10,80,128]{2,1,0:T(8,128)S(1)}, f32[10,80,128]{2,1,0:T(8,128)S(1)}, u32[]{:S(2)}, u32[]{:S(2)}) collective-permute-start(f32[10,80,128]{2,1,0:T(8,128)S(1)} %get-tuple-element.32), channel_id=1, source_target_pairs={{0,6},{1,4},{2,0},{3,2},{4,7},{5,5},{6,1},{7,3},{8,14},{9,12},{10,... | collective-permute-start | bytes 1228808 | tf_op jit(solution)/shard_map/ppermute | solution.py:406
  15.8 2.7 %collective-permute-start.3 = (f32[10,80,128]{2,1,0:T(8,128)S(1)}, f32[10,80,128]{2,1,0:T(8,128)S(1)}, u32[]{:S(2)}, u32[]{:S(2)}) collective-permute-start(f32[10,80,128]{2,1,0:T(8,128)S(1)} %get-tuple-element.33), channel_id=1, source_target_pairs={{0,4},{1,0},{2,2},{3,6},{4,5},{5,1},{6,3},{7,7},{8,12},{9,8},{10,1... | collective-permute-start | bytes 1228808 | tf_op jit(solution)/shard_map/ppermute | solution.py:406
  19.7 10.7 %collective-permute-done.1.refs_1_ = f32[10,80,128]{2,1,0:T(8,128)S(1)} collective-permute-done((f32[10,80,128]{2,1,0:T(8,128)S(1)}, f32[10,80,128]{2,1,0:T(8,128)S(1)}, u32[]{:S(2)}, u32[]{:S(2)}) %collective-permute-start.1) | collective-permute-done | bytes 409632 | tf_op jit(solution)/shard_map/ppermute | solution.py:406
  30.3 7.2 %collective-permute-start.12 = (s32[2,256]{1,0:T(2,128)S(1)}, s32[2,256]{1,0:T(2,128)S(1)}, u32[]{:S(2)}, u32[]{:S(2)}) collective-permute-start(s32[2,256]{1,0:T(2,128)S(1)} %get-tuple-element.59), channel_id=1, source_target_pairs={{4,0},{5,2},{6,6},{7,4},{8,1},{9,3},{10,7},{11,5},{12,8},{13,10},{... | collective-permute-start | bytes 6152 | tf_op jit(solution)/shard_map/ppermute | solution.py:412
  37.5 1.7 %collective-permute-start.5 = (f32[10,80,128]{2,1,0:T(8,128)}, f32[10,80,128]{2,1,0:T(8,128)S(1)}, u32[]{:S(2)}, u32[]{:S(2)}) collective-permute-start(f32[10,80,128]{2,1,0:T(8,128)} %get-tuple-element.36), channel_id=1, source_target_pairs={{0,0},{1,2},{2,6},{3,4},{4,1},{5,3},{6,7},{7,5},{8,8},{9,10},{10,1... | collective-permute-start | bytes 1228808 | tf_op jit(solution)/shard_map/ppermute | solution.py:406
  40.5 3.5 %collective-permute-start.9 = (f32[2,80,1280]{2,1,0:T(8,128)S(1)}, f32[2,80,1280]{2,1,0:T(8,128)}, u32[]{:S(2)}, u32[]{:S(2)}) collective-permute-start(f32[2,80,1280]{2,1,0:T(8,128)S(1)} %get-tuple-element.35.top), channel_id=1, source_target_pairs={{1,0},{3,2},{7,6},{5,4},{8,1},{10,3},{14,7},{12,5},{9,8},{11,10},{... | collective-permute-start | bytes 2457608 | tf_op jit(solution)/shard_map/ppermute | solution.py:472
  44.2 1.9 %collective-permute-start.7 = (f32[10,80,128]{2,1,0:T(8,128)}, f32[10,80,128]{2,1,0:T(8,128)S(1)}, u32[]{:S(2)}, u32[]{:S(2)}) collective-permute-start(f32[10,80,128]{2,1,0:T(8,128)} %copy-done.4), channel_id=1, source_target_pairs={{0,6},{1,4},{2,0},{3,2},{4,7},{5,5},{6,1},{7,3},{8,14},{9,12},{10,... | collective-permute-start | bytes 1228808 | tf_op jit(solution)/shard_map/ppermute | solution.py:406
  46.1 5.4 %collective-permute-start.8 = (f32[10,80,128]{2,1,0:T(8,128)S(1)}, f32[10,80,128]{2,1,0:T(8,128)S(1)}, u32[]{:S(2)}, u32[]{:S(2)}) collective-permute-start(f32[10,80,128]{2,1,0:T(8,128)S(1)} %get-tuple-element.39), channel_id=1, source_target_pairs={{0,4},{1,0},{2,2},{3,6},{4,5},{5,1},{6,3},{7,7},{8,12},{9,8},{10,1... | collective-permute-start | bytes 1228808 | tf_op jit(solution)/shard_map/ppermute | solution.py:406
  51.6 1.7 %copy-done.2 = bf16[1152,1152]{1,0:T(8,128)(2,1)S(1)} copy-done((bf16[1152,1152]{1,0:T(8,128)(2,1)S(1)}, bf16[1152,1152]{1,0:T(8,128)(2,1)}, u32[]{:S(2)}) %copy-start.2) | copy-done | bytes 2654232
  53.3 1.7 %copy-done.3 = bf16[1152,1152]{1,0:T(8,128)(2,1)S(1)} copy-done((bf16[1152,1152]{1,0:T(8,128)(2,1)S(1)}, bf16[1152,1152]{1,0:T(8,128)(2,1)}, u32[]{:S(2)}) %copy-start.3) | copy-done | bytes 2654232
  57.7 3.7 %collective-permute-done.6.refs_1_ = f32[10,80,128]{2,1,0:T(8,128)S(1)} collective-permute-done((f32[10,80,128]{2,1,0:T(8,128)}, f32[10,80,128]{2,1,0:T(8,128)S(1)}, u32[]{:S(2)}, u32[]{:S(2)}) %collective-permute-start.6) | collective-permute-done | bytes 409632 | tf_op jit(solution)/shard_map/ppermute | solution.py:406
  63.0 8.1 %edge_kernel.3 = (f32[2,72,1280]{2,1,0:T(8,128)S(1)}, f32[2,72,1280]{2,1,0:T(8,128)S(1)}) custom-call(f32[2,80,1280]{2,1,0:T(8,128)S(1)} %collective-permute-done.4.up, f32[2,80,1280]{2,1,0:T(8,128)S(1)} %get-tuple-element.35.top, f32[4,80,1280]{2,1,0:T(8,128)S(1)} %unpack.3.inner, f32[2,80,1280]{2,1,0:T(8,128)} %get-tuple-element.34.bottom, ...), custom_call_target="tpu_custom_call" | custom-call | flops 6000000000 | bytes 8000000 | tf_op jit(solution)/shard_map/edge_kernel/pallas_call | solution.py:451
  72.1 2.7 %collective-permute-start.14 = (f32[2,72,1280]{2,1,0:T(8,128)S(1)}, f32[2,72,1280]{2,1,0:T(8,128)S(1)}, u32[]{:S(2)}, u32[]{:S(2)}) collective-permute-start(f32[2,72,1280]{2,1,0:T(8,128)S(1)} %get-tuple-element.43.top), channel_id=1, source_target_pairs={{1,0},{3,2},{7,6},{5,4},{8,1},{10,3},{14,7},{12,5},{9,8},{11,10},{... | collective-permute-start | bytes 2211848 | tf_op jit(solution)/shard_map/ppermute | solution.py:472
  74.8 7.0 %inner_kernel.3.inner = f32[4,72,1280]{2,1,0:T(8,128)S(1)} custom-call(f32[2,80,1280]{2,1,0:T(8,128)S(1)} %get-tuple-element.35.top, f32[4,80,1280]{2,1,0:T(8,128)S(1)} %unpack.3.inner, f32[2,80,1280]{2,1,0:T(8,128)} %get-tuple-element.34.bottom, f32[12,80,128]{2,1,0:T(8,128)S(1)} %broadcast_in_dim.2.sea, f32[8,1152]{1,0:T(8,128)S(1)} %maximum_maximum_fusion.refs_0_, ...), custom_call_target="tpu_custom_call" | custom-call | flops 6000000000 | bytes 8000000 | tf_op jit(solution)/shard_map/inner_kernel/pallas_call | solution.py:451
  81.8 8.6 %collective-permute-done.13.up = f32[2,72,1280]{2,1,0:T(8,128)S(1)} collective-permute-done((f32[2,72,1280]{2,1,0:T(8,128)S(1)}, f32[2,72,1280]{2,1,0:T(8,128)S(1)}, u32[]{:S(2)}, u32[]{:S(2)}) %collective-permute-start.13) | collective-permute-done | bytes 737312 | tf_op jit(solution)/shard_map/ppermute | solution.py:471
  90.4 6.2 %edge_kernel.4 = (f32[2,72,1280]{2,1,0:T(8,128)S(1)}, f32[2,72,1280]{2,1,0:T(8,128)S(1)}) custom-call(f32[2,72,1280]{2,1,0:T(8,128)S(1)} %collective-permute-done.13.up, f32[2,72,1280]{2,1,0:T(8,128)S(1)} %get-tuple-element.43.top, f32[4,72,1280]{2,1,0:T(8,128)S(1)} %inner_kernel.3.inner, f32[2,72,1280]{2,1,0:T(8,128)S(1)} %get-tuple-element.42.bottom, ...), custom_call_target="tpu_custom_call" | custom-call | flops 6000000000 | bytes 8000000 | tf_op jit(solution)/shard_map/edge_kernel/pallas_call | solution.py:451
  97.4 2.8 %collective-permute-start.16 = (f32[2,72,1280]{2,1,0:T(8,128)S(1)}, f32[2,72,1280]{2,1,0:T(8,128)S(1)}, u32[]{:S(2)}, u32[]{:S(2)}) collective-permute-start(f32[2,72,1280]{2,1,0:T(8,128)S(1)} %get-tuple-element.45.top), channel_id=1, source_target_pairs={{1,0},{3,2},{7,6},{5,4},{8,1},{10,3},{14,7},{12,5},{9,8},{11,10},{... | collective-permute-start | bytes 2211848 | tf_op jit(solution)/shard_map/ppermute | solution.py:472
  100.2 5.4 %inner_kernel.4.inner = f32[4,72,1280]{2,1,0:T(8,128)S(1)} custom-call(f32[2,72,1280]{2,1,0:T(8,128)S(1)} %get-tuple-element.43.top, f32[4,72,1280]{2,1,0:T(8,128)S(1)} %inner_kernel.3.inner, f32[2,72,1280]{2,1,0:T(8,128)S(1)} %get-tuple-element.42.bottom, f32[12,80,128]{2,1,0:T(8,128)S(1)} %broadcast_in_dim.2.sea, ...), custom_call_target="tpu_custom_call" | custom-call | flops 6000000000 | bytes 8000000 | tf_op jit(solution)/shard_map/inner_kernel/pallas_call | solution.py:451
  105.6 5.2 %inner_kernel.5.refs_0_ = f32[4,64,1280]{2,1,0:T(8,128)S(1)} custom-call(f32[2,72,1280]{2,1,0:T(8,128)S(1)} %get-tuple-element.45.top, f32[4,72,1280]{2,1,0:T(8,128)S(1)} %inner_kernel.4.inner, f32[2,72,1280]{2,1,0:T(8,128)S(1)} %get-tuple-element.44.bottom, f32[12,80,128]{2,1,0:T(8,128)S(1)} %broadcast_in_dim.2.sea, ...), custom_call_target="tpu_custom_call" | custom-call | flops 6000000000 | bytes 8000000 | tf_op jit(solution)/shard_map/inner_kernel/pallas_call | solution.py:451
  111.9 2.1 %collective-permute-start.22 = (f32[10,64,128]{2,1,0:T(8,128)S(1)}, f32[10,64,128]{2,1,0:T(8,128)S(1)}, u32[]{:S(2)}, u32[]{:S(2)}) collective-permute-start(f32[10,64,128]{2,1,0:T(8,128)S(1)} %get-tuple-element.53), channel_id=1, source_target_pairs={{2,0},{6,1},{4,2},{0,3},{3,4},{7,5},{5,6},{1,7},{10,8},{14,9},{12,... | collective-permute-start | bytes 983048 | tf_op jit(solution)/shard_map/ppermute | solution.py:497
  113.9 3.6 %collective-permute-start.23 = (f32[10,64,128]{2,1,0:T(8,128)S(1)}, f32[10,64,128]{2,1,0:T(8,128)S(1)}, u32[]{:S(2)}, u32[]{:S(2)}) collective-permute-start(f32[10,64,128]{2,1,0:T(8,128)S(1)} %get-tuple-element.54), channel_id=1, source_target_pairs={{6,0},{4,1},{0,2},{2,3},{7,4},{5,5},{1,6},{3,7},{14,8},{12,9},{8,1... | collective-permute-start | bytes 983048 | tf_op jit(solution)/shard_map/ppermute | solution.py:497
  117.6 4.8 %collective-permute-start.24 = (f32[10,64,128]{2,1,0:T(8,128)S(1)}, f32[10,64,128]{2,1,0:T(8,128)S(1)}, u32[]{:S(2)}, u32[]{:S(2)}) collective-permute-start(f32[10,64,128]{2,1,0:T(8,128)S(1)} %get-tuple-element.55), channel_id=1, source_target_pairs={{4,0},{0,1},{2,2},{6,3},{5,4},{1,5},{3,6},{7,7},{12,8},{8,9},{10,1... | collective-permute-start | bytes 983048 | tf_op jit(solution)/shard_map/ppermute | solution.py:497
  122.4 5.9 %edge_kernel.5 = (f32[2,64,1280]{2,1,0:T(8,128)S(1)}, f32[2,64,1280]{2,1,0:T(8,128)S(1)}) custom-call(f32[2,72,1280]{2,1,0:T(8,128)S(1)} %collective-permute-done.15.up, f32[2,72,1280]{2,1,0:T(8,128)S(1)} %get-tuple-element.45.top, f32[4,72,1280]{2,1,0:T(8,128)S(1)} %inner_kernel.4.inner, f32[2,72,1280]{2,1,0:T(8,128)S(1)} %get-tuple-element.44.bottom, ...), custom_call_target="tpu_custom_call" | custom-call | flops 6000000000 | bytes 8000000 | tf_op jit(solution)/shard_map/edge_kernel/pallas_call | solution.py:451
  129.4 1.6 %collective-permute-start.18 = (f32[10,64,128]{2,1,0:T(8,128)S(1)}, f32[10,64,128]{2,1,0:T(8,128)S(1)}, u32[]{:S(2)}, u32[]{:S(2)}) collective-permute-start(f32[10,64,128]{2,1,0:T(8,128)S(1)} %get-tuple-element.49), channel_id=1, source_target_pairs={{2,0},{6,1},{4,2},{0,3},{3,4},{7,5},{5,6},{1,7},{10,8},{14,9},{12,... | collective-permute-start | bytes 983048 | tf_op jit(solution)/shard_map/ppermute | solution.py:497
  131.1 3.1 %collective-permute-start.19 = (f32[10,64,128]{2,1,0:T(8,128)S(1)}, f32[10,64,128]{2,1,0:T(8,128)S(1)}, u32[]{:S(2)}, u32[]{:S(2)}) collective-permute-start(f32[10,64,128]{2,1,0:T(8,128)S(1)} %get-tuple-element.50), channel_id=1, source_target_pairs={{6,0},{4,1},{0,2},{2,3},{7,4},{5,5},{1,6},{3,7},{14,8},{12,9},{8,1... | collective-permute-start | bytes 983048 | tf_op jit(solution)/shard_map/ppermute | solution.py:497
  134.3 2.9 %collective-permute-start.20 = (f32[10,64,128]{2,1,0:T(8,128)S(1)}, f32[10,64,128]{2,1,0:T(8,128)S(1)}, u32[]{:S(2)}, u32[]{:S(2)}) collective-permute-start(f32[10,64,128]{2,1,0:T(8,128)S(1)} %get-tuple-element.51), channel_id=1, source_target_pairs={{4,0},{0,1},{2,2},{6,3},{5,4},{1,5},{3,6},{7,7},{12,8},{8,9},{10,1... | collective-permute-start | bytes 983048 | tf_op jit(solution)/shard_map/ppermute | solution.py:497
  137.2 10.6 %collective-permute-done.18.refs_1_ = f32[10,64,128]{2,1,0:T(8,128)S(1)} collective-permute-done((f32[10,64,128]{2,1,0:T(8,128)S(1)}, f32[10,64,128]{2,1,0:T(8,128)S(1)}, u32[]{:S(2)}, u32[]{:S(2)}) %collective-permute-start.18) | collective-permute-done | bytes 327712 | tf_op jit(solution)/shard_map/ppermute | solution.py:497
  147.9 2.9 %restore.1 = (f32[2304,256]{1,0:T(8,128)}, f32[256,256]{1,0:T(8,128)}) custom-call(s32[1]{0:T(128)} %bitcast.who, f32[10,64,128]{2,1,0:T(8,128)S(1)} %collective-permute-done.17.refs_0_, f32[10,64,128]{2,1,0:T(8,128)S(1)} %collective-permute-done.18.refs_1_, f32[10,64,128]{2,1,0:T(8,128)S(1)} %collective-permute-done.19.refs_2_, ...), custom_call_target="tpu_custom_call" | custom-call | tf_op jit(solution)/shard_map/restore/pallas_call | solution.py:499
  (57 shorter events, 13.3 us)
Async XLA Ops:
  0.6 17.9 %copy-start.7 = (s32[8,256]{1,0:T(8,128)S(1)}, s32[8,256]{1,0:T(8,128)}, u32[]{:S(2)}) copy-start(s32[8,256]{1,0:T(8,128)} %param.7) | copy-start | bytes 24580
  0.6 1.7 %copy-start = (f32[288,8,256]{2,1,0:T(8,128)S(1)}, f32[288,8,256]{2,1,0:T(8,128)}, u32[]{:S(2)}) copy-start(f32[288,8,256]{2,1,0:T(8,128)} %param.6) | copy-start | bytes 7077892
  2.3 0.9 copy-start.1
  6.1 0.8 copy-start.5
  6.8 12.2 %collective-permute-start = (f32[10,80,128]{2,1,0:T(8,128)}, f32[10,80,128]{2,1,0:T(8,128)S(1)}, u32[]{:S(2)}, u32[]{:S(2)}) collective-permute-start(f32[10,80,128]{2,1,0:T(8,128)} %get-tuple-element.30), channel_id=1, source_target_pairs={{0,0},{1,2},{2,6},{3,4},{4,1},{5,3},{6,7},{7,5},{8,8},{9,10},{10,1... | collective-permute-start | bytes 1228808 | tf_op jit(solution)/shard_map/ppermute | solution.py:406
  8.5 21.9 %collective-permute-start.1 = (f32[10,80,128]{2,1,0:T(8,128)S(1)}, f32[10,80,128]{2,1,0:T(8,128)S(1)}, u32[]{:S(2)}, u32[]{:S(2)}) collective-permute-start(f32[10,80,128]{2,1,0:T(8,128)S(1)} %get-tuple-element.31), channel_id=1, source_target_pairs={{0,2},{1,6},{2,4},{3,0},{4,3},{5,7},{6,5},{7,1},{8,10},{9,14},{10,... | collective-permute-start | bytes 1228808 | tf_op jit(solution)/shard_map/ppermute | solution.py:406
  13.3 24.3 %collective-permute-start.2 = (f32[10,80,128]{2,1,0:T(8,128)S(1)}, f32[10,80,128]{2,1,0:T(8,128)S(1)}, u32[]{:S(2)}, u32[]{:S(2)}) collective-permute-start(f32[10,80,128]{2,1,0:T(8,128)S(1)} %get-tuple-element.32), channel_id=1, source_target_pairs={{0,6},{1,4},{2,0},{3,2},{4,7},{5,5},{6,1},{7,3},{8,14},{9,12},{10,... | collective-permute-start | bytes 1228808 | tf_op jit(solution)/shard_map/ppermute | solution.py:406
  15.8 23.4 %collective-permute-start.3 = (f32[10,80,128]{2,1,0:T(8,128)S(1)}, f32[10,80,128]{2,1,0:T(8,128)S(1)}, u32[]{:S(2)}, u32[]{:S(2)}) collective-permute-start(f32[10,80,128]{2,1,0:T(8,128)S(1)} %get-tuple-element.33), channel_id=1, source_target_pairs={{0,4},{1,0},{2,2},{3,6},{4,5},{5,1},{6,3},{7,7},{8,12},{9,8},{10,1... | collective-permute-start | bytes 1228808 | tf_op jit(solution)/shard_map/ppermute | solution.py:406
  18.5 22.0 %collective-permute-start.10 = (s32[2,256]{1,0:T(2,128)S(1)}, s32[2,256]{1,0:T(2,128)S(1)}, u32[]{:S(2)}, u32[]{:S(2)}) collective-permute-start(s32[2,256]{1,0:T(2,128)S(1)} %get-tuple-element.58), channel_id=1, source_target_pairs={{28,0},{29,2},{30,6},{31,4},{0,1},{1,3},{2,7},{3,5},{4,8},{5,10},{... | collective-permute-start | bytes 6152 | tf_op jit(solution)/shard_map/ppermute | solution.py:412
  19.0 25.2 %collective-permute-start.11 = (s32[8,256]{1,0:T(8,128)S(1)}, s32[8,256]{1,0:T(8,128)S(1)}, u32[]{:S(2)}, u32[]{:S(2)}) collective-permute-start(s32[8,256]{1,0:T(8,128)S(1)} %copy-done.7), channel_id=1, source_target_pairs={{0,0},{1,2},{2,6},{3,4},{4,1},{5,3},{6,7},{7,5},{8,8},{9,10},{10,1... | collective-permute-start | bytes 24584 | tf_op jit(solution)/shard_map/ppermute | solution.py:412
  30.3 13.8 %collective-permute-start.12 = (s32[2,256]{1,0:T(2,128)S(1)}, s32[2,256]{1,0:T(2,128)S(1)}, u32[]{:S(2)}, u32[]{:S(2)}) collective-permute-start(s32[2,256]{1,0:T(2,128)S(1)} %get-tuple-element.59), channel_id=1, source_target_pairs={{4,0},{5,2},{6,6},{7,4},{8,1},{9,3},{10,7},{11,5},{12,8},{13,10},{... | collective-permute-start | bytes 6152 | tf_op jit(solution)/shard_map/ppermute | solution.py:412
  37.5 8.6 %collective-permute-start.5 = (f32[10,80,128]{2,1,0:T(8,128)}, f32[10,80,128]{2,1,0:T(8,128)S(1)}, u32[]{:S(2)}, u32[]{:S(2)}) collective-permute-start(f32[10,80,128]{2,1,0:T(8,128)} %get-tuple-element.36), channel_id=1, source_target_pairs={{0,0},{1,2},{2,6},{3,4},{4,1},{5,3},{6,7},{7,5},{8,8},{9,10},{10,1... | collective-permute-start | bytes 1228808 | tf_op jit(solution)/shard_map/ppermute | solution.py:406
  40.5 22.3 %collective-permute-start.4 = (f32[2,80,1280]{2,1,0:T(8,128)}, f32[2,80,1280]{2,1,0:T(8,128)S(1)}, u32[]{:S(2)}, u32[]{:S(2)}) collective-permute-start(f32[2,80,1280]{2,1,0:T(8,128)} %get-tuple-element.34.bottom), channel_id=1, source_target_pairs={{0,1},{2,3},{6,7},{4,5},{1,8},{3,10},{7,14},{5,12},{8,9},{10,11},{... | collective-permute-start | bytes 2457608 | tf_op jit(solution)/shard_map/ppermute | solution.py:471
  40.5 22.3 %collective-permute-start.9 = (f32[2,80,1280]{2,1,0:T(8,128)S(1)}, f32[2,80,1280]{2,1,0:T(8,128)}, u32[]{:S(2)}, u32[]{:S(2)}) collective-permute-start(f32[2,80,1280]{2,1,0:T(8,128)S(1)} %get-tuple-element.35.top), channel_id=1, source_target_pairs={{1,0},{3,2},{7,6},{5,4},{8,1},{10,3},{14,7},{12,5},{9,8},{11,10},{... | collective-permute-start | bytes 2457608 | tf_op jit(solution)/shard_map/ppermute | solution.py:472
  44.1 17.3 %collective-permute-start.6 = (f32[10,80,128]{2,1,0:T(8,128)}, f32[10,80,128]{2,1,0:T(8,128)S(1)}, u32[]{:S(2)}, u32[]{:S(2)}) collective-permute-start(f32[10,80,128]{2,1,0:T(8,128)} %copy-done.5), channel_id=1, source_target_pairs={{0,2},{1,6},{2,4},{3,0},{4,3},{5,7},{6,5},{7,1},{8,10},{9,14},{10,... | collective-permute-start | bytes 1228808 | tf_op jit(solution)/shard_map/ppermute | solution.py:406
  44.2 18.2 %collective-permute-start.7 = (f32[10,80,128]{2,1,0:T(8,128)}, f32[10,80,128]{2,1,0:T(8,128)S(1)}, u32[]{:S(2)}, u32[]{:S(2)}) collective-permute-start(f32[10,80,128]{2,1,0:T(8,128)} %copy-done.4), channel_id=1, source_target_pairs={{0,6},{1,4},{2,0},{3,2},{4,7},{5,5},{6,1},{7,3},{8,14},{9,12},{10,... | collective-permute-start | bytes 1228808 | tf_op jit(solution)/shard_map/ppermute | solution.py:406
  46.1 16.3 %collective-permute-start.8 = (f32[10,80,128]{2,1,0:T(8,128)S(1)}, f32[10,80,128]{2,1,0:T(8,128)S(1)}, u32[]{:S(2)}, u32[]{:S(2)}) collective-permute-start(f32[10,80,128]{2,1,0:T(8,128)S(1)} %get-tuple-element.39), channel_id=1, source_target_pairs={{0,4},{1,0},{2,2},{3,6},{4,5},{5,1},{6,3},{7,7},{8,12},{9,8},{10,1... | collective-permute-start | bytes 1228808 | tf_op jit(solution)/shard_map/ppermute | solution.py:406
  51.6 1.8 %copy-start.2 = (bf16[1152,1152]{1,0:T(8,128)(2,1)S(1)}, bf16[1152,1152]{1,0:T(8,128)(2,1)}, u32[]{:S(2)}) copy-start(bf16[1152,1152]{1,0:T(8,128)(2,1)} %linear.1) | copy-start | bytes 7962628
  53.3 1.7 %copy-start.3 = (bf16[1152,1152]{1,0:T(8,128)(2,1)S(1)}, bf16[1152,1152]{1,0:T(8,128)(2,1)}, u32[]{:S(2)}) copy-start(bf16[1152,1152]{1,0:T(8,128)(2,1)} %square.1) | copy-start | bytes 7962628
  55.1 1.0 copy-start.6
  71.1 19.3 %collective-permute-start.13 = (f32[2,72,1280]{2,1,0:T(8,128)S(1)}, f32[2,72,1280]{2,1,0:T(8,128)S(1)}, u32[]{:S(2)}, u32[]{:S(2)}) collective-permute-start(f32[2,72,1280]{2,1,0:T(8,128)S(1)} %get-tuple-element.42.bottom), channel_id=1, source_target_pairs={{0,1},{2,3},{6,7},{4,5},{1,8},{3,10},{7,14},{5,12},{8,9},{10,11},{... | collective-permute-start | bytes 2211848 | tf_op jit(solution)/shard_map/ppermute | solution.py:471
  72.1 18.3 %collective-permute-start.14 = (f32[2,72,1280]{2,1,0:T(8,128)S(1)}, f32[2,72,1280]{2,1,0:T(8,128)S(1)}, u32[]{:S(2)}, u32[]{:S(2)}) collective-permute-start(f32[2,72,1280]{2,1,0:T(8,128)S(1)} %get-tuple-element.43.top), channel_id=1, source_target_pairs={{1,0},{3,2},{7,6},{5,4},{8,1},{10,3},{14,7},{12,5},{9,8},{11,10},{... | collective-permute-start | bytes 2211848 | tf_op jit(solution)/shard_map/ppermute | solution.py:472
  96.6 20.9 %collective-permute-start.15 = (f32[2,72,1280]{2,1,0:T(8,128)S(1)}, f32[2,72,1280]{2,1,0:T(8,128)S(1)}, u32[]{:S(2)}, u32[]{:S(2)}) collective-permute-start(f32[2,72,1280]{2,1,0:T(8,128)S(1)} %get-tuple-element.44.bottom), channel_id=1, source_target_pairs={{0,1},{2,3},{6,7},{4,5},{1,8},{3,10},{7,14},{5,12},{8,9},{10,11},{... | collective-permute-start | bytes 2211848 | tf_op jit(solution)/shard_map/ppermute | solution.py:471
  97.4 24.9 %collective-permute-start.16 = (f32[2,72,1280]{2,1,0:T(8,128)S(1)}, f32[2,72,1280]{2,1,0:T(8,128)S(1)}, u32[]{:S(2)}, u32[]{:S(2)}) collective-permute-start(f32[2,72,1280]{2,1,0:T(8,128)S(1)} %get-tuple-element.45.top), channel_id=1, source_target_pairs={{1,0},{3,2},{7,6},{5,4},{8,1},{10,3},{14,7},{12,5},{9,8},{11,10},{... | collective-permute-start | bytes 2211848 | tf_op jit(solution)/shard_map/ppermute | solution.py:472
  111.2 18.2 %collective-permute-start.21 = (f32[10,64,128]{2,1,0:T(8,128)S(1)}, f32[10,64,128]{2,1,0:T(8,128)S(1)}, u32[]{:S(2)}, u32[]{:S(2)}) collective-permute-start(f32[10,64,128]{2,1,0:T(8,128)S(1)} %get-tuple-element.52), channel_id=1, source_target_pairs={{0,0},{2,1},{6,2},{4,3},{1,4},{3,5},{7,6},{5,7},{8,8},{10,9},{14,1... | collective-permute-start | bytes 983048 | tf_op jit(solution)/shard_map/ppermute | solution.py:497
  111.9 19.3 %collective-permute-start.22 = (f32[10,64,128]{2,1,0:T(8,128)S(1)}, f32[10,64,128]{2,1,0:T(8,128)S(1)}, u32[]{:S(2)}, u32[]{:S(2)}) collective-permute-start(f32[10,64,128]{2,1,0:T(8,128)S(1)} %get-tuple-element.53), channel_id=1, source_target_pairs={{2,0},{6,1},{4,2},{0,3},{3,4},{7,5},{5,6},{1,7},{10,8},{14,9},{12,... | collective-permute-start | bytes 983048 | tf_op jit(solution)/shard_map/ppermute | solution.py:497
  113.9 20.3 %collective-permute-start.23 = (f32[10,64,128]{2,1,0:T(8,128)S(1)}, f32[10,64,128]{2,1,0:T(8,128)S(1)}, u32[]{:S(2)}, u32[]{:S(2)}) collective-permute-start(f32[10,64,128]{2,1,0:T(8,128)S(1)} %get-tuple-element.54), channel_id=1, source_target_pairs={{6,0},{4,1},{0,2},{2,3},{7,4},{5,5},{1,6},{3,7},{14,8},{12,9},{8,1... | collective-permute-start | bytes 983048 | tf_op jit(solution)/shard_map/ppermute | solution.py:497
  117.6 19.6 %collective-permute-start.24 = (f32[10,64,128]{2,1,0:T(8,128)S(1)}, f32[10,64,128]{2,1,0:T(8,128)S(1)}, u32[]{:S(2)}, u32[]{:S(2)}) collective-permute-start(f32[10,64,128]{2,1,0:T(8,128)S(1)} %get-tuple-element.55), channel_id=1, source_target_pairs={{4,0},{0,1},{2,2},{6,3},{5,4},{1,5},{3,6},{7,7},{12,8},{8,9},{10,1... | collective-permute-start | bytes 983048 | tf_op jit(solution)/shard_map/ppermute | solution.py:497
  128.7 8.5 %collective-permute-start.17 = (f32[10,64,128]{2,1,0:T(8,128)S(1)}, f32[10,64,128]{2,1,0:T(8,128)S(1)}, u32[]{:S(2)}, u32[]{:S(2)}) collective-permute-start(f32[10,64,128]{2,1,0:T(8,128)S(1)} %get-tuple-element.48), channel_id=1, source_target_pairs={{0,0},{2,1},{6,2},{4,3},{1,4},{3,5},{7,6},{5,7},{8,8},{10,9},{14,1... | collective-permute-start | bytes 983048 | tf_op jit(solution)/shard_map/ppermute | solution.py:497
  129.4 18.4 %collective-permute-start.18 = (f32[10,64,128]{2,1,0:T(8,128)S(1)}, f32[10,64,128]{2,1,0:T(8,128)S(1)}, u32[]{:S(2)}, u32[]{:S(2)}) collective-permute-start(f32[10,64,128]{2,1,0:T(8,128)S(1)} %get-tuple-element.49), channel_id=1, source_target_pairs={{2,0},{6,1},{4,2},{0,3},{3,4},{7,5},{5,6},{1,7},{10,8},{14,9},{12,... | collective-permute-start | bytes 983048 | tf_op jit(solution)/shard_map/ppermute | solution.py:497
  131.1 16.7 %collective-permute-start.19 = (f32[10,64,128]{2,1,0:T(8,128)S(1)}, f32[10,64,128]{2,1,0:T(8,128)S(1)}, u32[]{:S(2)}, u32[]{:S(2)}) collective-permute-start(f32[10,64,128]{2,1,0:T(8,128)S(1)} %get-tuple-element.50), channel_id=1, source_target_pairs={{6,0},{4,1},{0,2},{2,3},{7,4},{5,5},{1,6},{3,7},{14,8},{12,9},{8,1... | collective-permute-start | bytes 983048 | tf_op jit(solution)/shard_map/ppermute | solution.py:497
  134.3 13.6 %collective-permute-start.20 = (f32[10,64,128]{2,1,0:T(8,128)S(1)}, f32[10,64,128]{2,1,0:T(8,128)S(1)}, u32[]{:S(2)}, u32[]{:S(2)}) collective-permute-start(f32[10,64,128]{2,1,0:T(8,128)S(1)} %get-tuple-element.51), channel_id=1, source_target_pairs={{4,0},{0,1},{2,2},{6,3},{5,4},{1,5},{3,6},{7,7},{12,8},{8,9},{10,1... | collective-permute-start | bytes 983048 | tf_op jit(solution)/shard_map/ppermute | solution.py:497
  (1 other events, 0.7 us)

commit v3 on v2

--- a/solution.py
+++ b/solution.py
@@ -42,6 +42,8 @@
         self.CH = self.NB + LANES
         self.edge_rows = (0, 1, rows - 2, rows - 1)
         self.inner_rows = tuple(range(2, rows - 2))
+        self.half = parts // 2
+        assert self.half & (self.half - 1) == 0 and self.half > 1
         assert self.nr * parts == LANES and self.no * parts == LANES
 
     def folds(self, rows):
@@ -58,15 +60,29 @@
         return self.folds(rows)[1]
 
 
+def exchange_share(z, k, odd, part):
+    core = part % 2
+    flip, delta = (k // z.half) ^ core, (k % z.half) ^ core
+    return (odd ^ flip) * z.half + ((part // 2) ^ delta)
+
+
+def exchange_part(z, k, odd, part):
+    core = (k // z.half) ^ odd ^ (part % 2)
+    delta = (k % z.half) ^ core
+    return ((part // 2) ^ delta) * 2 + core
+
+
 def lane_group(width):
     return lax.broadcasted_iota(jnp.int32, (1, LANES), 1) // width
 
 
-def pack_kernel(z, who, spec_in, ocean_in, *refs):
+def pack_kernel(z, odd, part, spec_in, ocean_in, mask, *refs):
     B, R, C, W, mt = z.B, z.R, z.C, z.W, z.mt
     outs, (spec, ocean, wide) = refs[: 2 * B], refs[2 * B :]
-    mine = who[0]
+    E = C + 2 * PAD
     at = 0
+    sea = mask[...].astype(F32)
+    sea = jnp.concatenate([sea, jnp.zeros((R, LANES), F32)], axis=1)
     for half in range(W // LANES):
         spec[half] = spec_in[:, half * LANES : (half + 1) * LANES]
         ocean[half] = ocean_in[:, half * LANES : (half + 1) * LANES]
@@ -90,40 +106,56 @@
                         pieces.append(jnp.zeros((LANES - used * count, LANES), F32))
                     wide[at + base + rr, cols] = jnp.concatenate(pieces, axis=0).T
         for k in range(B):
-            start = pl.multiple_of(lax.rem(mine + k, B) * C, PAD)
-            outs[which * B + k][...] = wide[at : at + slabs, pl.ds(start, C + 2 * PAD), :]
+            out = outs[which * B + k]
+            share = exchange_share(z, k, odd[0], part[0])
+            start = pl.multiple_of(share * C, PAD)
+            block = wide[at : at + slabs, pl.ds(start, E), :]
+            out[0 : slabs * E] = block.reshape(slabs * E, LANES)
+            if which == 0:
+                shift = lax.rem(W + LANES + PAD - start, W + LANES)
+                out[slabs * E : slabs * E + R] = pltpu.roll(sea, shift, axis=1)[:, :LANES]
         at += slabs
 
 
-def unpack_kernel(z, rows, who, *refs):
+def unpack_kernel(z, rows, odd, part, *refs):
     B, mt = z.B, z.mt
     got, outs = refs[:B], refs[B:]
-    share = who[0]
+    E = z.C + 2 * PAD
+    if rows == z.edge_rows:
+        sea = outs[-1]
+        outs = outs[:-1]
+        at = z.slabs(rows) * E
+        for r in range(z.R):
+            line = jnp.broadcast_to(got[0][at + r : at + r + 1], (LANES, LANES))
+            sea[r] = line.T[:E]
+        for ref, first in zip(outs, (0, z.R - EDGE)):
+            for i in range(EDGE):
+                ref[i, :, z.CH :] = sea[first + i]
     places = [(ref, i) for ref in outs for i in range(ref.shape[0])]
-    src = [lax.rem(share - k + B, B) for k in range(B)]
+    src = [exchange_part(z, k, odd[0], part[0]) for k in range(B)]
     for k in range(B):
         for t in range(mt):
             lanes = pl.ds(pl.multiple_of(src[k] * z.main + t * LANES, LANES), LANES)
             for i, (ref, at) in enumerate(places):
-                ref[at, :, lanes] = got[k][i * mt + t]
+                ref[at, :, lanes] = got[k][(i * mt + t) * E : (i * mt + t + 1) * E]
     for count, used, deep, base, lane in z.folds(rows)[0]:
         group = lane_group(count)
         for i, (ref, at) in enumerate(places):
             tile = jnp.zeros(ref.shape[1:2] + (LANES,), F32)
             for k in range(B):
                 shift = lax.rem((src[k] - i // deep) * count + LANES, LANES)
-                moved = pltpu.roll(got[k][base + i % deep], shift, axis=1)
+                slab = base + i % deep
+                moved = pltpu.roll(got[k][slab * E : (slab + 1) * E], shift, axis=1)
                 tile = jnp.where(group == src[k], moved, tile)
             ref[at, :, lane : lane + LANES] = tile
 
 
-def send_back_kernel(z, rows, who, *refs):
+def send_back_kernel(z, rows, odd, part, *refs):
     B, mt = z.B, z.mt
     states, outs = refs[:-B], refs[-B:]
-    share = who[0]
     places = [(ref, i) for ref in states for i in range(ref.shape[0])]
     for k in range(B):
-        src = lax.rem(share - k + B, B)
+        src = exchange_part(z, k, odd[0], part[0])
         for t in range(mt):
             lanes = pl.ds(pl.multiple_of(src * z.main + t * LANES, LANES), LANES)
             for i, (ref, at) in enumerate(places):
@@ -140,15 +172,14 @@
                 outs[k][base + rr] = tile
 
 
-def restore_kernel(z, who, *refs):
+def restore_kernel(z, odd, part, *refs):
     B, R, C, mt = z.B, z.R, z.C, z.mt
     got, (spec_out, ocean_out, wide, spec, ocean) = refs[: 2 * B], refs[2 * B :]
-    mine = who[0]
     at = 0
     for which, rows in enumerate((z.edge_rows, z.inner_rows)):
         folds, slabs = z.folds(rows)
         for k in range(B):
-            c = lax.rem(mine + k, B)
+            c = exchange_share(z, k, odd[0], part[0])
             wide[at : at + slabs, pl.ds(pl.multiple_of(c * C, PAD), C), :] = got[which * B + k][...]
         for half in range(z.W // LANES):
             cols = slice(half * LANES, (half + 1) * LANES)
@@ -198,7 +229,7 @@
     put(drift_weights, 0, slice(0, LANES), turned)
 
 
-def advance(z, groups, outs, cut, sea_at, sea, speed, weights, drift_weights, moved, moved_twice):
+def advance(z, groups, outs, cut, sea_at, speed, weights, drift_weights, moved, moved_twice):
     NB, CH, L = z.NB, z.CH, z.L
     E = groups[0][1][0][0].shape[1]
     N = E - 2 * cut
@@ -206,17 +237,17 @@
     sea_cols = pl.ds(sea_at, E)
     places = [(ref, i) for ref in outs for i in range(ref.shape[0])]
 
-    def sea_row(r):
-        return sea[r, sea_cols]
-
-    for g, (sea_first, rows) in enumerate(groups):
+    def sea_row(place):
+        return place[0][place[1], sea_cols]
+
+    for g, (sea_rows, rows) in enumerate(groups):
         n = len(rows)
         tops = [ref[i, :, NB:CH] for ref, i in rows]
         for r in range(n):
             moved[g, 0, r] = DOPPLER * jnp.tanh(jnp.broadcast_to(tops[r][:, 0:1], (E, LANES)))
             moved[g, 1, r] = DOPPLER * jnp.tanh(jnp.broadcast_to(tops[r][:, L : L + 1], (E, LANES)))
 
-    def advect(g, sea_first, read, write, first, last, speed_cx, speed_cy):
+    def advect(g, sea_rows, read, write, first, last, speed_cx, speed_cy):
         def along_x(r):
             energy = read(r)
             speed_x = speed_cx + moved[g, 0, r]
@@ -241,7 +272,7 @@
                     + (pltpu.roll(minus_y, E - 1, axis=0) - minus_y)
                 )
             )
-            write(r, result * sea_row(sea_first + r))
+            write(r, result * sea_row(sea_rows[r]))
             plus_before, energy, plus, minus = plus, energy_next, plus_next, minus_next
 
     def one_tile(j, carry):
@@ -249,7 +280,7 @@
         speed_cx = speed[0:1, lanes]
         speed_cy = speed[1:2, lanes]
         done = 0
-        for g, (sea_first, rows) in enumerate(groups):
+        for g, (sea_rows, rows) in enumerate(groups):
             n = len(rows)
 
             def read_state(r):
@@ -262,9 +293,9 @@
             def write_second(r, value):
                 moved_twice[done + r - 2, :, lanes] = value[keep]
 
-            advect(g, sea_first, read_state, write_first, 1, n - 1, speed_cx, speed_cy)
+            advect(g, sea_rows, read_state, write_first, 1, n - 1, speed_cx, speed_cy)
             advect(
-                g, sea_first, lambda r: moved[g, 2, r], write_second, 2, n - 2, speed_cx, speed_cy
+                g, sea_rows, lambda r: moved[g, 2, r], write_second, 2, n - 2, speed_cx, speed_cy
             )
             done += n - 4
         return carry
@@ -272,14 +303,14 @@
     lax.fori_loop(0, NB // LANES, one_tile, 0)
 
     count = len(places)
-    sea_rows = [f + r for f, rows in groups for r in range(2, len(rows) - 2)]
+    own_sea = [place for sea_rows, rows in groups for place in sea_rows[2 : len(rows) - 2]]
     energy = moved_twice[...].reshape(count * N, NB)
     squares = energy * energy
     interaction = jnp.dot(
         energy.astype(BF16), weights[:NB], preferred_element_type=F32
     ) + jnp.dot(squares.astype(BF16), weights[NB:], preferred_element_type=F32)
     total = jnp.sum(squares, axis=1, keepdims=True)
-    sea_here = jnp.concatenate([sea_row(r)[keep] for r in sea_rows], axis=0)
+    sea_here = jnp.concatenate([sea_row(place)[keep] for place in own_sea], axis=0)
     scale = (DT_SOURCE * sea_here[:, 0:1]) / (1.0 + total / NB)
     fresh = energy + scale * (interaction * energy)
     for i, (ref, at) in enumerate(places):
@@ -289,7 +320,7 @@
     comp = (lax.broadcasted_iota(jnp.int32, (1, LANES), 1) // L) % 2
     sign = jnp.where(comp == 0, 1.0, -1.0).astype(F32)
     i = 0
-    for sea_first, rows in groups:
+    for _, rows in groups:
         for r in range(2, len(rows) - 2):
             here, before, after = [
                 rows[r + d][0][rows[r + d][1], :, NB:CH] for d in (0, -1, 1)
@@ -307,7 +338,7 @@
             ref, at = places[i]
             ref[at, :, NB:CH] = (
                 centre + DT_OCEAN * (turn + VISCOSITY * lap)
-            ) * sea_row(sea_first + r)[keep]
+            ) * sea_row(own_sea[i])[keep]
             i += 1
 
 
@@ -317,23 +348,20 @@
 
 def inner_kernel(z, cut, sea_at, top, inner, bottom, sea, *refs):
     (speed, weights, drift_weights, out, moved, moved_twice) = refs
-    groups = [(EDGE, listed(top, inner, bottom))]
-    advance(
-        z, groups, [out], cut, sea_at, sea, speed, weights, drift_weights, moved, moved_twice
-    )
-
-
-def edge_kernel(z, cut, sea_at, up, top, inner, bottom, down, sea, *refs):
+    groups = [(listed(sea), listed(top, inner, bottom))]
+    advance(z, groups, [out], cut, sea_at, speed, weights, drift_weights, moved, moved_twice)
+
+
+def edge_kernel(z, cut, sea_at, up, top, inner, bottom, down, sea_up, sea, sea_down, *refs):
     (speed, weights, drift_weights, new_top, new_bottom, moved, moved_twice) = refs
     inside = listed(inner)
+    sea_rows = listed(sea_up, sea, sea_down)
     groups = [
-        (0, listed(up, top) + inside[:EDGE]),
-        (z.R - EDGE, inside[-EDGE:] + listed(bottom, down)),
+        (sea_rows[: 3 * EDGE], listed(up, top) + inside[:EDGE]),
+        (sea_rows[-3 * EDGE :], inside[-EDGE:] + listed(bottom, down)),
     ]
     outs = [new_top, new_bottom]
-    advance(
-        z, groups, outs, cut, sea_at, sea, speed, weights, drift_weights, moved, moved_twice
-    )
+    advance(z, groups, outs, cut, sea_at, speed, weights, drift_weights, moved, moved_twice)
 
 
 def speeds(z):
@@ -365,30 +393,27 @@
     geo, part = lax.axis_index("geo"), lax.axis_index("bins")
 
     def device_at(q, c):
-        m, along = c // half, c % half
-        along = along if m == 0 else half - 1 - along
-        return ((q // 2) * 2 + m) * B + 2 * along + q % 2
-
-    along, odd = part // 2, geo % 2
-    tile = geo - odd + part % 2
-    share = along + (half + half - 1 - 2 * along) * odd
+        return ((q // 2) * 2 + c // half) * B + 2 * (c % half) + q % 2
+
     forward = [
-        [(g * B + b, device_at(g, (b + k) % B)) for g in range(G) for b in range(B)]
+        [
+            (g * B + b, device_at(g, exchange_share(z, k, g % 2, b)))
+            for g in range(G)
+            for b in range(B)
+        ]
         for k in range(B)
     ]
     pairs = [(q, c) for q in range(G) for c in range(B)]
     to_next_row = [(device_at(q, c), device_at((q + 1) % G, c)) for q, c in pairs]
     to_prev_row = [(t, s) for s, t in to_next_row]
-    part_id = part.astype(jnp.int32).reshape(1)
-    share_id = share.astype(jnp.int32).reshape(1)
-
-    def blocks(width):
-        return [
-            jax.ShapeDtypeStruct((z.slabs(rows), width, LANES), F32)
-            for rows in (z.edge_rows, z.inner_rows)
-            for _ in range(B)
-        ]
-
+    who = ((geo % 2).astype(jnp.int32).reshape(1), part.astype(jnp.int32).reshape(1))
+
+    width = C + 2 * PAD
+    blocks = [
+        jax.ShapeDtypeStruct((z.slabs(rows) * width + more, LANES), F32)
+        for rows, more in ((z.edge_rows, R), (z.inner_rows, 0))
+        for _ in range(B)
+    ]
     all_slabs = z.slabs(z.edge_rows) + z.slabs(z.inner_rows)
     columns_scratch = [
         pltpu.VMEM((W // LANES, nb * R, LANES), F32),
@@ -396,28 +421,14 @@
     ]
     packed = pl.pallas_call(
         functools.partial(pack_kernel, z),
-        out_shape=blocks(C + 2 * PAD),
-        in_specs=[SMEM, VMEM, VMEM],
+        out_shape=blocks,
+        in_specs=[SMEM] * 2 + [VMEM] * 3,
         out_specs=[VMEM] * (2 * B),
         scratch_shapes=columns_scratch + [pltpu.VMEM((all_slabs, W + 2 * PAD, LANES), F32)],
         compiler_params=params(24),
         name="pack",
-    )(part_id, spectrum.reshape(nb * R, W), ocean.reshape(2 * L * R, W))
+    )(*who, spectrum.reshape(nb * R, W), ocean.reshape(2 * L * R, W), sea_mask)
     got = [lax.ppermute(packed[i], axes, forward[i % B]) for i in range(2 * B)]
-
-    def mask_of(offset, block):
-        perm = [
-            (((q + offset) % G) * B + c, device_at(q, c)) for q in range(G) for c in range(B)
-        ]
-        return lax.ppermute(block, axes, perm)
-
-    mask = jnp.concatenate(
-        [mask_of(-1, sea_mask[R - EDGE :]), mask_of(0, sea_mask), mask_of(1, sea_mask[:EDGE])],
-        axis=0,
-    )
-    mask = jnp.pad(mask, ((0, 0), (PAD, PAD)))
-    mask = lax.dynamic_slice_in_dim(mask, share * C, C + 2 * PAD, axis=1)
-    sea = jnp.broadcast_to(mask.astype(F32)[..., None], mask.shape + (LANES,))
 
     weights, drift_weights = pl.pallas_call(
         functools.partial(weights_kernel, z),
@@ -433,25 +444,27 @@
     )(kernel_linear, kernel_square, drift_kernel)
     speed = speeds(z)
 
-    def unpack(rows, received, counts):
+    def unpack(rows, received, shapes):
         return pl.pallas_call(
             functools.partial(unpack_kernel, z, rows),
-            out_shape=[jax.ShapeDtypeStruct((n, C + 2 * PAD, CH), F32) for n in counts],
-            in_specs=[SMEM] + [VMEM] * B,
-            out_specs=[VMEM] * len(counts),
+            out_shape=[jax.ShapeDtypeStruct((n, width, lanes), F32) for n, lanes in shapes],
+            in_specs=[SMEM] * 2 + [VMEM] * B,
+            out_specs=[VMEM] * len(shapes),
             compiler_params=params(16),
             name="unpack",
-        )(share_id, *received)
-
-    top, bottom = unpack(z.edge_rows, got[:B], (EDGE, EDGE))
-    (inner,) = unpack(z.inner_rows, got[B:], (R - 2 * EDGE,))
+        )(*who, *received)
+
+    top, bottom, sea = unpack(
+        z.edge_rows, got[:B], [(EDGE, CH + LANES), (EDGE, CH + LANES), (R, LANES)]
+    )
+    (inner,) = unpack(z.inner_rows, got[B:], [(R - 2 * EDGE, CH)])
 
     def step_call(body, width, cut, sea_at, counts, groups, deepest, inputs):
         n = width - 2 * cut
         return pl.pallas_call(
             functools.partial(body, z, cut, sea_at),
             out_shape=[jax.ShapeDtypeStruct((k, n, CH), F32) for k in counts],
-            in_specs=[VMEM] * (len(inputs) + 4),
+            in_specs=[VMEM] * (len(inputs) + 3),
             out_specs=[VMEM] * len(counts),
             scratch_shapes=[
                 pltpu.VMEM((groups, 3, deepest, width, LANES), F32),
@@ -460,9 +473,8 @@
             compiler_params=params(32),
             cost_estimate=cost(6e9, 8e6),
             name=body.__name__,
-        )(*inputs, sea, speed, weights, drift_weights)
-
-    width = C + 2 * PAD
+        )(*inputs, speed, weights, drift_weights)
+
     for step in range(STEPS):
         valid = EDGE * (STEPS - 1 - step)
         margin = (width - C) // 2
@@ -471,11 +483,13 @@
         up = lax.ppermute(bottom, axes, to_next_row)
         down = lax.ppermute(top, axes, to_prev_row)
         (new_inner,) = step_call(
-            inner_kernel, width, cut, sea_at, (R - 2 * EDGE,), 1, R, (top, inner, bottom)
+            inner_kernel, width, cut, sea_at, (R - 2 * EDGE,), 1, R, (top, inner, bottom, sea)
         )
+        if step == 0:
+            sea_up, sea_down = up[:, :, CH:], down[:, :, CH:]
         top, bottom = step_call(
             edge_kernel, width, cut, sea_at, (EDGE, EDGE), 2, 3 * EDGE,
-            (up, top, inner, bottom, down),
+            (up, top, inner, bottom, down, sea_up, sea, sea_down),
         )
         inner = new_inner
         width -= 2 * cut
@@ -485,11 +499,11 @@
         return pl.pallas_call(
             functools.partial(send_back_kernel, z, rows),
             out_shape=[shape] * B,
-            in_specs=[SMEM] + [VMEM] * len(states),
+            in_specs=[SMEM] * 2 + [VMEM] * len(states),
             out_specs=[VMEM] * B,
             compiler_params=params(16),
             name="send_back",
-        )(share_id, *states)
+        )(*who, *states)
 
     packed = send_back(z.inner_rows, [inner]), send_back(z.edge_rows, [top, bottom])
     packed = list(packed[1]) + list(packed[0])
@@ -502,12 +516,12 @@
             jax.ShapeDtypeStruct((nb * R, W), F32),
             jax.ShapeDtypeStruct((2 * L * R, W), F32),
         ),
-        in_specs=[SMEM] + [VMEM] * (2 * B),
+        in_specs=[SMEM] * 2 + [VMEM] * (2 * B),
         out_specs=(VMEM,) * 2,
         scratch_shapes=[pltpu.VMEM((all_slabs, W, LANES), F32)] + columns_scratch,
         compiler_params=params(24),
         name="restore",
-    )(part_id, *back)
+    )(*who, *back)
     return spectrum_out.reshape(nb, R, W), ocean_out.reshape(2, L, R, W)
 
 

time: 152 us -> 147 us (0.967)
  waiting for transfers between devices: 34.8 us -> 45.1 us
  starting transfers between devices: 58.9 us -> 52.2 us
  Pallas kernels: 46.7 us -> 43 us
  local copies, waits for them, and re-layouts: 8.9 us -> 5.23 us
    ppermute x3 -> x0, starting transfers between devices: 7.9 us -> none  [mask_of(): return lax.ppermute(block, axes, perm)]
    ppermute x8, starting transfers between devices: 20.7 us -> 25.6 us  [per_device(): got = [lax.ppermute(packed[i], axes, forward[i % B]) for i in range(2 * B)]]
    ppermute x8, waiting for transfers between devices: 15.4 us -> 19.9 us  [per_device(): got = [lax.ppermute(packed[i], axes, forward[i % B]) for i in range(2 * B)]]
    ppermute x8, starting transfers between devices: 19.5 us -> 15.9 us  [per_device(): lax.ppermute(packed[i], axes, [(t, s) for s, t in forward[i % B]])]
    ppermute x8, waiting for transfers between devices: 10.8 us -> 14.4 us  [per_device(): lax.ppermute(packed[i], axes, [(t, s) for s, t in forward[i % B]])]
    unnamed x16 -> x12, local copies, waits for them, and re-layouts: 8.56 us -> 5.06 us
    ppermute x3, waiting for transfers between devices: 8.59 us -> 10.8 us  [per_device(): up = lax.ppermute(bottom, axes, to_next_row)]
    pallas_call x6, Pallas kernels: 37.8 us -> 35.9 us  [step_call(): pl.pallas_call(functools.partial(body, z, cut, sea_at), out_shape=[jax.Sh...]
  transfers between devices with their start and end apart: 25 -> 22, of which waited for: 6 -> 8; matrix products, arithmetic and copies ran while one was open for 0% -> 0% of each run, Pallas kernels for 18% -> 17%
where the time goes in v3:
time: 147 us
  starting transfers between devices  52.2 us (36%)
  waiting for transfers between devices  45.1 us (31%)
  Pallas kernels  43 us (29%)
  local copies, waits for them, and re-layouts  5.23 us (4%)
    pallas_call x6, Pallas kernels, step_call(): pl.pallas_call(functools.partial(body, z, cut, sea_at), out_shape=[jax.Sh...  35.9 us
    ppermute x8, starting transfers between devices, per_device(): got = [lax.ppermute(packed[i], axes, forward[i % B]) for i in range(2 * B)]  25.6 us
    ppermute x8, waiting for transfers between devices, per_device(): got = [lax.ppermute(packed[i], axes, forward[i % B]) for i in range(2 * B)]  19.9 us
    ppermute x8, starting transfers between devices, per_device(): lax.ppermute(packed[i], axes, [(t, s) for s, t in forward[i % B]])  15.9 us
    ppermute x8, waiting for transfers between devices, per_device(): lax.ppermute(packed[i], axes, [(t, s) for s, t in forward[i % B]])  14.4 us
    ppermute x3, waiting for transfers between devices, per_device(): up = lax.ppermute(bottom, axes, to_next_row)  10.8 us
    ppermute x3, starting transfers between devices, per_device(): down = lax.ppermute(top, axes, to_prev_row)  10.3 us
    unnamed x12, local copies, waits for them, and re-layouts  5.06 us
  transfers between devices with their start and end apart: 22, of which 8 were waited for; matrix products, arithmetic and copies ran while one was open for 0% of the time, Pallas kernels for 17%

profile of v3, /device:TPU:0, one launch (start us, length us, event | category | flops | bytes accessed | tf_op | source)
XLA Modules:
  0.0 146.7 jit_solution(791401739103271844)
XLA Ops:
  0.7 1.7 %copy-done = f32[288,8,256]{2,1,0:T(8,128)S(1)} copy-done((f32[288,8,256]{2,1,0:T(8,128)S(1)}, f32[288,8,256]{2,1,0:T(8,128)}, u32[]{:S(2)}) %copy-start) | copy-done | bytes 2359320
  4.0 1.1 pack.1
  5.7 3.0 %collective-permute-start.1 = (f32[808,128]{1,0:T(8,128)S(1)}, f32[808,128]{1,0:T(8,128)S(1)}, u32[]{:S(2)}, u32[]{:S(2)}) collective-permute-start(f32[808,128]{1,0:T(8,128)S(1)} %get-tuple-element.32), channel_id=1, source_target_pairs={{0,2},{1,4},{2,0},{3,6},{4,7},{5,1},{6,5},{7,3},{8,10},{9,12},{10,... | collective-permute-start | bytes 1241096 | tf_op jit(solution)/shard_map/ppermute | solution.py:431
  8.8 2.2 %collective-permute-start.2 = (f32[808,128]{1,0:T(8,128)S(1)}, f32[808,128]{1,0:T(8,128)S(1)}, u32[]{:S(2)}, u32[]{:S(2)}) collective-permute-start(f32[808,128]{1,0:T(8,128)S(1)} %get-tuple-element.33), channel_id=1, source_target_pairs={{0,4},{1,2},{2,6},{3,0},{4,1},{5,7},{6,3},{7,5},{8,12},{9,10},{10,... | collective-permute-start | bytes 1241096 | tf_op jit(solution)/shard_map/ppermute | solution.py:431
  10.9 3.6 %collective-permute-start.3 = (f32[808,128]{1,0:T(8,128)S(1)}, f32[808,128]{1,0:T(8,128)S(1)}, u32[]{:S(2)}, u32[]{:S(2)}) collective-permute-start(f32[808,128]{1,0:T(8,128)S(1)} %get-tuple-element.34), channel_id=1, source_target_pairs={{0,6},{1,0},{2,4},{3,2},{4,3},{5,5},{6,1},{7,7},{8,14},{9,8},{10,1... | collective-permute-start | bytes 1241096 | tf_op jit(solution)/shard_map/ppermute | solution.py:431
  14.6 7.6 %collective-permute-done.1.refs_1_ = f32[808,128]{1,0:T(8,128)S(1)} collective-permute-done((f32[808,128]{1,0:T(8,128)S(1)}, f32[808,128]{1,0:T(8,128)S(1)}, u32[]{:S(2)}, u32[]{:S(2)}) %collective-permute-start.1) | collective-permute-done | bytes 413728 | tf_op jit(solution)/shard_map/ppermute | solution.py:431
  22.2 1.8 %collective-permute-done.2.refs_2_ = f32[808,128]{1,0:T(8,128)S(1)} collective-permute-done((f32[808,128]{1,0:T(8,128)S(1)}, f32[808,128]{1,0:T(8,128)S(1)}, u32[]{:S(2)}, u32[]{:S(2)}) %collective-permute-start.2) | collective-permute-done | bytes 413728 | tf_op jit(solution)/shard_map/ppermute | solution.py:431
  24.1 5.0 %collective-permute-done.3.refs_3_ = f32[808,128]{1,0:T(8,128)S(1)} collective-permute-done((f32[808,128]{1,0:T(8,128)S(1)}, f32[808,128]{1,0:T(8,128)S(1)}, u32[]{:S(2)}, u32[]{:S(2)}) %collective-permute-start.3) | collective-permute-done | bytes 413728 | tf_op jit(solution)/shard_map/ppermute | solution.py:431
  29.8 3.5 %collective-permute-start.9 = (f32[2,80,1408]{2,1,0:T(8,128)S(1)}, f32[2,80,1408]{2,1,0:T(8,128)S(1)}, u32[]{:S(2)}, u32[]{:S(2)}) collective-permute-start(f32[2,80,1408]{2,1,0:T(8,128)S(1)} %get-tuple-element.36.top), channel_id=1, source_target_pairs={{1,0},{3,2},{5,4},{7,6},{8,1},{10,3},{12,5},{14,7},{9,8},{11,10},{... | collective-permute-start | bytes 2703368 | tf_op jit(solution)/shard_map/ppermute | solution.py:484
  33.9 1.5 %collective-permute-start.6 = (f32[800,128]{1,0:T(8,128)S(1)}, f32[800,128]{1,0:T(8,128)S(1)}, u32[]{:S(2)}, u32[]{:S(2)}) collective-permute-start(f32[800,128]{1,0:T(8,128)S(1)} %get-tuple-element.38), channel_id=1, source_target_pairs={{0,2},{1,4},{2,0},{3,6},{4,7},{5,1},{6,5},{7,3},{8,10},{9,12},{10,... | collective-permute-start | bytes 1228808 | tf_op jit(solution)/shard_map/ppermute | solution.py:431
  35.5 2.2 %collective-permute-start.7 = (f32[800,128]{1,0:T(8,128)S(1)}, f32[800,128]{1,0:T(8,128)S(1)}, u32[]{:S(2)}, u32[]{:S(2)}) collective-permute-start(f32[800,128]{1,0:T(8,128)S(1)} %get-tuple-element.39), channel_id=1, source_target_pairs={{0,4},{1,2},{2,6},{3,0},{4,1},{5,7},{6,3},{7,5},{8,12},{9,10},{10,... | collective-permute-start | bytes 1228808 | tf_op jit(solution)/shard_map/ppermute | solution.py:431
  37.9 1.7 %copy-done.4 = bf16[1152,1152]{1,0:T(8,128)(2,1)S(1)} copy-done((bf16[1152,1152]{1,0:T(8,128)(2,1)S(1)}, bf16[1152,1152]{1,0:T(8,128)(2,1)}, u32[]{:S(2)}) %copy-start.4) | copy-done | bytes 2654232
  39.7 1.5 %weights.1 = (bf16[2304,1152]{1,0:T(8,128)(2,1)S(1)}, bf16[1152,128]{1,0:T(8,128)(2,1)S(1)}) custom-call(bf16[1152,1152]{1,0:T(8,128)(2,1)S(1)} %copy-done.3, bf16[1152,1152]{1,0:T(8,128)(2,1)S(1)} %copy-done.4, bf16[128,1152]{1,0:T(8,128)(2,1)S(1)} %copy-done.5), custom_call_target="tpu_custom_call" | custom-call | flops 2000000000 | bytes 10616832 | tf_op jit(solution)/shard_map/weights/pallas_call | solution.py:433
  41.4 11.6 %collective-permute-start.8 = (f32[800,128]{1,0:T(8,128)S(1)}, f32[800,128]{1,0:T(8,128)S(1)}, u32[]{:S(2)}, u32[]{:S(2)}) collective-permute-start(f32[800,128]{1,0:T(8,128)S(1)} %get-tuple-element.40), channel_id=1, source_target_pairs={{0,6},{1,0},{2,4},{3,2},{4,3},{5,5},{6,1},{7,7},{8,14},{9,8},{10,1... | collective-permute-start | bytes 1228808 | tf_op jit(solution)/shard_map/ppermute | solution.py:431
  53.1 5.4 %collective-permute-done.8.refs_3_ = f32[800,128]{1,0:T(8,128)S(1)} collective-permute-done((f32[800,128]{1,0:T(8,128)S(1)}, f32[800,128]{1,0:T(8,128)S(1)}, u32[]{:S(2)}, u32[]{:S(2)}) %collective-permute-start.8) | collective-permute-done | bytes 409632 | tf_op jit(solution)/shard_map/ppermute | solution.py:431
  59.0 6.8 %edge_kernel.3 = (f32[2,72,1280]{2,1,0:T(8,128)S(1)}, f32[2,72,1280]{2,1,0:T(8,128)S(1)}) custom-call(f32[2,80,1408]{2,1,0:T(8,128)S(1)} %collective-permute-done.4.up, f32[2,80,1408]{2,1,0:T(8,128)S(1)} %get-tuple-element.36.top, f32[4,80,1280]{2,1,0:T(8,128)S(1)} %unpack.3.inner, f32[2,80,1408]{2,1,0:T(8,128)S(1)} %get-tuple-element.35.bottom, ...), custom_call_target="tpu_custom_call" | custom-call | flops 6000000000 | bytes 8000000 | tf_op jit(solution)/shard_map/edge_kernel/pallas_call | solution.py:464
  66.1 3.3 %collective-permute-start.11 = (f32[2,72,1280]{2,1,0:T(8,128)S(1)}, f32[2,72,1280]{2,1,0:T(8,128)S(1)}, u32[]{:S(2)}, u32[]{:S(2)}) collective-permute-start(f32[2,72,1280]{2,1,0:T(8,128)S(1)} %get-tuple-element.45.top), channel_id=1, source_target_pairs={{1,0},{3,2},{5,4},{7,6},{8,1},{10,3},{12,5},{14,7},{9,8},{11,10},{... | collective-permute-start | bytes 2211848 | tf_op jit(solution)/shard_map/ppermute | solution.py:484
  69.4 5.9 %inner_kernel.3.inner = f32[4,72,1280]{2,1,0:T(8,128)S(1)} custom-call(f32[2,80,1408]{2,1,0:T(8,128)S(1)} %get-tuple-element.36.top, f32[4,80,1280]{2,1,0:T(8,128)S(1)} %unpack.3.inner, f32[2,80,1408]{2,1,0:T(8,128)S(1)} %get-tuple-element.35.bottom, f32[8,80,128]{2,1,0:T(8,128)S(1)} %get-tuple-element.41.sea, f32[8,1152]{1,0:T(8,128)S(1)} %maximum_maximum_fusion.refs_0_, ...), custom_call_target="tpu_custom_call" | custom-call | flops 6000000000 | bytes 8000000 | tf_op jit(solution)/shard_map/inner_kernel/pallas_call | solution.py:464
  75.3 10.8 %collective-permute-done.10.up = f32[2,72,1280]{2,1,0:T(8,128)S(1)} collective-permute-done((f32[2,72,1280]{2,1,0:T(8,128)S(1)}, f32[2,72,1280]{2,1,0:T(8,128)S(1)}, u32[]{:S(2)}, u32[]{:S(2)}) %collective-permute-start.10) | collective-permute-done | bytes 737312 | tf_op jit(solution)/shard_map/ppermute | solution.py:483
  86.1 6.3 %edge_kernel.4 = (f32[2,72,1280]{2,1,0:T(8,128)S(1)}, f32[2,72,1280]{2,1,0:T(8,128)S(1)}) custom-call(f32[2,72,1280]{2,1,0:T(8,128)S(1)} %collective-permute-done.10.up, f32[2,72,1280]{2,1,0:T(8,128)S(1)} %get-tuple-element.45.top, f32[4,72,1280]{2,1,0:T(8,128)S(1)} %inner_kernel.3.inner, f32[2,72,1280]{2,1,0:T(8,128)S(1)} %get-tuple-element.44.bottom, ...), custom_call_target="tpu_custom_call" | custom-call | flops 6000000000 | bytes 8000000 | tf_op jit(solution)/shard_map/edge_kernel/pallas_call | solution.py:464
  92.5 3.5 %collective-permute-start.13 = (f32[2,72,1280]{2,1,0:T(8,128)S(1)}, f32[2,72,1280]{2,1,0:T(8,128)S(1)}, u32[]{:S(2)}, u32[]{:S(2)}) collective-permute-start(f32[2,72,1280]{2,1,0:T(8,128)S(1)} %get-tuple-element.47.top), channel_id=1, source_target_pairs={{1,0},{3,2},{5,4},{7,6},{8,1},{10,3},{12,5},{14,7},{9,8},{11,10},{... | collective-permute-start | bytes 2211848 | tf_op jit(solution)/shard_map/ppermute | solution.py:484
  96.0 5.5 %inner_kernel.4.inner = f32[4,72,1280]{2,1,0:T(8,128)S(1)} custom-call(f32[2,72,1280]{2,1,0:T(8,128)S(1)} %get-tuple-element.45.top, f32[4,72,1280]{2,1,0:T(8,128)S(1)} %inner_kernel.3.inner, f32[2,72,1280]{2,1,0:T(8,128)S(1)} %get-tuple-element.44.bottom, f32[8,80,128]{2,1,0:T(8,128)S(1)} %get-tuple-element.41.sea, ...), custom_call_target="tpu_custom_call" | custom-call | flops 6000000000 | bytes 8000000 | tf_op jit(solution)/shard_map/inner_kernel/pallas_call | solution.py:464
  101.6 5.3 %inner_kernel.5.refs_0_ = f32[4,64,1280]{2,1,0:T(8,128)S(1)} custom-call(f32[2,72,1280]{2,1,0:T(8,128)S(1)} %get-tuple-element.47.top, f32[4,72,1280]{2,1,0:T(8,128)S(1)} %inner_kernel.4.inner, f32[2,72,1280]{2,1,0:T(8,128)S(1)} %get-tuple-element.46.bottom, f32[8,80,128]{2,1,0:T(8,128)S(1)} %get-tuple-element.41.sea, ...), custom_call_target="tpu_custom_call" | custom-call | flops 6000000000 | bytes 8000000 | tf_op jit(solution)/shard_map/inner_kernel/pallas_call | solution.py:464
  108.0 5.0 %collective-permute-start.20 = (f32[10,64,128]{2,1,0:T(8,128)S(1)}, f32[10,64,128]{2,1,0:T(8,128)S(1)}, u32[]{:S(2)}, u32[]{:S(2)}) collective-permute-start(f32[10,64,128]{2,1,0:T(8,128)S(1)} %get-tuple-element.56), channel_id=1, source_target_pairs={{4,0},{2,1},{6,2},{0,3},{1,4},{7,5},{3,6},{5,7},{12,8},{10,9},{14,... | collective-permute-start | bytes 983048 | tf_op jit(solution)/shard_map/ppermute | solution.py:511
  113.0 2.1 %collective-permute-start.21 = (f32[10,64,128]{2,1,0:T(8,128)S(1)}, f32[10,64,128]{2,1,0:T(8,128)S(1)}, u32[]{:S(2)}, u32[]{:S(2)}) collective-permute-start(f32[10,64,128]{2,1,0:T(8,128)S(1)} %get-tuple-element.57), channel_id=1, source_target_pairs={{6,0},{0,1},{4,2},{2,3},{3,4},{5,5},{1,6},{7,7},{14,8},{8,9},{12,1... | collective-permute-start | bytes 983048 | tf_op jit(solution)/shard_map/ppermute | solution.py:511
  115.2 6.1 %edge_kernel.5 = (f32[2,64,1280]{2,1,0:T(8,128)S(1)}, f32[2,64,1280]{2,1,0:T(8,128)S(1)}) custom-call(f32[2,72,1280]{2,1,0:T(8,128)S(1)} %collective-permute-done.12.up, f32[2,72,1280]{2,1,0:T(8,128)S(1)} %get-tuple-element.47.top, f32[4,72,1280]{2,1,0:T(8,128)S(1)} %inner_kernel.4.inner, f32[2,72,1280]{2,1,0:T(8,128)S(1)} %get-tuple-element.46.bottom, ...), custom_call_target="tpu_custom_call" | custom-call | flops 6000000000 | bytes 8000000 | tf_op jit(solution)/shard_map/edge_kernel/pallas_call | solution.py:464
  122.7 4.2 %collective-permute-start.16 = (f32[10,64,128]{2,1,0:T(8,128)S(1)}, f32[10,64,128]{2,1,0:T(8,128)S(1)}, u32[]{:S(2)}, u32[]{:S(2)}) collective-permute-start(f32[10,64,128]{2,1,0:T(8,128)S(1)} %get-tuple-element.52), channel_id=1, source_target_pairs={{4,0},{2,1},{6,2},{0,3},{1,4},{7,5},{3,6},{5,7},{12,8},{10,9},{14,... | collective-permute-start | bytes 983048 | tf_op jit(solution)/shard_map/ppermute | solution.py:511
  126.9 2.7 %collective-permute-start.17 = (f32[10,64,128]{2,1,0:T(8,128)S(1)}, f32[10,64,128]{2,1,0:T(8,128)S(1)}, u32[]{:S(2)}, u32[]{:S(2)}) collective-permute-start(f32[10,64,128]{2,1,0:T(8,128)S(1)} %get-tuple-element.53), channel_id=1, source_target_pairs={{6,0},{0,1},{4,2},{2,3},{3,4},{5,5},{1,6},{7,7},{14,8},{8,9},{12,1... | collective-permute-start | bytes 983048 | tf_op jit(solution)/shard_map/ppermute | solution.py:511
  129.6 5.5 %collective-permute-done.15.refs_1_ = f32[10,64,128]{2,1,0:T(8,128)S(1)} collective-permute-done((f32[10,64,128]{2,1,0:T(8,128)S(1)}, f32[10,64,128]{2,1,0:T(8,128)S(1)}, u32[]{:S(2)}, u32[]{:S(2)}) %collective-permute-start.15) | collective-permute-done | bytes 327712 | tf_op jit(solution)/shard_map/ppermute | solution.py:511
  135.2 3.7 %collective-permute-done.16.refs_2_ = f32[10,64,128]{2,1,0:T(8,128)S(1)} collective-permute-done((f32[10,64,128]{2,1,0:T(8,128)S(1)}, f32[10,64,128]{2,1,0:T(8,128)S(1)}, u32[]{:S(2)}, u32[]{:S(2)}) %collective-permute-start.16) | collective-permute-done | bytes 327712 | tf_op jit(solution)/shard_map/ppermute | solution.py:511
  138.9 5.1 %collective-permute-done.17.refs_3_ = f32[10,64,128]{2,1,0:T(8,128)S(1)} collective-permute-done((f32[10,64,128]{2,1,0:T(8,128)S(1)}, f32[10,64,128]{2,1,0:T(8,128)S(1)}, u32[]{:S(2)}, u32[]{:S(2)}) %collective-permute-start.17) | collective-permute-done | bytes 327712 | tf_op jit(solution)/shard_map/ppermute | solution.py:511
  144.0 2.7 %restore.1 = (f32[2304,256]{1,0:T(8,128)}, f32[256,256]{1,0:T(8,128)}) custom-call(s32[1]{0:T(128)} %bitcast.odd, s32[1]{0:T(128)} %bitcast.1.part, f32[10,64,128]{2,1,0:T(8,128)S(1)} %collective-permute-done.14.refs_0_, f32[10,64,128]{2,1,0:T(8,128)S(1)} %collective-permute-done.15.refs_1_, f32[10,64,128]{2,1,0:T(8,128)S(1)} %collective-permute-done.16.refs_2_, ...), custom_call_target="tpu_custom_call" | custom-call | tf_op jit(solution)/shard_map/restore/pallas_call | solution.py:513
  (45 shorter events, 7.7 us)
Async XLA Ops:
  0.6 1.7 %copy-start = (f32[288,8,256]{2,1,0:T(8,128)S(1)}, f32[288,8,256]{2,1,0:T(8,128)}, u32[]{:S(2)}) copy-start(f32[288,8,256]{2,1,0:T(8,128)} %param.6) | copy-start | bytes 7077892
  2.3 0.9 copy-start.1
  3.3 0.7 copy-start.2
  4.0 33.9 %copy-start.3 = (bf16[1152,1152]{1,0:T(8,128)(2,1)S(1)}, bf16[1152,1152]{1,0:T(8,128)(2,1)}, u32[]{:S(2)}) copy-start(bf16[1152,1152]{1,0:T(8,128)(2,1)} %linear.1) | copy-start | bytes 7962628
  4.0 33.9 %copy-start.5 = (bf16[128,1152]{1,0:T(8,128)(2,1)S(1)}, bf16[128,1152]{1,0:T(8,128)(2,1)}, u32[]{:S(2)}) copy-start(bf16[128,1152]{1,0:T(8,128)(2,1)} %drift.1) | copy-start | bytes 884740
  5.0 9.5 %collective-permute-start = (f32[808,128]{1,0:T(8,128)S(1)}, f32[808,128]{1,0:T(8,128)S(1)}, u32[]{:S(2)}, u32[]{:S(2)}) collective-permute-start(f32[808,128]{1,0:T(8,128)S(1)} %get-tuple-element.31), channel_id=1, source_target_pairs={{0,0},{1,6},{2,2},{3,4},{4,5},{5,3},{6,7},{7,1},{8,8},{9,14},{10,1... | collective-permute-start | bytes 1241096 | tf_op jit(solution)/shard_map/ppermute | solution.py:431
  5.7 16.5 %collective-permute-start.1 = (f32[808,128]{1,0:T(8,128)S(1)}, f32[808,128]{1,0:T(8,128)S(1)}, u32[]{:S(2)}, u32[]{:S(2)}) collective-permute-start(f32[808,128]{1,0:T(8,128)S(1)} %get-tuple-element.32), channel_id=1, source_target_pairs={{0,2},{1,4},{2,0},{3,6},{4,7},{5,1},{6,5},{7,3},{8,10},{9,12},{10,... | collective-permute-start | bytes 1241096 | tf_op jit(solution)/shard_map/ppermute | solution.py:431
  8.8 15.3 %collective-permute-start.2 = (f32[808,128]{1,0:T(8,128)S(1)}, f32[808,128]{1,0:T(8,128)S(1)}, u32[]{:S(2)}, u32[]{:S(2)}) collective-permute-start(f32[808,128]{1,0:T(8,128)S(1)} %get-tuple-element.33), channel_id=1, source_target_pairs={{0,4},{1,2},{2,6},{3,0},{4,1},{5,7},{6,3},{7,5},{8,12},{9,10},{10,... | collective-permute-start | bytes 1241096 | tf_op jit(solution)/shard_map/ppermute | solution.py:431
  10.9 18.1 %collective-permute-start.3 = (f32[808,128]{1,0:T(8,128)S(1)}, f32[808,128]{1,0:T(8,128)S(1)}, u32[]{:S(2)}, u32[]{:S(2)}) collective-permute-start(f32[808,128]{1,0:T(8,128)S(1)} %get-tuple-element.34), channel_id=1, source_target_pairs={{0,6},{1,0},{2,4},{3,2},{4,3},{5,5},{6,1},{7,7},{8,14},{9,8},{10,1... | collective-permute-start | bytes 1241096 | tf_op jit(solution)/shard_map/ppermute | solution.py:431
  29.7 29.2 %collective-permute-start.4 = (f32[2,80,1408]{2,1,0:T(8,128)S(1)}, f32[2,80,1408]{2,1,0:T(8,128)S(1)}, u32[]{:S(2)}, u32[]{:S(2)}) collective-permute-start(f32[2,80,1408]{2,1,0:T(8,128)S(1)} %get-tuple-element.35.bottom), channel_id=1, source_target_pairs={{0,1},{2,3},{4,5},{6,7},{1,8},{3,10},{5,12},{7,14},{8,9},{10,11},{... | collective-permute-start | bytes 2703368 | tf_op jit(solution)/shard_map/ppermute | solution.py:483
  29.8 29.2 %collective-permute-start.9 = (f32[2,80,1408]{2,1,0:T(8,128)S(1)}, f32[2,80,1408]{2,1,0:T(8,128)S(1)}, u32[]{:S(2)}, u32[]{:S(2)}) collective-permute-start(f32[2,80,1408]{2,1,0:T(8,128)S(1)} %get-tuple-element.36.top), channel_id=1, source_target_pairs={{1,0},{3,2},{5,4},{7,6},{8,1},{10,3},{12,5},{14,7},{9,8},{11,10},{... | collective-permute-start | bytes 2703368 | tf_op jit(solution)/shard_map/ppermute | solution.py:484
  33.3 8.1 %collective-permute-start.5 = (f32[800,128]{1,0:T(8,128)S(1)}, f32[800,128]{1,0:T(8,128)S(1)}, u32[]{:S(2)}, u32[]{:S(2)}) collective-permute-start(f32[800,128]{1,0:T(8,128)S(1)} %get-tuple-element.37), channel_id=1, source_target_pairs={{0,0},{1,6},{2,2},{3,4},{4,5},{5,3},{6,7},{7,1},{8,8},{9,14},{10,1... | collective-permute-start | bytes 1228808 | tf_op jit(solution)/shard_map/ppermute | solution.py:431
  33.9 19.1 %collective-permute-start.6 = (f32[800,128]{1,0:T(8,128)S(1)}, f32[800,128]{1,0:T(8,128)S(1)}, u32[]{:S(2)}, u32[]{:S(2)}) collective-permute-start(f32[800,128]{1,0:T(8,128)S(1)} %get-tuple-element.38), channel_id=1, source_target_pairs={{0,2},{1,4},{2,0},{3,6},{4,7},{5,1},{6,5},{7,3},{8,10},{9,12},{10,... | collective-permute-start | bytes 1228808 | tf_op jit(solution)/shard_map/ppermute | solution.py:431
  35.5 17.6 %collective-permute-start.7 = (f32[800,128]{1,0:T(8,128)S(1)}, f32[800,128]{1,0:T(8,128)S(1)}, u32[]{:S(2)}, u32[]{:S(2)}) collective-permute-start(f32[800,128]{1,0:T(8,128)S(1)} %get-tuple-element.39), channel_id=1, source_target_pairs={{0,4},{1,2},{2,6},{3,0},{4,1},{5,7},{6,3},{7,5},{8,12},{9,10},{10,... | collective-permute-start | bytes 1228808 | tf_op jit(solution)/shard_map/ppermute | solution.py:431
  37.9 1.8 %copy-start.4 = (bf16[1152,1152]{1,0:T(8,128)(2,1)S(1)}, bf16[1152,1152]{1,0:T(8,128)(2,1)}, u32[]{:S(2)}) copy-start(bf16[1152,1152]{1,0:T(8,128)(2,1)} %square.1) | copy-start | bytes 7962628
  41.4 17.0 %collective-permute-start.8 = (f32[800,128]{1,0:T(8,128)S(1)}, f32[800,128]{1,0:T(8,128)S(1)}, u32[]{:S(2)}, u32[]{:S(2)}) collective-permute-start(f32[800,128]{1,0:T(8,128)S(1)} %get-tuple-element.40), channel_id=1, source_target_pairs={{0,6},{1,0},{2,4},{3,2},{4,3},{5,5},{6,1},{7,7},{8,14},{9,8},{10,1... | collective-permute-start | bytes 1228808 | tf_op jit(solution)/shard_map/ppermute | solution.py:431
  65.8 20.3 %collective-permute-start.10 = (f32[2,72,1280]{2,1,0:T(8,128)S(1)}, f32[2,72,1280]{2,1,0:T(8,128)S(1)}, u32[]{:S(2)}, u32[]{:S(2)}) collective-permute-start(f32[2,72,1280]{2,1,0:T(8,128)S(1)} %get-tuple-element.44.bottom), channel_id=1, source_target_pairs={{0,1},{2,3},{4,5},{6,7},{1,8},{3,10},{5,12},{7,14},{8,9},{10,11},{... | collective-permute-start | bytes 2211848 | tf_op jit(solution)/shard_map/ppermute | solution.py:483
  66.1 20.0 %collective-permute-start.11 = (f32[2,72,1280]{2,1,0:T(8,128)S(1)}, f32[2,72,1280]{2,1,0:T(8,128)S(1)}, u32[]{:S(2)}, u32[]{:S(2)}) collective-permute-start(f32[2,72,1280]{2,1,0:T(8,128)S(1)} %get-tuple-element.45.top), channel_id=1, source_target_pairs={{1,0},{3,2},{5,4},{7,6},{8,1},{10,3},{12,5},{14,7},{9,8},{11,10},{... | collective-permute-start | bytes 2211848 | tf_op jit(solution)/shard_map/ppermute | solution.py:484
  92.4 20.6 %collective-permute-start.12 = (f32[2,72,1280]{2,1,0:T(8,128)S(1)}, f32[2,72,1280]{2,1,0:T(8,128)S(1)}, u32[]{:S(2)}, u32[]{:S(2)}) collective-permute-start(f32[2,72,1280]{2,1,0:T(8,128)S(1)} %get-tuple-element.46.bottom), channel_id=1, source_target_pairs={{0,1},{2,3},{4,5},{6,7},{1,8},{3,10},{5,12},{7,14},{8,9},{10,11},{... | collective-permute-start | bytes 2211848 | tf_op jit(solution)/shard_map/ppermute | solution.py:483
  92.5 22.6 %collective-permute-start.13 = (f32[2,72,1280]{2,1,0:T(8,128)S(1)}, f32[2,72,1280]{2,1,0:T(8,128)S(1)}, u32[]{:S(2)}, u32[]{:S(2)}) collective-permute-start(f32[2,72,1280]{2,1,0:T(8,128)S(1)} %get-tuple-element.47.top), channel_id=1, source_target_pairs={{1,0},{3,2},{5,4},{7,6},{8,1},{10,3},{12,5},{14,7},{9,8},{11,10},{... | collective-permute-start | bytes 2211848 | tf_op jit(solution)/shard_map/ppermute | solution.py:484
  107.2 15.0 %collective-permute-start.18 = (f32[10,64,128]{2,1,0:T(8,128)S(1)}, f32[10,64,128]{2,1,0:T(8,128)S(1)}, u32[]{:S(2)}, u32[]{:S(2)}) collective-permute-start(f32[10,64,128]{2,1,0:T(8,128)S(1)} %get-tuple-element.54), channel_id=1, source_target_pairs={{0,0},{6,1},{2,2},{4,3},{5,4},{3,5},{7,6},{1,7},{8,8},{14,9},{10,1... | collective-permute-start | bytes 983048 | tf_op jit(solution)/shard_map/ppermute | solution.py:511
  107.9 14.8 %collective-permute-start.19 = (f32[10,64,128]{2,1,0:T(8,128)S(1)}, f32[10,64,128]{2,1,0:T(8,128)S(1)}, u32[]{:S(2)}, u32[]{:S(2)}) collective-permute-start(f32[10,64,128]{2,1,0:T(8,128)S(1)} %get-tuple-element.55), channel_id=1, source_target_pairs={{2,0},{4,1},{0,2},{6,3},{7,4},{1,5},{5,6},{3,7},{10,8},{12,9},{8,1... | collective-permute-start | bytes 983048 | tf_op jit(solution)/shard_map/ppermute | solution.py:511
  108.0 18.9 %collective-permute-start.20 = (f32[10,64,128]{2,1,0:T(8,128)S(1)}, f32[10,64,128]{2,1,0:T(8,128)S(1)}, u32[]{:S(2)}, u32[]{:S(2)}) collective-permute-start(f32[10,64,128]{2,1,0:T(8,128)S(1)} %get-tuple-element.56), channel_id=1, source_target_pairs={{4,0},{2,1},{6,2},{0,3},{1,4},{7,5},{3,6},{5,7},{12,8},{10,9},{14,... | collective-permute-start | bytes 983048 | tf_op jit(solution)/shard_map/ppermute | solution.py:511
  113.0 16.6 %collective-permute-start.21 = (f32[10,64,128]{2,1,0:T(8,128)S(1)}, f32[10,64,128]{2,1,0:T(8,128)S(1)}, u32[]{:S(2)}, u32[]{:S(2)}) collective-permute-start(f32[10,64,128]{2,1,0:T(8,128)S(1)} %get-tuple-element.57), channel_id=1, source_target_pairs={{6,0},{0,1},{4,2},{2,3},{3,4},{5,5},{1,6},{7,7},{14,8},{8,9},{12,1... | collective-permute-start | bytes 983048 | tf_op jit(solution)/shard_map/ppermute | solution.py:511
  121.6 8.0 %collective-permute-start.14 = (f32[10,64,128]{2,1,0:T(8,128)S(1)}, f32[10,64,128]{2,1,0:T(8,128)S(1)}, u32[]{:S(2)}, u32[]{:S(2)}) collective-permute-start(f32[10,64,128]{2,1,0:T(8,128)S(1)} %get-tuple-element.50), channel_id=1, source_target_pairs={{0,0},{6,1},{2,2},{4,3},{5,4},{3,5},{7,6},{1,7},{8,8},{14,9},{10,1... | collective-permute-start | bytes 983048 | tf_op jit(solution)/shard_map/ppermute | solution.py:511
  122.3 12.9 %collective-permute-start.15 = (f32[10,64,128]{2,1,0:T(8,128)S(1)}, f32[10,64,128]{2,1,0:T(8,128)S(1)}, u32[]{:S(2)}, u32[]{:S(2)}) collective-permute-start(f32[10,64,128]{2,1,0:T(8,128)S(1)} %get-tuple-element.51), channel_id=1, source_target_pairs={{2,0},{4,1},{0,2},{6,3},{7,4},{1,5},{5,6},{3,7},{10,8},{12,9},{8,1... | collective-permute-start | bytes 983048 | tf_op jit(solution)/shard_map/ppermute | solution.py:511
  122.7 16.2 %collective-permute-start.16 = (f32[10,64,128]{2,1,0:T(8,128)S(1)}, f32[10,64,128]{2,1,0:T(8,128)S(1)}, u32[]{:S(2)}, u32[]{:S(2)}) collective-permute-start(f32[10,64,128]{2,1,0:T(8,128)S(1)} %get-tuple-element.52), channel_id=1, source_target_pairs={{4,0},{2,1},{6,2},{0,3},{1,4},{7,5},{3,6},{5,7},{12,8},{10,9},{14,... | collective-permute-start | bytes 983048 | tf_op jit(solution)/shard_map/ppermute | solution.py:511
  126.9 17.1 %collective-permute-start.17 = (f32[10,64,128]{2,1,0:T(8,128)S(1)}, f32[10,64,128]{2,1,0:T(8,128)S(1)}, u32[]{:S(2)}, u32[]{:S(2)}) collective-permute-start(f32[10,64,128]{2,1,0:T(8,128)S(1)} %get-tuple-element.53), channel_id=1, source_target_pairs={{6,0},{0,1},{4,2},{2,3},{3,4},{5,5},{1,6},{7,7},{14,8},{8,9},{12,1... | collective-permute-start | bytes 983048 | tf_op jit(solution)/shard_map/ppermute | solution.py:511

commit v4 on v3

--- a/solution.py
+++ b/solution.py
@@ -22,6 +22,7 @@
 EDGE = 2
 VMEM = pl.BlockSpec(memory_space=pltpu.VMEM)
 SMEM = pl.BlockSpec(memory_space=pltpu.SMEM)
+ANY = pl.BlockSpec(memory_space=pl.ANY)
 F32 = jnp.float32
 BF16 = jnp.bfloat16
 
@@ -122,6 +123,7 @@
     got, outs = refs[:B], refs[B:]
     E = z.C + 2 * PAD
     if rows == z.edge_rows:
+        outs = outs[1:]
         sea = outs[-1]
         outs = outs[:-1]
         at = z.slabs(rows) * E
@@ -229,9 +231,16 @@
     put(drift_weights, 0, slice(0, LANES), turned)
 
 
-def advance(z, groups, outs, cut, sea_at, speed, weights, drift_weights, moved, moved_twice):
+def advance(
+    z, sea_rows, rows, outs, cut, sea_at, speed, weights, drift_weights, moved, moved_twice,
+    known=None, kept=None,
+):
     NB, CH, L = z.NB, z.CH, z.L
-    E = groups[0][1][0][0].shape[1]
+    known, kept = known or {}, kept or {}
+    n = len(rows)
+    first = [r for r in range(1, n - 1) if r not in known]
+    assert first == list(range(first[0], first[-1] + 1))
+    E = rows[0][0].shape[1]
     N = E - 2 * cut
     keep = slice(cut, cut + N)
     sea_cols = pl.ds(sea_at, E)
@@ -240,28 +249,27 @@
     def sea_row(place):
         return place[0][place[1], sea_cols]
 
-    for g, (sea_rows, rows) in enumerate(groups):
-        n = len(rows)
-        tops = [ref[i, :, NB:CH] for ref, i in rows]
-        for r in range(n):
-            moved[g, 0, r] = DOPPLER * jnp.tanh(jnp.broadcast_to(tops[r][:, 0:1], (E, LANES)))
-            moved[g, 1, r] = DOPPLER * jnp.tanh(jnp.broadcast_to(tops[r][:, L : L + 1], (E, LANES)))
-
-    def advect(g, sea_rows, read, write, first, last, speed_cx, speed_cy):
+    for r in range(min(first[0] - 1, 1), max(first[-1] + 2, n - 1)):
+        ref, i = rows[r]
+        surface = ref[i, :, NB:CH]
+        moved[0, r] = DOPPLER * jnp.tanh(jnp.broadcast_to(surface[:, 0:1], (E, LANES)))
+        moved[1, r] = DOPPLER * jnp.tanh(jnp.broadcast_to(surface[:, L : L + 1], (E, LANES)))
+
+    def advect(read, write, start, stop, speed_cx, speed_cy):
         def along_x(r):
             energy = read(r)
-            speed_x = speed_cx + moved[g, 0, r]
+            speed_x = speed_cx + moved[0, r]
             return (
                 energy,
                 jnp.maximum(speed_x, 0.0) * energy,
                 jnp.minimum(speed_x, 0.0) * energy,
             )
 
-        _, plus_before, _ = along_x(first - 1)
-        energy, plus, minus = along_x(first)
-        for r in range(first, last):
+        _, plus_before, _ = along_x(start - 1)
+        energy, plus, minus = along_x(start)
+        for r in range(start, stop):
             energy_next, plus_next, minus_next = along_x(r + 1)
-            speed_y = speed_cy + moved[g, 1, r]
+            speed_y = speed_cy + moved[1, r]
             plus_y = jnp.maximum(speed_y, 0.0) * energy
             minus_y = jnp.minimum(speed_y, 0.0) * energy
             result = (
@@ -279,31 +287,34 @@
         lanes = pl.ds(pl.multiple_of(j * LANES, LANES), LANES)
         speed_cx = speed[0:1, lanes]
         speed_cy = speed[1:2, lanes]
-        done = 0
-        for g, (sea_rows, rows) in enumerate(groups):
-            n = len(rows)
-
-            def read_state(r):
-                ref, i = rows[r]
+
+        def read_first(r):
+            ref, i = rows[r]
+            return ref[i, :, lanes]
+
+        def write_first(r, value):
+            moved[2, r] = value
+            if r in kept:
+                ref, i = kept[r]
+                ref[i, :, lanes] = value
+
+        def read_second(r):
+            if r in known:
+                ref, i = known[r]
                 return ref[i, :, lanes]
-
-            def write_first(r, value):
-                moved[g, 2, r] = value
-
-            def write_second(r, value):
-                moved_twice[done + r - 2, :, lanes] = value[keep]
-
-            advect(g, sea_rows, read_state, write_first, 1, n - 1, speed_cx, speed_cy)
-            advect(
-                g, sea_rows, lambda r: moved[g, 2, r], write_second, 2, n - 2, speed_cx, speed_cy
-            )
-            done += n - 4
+            return moved[2, r]
+
+        def write_second(r, value):
+            moved_twice[r - 2, :, lanes] = value[keep]
+
+        advect(read_first, write_first, first[0], first[-1] + 1, speed_cx, speed_cy)
+        advect(read_second, write_second, 2, n - 2, speed_cx, speed_cy)
         return carry
 
     lax.fori_loop(0, NB // LANES, one_tile, 0)
 
     count = len(places)
-    own_sea = [place for sea_rows, rows in groups for place in sea_rows[2 : len(rows) - 2]]
+    own_sea = sea_rows[2 : n - 2]
     energy = moved_twice[...].reshape(count * N, NB)
     squares = energy * energy
     interaction = jnp.dot(
@@ -319,49 +330,61 @@
 
     comp = (lax.broadcasted_iota(jnp.int32, (1, LANES), 1) // L) % 2
     sign = jnp.where(comp == 0, 1.0, -1.0).astype(F32)
-    i = 0
-    for _, rows in groups:
-        for r in range(2, len(rows) - 2):
-            here, before, after = [
-                rows[r + d][0][rows[r + d][1], :, NB:CH] for d in (0, -1, 1)
-            ]
-            lap = (
-                (after + before)
-                + (pltpu.roll(here, E - 1, axis=0) + pltpu.roll(here, 1, axis=0))
-                - 4.0 * here
-            )[keep]
-            centre = here[keep]
-            other = jnp.where(
-                comp == 0, pltpu.roll(centre, LANES - L, axis=1), pltpu.roll(centre, L, axis=1)
-            )
-            turn = sign * (CORIOLIS * (other + drift[i * N : (i + 1) * N]))
-            ref, at = places[i]
-            ref[at, :, NB:CH] = (
-                centre + DT_OCEAN * (turn + VISCOSITY * lap)
-            ) * sea_row(own_sea[i])[keep]
-            i += 1
+    for i, (out, at) in enumerate(places):
+        here, before, after = [
+            ref[row, :, NB:CH] for ref, row in (rows[i + 2], rows[i + 1], rows[i + 3])
+        ]
+        lap = (
+            (after + before)
+            + (pltpu.roll(here, E - 1, axis=0) + pltpu.roll(here, 1, axis=0))
+            - 4.0 * here
+        )[keep]
+        centre = here[keep]
+        other = jnp.where(
+            comp == 0, pltpu.roll(centre, LANES - L, axis=1), pltpu.roll(centre, L, axis=1)
+        )
+        turn = sign * (CORIOLIS * (other + drift[i * N : (i + 1) * N]))
+        out[at, :, NB:CH] = (
+            centre + DT_OCEAN * (turn + VISCOSITY * lap)
+        ) * sea_row(own_sea[i])[keep]
 
 
 def listed(*refs):
     return [(ref, i) for ref in refs for i in range(ref.shape[0])]
 
 
-def inner_kernel(z, cut, sea_at, top, inner, bottom, sea, *refs):
-    (speed, weights, drift_weights, out, moved, moved_twice) = refs
-    groups = [(listed(sea), listed(top, inner, bottom))]
-    advance(z, groups, [out], cut, sea_at, speed, weights, drift_weights, moved, moved_twice)
-
-
-def edge_kernel(z, cut, sea_at, up, top, inner, bottom, down, sea_up, sea, sea_down, *refs):
-    (speed, weights, drift_weights, new_top, new_bottom, moved, moved_twice) = refs
-    inside = listed(inner)
-    sea_rows = listed(sea_up, sea, sea_down)
-    groups = [
-        (sea_rows[: 3 * EDGE], listed(up, top) + inside[:EDGE]),
-        (sea_rows[-3 * EDGE :], inside[-EDGE:] + listed(bottom, down)),
-    ]
-    outs = [new_top, new_bottom]
-    advance(z, groups, outs, cut, sea_at, speed, weights, drift_weights, moved, moved_twice)
+def inner_kernel(z, cut, sea_at, top, inner, bottom, sea, speed, weights, drift_weights, *refs):
+    out, for_edges, (moved, moved_twice) = refs[0], refs[1:-2], refs[-2:]
+    kept = {}
+    if for_edges:
+        kept = {1 + i: (for_edges[0], i) for i in range(EDGE)}
+        kept |= {z.R - 1 - EDGE + i: (for_edges[1], i) for i in range(EDGE)}
+    advance(
+        z, listed(sea), listed(top, inner, bottom), [out], cut, sea_at, speed, weights,
+        drift_weights, moved, moved_twice, kept=kept,
+    )
+
+
+def top_kernel(z, cut, sea_at, up, top, inner, sea_up, sea, *refs):
+    given, (speed, weights, drift_weights, out, moved, moved_twice) = refs[:-6], refs[-6:]
+    known = {3 + i: (given[0], i) for i in range(EDGE)} if given else {}
+    rows = listed(up, top) + listed(inner)[:EDGE]
+    sea_rows = (listed(sea_up) + listed(sea))[: len(rows)]
+    advance(
+        z, sea_rows, rows, [out], cut, sea_at, speed, weights, drift_weights, moved,
+        moved_twice, known=known,
+    )
+
+
+def bottom_kernel(z, cut, sea_at, down, bottom, inner, sea_down, sea, *refs):
+    given, (speed, weights, drift_weights, out, moved, moved_twice) = refs[:-6], refs[-6:]
+    known = {1 + i: (given[0], i) for i in range(EDGE)} if given else {}
+    rows = listed(inner)[-EDGE:] + listed(bottom, down)
+    sea_rows = (listed(sea) + listed(sea_down))[-len(rows) :]
+    advance(
+        z, sea_rows, rows, [out], cut, sea_at, speed, weights, drift_weights, moved,
+        moved_twice, known=known,
+    )
 
 
 def speeds(z):
@@ -448,30 +471,32 @@
         return pl.pallas_call(
             functools.partial(unpack_kernel, z, rows),
             out_shape=[jax.ShapeDtypeStruct((n, width, lanes), F32) for n, lanes in shapes],
-            in_specs=[SMEM] * 2 + [VMEM] * B,
+            in_specs=[SMEM] * 2 + [VMEM] * B + [ANY] * (len(received) - B),
             out_specs=[VMEM] * len(shapes),
             compiler_params=params(16),
             name="unpack",
         )(*who, *received)
 
     top, bottom, sea = unpack(
-        z.edge_rows, got[:B], [(EDGE, CH + LANES), (EDGE, CH + LANES), (R, LANES)]
+        z.edge_rows, got[: B + 1], [(EDGE, CH + LANES), (EDGE, CH + LANES), (R, LANES)]
     )
     (inner,) = unpack(z.inner_rows, got[B:], [(R - 2 * EDGE, CH)])
 
-    def step_call(body, width, cut, sea_at, counts, groups, deepest, inputs):
+    def step_call(body, cut, sea_at, count, deepest, inputs, more=0):
+        width = inputs[0].shape[1]
         n = width - 2 * cut
+        shapes = [(count, n, CH)] + [(EDGE, width, NB)] * more
         return pl.pallas_call(
             functools.partial(body, z, cut, sea_at),
-            out_shape=[jax.ShapeDtypeStruct((k, n, CH), F32) for k in counts],
+            out_shape=[jax.ShapeDtypeStruct(shape, F32) for shape in shapes],
             in_specs=[VMEM] * (len(inputs) + 3),
-            out_specs=[VMEM] * len(counts),
+            out_specs=[VMEM] * len(shapes),
             scratch_shapes=[
-                pltpu.VMEM((groups, 3, deepest, width, LANES), F32),
-                pltpu.VMEM((sum(counts), n, NB), F32),
+                pltpu.VMEM((3, deepest, width, LANES), F32),
+                pltpu.VMEM((count, n, NB), F32),
             ],
-            compiler_params=params(32),
-            cost_estimate=cost(6e9, 8e6),
+            compiler_params=params(24),
+            cost_estimate=cost(count * 1.5e9, count * 2e6),
             name=body.__name__,
         )(*inputs, speed, weights, drift_weights)
 
@@ -480,18 +505,22 @@
         margin = (width - C) // 2
         cut = margin - valid if valid == 0 or (margin - valid) % 4 == 0 else 0
         sea_at = PAD - margin
+        down = lax.ppermute(top, axes, to_prev_row)
         up = lax.ppermute(bottom, axes, to_next_row)
-        down = lax.ppermute(top, axes, to_prev_row)
-        (new_inner,) = step_call(
-            inner_kernel, width, cut, sea_at, (R - 2 * EDGE,), 1, R, (top, inner, bottom, sea)
-        )
         if step == 0:
             sea_up, sea_down = up[:, :, CH:], down[:, :, CH:]
-        top, bottom = step_call(
-            edge_kernel, width, cut, sea_at, (EDGE, EDGE), 2, 3 * EDGE,
-            (up, top, inner, bottom, down, sea_up, sea, sea_down),
+        new_inner, *given = step_call(
+            inner_kernel, cut, sea_at, R - 2 * EDGE, R, (top, inner, bottom, sea),
+            2 if step > 0 else 0,
         )
-        inner = new_inner
+        (new_bottom,) = step_call(
+            bottom_kernel, cut, sea_at, EDGE, 3 * EDGE,
+            (down, bottom, inner, sea_down, sea, *given[1:]),
+        )
+        (new_top,) = step_call(
+            top_kernel, cut, sea_at, EDGE, 3 * EDGE, (up, top, inner, sea_up, sea, *given[:1])
+        )
+        top, inner, bottom = new_top, new_inner, new_bottom
         width -= 2 * cut
 
     def send_back(rows, states):

time: 147 us -> 139 us (0.946)
  waiting for transfers between devices: 45.1 us -> 31.1 us
  starting transfers between devices: 52.2 us -> 58.8 us
    ppermute x8, waiting for transfers between devices: 19.9 us -> 3.94 us  [per_device(): got = [lax.ppermute(packed[i], axes, forward[i % B]) for i in range(2 * B)]]
    ppermute x8, starting transfers between devices: 25.6 us -> 35 us  [per_device(): got = [lax.ppermute(packed[i], axes, forward[i % B]) for i in range(2 * B)]]
    ppermute x3, waiting for transfers between devices: 0.01 us -> 7.21 us  [per_device(): down = lax.ppermute(top, axes, to_prev_row)]
    ppermute x3, starting transfers between devices: 10.3 us -> 5.1 us  [per_device(): down = lax.ppermute(top, axes, to_prev_row)]
    ppermute x3, waiting for transfers between devices: 10.8 us -> 6.72 us  [per_device(): up = lax.ppermute(bottom, axes, to_next_row)]
    pallas_call x6 -> x9, Pallas kernels: 35.9 us -> 34.7 us  [step_call(): pl.pallas_call(functools.partial(body, z, cut, sea_at), out_shape=[jax.Sh...]
  transfers between devices with their start and end apart: 22 -> 22, of which waited for: 8 -> 7; matrix products, arithmetic and copies ran while one was open for 0% -> 0% of each run, Pallas kernels for 17% -> 27%
where the time goes in v4:
time: 139 us; the launch traced here: 138 us
  starting transfers between devices  58.8 us (42%)
  Pallas kernels  41.8 us (30%)
  waiting for transfers between devices  31.1 us (22%)
  local copies, waits for them, and re-layouts  5.23 us (4%)
    ppermute x8, starting transfers between devices, per_device(): got = [lax.ppermute(packed[i], axes, forward[i % B]) for i in range(2 * B)]  35 us
    pallas_call x9, Pallas kernels, step_call(): pl.pallas_call(functools.partial(body, z, cut, sea_at), out_shape=[jax.Sh...  34.7 us
    ppermute x8, starting transfers between devices, per_device(): lax.ppermute(packed[i], axes, [(t, s) for s, t in forward[i % B]])  17 us
    ppermute x8, waiting for transfers between devices, per_device(): lax.ppermute(packed[i], axes, [(t, s) for s, t in forward[i % B]])  13.2 us
    ppermute x3, waiting for transfers between devices, per_device(): down = lax.ppermute(top, axes, to_prev_row)  7.21 us
    ppermute x3, waiting for transfers between devices, per_device(): up = lax.ppermute(bottom, axes, to_next_row)  6.72 us
    ppermute x3, starting transfers between devices, per_device(): down = lax.ppermute(top, axes, to_prev_row)  5.1 us
    unnamed x12, local copies, waits for them, and re-layouts  5.06 us
  transfers between devices with their start and end apart: 22, of which 7 were waited for; matrix products, arithmetic and copies ran while one was open for 0% of the time, Pallas kernels for 27%

profile of v4, /device:TPU:0, one launch (start us, length us, event | category | flops | bytes accessed | tf_op | source)
XLA Modules:
  0.0 138.2 jit_solution(13041231926265867618)
XLA Ops:
  0.7 1.7 %copy-done = f32[288,8,256]{2,1,0:T(8,128)S(1)} copy-done((f32[288,8,256]{2,1,0:T(8,128)S(1)}, f32[288,8,256]{2,1,0:T(8,128)}, u32[]{:S(2)}) %copy-start) | copy-done | bytes 2359320
  4.0 1.1 pack.1
  5.7 3.0 %collective-permute-start.1 = (f32[808,128]{1,0:T(8,128)S(1)}, f32[808,128]{1,0:T(8,128)S(1)}, u32[]{:S(2)}, u32[]{:S(2)}) collective-permute-start(f32[808,128]{1,0:T(8,128)S(1)} %get-tuple-element.32), channel_id=1, source_target_pairs={{0,2},{1,4},{2,0},{3,6},{4,7},{5,1},{6,5},{7,3},{8,10},{9,12},{10,... | collective-permute-start | bytes 1241096 | tf_op jit(solution)/shard_map/ppermute | solution.py:454
  8.8 2.2 %collective-permute-start.2 = (f32[808,128]{1,0:T(8,128)S(1)}, f32[808,128]{1,0:T(8,128)S(1)}, u32[]{:S(2)}, u32[]{:S(2)}) collective-permute-start(f32[808,128]{1,0:T(8,128)S(1)} %get-tuple-element.33), channel_id=1, source_target_pairs={{0,4},{1,2},{2,6},{3,0},{4,1},{5,7},{6,3},{7,5},{8,12},{9,10},{10,... | collective-permute-start | bytes 1241096 | tf_op jit(solution)/shard_map/ppermute | solution.py:454
  10.9 3.6 %collective-permute-start.3 = (f32[808,128]{1,0:T(8,128)S(1)}, f32[808,128]{1,0:T(8,128)S(1)}, u32[]{:S(2)}, u32[]{:S(2)}) collective-permute-start(f32[808,128]{1,0:T(8,128)S(1)} %get-tuple-element.34), channel_id=1, source_target_pairs={{0,6},{1,0},{2,4},{3,2},{4,3},{5,5},{6,1},{7,7},{8,14},{9,8},{10,1... | collective-permute-start | bytes 1241096 | tf_op jit(solution)/shard_map/ppermute | solution.py:454
  15.6 1.6 %collective-permute-start.6 = (f32[800,128]{1,0:T(8,128)S(1)}, f32[800,128]{1,0:T(8,128)S(1)}, u32[]{:S(2)}, u32[]{:S(2)}) collective-permute-start(f32[800,128]{1,0:T(8,128)S(1)} %get-tuple-element.38), channel_id=1, source_target_pairs={{0,2},{1,4},{2,0},{3,6},{4,7},{5,1},{6,5},{7,3},{8,10},{9,12},{10,... | collective-permute-start | bytes 1228808 | tf_op jit(solution)/shard_map/ppermute | solution.py:454
  17.2 18.7 %collective-permute-start.7 = (f32[800,128]{1,0:T(8,128)S(1)}, f32[800,128]{1,0:T(8,128)S(1)}, u32[]{:S(2)}, u32[]{:S(2)}) collective-permute-start(f32[800,128]{1,0:T(8,128)S(1)} %get-tuple-element.39), channel_id=1, source_target_pairs={{0,4},{1,2},{2,6},{3,0},{4,1},{5,7},{6,3},{7,5},{8,12},{9,10},{10,... | collective-permute-start | bytes 1228808 | tf_op jit(solution)/shard_map/ppermute | solution.py:454
  35.9 4.6 %collective-permute-start.8 = (f32[800,128]{1,0:T(8,128)S(1)}, f32[800,128]{1,0:T(8,128)S(1)}, u32[]{:S(2)}, u32[]{:S(2)}) collective-permute-start(f32[800,128]{1,0:T(8,128)S(1)} %get-tuple-element.40), channel_id=1, source_target_pairs={{0,6},{1,0},{2,4},{3,2},{4,3},{5,5},{6,1},{7,7},{8,14},{9,8},{10,1... | collective-permute-start | bytes 1228808 | tf_op jit(solution)/shard_map/ppermute | solution.py:454
  41.1 1.1 collective-permute-start.10
  42.3 1.7 %copy-done.4 = bf16[1152,1152]{1,0:T(8,128)(2,1)S(1)} copy-done((bf16[1152,1152]{1,0:T(8,128)(2,1)S(1)}, bf16[1152,1152]{1,0:T(8,128)(2,1)}, u32[]{:S(2)}) %copy-start.4) | copy-done | bytes 2654232
  44.1 1.5 %weights.1 = (bf16[2304,1152]{1,0:T(8,128)(2,1)S(1)}, bf16[1152,128]{1,0:T(8,128)(2,1)S(1)}) custom-call(bf16[1152,1152]{1,0:T(8,128)(2,1)S(1)} %copy-done.3, bf16[1152,1152]{1,0:T(8,128)(2,1)S(1)} %copy-done.4, bf16[128,1152]{1,0:T(8,128)(2,1)S(1)} %copy-done.5), custom_call_target="tpu_custom_call" | custom-call | flops 2000000000 | bytes 10616832 | tf_op jit(solution)/shard_map/weights/pallas_call | solution.py:456
  45.6 3.9 %collective-permute-done.8.refs_3_ = f32[800,128]{1,0:T(8,128)S(1)} collective-permute-done((f32[800,128]{1,0:T(8,128)S(1)}, f32[800,128]{1,0:T(8,128)S(1)}, u32[]{:S(2)}, u32[]{:S(2)}) %collective-permute-start.8) | collective-permute-done | bytes 409632 | tf_op jit(solution)/shard_map/ppermute | solution.py:454
  50.0 5.9 %inner_kernel.3.inner = f32[4,72,1280]{2,1,0:T(8,128)S(1)} custom-call(f32[2,80,1408]{2,1,0:T(8,128)S(1)} %get-tuple-element.37.top, f32[4,80,1280]{2,1,0:T(8,128)S(1)} %unpack.3.inner, f32[2,80,1408]{2,1,0:T(8,128)S(1)} %get-tuple-element.36.bottom, f32[8,80,128]{2,1,0:T(8,128)S(1)} %get-tuple-element.41.sea, ...), custom_call_target="tpu_custom_call" | custom-call | flops 6000000000 | bytes 8000000 | tf_op jit(solution)/shard_map/inner_kernel/pallas_call | solution.py:489
  56.0 6.6 %collective-permute-done.10.down = f32[2,80,1408]{2,1,0:T(8,128)S(1)} collective-permute-done((f32[2,80,1408]{2,1,0:T(8,128)S(1)}, f32[2,80,1408]{2,1,0:T(8,128)S(1)}, u32[]{:S(2)}, u32[]{:S(2)}) %collective-permute-start.10) | collective-permute-done | bytes 901152 | tf_op jit(solution)/shard_map/ppermute | solution.py:508
  62.6 3.6 %bottom_kernel.3.bottom = f32[2,72,1280]{2,1,0:T(8,128)S(1)} custom-call(f32[2,80,1408]{2,1,0:T(8,128)S(1)} %collective-permute-done.10.down, f32[2,80,1408]{2,1,0:T(8,128)S(1)} %get-tuple-element.36.bottom, f32[4,80,1280]{2,1,0:T(8,128)S(1)} %unpack.3.inner, f32[2,80,128]{2,1,0:T(8,128)S(1)} %slice.9.sea_down, f32[8,80,128]{2,1,0:T(8,128)S(1)} %get-tuple-element.41.sea, ...), custom_call_target="tpu_custom_call" | custom-call | flops 3000000000 | bytes 4000000 | tf_op jit(solution)/shard_map/bottom_kernel/pallas_call | solution.py:489
  66.2 3.6 %top_kernel.3.top = f32[2,72,1280]{2,1,0:T(8,128)S(1)} custom-call(f32[2,80,1408]{2,1,0:T(8,128)S(1)} %collective-permute-done.5.up, f32[2,80,1408]{2,1,0:T(8,128)S(1)} %get-tuple-element.37.top, f32[4,80,1280]{2,1,0:T(8,128)S(1)} %unpack.3.inner, f32[2,80,128]{2,1,0:T(8,128)S(1)} %slice.8.sea_up, f32[8,80,128]{2,1,0:T(8,128)S(1)} %get-tuple-element.41.sea, ...), custom_call_target="tpu_custom_call" | custom-call | flops 3000000000 | bytes 4000000 | tf_op jit(solution)/shard_map/top_kernel/pallas_call | solution.py:489
  69.8 3.9 %collective-permute-start.9 = (f32[2,72,1280]{2,1,0:T(8,128)S(1)}, f32[2,72,1280]{2,1,0:T(8,128)S(1)}, u32[]{:S(2)}, u32[]{:S(2)}) collective-permute-start(f32[2,72,1280]{2,1,0:T(8,128)S(1)} %top_kernel.3.top), channel_id=1, source_target_pairs={{1,0},{3,2},{5,4},{7,6},{8,1},{10,3},{12,5},{14,7},{9,8},{11,10},{... | collective-permute-start | bytes 2211848 | tf_op jit(solution)/shard_map/ppermute | solution.py:508
  73.7 5.5 %inner_kernel.4 = (f32[4,72,1280]{2,1,0:T(8,128)S(1)}, f32[2,72,1152]{2,1,0:T(8,128)S(1)}, f32[2,72,1152]{2,1,0:T(8,128)S(1)}) custom-call(f32[2,72,1280]{2,1,0:T(8,128)S(1)} %top_kernel.3.top, f32[4,72,1280]{2,1,0:T(8,128)S(1)} %inner_kernel.3.inner, f32[2,72,1280]{2,1,0:T(8,128)S(1)} %bottom_kernel.3.bottom, f32[8,80,128]{2,1,0:T(8,128)S(1)} %get-tuple-element.41.sea, ...), custom_call_target="tpu_custom_call" | custom-call | flops 6000000000 | bytes 8000000 | tf_op jit(solution)/shard_map/inner_kernel/pallas_call | solution.py:489
  79.3 3.1 %collective-permute-done.12.up = f32[2,72,1280]{2,1,0:T(8,128)S(1)} collective-permute-done((f32[2,72,1280]{2,1,0:T(8,128)S(1)}, f32[2,72,1280]{2,1,0:T(8,128)S(1)}, u32[]{:S(2)}, u32[]{:S(2)}) %collective-permute-start.12) | collective-permute-done | bytes 737312 | tf_op jit(solution)/shard_map/ppermute | solution.py:509
  82.4 2.7 %top_kernel.4.top = f32[2,72,1280]{2,1,0:T(8,128)S(1)} custom-call(f32[2,72,1280]{2,1,0:T(8,128)S(1)} %collective-permute-done.12.up, f32[2,72,1280]{2,1,0:T(8,128)S(1)} %top_kernel.3.top, f32[4,72,1280]{2,1,0:T(8,128)S(1)} %inner_kernel.3.inner, f32[2,80,128]{2,1,0:T(8,128)S(1)} %slice.8.sea_up, f32[8,80,128]{2,1,0:T(8,128)S(1)} %get-tuple-element.41.sea, ...), custom_call_target="tpu_custom_call" | custom-call | flops 3000000000 | bytes 4000000 | tf_op jit(solution)/shard_map/top_kernel/pallas_call | solution.py:489
  85.2 2.8 %bottom_kernel.4.bottom = f32[2,72,1280]{2,1,0:T(8,128)S(1)} custom-call(f32[2,72,1280]{2,1,0:T(8,128)S(1)} %collective-permute-done.9.down, f32[2,72,1280]{2,1,0:T(8,128)S(1)} %bottom_kernel.3.bottom, f32[4,72,1280]{2,1,0:T(8,128)S(1)} %inner_kernel.3.inner, f32[2,80,128]{2,1,0:T(8,128)S(1)} %slice.9.sea_down, f32[8,80,128]{2,1,0:T(8,128)S(1)} %get-tuple-element.41.sea, ...), custom_call_target="tpu_custom_call" | custom-call | flops 3000000000 | bytes 4000000 | tf_op jit(solution)/shard_map/bottom_kernel/pallas_call | solution.py:489
  88.0 1.6 %collective-permute-start.11 = (f32[2,72,1280]{2,1,0:T(8,128)S(1)}, f32[2,72,1280]{2,1,0:T(8,128)S(1)}, u32[]{:S(2)}, u32[]{:S(2)}) collective-permute-start(f32[2,72,1280]{2,1,0:T(8,128)S(1)} %bottom_kernel.4.bottom), channel_id=1, source_target_pairs={{0,1},{2,3},{4,5},{6,7},{1,8},{3,10},{5,12},{7,14},{8,9},{10,11},{... | collective-permute-start | bytes 2211848 | tf_op jit(solution)/shard_map/ppermute | solution.py:509
  89.6 5.3 %inner_kernel.5 = (f32[4,64,1280]{2,1,0:T(8,128)S(1)}, f32[2,72,1152]{2,1,0:T(8,128)S(1)}, f32[2,72,1152]{2,1,0:T(8,128)S(1)}) custom-call(f32[2,72,1280]{2,1,0:T(8,128)S(1)} %top_kernel.4.top, f32[4,72,1280]{2,1,0:T(8,128)S(1)} %get-tuple-element.46.inner, f32[2,72,1280]{2,1,0:T(8,128)S(1)} %bottom_kernel.4.bottom, ...), custom_call_target="tpu_custom_call" | custom-call | flops 6000000000 | bytes 8000000 | tf_op jit(solution)/shard_map/inner_kernel/pallas_call | solution.py:489
  98.2 2.9 %collective-permute-start.21 = (f32[10,64,128]{2,1,0:T(8,128)S(1)}, f32[10,64,128]{2,1,0:T(8,128)S(1)}, u32[]{:S(2)}, u32[]{:S(2)}) collective-permute-start(f32[10,64,128]{2,1,0:T(8,128)S(1)} %get-tuple-element.57), channel_id=1, source_target_pairs={{6,0},{0,1},{4,2},{2,3},{3,4},{5,5},{1,6},{7,7},{14,8},{8,9},{12,1... | collective-permute-start | bytes 983048 | tf_op jit(solution)/shard_map/ppermute | solution.py:540
  101.1 2.7 %bottom_kernel.5.refs_1_ = f32[2,64,1280]{2,1,0:T(8,128)S(1)} custom-call(f32[2,72,1280]{2,1,0:T(8,128)S(1)} %collective-permute-done.13.down, f32[2,72,1280]{2,1,0:T(8,128)S(1)} %bottom_kernel.4.bottom, f32[4,72,1280]{2,1,0:T(8,128)S(1)} %get-tuple-element.46.inner, f32[2,80,128]{2,1,0:T(8,128)S(1)} %slice.9.sea_down, ...), custom_call_target="tpu_custom_call" | custom-call | flops 3000000000 | bytes 4000000 | tf_op jit(solution)/shard_map/bottom_kernel/pallas_call | solution.py:489
  103.8 3.6 %collective-permute-done.11.up = f32[2,72,1280]{2,1,0:T(8,128)S(1)} collective-permute-done((f32[2,72,1280]{2,1,0:T(8,128)S(1)}, f32[2,72,1280]{2,1,0:T(8,128)S(1)}, u32[]{:S(2)}, u32[]{:S(2)}) %collective-permute-start.11) | collective-permute-done | bytes 737312 | tf_op jit(solution)/shard_map/ppermute | solution.py:509
  107.4 2.6 %top_kernel.5.refs_0_ = f32[2,64,1280]{2,1,0:T(8,128)S(1)} custom-call(f32[2,72,1280]{2,1,0:T(8,128)S(1)} %collective-permute-done.11.up, f32[2,72,1280]{2,1,0:T(8,128)S(1)} %top_kernel.4.top, f32[4,72,1280]{2,1,0:T(8,128)S(1)} %get-tuple-element.46.inner, f32[2,80,128]{2,1,0:T(8,128)S(1)} %slice.8.sea_up, f32[8,80,128]{2,1,0:T(8,128)S(1)} %get-tuple-element.41.sea, ...), custom_call_target="tpu_custom_call" | custom-call | flops 3000000000 | bytes 4000000 | tf_op jit(solution)/shard_map/top_kernel/pallas_call | solution.py:489
  111.2 9.1 %collective-permute-start.16 = (f32[10,64,128]{2,1,0:T(8,128)S(1)}, f32[10,64,128]{2,1,0:T(8,128)S(1)}, u32[]{:S(2)}, u32[]{:S(2)}) collective-permute-start(f32[10,64,128]{2,1,0:T(8,128)S(1)} %get-tuple-element.51), channel_id=1, source_target_pairs={{4,0},{2,1},{6,2},{0,3},{1,4},{7,5},{3,6},{5,7},{12,8},{10,9},{14,... | collective-permute-start | bytes 983048 | tf_op jit(solution)/shard_map/ppermute | solution.py:540
  120.4 1.9 %collective-permute-start.17 = (f32[10,64,128]{2,1,0:T(8,128)S(1)}, f32[10,64,128]{2,1,0:T(8,128)S(1)}, u32[]{:S(2)}, u32[]{:S(2)}) collective-permute-start(f32[10,64,128]{2,1,0:T(8,128)S(1)} %get-tuple-element.52), channel_id=1, source_target_pairs={{6,0},{0,1},{4,2},{2,3},{3,4},{5,5},{1,6},{7,7},{14,8},{8,9},{12,1... | collective-permute-start | bytes 983048 | tf_op jit(solution)/shard_map/ppermute | solution.py:540
  122.3 9.2 %collective-permute-done.16.refs_2_ = f32[10,64,128]{2,1,0:T(8,128)S(1)} collective-permute-done((f32[10,64,128]{2,1,0:T(8,128)S(1)}, f32[10,64,128]{2,1,0:T(8,128)S(1)}, u32[]{:S(2)}, u32[]{:S(2)}) %collective-permute-start.16) | collective-permute-done | bytes 327712 | tf_op jit(solution)/shard_map/ppermute | solution.py:540
  131.5 4.0 %collective-permute-done.17.refs_3_ = f32[10,64,128]{2,1,0:T(8,128)S(1)} collective-permute-done((f32[10,64,128]{2,1,0:T(8,128)S(1)}, f32[10,64,128]{2,1,0:T(8,128)S(1)}, u32[]{:S(2)}, u32[]{:S(2)}) %collective-permute-start.17) | collective-permute-done | bytes 327712 | tf_op jit(solution)/shard_map/ppermute | solution.py:540
  135.5 2.7 %restore.1 = (f32[2304,256]{1,0:T(8,128)}, f32[256,256]{1,0:T(8,128)}) custom-call(s32[1]{0:T(128)} %bitcast.odd, s32[1]{0:T(128)} %bitcast.1.part, f32[10,64,128]{2,1,0:T(8,128)S(1)} %collective-permute-done.14.refs_0_, f32[10,64,128]{2,1,0:T(8,128)S(1)} %collective-permute-done.15.refs_1_, f32[10,64,128]{2,1,0:T(8,128)S(1)} %collective-permute-done.16.refs_2_, ...), custom_call_target="tpu_custom_call" | custom-call | tf_op jit(solution)/shard_map/restore/pallas_call | solution.py:542
  (48 shorter events, 9.2 us)
Async XLA Ops:
  0.6 1.7 %copy-start = (f32[288,8,256]{2,1,0:T(8,128)S(1)}, f32[288,8,256]{2,1,0:T(8,128)}, u32[]{:S(2)}) copy-start(f32[288,8,256]{2,1,0:T(8,128)} %param.6) | copy-start | bytes 7077892
  2.3 0.9 copy-start.1
  3.3 0.7 copy-start.2
  4.0 38.4 %copy-start.3 = (bf16[1152,1152]{1,0:T(8,128)(2,1)S(1)}, bf16[1152,1152]{1,0:T(8,128)(2,1)}, u32[]{:S(2)}) copy-start(bf16[1152,1152]{1,0:T(8,128)(2,1)} %linear.1) | copy-start | bytes 7962628
  4.0 38.4 %copy-start.5 = (bf16[128,1152]{1,0:T(8,128)(2,1)S(1)}, bf16[128,1152]{1,0:T(8,128)(2,1)}, u32[]{:S(2)}) copy-start(bf16[128,1152]{1,0:T(8,128)(2,1)} %drift.1) | copy-start | bytes 884740
  5.0 12.2 %collective-permute-start = (f32[808,128]{1,0:T(8,128)S(1)}, f32[808,128]{1,0:T(8,128)S(1)}, u32[]{:S(2)}, u32[]{:S(2)}) collective-permute-start(f32[808,128]{1,0:T(8,128)S(1)} %get-tuple-element.31), channel_id=1, source_target_pairs={{0,0},{1,6},{2,2},{3,4},{4,5},{5,3},{6,7},{7,1},{8,8},{9,14},{10,1... | collective-permute-start | bytes 1241096 | tf_op jit(solution)/shard_map/ppermute | solution.py:454
  5.7 30.2 %collective-permute-start.1 = (f32[808,128]{1,0:T(8,128)S(1)}, f32[808,128]{1,0:T(8,128)S(1)}, u32[]{:S(2)}, u32[]{:S(2)}) collective-permute-start(f32[808,128]{1,0:T(8,128)S(1)} %get-tuple-element.32), channel_id=1, source_target_pairs={{0,2},{1,4},{2,0},{3,6},{4,7},{5,1},{6,5},{7,3},{8,10},{9,12},{10,... | collective-permute-start | bytes 1241096 | tf_op jit(solution)/shard_map/ppermute | solution.py:454
  8.8 31.7 %collective-permute-start.2 = (f32[808,128]{1,0:T(8,128)S(1)}, f32[808,128]{1,0:T(8,128)S(1)}, u32[]{:S(2)}, u32[]{:S(2)}) collective-permute-start(f32[808,128]{1,0:T(8,128)S(1)} %get-tuple-element.33), channel_id=1, source_target_pairs={{0,4},{1,2},{2,6},{3,0},{4,1},{5,7},{6,3},{7,5},{8,12},{9,10},{10,... | collective-permute-start | bytes 1241096 | tf_op jit(solution)/shard_map/ppermute | solution.py:454
  10.9 29.6 %collective-permute-start.3 = (f32[808,128]{1,0:T(8,128)S(1)}, f32[808,128]{1,0:T(8,128)S(1)}, u32[]{:S(2)}, u32[]{:S(2)}) collective-permute-start(f32[808,128]{1,0:T(8,128)S(1)} %get-tuple-element.34), channel_id=1, source_target_pairs={{0,6},{1,0},{2,4},{3,2},{4,3},{5,5},{6,1},{7,7},{8,14},{9,8},{10,1... | collective-permute-start | bytes 1241096 | tf_op jit(solution)/shard_map/ppermute | solution.py:454
  14.6 1.1 collective-permute-start.4
  15.6 30.0 %collective-permute-start.6 = (f32[800,128]{1,0:T(8,128)S(1)}, f32[800,128]{1,0:T(8,128)S(1)}, u32[]{:S(2)}, u32[]{:S(2)}) collective-permute-start(f32[800,128]{1,0:T(8,128)S(1)} %get-tuple-element.38), channel_id=1, source_target_pairs={{0,2},{1,4},{2,0},{3,6},{4,7},{5,1},{6,5},{7,3},{8,10},{9,12},{10,... | collective-permute-start | bytes 1228808 | tf_op jit(solution)/shard_map/ppermute | solution.py:454
  17.2 28.4 %collective-permute-start.7 = (f32[800,128]{1,0:T(8,128)S(1)}, f32[800,128]{1,0:T(8,128)S(1)}, u32[]{:S(2)}, u32[]{:S(2)}) collective-permute-start(f32[800,128]{1,0:T(8,128)S(1)} %get-tuple-element.39), channel_id=1, source_target_pairs={{0,4},{1,2},{2,6},{3,0},{4,1},{5,7},{6,3},{7,5},{8,12},{9,10},{10,... | collective-permute-start | bytes 1228808 | tf_op jit(solution)/shard_map/ppermute | solution.py:454
  35.9 13.6 %collective-permute-start.8 = (f32[800,128]{1,0:T(8,128)S(1)}, f32[800,128]{1,0:T(8,128)S(1)}, u32[]{:S(2)}, u32[]{:S(2)}) collective-permute-start(f32[800,128]{1,0:T(8,128)S(1)} %get-tuple-element.40), channel_id=1, source_target_pairs={{0,6},{1,0},{2,4},{3,2},{4,3},{5,5},{6,1},{7,7},{8,14},{9,8},{10,1... | collective-permute-start | bytes 1228808 | tf_op jit(solution)/shard_map/ppermute | solution.py:454
  41.1 21.4 %collective-permute-start.10 = (f32[2,80,1408]{2,1,0:T(8,128)S(1)}, f32[2,80,1408]{2,1,0:T(8,128)S(1)}, u32[]{:S(2)}, u32[]{:S(2)}) collective-permute-start(f32[2,80,1408]{2,1,0:T(8,128)S(1)} %get-tuple-element.37.top), channel_id=1, source_target_pairs={{1,0},{3,2},{5,4},{7,6},{8,1},{10,3},{12,5},{14,7},{9,8},{11,10},{... | collective-permute-start | bytes 2703368 | tf_op jit(solution)/shard_map/ppermute | solution.py:508
  42.3 23.9 %collective-permute-start.5 = (f32[2,80,1408]{2,1,0:T(8,128)S(1)}, f32[2,80,1408]{2,1,0:T(8,128)S(1)}, u32[]{:S(2)}, u32[]{:S(2)}) collective-permute-start(f32[2,80,1408]{2,1,0:T(8,128)S(1)} %get-tuple-element.36.bottom), channel_id=1, source_target_pairs={{0,1},{2,3},{4,5},{6,7},{1,8},{3,10},{5,12},{7,14},{8,9},{10,11},{... | collective-permute-start | bytes 2703368 | tf_op jit(solution)/shard_map/ppermute | solution.py:509
  42.3 1.8 %copy-start.4 = (bf16[1152,1152]{1,0:T(8,128)(2,1)S(1)}, bf16[1152,1152]{1,0:T(8,128)(2,1)}, u32[]{:S(2)}) copy-start(bf16[1152,1152]{1,0:T(8,128)(2,1)} %square.1) | copy-start | bytes 7962628
  66.1 16.2 %collective-permute-start.12 = (f32[2,72,1280]{2,1,0:T(8,128)S(1)}, f32[2,72,1280]{2,1,0:T(8,128)S(1)}, u32[]{:S(2)}, u32[]{:S(2)}) collective-permute-start(f32[2,72,1280]{2,1,0:T(8,128)S(1)} %bottom_kernel.3.bottom), channel_id=1, source_target_pairs={{0,1},{2,3},{4,5},{6,7},{1,8},{3,10},{5,12},{7,14},{8,9},{10,11},{... | collective-permute-start | bytes 2211848 | tf_op jit(solution)/shard_map/ppermute | solution.py:509
  69.8 15.4 %collective-permute-start.9 = (f32[2,72,1280]{2,1,0:T(8,128)S(1)}, f32[2,72,1280]{2,1,0:T(8,128)S(1)}, u32[]{:S(2)}, u32[]{:S(2)}) collective-permute-start(f32[2,72,1280]{2,1,0:T(8,128)S(1)} %top_kernel.3.top), channel_id=1, source_target_pairs={{1,0},{3,2},{5,4},{7,6},{8,1},{10,3},{12,5},{14,7},{9,8},{11,10},{... | collective-permute-start | bytes 2211848 | tf_op jit(solution)/shard_map/ppermute | solution.py:508
  85.1 13.1 %collective-permute-start.13 = (f32[2,72,1280]{2,1,0:T(8,128)S(1)}, f32[2,72,1280]{2,1,0:T(8,128)S(1)}, u32[]{:S(2)}, u32[]{:S(2)}) collective-permute-start(f32[2,72,1280]{2,1,0:T(8,128)S(1)} %top_kernel.4.top), channel_id=1, source_target_pairs={{1,0},{3,2},{5,4},{7,6},{8,1},{10,3},{12,5},{14,7},{9,8},{11,10},{... | collective-permute-start | bytes 2211848 | tf_op jit(solution)/shard_map/ppermute | solution.py:508
  88.0 19.5 %collective-permute-start.11 = (f32[2,72,1280]{2,1,0:T(8,128)S(1)}, f32[2,72,1280]{2,1,0:T(8,128)S(1)}, u32[]{:S(2)}, u32[]{:S(2)}) collective-permute-start(f32[2,72,1280]{2,1,0:T(8,128)S(1)} %bottom_kernel.4.bottom), channel_id=1, source_target_pairs={{0,1},{2,3},{4,5},{6,7},{1,8},{3,10},{5,12},{7,14},{8,9},{10,11},{... | collective-permute-start | bytes 2211848 | tf_op jit(solution)/shard_map/ppermute | solution.py:509
  95.2 15.9 %collective-permute-start.18 = (f32[10,64,128]{2,1,0:T(8,128)S(1)}, f32[10,64,128]{2,1,0:T(8,128)S(1)}, u32[]{:S(2)}, u32[]{:S(2)}) collective-permute-start(f32[10,64,128]{2,1,0:T(8,128)S(1)} %get-tuple-element.54), channel_id=1, source_target_pairs={{0,0},{6,1},{2,2},{4,3},{5,4},{3,5},{7,6},{1,7},{8,8},{14,9},{10,1... | collective-permute-start | bytes 983048 | tf_op jit(solution)/shard_map/ppermute | solution.py:540
  95.9 15.3 %collective-permute-start.19 = (f32[10,64,128]{2,1,0:T(8,128)S(1)}, f32[10,64,128]{2,1,0:T(8,128)S(1)}, u32[]{:S(2)}, u32[]{:S(2)}) collective-permute-start(f32[10,64,128]{2,1,0:T(8,128)S(1)} %get-tuple-element.55), channel_id=1, source_target_pairs={{2,0},{4,1},{0,2},{6,3},{7,4},{1,5},{5,6},{3,7},{10,8},{12,9},{8,1... | collective-permute-start | bytes 983048 | tf_op jit(solution)/shard_map/ppermute | solution.py:540
  96.7 23.7 %collective-permute-start.20 = (f32[10,64,128]{2,1,0:T(8,128)S(1)}, f32[10,64,128]{2,1,0:T(8,128)S(1)}, u32[]{:S(2)}, u32[]{:S(2)}) collective-permute-start(f32[10,64,128]{2,1,0:T(8,128)S(1)} %get-tuple-element.56), channel_id=1, source_target_pairs={{4,0},{2,1},{6,2},{0,3},{1,4},{7,5},{3,6},{5,7},{12,8},{10,9},{14,... | collective-permute-start | bytes 983048 | tf_op jit(solution)/shard_map/ppermute | solution.py:540
  98.2 24.0 %collective-permute-start.21 = (f32[10,64,128]{2,1,0:T(8,128)S(1)}, f32[10,64,128]{2,1,0:T(8,128)S(1)}, u32[]{:S(2)}, u32[]{:S(2)}) collective-permute-start(f32[10,64,128]{2,1,0:T(8,128)S(1)} %get-tuple-element.57), channel_id=1, source_target_pairs={{6,0},{0,1},{4,2},{2,3},{3,4},{5,5},{1,6},{7,7},{14,8},{8,9},{12,1... | collective-permute-start | bytes 983048 | tf_op jit(solution)/shard_map/ppermute | solution.py:540
  110.5 11.8 %collective-permute-start.14 = (f32[10,64,128]{2,1,0:T(8,128)S(1)}, f32[10,64,128]{2,1,0:T(8,128)S(1)}, u32[]{:S(2)}, u32[]{:S(2)}) collective-permute-start(f32[10,64,128]{2,1,0:T(8,128)S(1)} %get-tuple-element.49), channel_id=1, source_target_pairs={{0,0},{6,1},{2,2},{4,3},{5,4},{3,5},{7,6},{1,7},{8,8},{14,9},{10,1... | collective-permute-start | bytes 983048 | tf_op jit(solution)/shard_map/ppermute | solution.py:540
  111.2 11.1 %collective-permute-start.15 = (f32[10,64,128]{2,1,0:T(8,128)S(1)}, f32[10,64,128]{2,1,0:T(8,128)S(1)}, u32[]{:S(2)}, u32[]{:S(2)}) collective-permute-start(f32[10,64,128]{2,1,0:T(8,128)S(1)} %get-tuple-element.50), channel_id=1, source_target_pairs={{2,0},{4,1},{0,2},{6,3},{7,4},{1,5},{5,6},{3,7},{10,8},{12,9},{8,1... | collective-permute-start | bytes 983048 | tf_op jit(solution)/shard_map/ppermute | solution.py:540
  111.2 20.3 %collective-permute-start.16 = (f32[10,64,128]{2,1,0:T(8,128)S(1)}, f32[10,64,128]{2,1,0:T(8,128)S(1)}, u32[]{:S(2)}, u32[]{:S(2)}) collective-permute-start(f32[10,64,128]{2,1,0:T(8,128)S(1)} %get-tuple-element.51), channel_id=1, source_target_pairs={{4,0},{2,1},{6,2},{0,3},{1,4},{7,5},{3,6},{5,7},{12,8},{10,9},{14,... | collective-permute-start | bytes 983048 | tf_op jit(solution)/shard_map/ppermute | solution.py:540
  120.4 15.1 %collective-permute-start.17 = (f32[10,64,128]{2,1,0:T(8,128)S(1)}, f32[10,64,128]{2,1,0:T(8,128)S(1)}, u32[]{:S(2)}, u32[]{:S(2)}) collective-permute-start(f32[10,64,128]{2,1,0:T(8,128)S(1)} %get-tuple-element.52), channel_id=1, source_target_pairs={{6,0},{0,1},{4,2},{2,3},{3,4},{5,5},{1,6},{7,7},{14,8},{8,9},{12,1... | collective-permute-start | bytes 983048 | tf_op jit(solution)/shard_map/ppermute | solution.py:540

commit v5 on v4

--- a/solution.py
+++ b/solution.py
@@ -22,7 +22,7 @@
 EDGE = 2
 VMEM = pl.BlockSpec(memory_space=pltpu.VMEM)
 SMEM = pl.BlockSpec(memory_space=pltpu.SMEM)
-ANY = pl.BlockSpec(memory_space=pl.ANY)
+HBM = pl.BlockSpec(memory_space=pltpu.HBM)
 F32 = jnp.float32
 BF16 = jnp.bfloat16
 
@@ -79,19 +79,25 @@
 
 def pack_kernel(z, odd, part, spec_in, ocean_in, mask, *refs):
     B, R, C, W, mt = z.B, z.R, z.C, z.W, z.mt
-    outs, (spec, ocean, wide) = refs[: 2 * B], refs[2 * B :]
+    outs, (spec, ocean, wide, sems) = refs[: 2 * B], refs[2 * B :]
     E = C + 2 * PAD
     at = 0
+    copies = []
+    for half in range(W // LANES):
+        cols = pl.ds(half * LANES, LANES)
+        for n, (src, dst) in enumerate(((spec_in, spec), (ocean_in, ocean))):
+            copies.append(pltpu.make_async_copy(src.at[:, cols], dst.at[half], sems.at[n, half]))
+            copies[-1].start()
     sea = mask[...].astype(F32)
     sea = jnp.concatenate([sea, jnp.zeros((R, LANES), F32)], axis=1)
-    for half in range(W // LANES):
-        spec[half] = spec_in[:, half * LANES : (half + 1) * LANES]
-        ocean[half] = ocean_in[:, half * LANES : (half + 1) * LANES]
     wide[:, 0:PAD, :] = jnp.zeros((wide.shape[0], PAD, LANES), F32)
     wide[:, PAD + W : W + 2 * PAD, :] = jnp.zeros((wide.shape[0], PAD, LANES), F32)
     for which, rows in enumerate((z.edge_rows, z.inner_rows)):
         folds, slabs = z.folds(rows)
         for half in range(W // LANES):
+            if which == 0:
+                for copy in copies[2 * half : 2 * half + 2]:
+                    copy.wait()
             cols = slice(PAD + half * LANES, PAD + (half + 1) * LANES)
             for i, r in enumerate(rows):
                 for t in range(mt):
@@ -118,21 +124,20 @@
         at += slabs
 
 
+def spread_line(line):
+    return jnp.broadcast_to(line, (LANES, LANES)).T
+
+
 def unpack_kernel(z, rows, odd, part, *refs):
     B, mt = z.B, z.mt
     got, outs = refs[:B], refs[B:]
     E = z.C + 2 * PAD
     if rows == z.edge_rows:
-        outs = outs[1:]
         sea = outs[-1]
         outs = outs[:-1]
-        at = z.slabs(rows) * E
+        lines = got[0][z.slabs(rows) * E : z.slabs(rows) * E + z.R]
         for r in range(z.R):
-            line = jnp.broadcast_to(got[0][at + r : at + r + 1], (LANES, LANES))
-            sea[r] = line.T[:E]
-        for ref, first in zip(outs, (0, z.R - EDGE)):
-            for i in range(EDGE):
-                ref[i, :, z.CH :] = sea[first + i]
+            sea[r] = spread_line(lines[r : r + 1])[:E]
     places = [(ref, i) for ref in outs for i in range(ref.shape[0])]
     src = [exchange_part(z, k, odd[0], part[0]) for k in range(B)]
     for k in range(B):
@@ -150,6 +155,10 @@
                 moved = pltpu.roll(got[k][slab * E : (slab + 1) * E], shift, axis=1)
                 tile = jnp.where(group == src[k], moved, tile)
             ref[at, :, lane : lane + LANES] = tile
+    if rows == z.edge_rows:
+        for i, (ref, at) in enumerate(places):
+            r = rows[i]
+            ref[at, 0:1, 0:LANES] = lines[r : r + 1]
 
 
 def send_back_kernel(z, rows, odd, part, *refs):
@@ -353,7 +362,7 @@
     return [(ref, i) for ref in refs for i in range(ref.shape[0])]
 
 
-def inner_kernel(z, cut, sea_at, top, inner, bottom, sea, speed, weights, drift_weights, *refs):
+def inner_kernel(z, first, cut, sea_at, top, inner, bottom, sea, speed, weights, drift_weights, *refs):
     out, for_edges, (moved, moved_twice) = refs[0], refs[1:-2], refs[-2:]
     kept = {}
     if for_edges:
@@ -365,8 +374,17 @@
     )
 
 
-def top_kernel(z, cut, sea_at, up, top, inner, sea_up, sea, *refs):
-    given, (speed, weights, drift_weights, out, moved, moved_twice) = refs[:-6], refs[-6:]
+def read_sea(halo, sea):
+    for i in range(EDGE):
+        sea[i] = spread_line(halo[i, 0:1, 0:LANES])[: halo.shape[1]]
+    return sea
+
+
+def top_kernel(z, first, cut, sea_at, up, top, inner, sea, *refs):
+    inputs, outs = refs[:-4] if first else refs[:-3], refs[-4:] if first else refs[-3:]
+    *given, speed, weights, drift_weights = inputs
+    out, moved, moved_twice = outs[0], outs[-2], outs[-1]
+    sea_up = read_sea(up, outs[1]) if first else given.pop(0)
     known = {3 + i: (given[0], i) for i in range(EDGE)} if given else {}
     rows = listed(up, top) + listed(inner)[:EDGE]
     sea_rows = (listed(sea_up) + listed(sea))[: len(rows)]
@@ -376,8 +394,11 @@
     )
 
 
-def bottom_kernel(z, cut, sea_at, down, bottom, inner, sea_down, sea, *refs):
-    given, (speed, weights, drift_weights, out, moved, moved_twice) = refs[:-6], refs[-6:]
+def bottom_kernel(z, first, cut, sea_at, down, bottom, inner, sea, *refs):
+    inputs, outs = refs[:-4] if first else refs[:-3], refs[-4:] if first else refs[-3:]
+    *given, speed, weights, drift_weights = inputs
+    out, moved, moved_twice = outs[0], outs[-2], outs[-1]
+    sea_down = read_sea(down, outs[1]) if first else given.pop(0)
     known = {1 + i: (given[0], i) for i in range(EDGE)} if given else {}
     rows = listed(inner)[-EDGE:] + listed(bottom, down)
     sea_rows = (listed(sea) + listed(sea_down))[-len(rows) :]
@@ -445,13 +466,17 @@
     packed = pl.pallas_call(
         functools.partial(pack_kernel, z),
         out_shape=blocks,
-        in_specs=[SMEM] * 2 + [VMEM] * 3,
+        in_specs=[SMEM] * 2 + [HBM, HBM, VMEM],
         out_specs=[VMEM] * (2 * B),
-        scratch_shapes=columns_scratch + [pltpu.VMEM((all_slabs, W + 2 * PAD, LANES), F32)],
-        compiler_params=params(24),
+        scratch_shapes=columns_scratch
+        + [
+            pltpu.VMEM((all_slabs, W + 2 * PAD, LANES), F32),
+            pltpu.SemaphoreType.DMA((2, W // LANES)),
+        ],
+        compiler_params=params(58),
         name="pack",
     )(*who, spectrum.reshape(nb * R, W), ocean.reshape(2 * L * R, W), sea_mask)
-    got = [lax.ppermute(packed[i], axes, forward[i % B]) for i in range(2 * B)]
+    got = [lax.ppermute(packed[k], axes, forward[k]) for k in range(B)]
 
     weights, drift_weights = pl.pallas_call(
         functools.partial(weights_kernel, z),
@@ -466,28 +491,33 @@
         name="weights",
     )(kernel_linear, kernel_square, drift_kernel)
     speed = speeds(z)
+    *got, weights, drift_weights, speed = lax.optimization_barrier(
+        (*got, weights, drift_weights, speed)
+    )
 
     def unpack(rows, received, shapes):
         return pl.pallas_call(
             functools.partial(unpack_kernel, z, rows),
             out_shape=[jax.ShapeDtypeStruct((n, width, lanes), F32) for n, lanes in shapes],
-            in_specs=[SMEM] * 2 + [VMEM] * B + [ANY] * (len(received) - B),
+            in_specs=[SMEM] * 2 + [VMEM] * B,
             out_specs=[VMEM] * len(shapes),
             compiler_params=params(16),
             name="unpack",
         )(*who, *received)
 
     top, bottom, sea = unpack(
-        z.edge_rows, got[: B + 1], [(EDGE, CH + LANES), (EDGE, CH + LANES), (R, LANES)]
+        z.edge_rows, got[:B], [(EDGE, CH), (EDGE, CH), (R, LANES)]
     )
+    *blocks, top = lax.optimization_barrier((*packed[B:], top))
+    got += [lax.ppermute(blocks[k], axes, forward[k]) for k in range(B)]
     (inner,) = unpack(z.inner_rows, got[B:], [(R - 2 * EDGE, CH)])
 
-    def step_call(body, cut, sea_at, count, deepest, inputs, more=0):
+    def step_call(body, first, cut, sea_at, count, deepest, inputs, more=()):
         width = inputs[0].shape[1]
         n = width - 2 * cut
-        shapes = [(count, n, CH)] + [(EDGE, width, NB)] * more
+        shapes = [(count, n, CH)] + [(EDGE, width, lanes) for lanes in more]
         return pl.pallas_call(
-            functools.partial(body, z, cut, sea_at),
+            functools.partial(body, z, first, cut, sea_at),
             out_shape=[jax.ShapeDtypeStruct(shape, F32) for shape in shapes],
             in_specs=[VMEM] * (len(inputs) + 3),
             out_specs=[VMEM] * len(shapes),
@@ -496,10 +526,11 @@
                 pltpu.VMEM((count, n, NB), F32),
             ],
             compiler_params=params(24),
-            cost_estimate=cost(count * 1.5e9, count * 2e6),
+            cost_estimate=cost(count * 1e8, count * 1e5),
             name=body.__name__,
         )(*inputs, speed, weights, drift_weights)
 
+    sea_up, sea_down = [], []
     for step in range(STEPS):
         valid = EDGE * (STEPS - 1 - step)
         margin = (width - C) // 2
@@ -507,19 +538,32 @@
         sea_at = PAD - margin
         down = lax.ppermute(top, axes, to_prev_row)
         up = lax.ppermute(bottom, axes, to_next_row)
-        if step == 0:
-            sea_up, sea_down = up[:, :, CH:], down[:, :, CH:]
-        new_inner, *given = step_call(
-            inner_kernel, cut, sea_at, R - 2 * EDGE, R, (top, inner, bottom, sea),
-            2 if step > 0 else 0,
+        first = step == 0
+
+        def advance_inner():
+            return step_call(
+                inner_kernel, first, cut, sea_at, R - 2 * EDGE, R, (top, inner, bottom, sea),
+                () if first else (NB, NB),
+            )
+
+        given = ()
+        if not first:
+            new_inner, *given = advance_inner()
+        new_bottom, *found = step_call(
+            bottom_kernel, first, cut, sea_at, EDGE, 3 * EDGE,
+            (down, bottom, inner, sea, *sea_down, *given[1:]),
+            (LANES,) if first else (),
         )
-        (new_bottom,) = step_call(
-            bottom_kernel, cut, sea_at, EDGE, 3 * EDGE,
-            (down, bottom, inner, sea_down, sea, *given[1:]),
+        sea_down = sea_down or found
+        new_top, *found = step_call(
+            top_kernel, first, cut, sea_at, EDGE, 3 * EDGE,
+            (up, top, inner, sea, *sea_up, *given[:1]),
+            (LANES,) if first else (),
         )
-        (new_top,) = step_call(
-            top_kernel, cut, sea_at, EDGE, 3 * EDGE, (up, top, inner, sea_up, sea, *given[:1])
-        )
+        sea_up = sea_up or found
+        if first:
+            inner, new_top = lax.optimization_barrier((inner, new_top))
+            (new_inner,) = advance_inner()
         top, inner, bottom = new_top, new_inner, new_bottom
         width -= 2 * cut
 

time: 139 us -> 128 us (0.921)
  starting transfers between devices: 58.8 us -> 42.5 us
  waiting for transfers between devices: 31.1 us -> 36 us
  Pallas kernels: 41.8 us -> 45.1 us
  local copies, waits for them, and re-layouts: 5.23 us -> 2.89 us
    ppermute x8, starting transfers between devices: 35 us -> 17.1 us  [the longest x4 9.52 us: per_device(): got = [lax.ppermute(packed[k], axes, forward[k]) for k in range(B)]]
    ppermute x8, waiting for transfers between devices: 3.94 us -> 19.9 us  [the longest x4 10.1 us: per_device(): got = [lax.ppermute(packed[k], axes, forward[k]) for k in range(B)]]
    ppermute x3, starting transfers between devices: 5.1 us -> 11.8 us  [per_device(): down = lax.ppermute(top, axes, to_prev_row)]
    ppermute x3, waiting for transfers between devices: 6.72 us -> 0.01 us  [per_device(): up = lax.ppermute(bottom, axes, to_next_row)]
    ppermute x3, waiting for transfers between devices: 7.21 us -> 1.9 us  [per_device(): down = lax.ppermute(top, axes, to_prev_row)]
    ppermute x8, starting transfers between devices: 17 us -> 13.2 us  [per_device(): lax.ppermute(packed[i], axes, [(t, s) for s, t in forward[i % B]])]
    pallas_call x1, Pallas kernels: 1.08 us -> 4.6 us  [per_device(): pl.pallas_call(functools.partial(pack_kernel, z), out_shape=blocks, in_sp...]
    unnamed x12 -> x14, local copies, waits for them, and re-layouts: 5.06 us -> 2.73 us
  transfers between devices with their start and end apart: 22 -> 22, of which waited for: 7 -> 8; matrix products, arithmetic and copies ran while one was open for 0% -> 0% of each run, Pallas kernels for 27% -> 29%
where the time goes in v5:
time: 128 us
  Pallas kernels  45.1 us (35%)
  starting transfers between devices  42.5 us (33%)
  waiting for transfers between devices  36 us (28%)
  local copies, waits for them, and re-layouts  2.89 us (2%)
    pallas_call x9, Pallas kernels, step_call(): pl.pallas_call(functools.partial(body, z, first, cut, sea_at), out_shape=...  34.5 us
    ppermute x8, waiting for transfers between devices, per_device(): lax.ppermute(packed[i], axes, [(t, s) for s, t in forward[i % B]])  14.2 us
    ppermute x8, starting transfers between devices, per_device(): lax.ppermute(packed[i], axes, [(t, s) for s, t in forward[i % B]])  13.2 us
    ppermute x3, starting transfers between devices, per_device(): down = lax.ppermute(top, axes, to_prev_row)  11.8 us
    ppermute x4, waiting for transfers between devices, per_device(): got = [lax.ppermute(packed[k], axes, forward[k]) for k in range(B)]  10.1 us
    ppermute x4, waiting for transfers between devices, per_device(): got += [lax.ppermute(blocks[k], axes, forward[k]) for k in range(B)]  9.79 us
    ppermute x4, starting transfers between devices, per_device(): got = [lax.ppermute(packed[k], axes, forward[k]) for k in range(B)]  9.52 us
    ppermute x4, starting transfers between devices, per_device(): got += [lax.ppermute(blocks[k], axes, forward[k]) for k in range(B)]  7.55 us
  transfers between devices with their start and end apart: 22, of which 8 were waited for; matrix products, arithmetic and copies ran while one was open for 0% of the time, Pallas kernels for 29%

profile of v5, /device:TPU:0, one launch (start us, length us, event | category | flops | bytes accessed | tf_op | source)
XLA Modules:
  0.0 127.7 jit_solution(13144305523039518668)
XLA Ops:
  0.7 4.6 %pack.1 = (f32[808,128]{1,0:T(8,128)}, f32[808,128]{1,0:T(8,128)}, f32[808,128]{1,0:T(8,128)}, f32[808,128]{1,0:T(8,128)}, f32[800,128]{1,0:T(8,128)}, /*index=5...) custom-call(s32[1]{0:T(128)} %bitcast.odd, s32[1]{0:T(128)} %bitcast.1.part, f32[2304,256]{1,0:T(8,128)} %bitcast.6, ...), custom_call_target="tpu_custom_call" | custom-call | tf_op jit(solution)/shard_map/pack/pallas_call | solution.py:466
  5.3 1.7 %collective-permute-start = (f32[808,128]{1,0:T(8,128)}, f32[808,128]{1,0:T(8,128)S(1)}, u32[]{:S(2)}, u32[]{:S(2)}) collective-permute-start(f32[808,128]{1,0:T(8,128)} %get-tuple-element.53), channel_id=1, source_target_pairs={{0,0},{1,6},{2,2},{3,4},{4,5},{5,3},{6,7},{7,1},{8,8},{9,14},{10,1... | collective-permute-start | bytes 1241096 | tf_op jit(solution)/shard_map/ppermute | solution.py:479
  6.9 3.0 %collective-permute-start.1 = (f32[808,128]{1,0:T(8,128)}, f32[808,128]{1,0:T(8,128)S(1)}, u32[]{:S(2)}, u32[]{:S(2)}) collective-permute-start(f32[808,128]{1,0:T(8,128)} %get-tuple-element.54), channel_id=1, source_target_pairs={{0,2},{1,4},{2,0},{3,6},{4,7},{5,1},{6,5},{7,3},{8,10},{9,12},{10,... | collective-permute-start | bytes 1241096 | tf_op jit(solution)/shard_map/ppermute | solution.py:479
  9.9 1.3 collective-permute-start.2
  11.1 3.6 %collective-permute-start.3 = (f32[808,128]{1,0:T(8,128)}, f32[808,128]{1,0:T(8,128)S(1)}, u32[]{:S(2)}, u32[]{:S(2)}) collective-permute-start(f32[808,128]{1,0:T(8,128)} %get-tuple-element.56), channel_id=1, source_target_pairs={{0,6},{1,0},{2,4},{3,2},{4,3},{5,5},{6,1},{7,7},{8,14},{9,8},{10,1... | collective-permute-start | bytes 1241096 | tf_op jit(solution)/shard_map/ppermute | solution.py:479
  15.2 1.7 %copy-done.1 = bf16[1152,1152]{1,0:T(8,128)(2,1)S(1)} copy-done((bf16[1152,1152]{1,0:T(8,128)(2,1)S(1)}, bf16[1152,1152]{1,0:T(8,128)(2,1)}, u32[]{:S(2)}) %copy-start.1) | copy-done | bytes 2654232
  16.9 1.0 copy-done.2
  17.9 1.5 %weights.1 = (bf16[2304,1152]{1,0:T(8,128)(2,1)S(1)}, bf16[1152,128]{1,0:T(8,128)(2,1)S(1)}) custom-call(bf16[1152,1152]{1,0:T(8,128)(2,1)S(1)} %copy-done, bf16[1152,1152]{1,0:T(8,128)(2,1)S(1)} %copy-done.1, bf16[128,1152]{1,0:T(8,128)(2,1)S(1)} %copy-done.2), custom_call_target="tpu_custom_call" | custom-call | flops 2000000000 | bytes 10616832 | tf_op jit(solution)/shard_map/weights/pallas_call | solution.py:481
  19.5 6.3 %collective-permute-done.1.refs_1_ = f32[808,128]{1,0:T(8,128)S(1)} collective-permute-done((f32[808,128]{1,0:T(8,128)}, f32[808,128]{1,0:T(8,128)S(1)}, u32[]{:S(2)}, u32[]{:S(2)}) %collective-permute-start.1) | collective-permute-done | bytes 413728 | tf_op jit(solution)/shard_map/ppermute | solution.py:479
  26.3 3.3 %collective-permute-done.3.refs_3_ = f32[808,128]{1,0:T(8,128)S(1)} collective-permute-done((f32[808,128]{1,0:T(8,128)}, f32[808,128]{1,0:T(8,128)S(1)}, u32[]{:S(2)}, u32[]{:S(2)}) %collective-permute-start.3) | collective-permute-done | bytes 413728 | tf_op jit(solution)/shard_map/ppermute | solution.py:479
  31.0 7.9 %collective-permute-start.10 = (f32[2,80,1280]{2,1,0:T(8,128)S(1)}, f32[2,80,1280]{2,1,0:T(8,128)S(1)}, u32[]{:S(2)}, u32[]{:S(2)}) collective-permute-start(f32[2,80,1280]{2,1,0:T(8,128)S(1)} %get-tuple-element.69.top), channel_id=1, source_target_pairs={{1,0},{3,2},{5,4},{7,6},{8,1},{10,3},{12,5},{14,7},{9,8},{11,10},{... | collective-permute-start | bytes 2457608 | tf_op jit(solution)/shard_map/ppermute | solution.py:539
  39.4 6.3 %collective-permute-start.7 = (f32[800,128]{1,0:T(8,128)S(1)}, f32[800,128]{1,0:T(8,128)S(1)}, u32[]{:S(2)}, u32[]{:S(2)}) collective-permute-start(f32[800,128]{1,0:T(8,128)S(1)} %copy-done.3), channel_id=1, source_target_pairs={{0,6},{1,0},{2,4},{3,2},{4,3},{5,5},{6,1},{7,7},{8,14},{9,8},{10,1... | collective-permute-start | bytes 1228808 | tf_op jit(solution)/shard_map/ppermute | solution.py:512
  45.7 9.8 %collective-permute-done.5.refs_1_ = f32[800,128]{1,0:T(8,128)S(1)} collective-permute-done((f32[800,128]{1,0:T(8,128)S(1)}, f32[800,128]{1,0:T(8,128)S(1)}, u32[]{:S(2)}, u32[]{:S(2)}) %collective-permute-start.5) | collective-permute-done | bytes 409632 | tf_op jit(solution)/shard_map/ppermute | solution.py:512
  56.0 3.6 %bottom_kernel.3 = (f32[2,72,1280]{2,1,0:T(8,128)S(1)}, f32[2,80,128]{2,1,0:T(8,128)S(1)}) custom-call(f32[2,80,1280]{2,1,0:T(8,128)S(1)} %collective-permute-done.10.down, f32[2,80,1280]{2,1,0:T(8,128)S(1)} %get-tuple-element.68.bottom, f32[4,80,1280]{2,1,0:T(8,128)S(1)} %unpack.3.inner, f32[8,80,128]{2,1,0:T(8,128)S(1)} %get-tuple-element.70.sea, ...), custom_call_target="tpu_custom_call" | custom-call | flops 200000000 | bytes 200000 | tf_op jit(solution)/shard_map/bottom_kernel/pallas_call | solution.py:519
  59.7 3.6 %top_kernel.3 = (f32[2,72,1280]{2,1,0:T(8,128)S(1)}, f32[2,80,128]{2,1,0:T(8,128)S(1)}) custom-call(f32[2,80,1280]{2,1,0:T(8,128)S(1)} %collective-permute-done.8.up, f32[2,80,1280]{2,1,0:T(8,128)S(1)} %get-tuple-element.69.top, f32[4,80,1280]{2,1,0:T(8,128)S(1)} %unpack.3.inner, f32[8,80,128]{2,1,0:T(8,128)S(1)} %get-tuple-element.70.sea, ...), custom_call_target="tpu_custom_call" | custom-call | flops 200000000 | bytes 200000 | tf_op jit(solution)/shard_map/top_kernel/pallas_call | solution.py:519
  63.3 3.8 %collective-permute-start.9 = (f32[2,72,1280]{2,1,0:T(8,128)S(1)}, f32[2,72,1280]{2,1,0:T(8,128)S(1)}, u32[]{:S(2)}, u32[]{:S(2)}) collective-permute-start(f32[2,72,1280]{2,1,0:T(8,128)S(1)} %get-tuple-element.75.top), channel_id=1, source_target_pairs={{1,0},{3,2},{5,4},{7,6},{8,1},{10,3},{12,5},{14,7},{9,8},{11,10},{... | collective-permute-start | bytes 2211848 | tf_op jit(solution)/shard_map/ppermute | solution.py:539
  67.0 5.8 %inner_kernel.3.inner = f32[4,72,1280]{2,1,0:T(8,128)S(1)} custom-call(f32[2,80,1280]{2,1,0:T(8,128)S(1)} %get-tuple-element.69.top, f32[4,80,1280]{2,1,0:T(8,128)S(1)} %unpack.3.inner, f32[2,80,1280]{2,1,0:T(8,128)S(1)} %get-tuple-element.68.bottom, f32[8,80,128]{2,1,0:T(8,128)S(1)} %get-tuple-element.70.sea, ...), custom_call_target="tpu_custom_call" | custom-call | flops 400000000 | bytes 400000 | tf_op jit(solution)/shard_map/inner_kernel/pallas_call | solution.py:519
  72.9 5.4 %inner_kernel.4 = (f32[4,72,1280]{2,1,0:T(8,128)S(1)}, f32[2,72,1152]{2,1,0:T(8,128)S(1)}, f32[2,72,1152]{2,1,0:T(8,128)S(1)}) custom-call(f32[2,72,1280]{2,1,0:T(8,128)S(1)} %get-tuple-element.75.top, f32[4,72,1280]{2,1,0:T(8,128)S(1)} %inner_kernel.3.inner, f32[2,72,1280]{2,1,0:T(8,128)S(1)} %get-tuple-element.76.bottom, ...), custom_call_target="tpu_custom_call" | custom-call | flops 400000000 | bytes 400000 | tf_op jit(solution)/shard_map/inner_kernel/pallas_call | solution.py:519
  78.3 2.7 %top_kernel.4.top = f32[2,72,1280]{2,1,0:T(8,128)S(1)} custom-call(f32[2,72,1280]{2,1,0:T(8,128)S(1)} %collective-permute-done.12.up, f32[2,72,1280]{2,1,0:T(8,128)S(1)} %get-tuple-element.75.top, f32[4,72,1280]{2,1,0:T(8,128)S(1)} %inner_kernel.3.inner, f32[8,80,128]{2,1,0:T(8,128)S(1)} %get-tuple-element.70.sea, ...), custom_call_target="tpu_custom_call" | custom-call | flops 200000000 | bytes 200000 | tf_op jit(solution)/shard_map/top_kernel/pallas_call | solution.py:519
  81.3 2.8 %bottom_kernel.4.bottom = f32[2,72,1280]{2,1,0:T(8,128)S(1)} custom-call(f32[2,72,1280]{2,1,0:T(8,128)S(1)} %collective-permute-done.9.down, f32[2,72,1280]{2,1,0:T(8,128)S(1)} %get-tuple-element.76.bottom, f32[4,72,1280]{2,1,0:T(8,128)S(1)} %inner_kernel.3.inner, f32[8,80,128]{2,1,0:T(8,128)S(1)} %get-tuple-element.70.sea, ...), custom_call_target="tpu_custom_call" | custom-call | flops 200000000 | bytes 200000 | tf_op jit(solution)/shard_map/bottom_kernel/pallas_call | solution.py:519
  84.5 5.2 %inner_kernel.5 = (f32[4,64,1280]{2,1,0:T(8,128)S(1)}, f32[2,72,1152]{2,1,0:T(8,128)S(1)}, f32[2,72,1152]{2,1,0:T(8,128)S(1)}) custom-call(f32[2,72,1280]{2,1,0:T(8,128)S(1)} %top_kernel.4.top, f32[4,72,1280]{2,1,0:T(8,128)S(1)} %get-tuple-element.82.inner, f32[2,72,1280]{2,1,0:T(8,128)S(1)} %bottom_kernel.4.bottom, ...), custom_call_target="tpu_custom_call" | custom-call | flops 400000000 | bytes 400000 | tf_op jit(solution)/shard_map/inner_kernel/pallas_call | solution.py:519
  91.3 2.5 %collective-permute-start.20 = (f32[10,64,128]{2,1,0:T(8,128)S(1)}, f32[10,64,128]{2,1,0:T(8,128)S(1)}, u32[]{:S(2)}, u32[]{:S(2)}) collective-permute-start(f32[10,64,128]{2,1,0:T(8,128)S(1)} %get-tuple-element.92), channel_id=1, source_target_pairs={{4,0},{2,1},{6,2},{0,3},{1,4},{7,5},{3,6},{5,7},{12,8},{10,9},{14,... | collective-permute-start | bytes 983048 | tf_op jit(solution)/shard_map/ppermute | solution.py:584
  93.8 1.9 %collective-permute-done.13.down = f32[2,72,1280]{2,1,0:T(8,128)S(1)} collective-permute-done((f32[2,72,1280]{2,1,0:T(8,128)S(1)}, f32[2,72,1280]{2,1,0:T(8,128)S(1)}, u32[]{:S(2)}, u32[]{:S(2)}) %collective-permute-start.13) | collective-permute-done | bytes 737312 | tf_op jit(solution)/shard_map/ppermute | solution.py:539
  95.7 2.1 %collective-permute-start.21 = (f32[10,64,128]{2,1,0:T(8,128)S(1)}, f32[10,64,128]{2,1,0:T(8,128)S(1)}, u32[]{:S(2)}, u32[]{:S(2)}) collective-permute-start(f32[10,64,128]{2,1,0:T(8,128)S(1)} %get-tuple-element.93), channel_id=1, source_target_pairs={{6,0},{0,1},{4,2},{2,3},{3,4},{5,5},{1,6},{7,7},{14,8},{8,9},{12,1... | collective-permute-start | bytes 983048 | tf_op jit(solution)/shard_map/ppermute | solution.py:584
  97.8 2.7 %bottom_kernel.5.refs_1_ = f32[2,64,1280]{2,1,0:T(8,128)S(1)} custom-call(f32[2,72,1280]{2,1,0:T(8,128)S(1)} %collective-permute-done.13.down, f32[2,72,1280]{2,1,0:T(8,128)S(1)} %bottom_kernel.4.bottom, f32[4,72,1280]{2,1,0:T(8,128)S(1)} %get-tuple-element.82.inner, f32[8,80,128]{2,1,0:T(8,128)S(1)} %get-tuple-element.70.sea, ...), custom_call_target="tpu_custom_call" | custom-call | flops 200000000 | bytes 200000 | tf_op jit(solution)/shard_map/bottom_kernel/pallas_call | solution.py:519
  100.5 2.6 %top_kernel.5.refs_0_ = f32[2,64,1280]{2,1,0:T(8,128)S(1)} custom-call(f32[2,72,1280]{2,1,0:T(8,128)S(1)} %collective-permute-done.11.up, f32[2,72,1280]{2,1,0:T(8,128)S(1)} %top_kernel.4.top, f32[4,72,1280]{2,1,0:T(8,128)S(1)} %get-tuple-element.82.inner, f32[8,80,128]{2,1,0:T(8,128)S(1)} %get-tuple-element.70.sea, ...), custom_call_target="tpu_custom_call" | custom-call | flops 200000000 | bytes 200000 | tf_op jit(solution)/shard_map/top_kernel/pallas_call | solution.py:519
  105.2 3.7 %collective-permute-start.16 = (f32[10,64,128]{2,1,0:T(8,128)S(1)}, f32[10,64,128]{2,1,0:T(8,128)S(1)}, u32[]{:S(2)}, u32[]{:S(2)}) collective-permute-start(f32[10,64,128]{2,1,0:T(8,128)S(1)} %get-tuple-element.87), channel_id=1, source_target_pairs={{4,0},{2,1},{6,2},{0,3},{1,4},{7,5},{3,6},{5,7},{12,8},{10,9},{14,... | collective-permute-start | bytes 983048 | tf_op jit(solution)/shard_map/ppermute | solution.py:584
  108.9 1.9 %collective-permute-start.17 = (f32[10,64,128]{2,1,0:T(8,128)S(1)}, f32[10,64,128]{2,1,0:T(8,128)S(1)}, u32[]{:S(2)}, u32[]{:S(2)}) collective-permute-start(f32[10,64,128]{2,1,0:T(8,128)S(1)} %get-tuple-element.88), channel_id=1, source_target_pairs={{6,0},{0,1},{4,2},{2,3},{3,4},{5,5},{1,6},{7,7},{14,8},{8,9},{12,1... | collective-permute-start | bytes 983048 | tf_op jit(solution)/shard_map/ppermute | solution.py:584
  110.9 6.2 %collective-permute-done.15.refs_1_ = f32[10,64,128]{2,1,0:T(8,128)S(1)} collective-permute-done((f32[10,64,128]{2,1,0:T(8,128)S(1)}, f32[10,64,128]{2,1,0:T(8,128)S(1)}, u32[]{:S(2)}, u32[]{:S(2)}) %collective-permute-start.15) | collective-permute-done | bytes 327712 | tf_op jit(solution)/shard_map/ppermute | solution.py:584
  117.1 3.5 %collective-permute-done.16.refs_2_ = f32[10,64,128]{2,1,0:T(8,128)S(1)} collective-permute-done((f32[10,64,128]{2,1,0:T(8,128)S(1)}, f32[10,64,128]{2,1,0:T(8,128)S(1)}, u32[]{:S(2)}, u32[]{:S(2)}) %collective-permute-start.16) | collective-permute-done | bytes 327712 | tf_op jit(solution)/shard_map/ppermute | solution.py:584
  120.6 4.5 %collective-permute-done.17.refs_3_ = f32[10,64,128]{2,1,0:T(8,128)S(1)} collective-permute-done((f32[10,64,128]{2,1,0:T(8,128)S(1)}, f32[10,64,128]{2,1,0:T(8,128)S(1)}, u32[]{:S(2)}, u32[]{:S(2)}) %collective-permute-start.17) | collective-permute-done | bytes 327712 | tf_op jit(solution)/shard_map/ppermute | solution.py:584
  125.0 2.7 %restore.1 = (f32[2304,256]{1,0:T(8,128)}, f32[256,256]{1,0:T(8,128)}) custom-call(s32[1]{0:T(128)} %bitcast.odd, s32[1]{0:T(128)} %bitcast.1.part, f32[10,64,128]{2,1,0:T(8,128)S(1)} %collective-permute-done.14.refs_0_, f32[10,64,128]{2,1,0:T(8,128)S(1)} %collective-permute-done.15.refs_1_, f32[10,64,128]{2,1,0:T(8,128)S(1)} %collective-permute-done.16.refs_2_, ...), custom_call_target="tpu_custom_call" | custom-call | tf_op jit(solution)/shard_map/restore/pallas_call | solution.py:586
  (48 shorter events, 7.6 us)
Async XLA Ops:
  0.6 14.5 %copy-start = (bf16[1152,1152]{1,0:T(8,128)(2,1)S(1)}, bf16[1152,1152]{1,0:T(8,128)(2,1)}, u32[]{:S(2)}) copy-start(bf16[1152,1152]{1,0:T(8,128)(2,1)} %linear.1) | copy-start | bytes 7962628
  5.3 14.2 %collective-permute-start = (f32[808,128]{1,0:T(8,128)}, f32[808,128]{1,0:T(8,128)S(1)}, u32[]{:S(2)}, u32[]{:S(2)}) collective-permute-start(f32[808,128]{1,0:T(8,128)} %get-tuple-element.53), channel_id=1, source_target_pairs={{0,0},{1,6},{2,2},{3,4},{4,5},{5,3},{6,7},{7,1},{8,8},{9,14},{10,1... | collective-permute-start | bytes 1241096 | tf_op jit(solution)/shard_map/ppermute | solution.py:479
  6.9 18.9 %collective-permute-start.1 = (f32[808,128]{1,0:T(8,128)}, f32[808,128]{1,0:T(8,128)S(1)}, u32[]{:S(2)}, u32[]{:S(2)}) collective-permute-start(f32[808,128]{1,0:T(8,128)} %get-tuple-element.54), channel_id=1, source_target_pairs={{0,2},{1,4},{2,0},{3,6},{4,7},{5,1},{6,5},{7,3},{8,10},{9,12},{10,... | collective-permute-start | bytes 1241096 | tf_op jit(solution)/shard_map/ppermute | solution.py:479
  9.9 16.4 %collective-permute-start.2 = (f32[808,128]{1,0:T(8,128)}, f32[808,128]{1,0:T(8,128)S(1)}, u32[]{:S(2)}, u32[]{:S(2)}) collective-permute-start(f32[808,128]{1,0:T(8,128)} %get-tuple-element.55), channel_id=1, source_target_pairs={{0,4},{1,2},{2,6},{3,0},{4,1},{5,7},{6,3},{7,5},{8,12},{9,10},{10,... | collective-permute-start | bytes 1241096 | tf_op jit(solution)/shard_map/ppermute | solution.py:479
  11.1 18.5 %collective-permute-start.3 = (f32[808,128]{1,0:T(8,128)}, f32[808,128]{1,0:T(8,128)S(1)}, u32[]{:S(2)}, u32[]{:S(2)}) collective-permute-start(f32[808,128]{1,0:T(8,128)} %get-tuple-element.56), channel_id=1, source_target_pairs={{0,6},{1,0},{2,4},{3,2},{4,3},{5,5},{6,1},{7,7},{8,14},{9,8},{10,1... | collective-permute-start | bytes 1241096 | tf_op jit(solution)/shard_map/ppermute | solution.py:479
  15.2 1.8 %copy-start.1 = (bf16[1152,1152]{1,0:T(8,128)(2,1)S(1)}, bf16[1152,1152]{1,0:T(8,128)(2,1)}, u32[]{:S(2)}) copy-start(bf16[1152,1152]{1,0:T(8,128)(2,1)} %square.1) | copy-start | bytes 7962628
  16.9 1.0 copy-start.2
  17.9 12.4 %copy-start.6 = (f32[800,128]{1,0:T(8,128)S(1)}, f32[800,128]{1,0:T(8,128)}, u32[]{:S(2)}) copy-start(f32[800,128]{1,0:T(8,128)} %get-tuple-element.64) | copy-start | bytes 1228804
  17.9 21.0 %copy-start.5 = (f32[800,128]{1,0:T(8,128)S(1)}, f32[800,128]{1,0:T(8,128)}, u32[]{:S(2)}) copy-start(f32[800,128]{1,0:T(8,128)} %get-tuple-element.65) | copy-start | bytes 1228804
  17.9 21.5 %copy-start.4 = (f32[800,128]{1,0:T(8,128)S(1)}, f32[800,128]{1,0:T(8,128)}, u32[]{:S(2)}) copy-start(f32[800,128]{1,0:T(8,128)} %get-tuple-element.66) | copy-start | bytes 1228804
  17.9 21.5 %copy-start.3 = (f32[800,128]{1,0:T(8,128)S(1)}, f32[800,128]{1,0:T(8,128)}, u32[]{:S(2)}) copy-start(f32[800,128]{1,0:T(8,128)} %get-tuple-element.67) | copy-start | bytes 1228804
  30.3 9.1 %collective-permute-start.4 = (f32[800,128]{1,0:T(8,128)S(1)}, f32[800,128]{1,0:T(8,128)S(1)}, u32[]{:S(2)}, u32[]{:S(2)}) collective-permute-start(f32[800,128]{1,0:T(8,128)S(1)} %copy-done.6), channel_id=1, source_target_pairs={{0,0},{1,6},{2,2},{3,4},{4,5},{5,3},{6,7},{7,1},{8,8},{9,14},{10,1... | collective-permute-start | bytes 1228808 | tf_op jit(solution)/shard_map/ppermute | solution.py:512
  31.0 25.0 %collective-permute-start.10 = (f32[2,80,1280]{2,1,0:T(8,128)S(1)}, f32[2,80,1280]{2,1,0:T(8,128)S(1)}, u32[]{:S(2)}, u32[]{:S(2)}) collective-permute-start(f32[2,80,1280]{2,1,0:T(8,128)S(1)} %get-tuple-element.69.top), channel_id=1, source_target_pairs={{1,0},{3,2},{5,4},{7,6},{8,1},{10,3},{12,5},{14,7},{9,8},{11,10},{... | collective-permute-start | bytes 2457608 | tf_op jit(solution)/shard_map/ppermute | solution.py:539
  38.8 20.8 %collective-permute-start.8 = (f32[2,80,1280]{2,1,0:T(8,128)S(1)}, f32[2,80,1280]{2,1,0:T(8,128)S(1)}, u32[]{:S(2)}, u32[]{:S(2)}) collective-permute-start(f32[2,80,1280]{2,1,0:T(8,128)S(1)} %get-tuple-element.68.bottom), channel_id=1, source_target_pairs={{0,1},{2,3},{4,5},{6,7},{1,8},{3,10},{5,12},{7,14},{8,9},{10,11},{... | collective-permute-start | bytes 2457608 | tf_op jit(solution)/shard_map/ppermute | solution.py:540
  38.8 16.7 %collective-permute-start.5 = (f32[800,128]{1,0:T(8,128)S(1)}, f32[800,128]{1,0:T(8,128)S(1)}, u32[]{:S(2)}, u32[]{:S(2)}) collective-permute-start(f32[800,128]{1,0:T(8,128)S(1)} %copy-done.5), channel_id=1, source_target_pairs={{0,2},{1,4},{2,0},{3,6},{4,7},{5,1},{6,5},{7,3},{8,10},{9,12},{10,... | collective-permute-start | bytes 1228808 | tf_op jit(solution)/shard_map/ppermute | solution.py:512
  39.3 16.2 %collective-permute-start.6 = (f32[800,128]{1,0:T(8,128)S(1)}, f32[800,128]{1,0:T(8,128)S(1)}, u32[]{:S(2)}, u32[]{:S(2)}) collective-permute-start(f32[800,128]{1,0:T(8,128)S(1)} %copy-done.4), channel_id=1, source_target_pairs={{0,4},{1,2},{2,6},{3,0},{4,1},{5,7},{6,3},{7,5},{8,12},{9,10},{10,... | collective-permute-start | bytes 1228808 | tf_op jit(solution)/shard_map/ppermute | solution.py:512
  39.4 16.1 %collective-permute-start.7 = (f32[800,128]{1,0:T(8,128)S(1)}, f32[800,128]{1,0:T(8,128)S(1)}, u32[]{:S(2)}, u32[]{:S(2)}) collective-permute-start(f32[800,128]{1,0:T(8,128)S(1)} %copy-done.3), channel_id=1, source_target_pairs={{0,6},{1,0},{2,4},{3,2},{4,3},{5,5},{6,1},{7,7},{8,14},{9,8},{10,1... | collective-permute-start | bytes 1228808 | tf_op jit(solution)/shard_map/ppermute | solution.py:512
  59.6 18.7 %collective-permute-start.12 = (f32[2,72,1280]{2,1,0:T(8,128)S(1)}, f32[2,72,1280]{2,1,0:T(8,128)S(1)}, u32[]{:S(2)}, u32[]{:S(2)}) collective-permute-start(f32[2,72,1280]{2,1,0:T(8,128)S(1)} %get-tuple-element.76.bottom), channel_id=1, source_target_pairs={{0,1},{2,3},{4,5},{6,7},{1,8},{3,10},{5,12},{7,14},{8,9},{10,11},{... | collective-permute-start | bytes 2211848 | tf_op jit(solution)/shard_map/ppermute | solution.py:540
  63.3 18.0 %collective-permute-start.9 = (f32[2,72,1280]{2,1,0:T(8,128)S(1)}, f32[2,72,1280]{2,1,0:T(8,128)S(1)}, u32[]{:S(2)}, u32[]{:S(2)}) collective-permute-start(f32[2,72,1280]{2,1,0:T(8,128)S(1)} %get-tuple-element.75.top), channel_id=1, source_target_pairs={{1,0},{3,2},{5,4},{7,6},{8,1},{10,3},{12,5},{14,7},{9,8},{11,10},{... | collective-permute-start | bytes 2211848 | tf_op jit(solution)/shard_map/ppermute | solution.py:539
  81.1 14.6 %collective-permute-start.13 = (f32[2,72,1280]{2,1,0:T(8,128)S(1)}, f32[2,72,1280]{2,1,0:T(8,128)S(1)}, u32[]{:S(2)}, u32[]{:S(2)}) collective-permute-start(f32[2,72,1280]{2,1,0:T(8,128)S(1)} %top_kernel.4.top), channel_id=1, source_target_pairs={{1,0},{3,2},{5,4},{7,6},{8,1},{10,3},{12,5},{14,7},{9,8},{11,10},{... | collective-permute-start | bytes 2211848 | tf_op jit(solution)/shard_map/ppermute | solution.py:539
  84.0 16.5 %collective-permute-start.11 = (f32[2,72,1280]{2,1,0:T(8,128)S(1)}, f32[2,72,1280]{2,1,0:T(8,128)S(1)}, u32[]{:S(2)}, u32[]{:S(2)}) collective-permute-start(f32[2,72,1280]{2,1,0:T(8,128)S(1)} %bottom_kernel.4.bottom), channel_id=1, source_target_pairs={{0,1},{2,3},{4,5},{6,7},{1,8},{3,10},{5,12},{7,14},{8,9},{10,11},{... | collective-permute-start | bytes 2211848 | tf_op jit(solution)/shard_map/ppermute | solution.py:540
  90.0 14.2 %collective-permute-start.18 = (f32[10,64,128]{2,1,0:T(8,128)S(1)}, f32[10,64,128]{2,1,0:T(8,128)S(1)}, u32[]{:S(2)}, u32[]{:S(2)}) collective-permute-start(f32[10,64,128]{2,1,0:T(8,128)S(1)} %get-tuple-element.90), channel_id=1, source_target_pairs={{0,0},{6,1},{2,2},{4,3},{5,4},{3,5},{7,6},{1,7},{8,8},{14,9},{10,1... | collective-permute-start | bytes 983048 | tf_op jit(solution)/shard_map/ppermute | solution.py:584
  90.7 14.5 %collective-permute-start.19 = (f32[10,64,128]{2,1,0:T(8,128)S(1)}, f32[10,64,128]{2,1,0:T(8,128)S(1)}, u32[]{:S(2)}, u32[]{:S(2)}) collective-permute-start(f32[10,64,128]{2,1,0:T(8,128)S(1)} %get-tuple-element.91), channel_id=1, source_target_pairs={{2,0},{4,1},{0,2},{6,3},{7,4},{1,5},{5,6},{3,7},{10,8},{12,9},{8,1... | collective-permute-start | bytes 983048 | tf_op jit(solution)/shard_map/ppermute | solution.py:584
  91.3 17.6 %collective-permute-start.20 = (f32[10,64,128]{2,1,0:T(8,128)S(1)}, f32[10,64,128]{2,1,0:T(8,128)S(1)}, u32[]{:S(2)}, u32[]{:S(2)}) collective-permute-start(f32[10,64,128]{2,1,0:T(8,128)S(1)} %get-tuple-element.92), channel_id=1, source_target_pairs={{4,0},{2,1},{6,2},{0,3},{1,4},{7,5},{3,6},{5,7},{12,8},{10,9},{14,... | collective-permute-start | bytes 983048 | tf_op jit(solution)/shard_map/ppermute | solution.py:584
  95.7 15.2 %collective-permute-start.21 = (f32[10,64,128]{2,1,0:T(8,128)S(1)}, f32[10,64,128]{2,1,0:T(8,128)S(1)}, u32[]{:S(2)}, u32[]{:S(2)}) collective-permute-start(f32[10,64,128]{2,1,0:T(8,128)S(1)} %get-tuple-element.93), channel_id=1, source_target_pairs={{6,0},{0,1},{4,2},{2,3},{3,4},{5,5},{1,6},{7,7},{14,8},{8,9},{12,1... | collective-permute-start | bytes 983048 | tf_op jit(solution)/shard_map/ppermute | solution.py:584
  103.5 7.3 %collective-permute-start.14 = (f32[10,64,128]{2,1,0:T(8,128)S(1)}, f32[10,64,128]{2,1,0:T(8,128)S(1)}, u32[]{:S(2)}, u32[]{:S(2)}) collective-permute-start(f32[10,64,128]{2,1,0:T(8,128)S(1)} %get-tuple-element.85), channel_id=1, source_target_pairs={{0,0},{6,1},{2,2},{4,3},{5,4},{3,5},{7,6},{1,7},{8,8},{14,9},{10,1... | collective-permute-start | bytes 983048 | tf_op jit(solution)/shard_map/ppermute | solution.py:584
  104.2 12.9 %collective-permute-start.15 = (f32[10,64,128]{2,1,0:T(8,128)S(1)}, f32[10,64,128]{2,1,0:T(8,128)S(1)}, u32[]{:S(2)}, u32[]{:S(2)}) collective-permute-start(f32[10,64,128]{2,1,0:T(8,128)S(1)} %get-tuple-element.86), channel_id=1, source_target_pairs={{2,0},{4,1},{0,2},{6,3},{7,4},{1,5},{5,6},{3,7},{10,8},{12,9},{8,1... | collective-permute-start | bytes 983048 | tf_op jit(solution)/shard_map/ppermute | solution.py:584
  105.2 15.4 %collective-permute-start.16 = (f32[10,64,128]{2,1,0:T(8,128)S(1)}, f32[10,64,128]{2,1,0:T(8,128)S(1)}, u32[]{:S(2)}, u32[]{:S(2)}) collective-permute-start(f32[10,64,128]{2,1,0:T(8,128)S(1)} %get-tuple-element.87), channel_id=1, source_target_pairs={{4,0},{2,1},{6,2},{0,3},{1,4},{7,5},{3,6},{5,7},{12,8},{10,9},{14,... | collective-permute-start | bytes 983048 | tf_op jit(solution)/shard_map/ppermute | solution.py:584
  108.9 16.1 %collective-permute-start.17 = (f32[10,64,128]{2,1,0:T(8,128)S(1)}, f32[10,64,128]{2,1,0:T(8,128)S(1)}, u32[]{:S(2)}, u32[]{:S(2)}) collective-permute-start(f32[10,64,128]{2,1,0:T(8,128)S(1)} %get-tuple-element.88), channel_id=1, source_target_pairs={{6,0},{0,1},{4,2},{2,3},{3,4},{5,5},{1,6},{7,7},{14,8},{8,9},{12,1... | collective-permute-start | bytes 983048 | tf_op jit(solution)/shard_map/ppermute | solution.py:584

commit v6 on v5

--- a/solution.py
+++ b/solution.py
@@ -77,51 +77,48 @@
     return lax.broadcasted_iota(jnp.int32, (1, LANES), 1) // width
 
 
-def pack_kernel(z, odd, part, spec_in, ocean_in, mask, *refs):
+def pack_kernel(z, rows, odd, part, spec_in, ocean_in, mask_in, *refs):
     B, R, C, W, mt = z.B, z.R, z.C, z.W, z.mt
-    outs, (spec, ocean, wide, sems) = refs[: 2 * B], refs[2 * B :]
+    outs, (spec, ocean, mask, wide, sems) = refs[:B], refs[B:]
     E = C + 2 * PAD
-    at = 0
     copies = []
     for half in range(W // LANES):
         cols = pl.ds(half * LANES, LANES)
         for n, (src, dst) in enumerate(((spec_in, spec), (ocean_in, ocean))):
             copies.append(pltpu.make_async_copy(src.at[:, cols], dst.at[half], sems.at[n, half]))
             copies[-1].start()
-    sea = mask[...].astype(F32)
-    sea = jnp.concatenate([sea, jnp.zeros((R, LANES), F32)], axis=1)
+    mask_copy = pltpu.make_async_copy(mask_in, mask, sems.at[2, 0])
+    mask_copy.start()
     wide[:, 0:PAD, :] = jnp.zeros((wide.shape[0], PAD, LANES), F32)
     wide[:, PAD + W : W + 2 * PAD, :] = jnp.zeros((wide.shape[0], PAD, LANES), F32)
-    for which, rows in enumerate((z.edge_rows, z.inner_rows)):
-        folds, slabs = z.folds(rows)
-        for half in range(W // LANES):
-            if which == 0:
-                for copy in copies[2 * half : 2 * half + 2]:
-                    copy.wait()
-            cols = slice(PAD + half * LANES, PAD + (half + 1) * LANES)
-            for i, r in enumerate(rows):
-                for t in range(mt):
-                    block = spec[half, pl.ds(t * LANES * R + r, LANES, stride=R), :]
-                    wide[at + i * mt + t, cols] = block.T
-            for (count, used, deep, base, _), src, first in zip(folds, (spec, ocean), (z.main, 0)):
-                for rr in range(deep):
-                    pieces = [
-                        src[half, pl.ds(first * R + rows[rr + i * deep], count, stride=R), :]
-                        for i in range(used)
-                    ]
-                    if used * count < LANES:
-                        pieces.append(jnp.zeros((LANES - used * count, LANES), F32))
-                    wide[at + base + rr, cols] = jnp.concatenate(pieces, axis=0).T
-        for k in range(B):
-            out = outs[which * B + k]
-            share = exchange_share(z, k, odd[0], part[0])
-            start = pl.multiple_of(share * C, PAD)
-            block = wide[at : at + slabs, pl.ds(start, E), :]
-            out[0 : slabs * E] = block.reshape(slabs * E, LANES)
-            if which == 0:
-                shift = lax.rem(W + LANES + PAD - start, W + LANES)
-                out[slabs * E : slabs * E + R] = pltpu.roll(sea, shift, axis=1)[:, :LANES]
-        at += slabs
+    folds, slabs = z.folds(rows)
+    for half in range(W // LANES):
+        for copy in copies[2 * half : 2 * half + 2]:
+            copy.wait()
+        cols = slice(PAD + half * LANES, PAD + (half + 1) * LANES)
+        for i, r in enumerate(rows):
+            for t in range(mt):
+                block = spec[half, pl.ds(t * LANES * R + r, LANES, stride=R), :]
+                wide[i * mt + t, cols] = block.T
+        for (count, used, deep, base, _), src, first in zip(folds, (spec, ocean), (z.main, 0)):
+            for rr in range(deep):
+                pieces = [
+                    src[half, pl.ds(first * R + rows[rr + i * deep], count, stride=R), :]
+                    for i in range(used)
+                ]
+                if used * count < LANES:
+                    pieces.append(jnp.zeros((LANES - used * count, LANES), F32))
+                wide[base + rr, cols] = jnp.concatenate(pieces, axis=0).T
+    mask_copy.wait()
+    sea = jnp.concatenate([mask[...].astype(F32), jnp.zeros((R, LANES), F32)], axis=1)
+    for k, out in enumerate(outs):
+        share = exchange_share(z, k, odd[0], part[0])
+        start = pl.multiple_of(share * C, PAD)
+        block = wide[:, pl.ds(start, E), :]
+        out[0 : slabs * E] = block.reshape(slabs * E, LANES)
+        if rows == z.edge_rows:
+            shift = lax.rem(W + LANES + PAD - start, W + LANES)
+            out[slabs * E : slabs * E + R] = pltpu.roll(sea, shift, axis=1)[:, :LANES]
 
 
 def spread_line(line):
@@ -265,32 +262,29 @@
         moved[1, r] = DOPPLER * jnp.tanh(jnp.broadcast_to(surface[:, L : L + 1], (E, LANES)))
 
     def advect(read, write, start, stop, speed_cx, speed_cy):
-        def along_x(r):
+        plus_before, waiting = None, None
+        for r in range(start - 1, stop + 1):
             energy = read(r)
             speed_x = speed_cx + moved[0, r]
-            return (
-                energy,
-                jnp.maximum(speed_x, 0.0) * energy,
-                jnp.minimum(speed_x, 0.0) * energy,
-            )
-
-        _, plus_before, _ = along_x(start - 1)
-        energy, plus, minus = along_x(start)
-        for r in range(start, stop):
-            energy_next, plus_next, minus_next = along_x(r + 1)
-            speed_y = speed_cy + moved[1, r]
-            plus_y = jnp.maximum(speed_y, 0.0) * energy
-            minus_y = jnp.minimum(speed_y, 0.0) * energy
-            result = (
-                energy
-                - ((plus - plus_before) + (minus_next - minus))
-                - (
-                    (plus_y - pltpu.roll(plus_y, 1, axis=0))
-                    + (pltpu.roll(minus_y, E - 1, axis=0) - minus_y)
+            if r >= start:
+                minus = jnp.minimum(speed_x, 0.0) * energy
+            if r > start:
+                write(r - 1, (waiting - minus) * sea_row(sea_rows[r - 1]))
+            if r < stop:
+                plus = jnp.maximum(speed_x, 0.0) * energy
+            if start <= r < stop:
+                speed_y = speed_cy + moved[1, r]
+                plus_y = jnp.maximum(speed_y, 0.0) * energy
+                minus_y = jnp.minimum(speed_y, 0.0) * energy
+                waiting = (
+                    energy
+                    - ((plus - plus_before) - minus)
+                    - (
+                        (plus_y - pltpu.roll(plus_y, 1, axis=0))
+                        + (pltpu.roll(minus_y, E - 1, axis=0) - minus_y)
+                    )
                 )
-            )
-            write(r, result * sea_row(sea_rows[r]))
-            plus_before, energy, plus, minus = plus, energy_next, plus_next, minus_next
+            plus_before = plus
 
     def one_tile(j, carry):
         lanes = pl.ds(pl.multiple_of(j * LANES, LANES), LANES)
@@ -453,30 +447,32 @@
     who = ((geo % 2).astype(jnp.int32).reshape(1), part.astype(jnp.int32).reshape(1))
 
     width = C + 2 * PAD
-    blocks = [
-        jax.ShapeDtypeStruct((z.slabs(rows) * width + more, LANES), F32)
-        for rows, more in ((z.edge_rows, R), (z.inner_rows, 0))
-        for _ in range(B)
-    ]
     all_slabs = z.slabs(z.edge_rows) + z.slabs(z.inner_rows)
     columns_scratch = [
         pltpu.VMEM((W // LANES, nb * R, LANES), F32),
         pltpu.VMEM((W // LANES, 2 * L * R, LANES), F32),
     ]
-    packed = pl.pallas_call(
-        functools.partial(pack_kernel, z),
-        out_shape=blocks,
-        in_specs=[SMEM] * 2 + [HBM, HBM, VMEM],
-        out_specs=[VMEM] * (2 * B),
-        scratch_shapes=columns_scratch
-        + [
-            pltpu.VMEM((all_slabs, W + 2 * PAD, LANES), F32),
-            pltpu.SemaphoreType.DMA((2, W // LANES)),
-        ],
-        compiler_params=params(58),
-        name="pack",
-    )(*who, spectrum.reshape(nb * R, W), ocean.reshape(2 * L * R, W), sea_mask)
+    def pack(rows):
+        slabs = z.slabs(rows)
+        lines = slabs * width + (R if rows == z.edge_rows else 0)
+        return pl.pallas_call(
+            functools.partial(pack_kernel, z, rows),
+            out_shape=[jax.ShapeDtypeStruct((lines, LANES), F32)] * B,
+            in_specs=[SMEM] * 2 + [HBM] * 3,
+            out_specs=[VMEM] * B,
+            scratch_shapes=columns_scratch
+            + [
+                pltpu.VMEM((R, W), jnp.int32),
+                pltpu.VMEM((slabs, W + 2 * PAD, LANES), F32),
+                pltpu.SemaphoreType.DMA((3, W // LANES)),
+            ],
+            compiler_params=params(58),
+            name="pack",
+        )(*who, spectrum.reshape(nb * R, W), ocean.reshape(2 * L * R, W), sea_mask)
+
+    packed = pack(z.edge_rows)
     got = [lax.ppermute(packed[k], axes, forward[k]) for k in range(B)]
+    packed = pack(z.inner_rows)
 
     weights, drift_weights = pl.pallas_call(
         functools.partial(weights_kernel, z),
@@ -508,9 +504,10 @@
     top, bottom, sea = unpack(
         z.edge_rows, got[:B], [(EDGE, CH), (EDGE, CH), (R, LANES)]
     )
-    *blocks, top = lax.optimization_barrier((*packed[B:], top))
-    got += [lax.ppermute(blocks[k], axes, forward[k]) for k in range(B)]
-    (inner,) = unpack(z.inner_rows, got[B:], [(R - 2 * EDGE, CH)])
+    *blocks, top = lax.optimization_barrier((*packed[half:], top))
+    blocks = list(packed[:half]) + blocks
+    got = [lax.ppermute(blocks[k], axes, forward[k]) for k in range(B)]
+    (inner,) = unpack(z.inner_rows, got, [(R - 2 * EDGE, CH)])
 
     def step_call(body, first, cut, sea_at, count, deepest, inputs, more=()):
         width = inputs[0].shape[1]

time: 128 us -> 124 us (0.969)
  starting transfers between devices: 42.5 us -> 37 us
  Pallas kernels: 45.1 us -> 47.4 us
    ppermute x4, waiting for transfers between devices: 9.79 us -> 13.3 us  [per_device(): got = [lax.ppermute(blocks[k], axes, forward[k]) for k in range(B)]]
    ppermute x4, waiting for transfers between devices: 10.1 us -> 6.76 us  [per_device(): got = [lax.ppermute(packed[k], axes, forward[k]) for k in range(B)]]
    ppermute x4, starting transfers between devices: 7.55 us -> 5.1 us  [per_device(): got = [lax.ppermute(blocks[k], axes, forward[k]) for k in range(B)]]
    ppermute x3, starting transfers between devices: 11.8 us -> 9.4 us  [per_device(): down = lax.ppermute(top, axes, to_prev_row)]
    pallas_call x1 -> x2, Pallas kernels: 4.6 us -> 6.62 us  [pack(): pl.pallas_call(functools.partial(pack_kernel, z, rows), out_shape=[jax.Sh...]
    unnamed x14 -> x12, local copies, waits for them, and re-layouts: 2.73 us -> 1.77 us
  transfers between devices with their start and end apart: 22 -> 22, of which waited for: 8 -> 9; matrix products, arithmetic and copies ran while one was open for 0% -> 0% of each run, Pallas kernels for 29% -> 34%
where the time goes in v6:
time: 124 us; the launch traced here: 123 us
  Pallas kernels  47.4 us (38%)
  starting transfers between devices  37 us (30%)
  waiting for transfers between devices  35.8 us (29%)
  local copies, waits for them, and re-layouts  1.92 us (2%)
    pallas_call x9, Pallas kernels, step_call(): pl.pallas_call(functools.partial(body, z, first, cut, sea_at), out_shape=...  34.7 us
    ppermute x4, waiting for transfers between devices, per_device(): got = [lax.ppermute(blocks[k], axes, forward[k]) for k in range(B)]  13.3 us
    ppermute x8, waiting for transfers between devices, per_device(): lax.ppermute(packed[i], axes, [(t, s) for s, t in forward[i % B]])  12.9 us
    ppermute x8, starting transfers between devices, per_device(): lax.ppermute(packed[i], axes, [(t, s) for s, t in forward[i % B]])  12.7 us
    ppermute x4, starting transfers between devices, per_device(): got = [lax.ppermute(packed[k], axes, forward[k]) for k in range(B)]  9.52 us
    ppermute x3, starting transfers between devices, per_device(): down = lax.ppermute(top, axes, to_prev_row)  9.4 us
    ppermute x4, waiting for transfers between devices, per_device(): got = [lax.ppermute(packed[k], axes, forward[k]) for k in range(B)]  6.76 us
    pallas_call x2, Pallas kernels, pack(): pl.pallas_call(functools.partial(pack_kernel, z, rows), out_shape=[jax.Sh...  6.62 us
  transfers between devices with their start and end apart: 22, of which 9 were waited for; matrix products, arithmetic and copies ran while one was open for 0% of the time, Pallas kernels for 34%

profile of v6, /device:TPU:0, one launch (start us, length us, event | category | flops | bytes accessed | tf_op | source)
XLA Modules:
  0.0 123.3 jit_solution(3273326546749566183)
XLA Ops:
  0.7 3.4 %pack.3 = (f32[808,128]{1,0:T(8,128)}, f32[808,128]{1,0:T(8,128)}, f32[808,128]{1,0:T(8,128)}, f32[808,128]{1,0:T(8,128)}) custom-call(s32[1]{0:T(128)} %bitcast.odd, s32[1]{0:T(128)} %bitcast.1.part, f32[2304,256]{1,0:T(8,128)} %bitcast.6, f32[256,256]{1,0:T(8,128)} %bitcast.8, s32[8,256]{1,0:T(8,128)} %mask_in.3), custom_call_target="tpu_custom_call" | custom-call | tf_op jit(solution)/shard_map/pack/pallas_call | solution.py:458
  4.0 1.7 %collective-permute-start.2 = (f32[808,128]{1,0:T(8,128)}, f32[808,128]{1,0:T(8,128)S(1)}, u32[]{:S(2)}, u32[]{:S(2)}) collective-permute-start(f32[808,128]{1,0:T(8,128)} %get-tuple-element.51), channel_id=1, source_target_pairs={{0,0},{1,6},{2,2},{3,4},{4,5},{5,3},{6,7},{7,1},{8,8},{9,14},{10,1... | collective-permute-start | bytes 1241096 | tf_op jit(solution)/shard_map/ppermute | solution.py:474
  5.7 3.0 %collective-permute-start.3 = (f32[808,128]{1,0:T(8,128)}, f32[808,128]{1,0:T(8,128)S(1)}, u32[]{:S(2)}, u32[]{:S(2)}) collective-permute-start(f32[808,128]{1,0:T(8,128)} %get-tuple-element.52), channel_id=1, source_target_pairs={{0,2},{1,4},{2,0},{3,6},{4,7},{5,1},{6,5},{7,3},{8,10},{9,12},{10,... | collective-permute-start | bytes 1241096 | tf_op jit(solution)/shard_map/ppermute | solution.py:474
  9.9 3.6 %collective-permute-start.5 = (f32[808,128]{1,0:T(8,128)}, f32[808,128]{1,0:T(8,128)S(1)}, u32[]{:S(2)}, u32[]{:S(2)}) collective-permute-start(f32[808,128]{1,0:T(8,128)} %get-tuple-element.54), channel_id=1, source_target_pairs={{0,6},{1,0},{2,4},{3,2},{4,3},{5,5},{6,1},{7,7},{8,14},{9,8},{10,1... | collective-permute-start | bytes 1241096 | tf_op jit(solution)/shard_map/ppermute | solution.py:474
  13.6 3.3 %pack.2 = (f32[800,128]{1,0:T(8,128)}, f32[800,128]{1,0:T(8,128)}, f32[800,128]{1,0:T(8,128)}, f32[800,128]{1,0:T(8,128)}) custom-call(s32[1]{0:T(128)} %bitcast.odd, s32[1]{0:T(128)} %bitcast.1.part, f32[2304,256]{1,0:T(8,128)} %bitcast.7, f32[256,256]{1,0:T(8,128)} %bitcast.9, s32[8,256]{1,0:T(8,128)} %mask_in.3), custom_call_target="tpu_custom_call" | custom-call | tf_op jit(solution)/shard_map/pack/pallas_call | solution.py:458
  16.8 1.7 %collective-permute-start = (f32[800,128]{1,0:T(8,128)}, f32[800,128]{1,0:T(8,128)S(1)}, u32[]{:S(2)}, u32[]{:S(2)}) collective-permute-start(f32[800,128]{1,0:T(8,128)} %get-tuple-element.47), channel_id=1, source_target_pairs={{0,0},{1,6},{2,2},{3,4},{4,5},{5,3},{6,7},{7,1},{8,8},{9,14},{10,1... | collective-permute-start | bytes 1228808 | tf_op jit(solution)/shard_map/ppermute | solution.py:509
  18.9 1.7 %copy-done.1 = bf16[1152,1152]{1,0:T(8,128)(2,1)S(1)} copy-done((bf16[1152,1152]{1,0:T(8,128)(2,1)S(1)}, bf16[1152,1152]{1,0:T(8,128)(2,1)}, u32[]{:S(2)}) %copy-start.1) | copy-done | bytes 2654232
  20.6 1.5 %weights.1 = (bf16[2304,1152]{1,0:T(8,128)(2,1)S(1)}, bf16[1152,128]{1,0:T(8,128)(2,1)S(1)}) custom-call(bf16[1152,1152]{1,0:T(8,128)(2,1)S(1)} %copy-done, bf16[1152,1152]{1,0:T(8,128)(2,1)S(1)} %copy-done.1, bf16[128,1152]{1,0:T(8,128)(2,1)S(1)} %copy-done.2), custom_call_target="tpu_custom_call" | custom-call | flops 2000000000 | bytes 10616832 | tf_op jit(solution)/shard_map/weights/pallas_call | solution.py:477
  22.2 2.3 %collective-permute-done.3.refs_1_ = f32[808,128]{1,0:T(8,128)S(1)} collective-permute-done((f32[808,128]{1,0:T(8,128)}, f32[808,128]{1,0:T(8,128)S(1)}, u32[]{:S(2)}, u32[]{:S(2)}) %collective-permute-start.3) | collective-permute-done | bytes 413728 | tf_op jit(solution)/shard_map/ppermute | solution.py:474
  25.1 3.9 %collective-permute-done.5.refs_3_ = f32[808,128]{1,0:T(8,128)S(1)} collective-permute-done((f32[808,128]{1,0:T(8,128)}, f32[808,128]{1,0:T(8,128)S(1)}, u32[]{:S(2)}, u32[]{:S(2)}) %collective-permute-start.5) | collective-permute-done | bytes 413728 | tf_op jit(solution)/shard_map/ppermute | solution.py:474
  29.6 5.3 %collective-permute-start.10 = (f32[2,80,1280]{2,1,0:T(8,128)S(1)}, f32[2,80,1280]{2,1,0:T(8,128)S(1)}, u32[]{:S(2)}, u32[]{:S(2)}) collective-permute-start(f32[2,80,1280]{2,1,0:T(8,128)S(1)} %get-tuple-element.65.top), channel_id=1, source_target_pairs={{1,0},{3,2},{5,4},{7,6},{8,1},{10,3},{12,5},{14,7},{9,8},{11,10},{... | collective-permute-start | bytes 2457608 | tf_op jit(solution)/shard_map/ppermute | solution.py:536
  34.9 1.5 %collective-permute-start.1 = (f32[800,128]{1,0:T(8,128)S(1)}, f32[800,128]{1,0:T(8,128)S(1)}, u32[]{:S(2)}, u32[]{:S(2)}) collective-permute-start(f32[800,128]{1,0:T(8,128)S(1)} %copy-done.5), channel_id=1, source_target_pairs={{0,2},{1,4},{2,0},{3,6},{4,7},{5,1},{6,5},{7,3},{8,10},{9,12},{10,... | collective-permute-start | bytes 1228808 | tf_op jit(solution)/shard_map/ppermute | solution.py:509
  36.5 1.9 %collective-permute-start.7 = (f32[800,128]{1,0:T(8,128)S(1)}, f32[800,128]{1,0:T(8,128)S(1)}, u32[]{:S(2)}, u32[]{:S(2)}) collective-permute-start(f32[800,128]{1,0:T(8,128)S(1)} %copy-done.3), channel_id=1, source_target_pairs={{0,6},{1,0},{2,4},{3,2},{4,3},{5,5},{6,1},{7,7},{8,14},{9,8},{10,1... | collective-permute-start | bytes 1228808 | tf_op jit(solution)/shard_map/ppermute | solution.py:509
  38.4 12.3 %collective-permute-done.1.refs_1_ = f32[800,128]{1,0:T(8,128)S(1)} collective-permute-done((f32[800,128]{1,0:T(8,128)S(1)}, f32[800,128]{1,0:T(8,128)S(1)}, u32[]{:S(2)}, u32[]{:S(2)}) %collective-permute-start.1) | collective-permute-done | bytes 409632 | tf_op jit(solution)/shard_map/ppermute | solution.py:509
  52.1 3.6 %bottom_kernel.3 = (f32[2,72,1280]{2,1,0:T(8,128)S(1)}, f32[2,80,128]{2,1,0:T(8,128)S(1)}) custom-call(f32[2,80,1280]{2,1,0:T(8,128)S(1)} %collective-permute-done.10.down, f32[2,80,1280]{2,1,0:T(8,128)S(1)} %get-tuple-element.64.bottom, f32[4,80,1280]{2,1,0:T(8,128)S(1)} %unpack.3.inner, f32[8,80,128]{2,1,0:T(8,128)S(1)} %get-tuple-element.66.sea, ...), custom_call_target="tpu_custom_call" | custom-call | flops 200000000 | bytes 200000 | tf_op jit(solution)/shard_map/bottom_kernel/pallas_call | solution.py:516
  55.9 3.6 %top_kernel.3 = (f32[2,72,1280]{2,1,0:T(8,128)S(1)}, f32[2,80,128]{2,1,0:T(8,128)S(1)}) custom-call(f32[2,80,1280]{2,1,0:T(8,128)S(1)} %collective-permute-done.8.up, f32[2,80,1280]{2,1,0:T(8,128)S(1)} %get-tuple-element.65.top, f32[4,80,1280]{2,1,0:T(8,128)S(1)} %unpack.3.inner, f32[8,80,128]{2,1,0:T(8,128)S(1)} %get-tuple-element.66.sea, ...), custom_call_target="tpu_custom_call" | custom-call | flops 200000000 | bytes 200000 | tf_op jit(solution)/shard_map/top_kernel/pallas_call | solution.py:516
  59.5 3.8 %collective-permute-start.9 = (f32[2,72,1280]{2,1,0:T(8,128)S(1)}, f32[2,72,1280]{2,1,0:T(8,128)S(1)}, u32[]{:S(2)}, u32[]{:S(2)}) collective-permute-start(f32[2,72,1280]{2,1,0:T(8,128)S(1)} %get-tuple-element.71.top), channel_id=1, source_target_pairs={{1,0},{3,2},{5,4},{7,6},{8,1},{10,3},{12,5},{14,7},{9,8},{11,10},{... | collective-permute-start | bytes 2211848 | tf_op jit(solution)/shard_map/ppermute | solution.py:536
  63.3 5.9 %inner_kernel.3.inner = f32[4,72,1280]{2,1,0:T(8,128)S(1)} custom-call(f32[2,80,1280]{2,1,0:T(8,128)S(1)} %get-tuple-element.65.top, f32[4,80,1280]{2,1,0:T(8,128)S(1)} %unpack.3.inner, f32[2,80,1280]{2,1,0:T(8,128)S(1)} %get-tuple-element.64.bottom, f32[8,80,128]{2,1,0:T(8,128)S(1)} %get-tuple-element.66.sea, ...), custom_call_target="tpu_custom_call" | custom-call | flops 400000000 | bytes 400000 | tf_op jit(solution)/shard_map/inner_kernel/pallas_call | solution.py:516
  69.2 5.5 %inner_kernel.4 = (f32[4,72,1280]{2,1,0:T(8,128)S(1)}, f32[2,72,1152]{2,1,0:T(8,128)S(1)}, f32[2,72,1152]{2,1,0:T(8,128)S(1)}) custom-call(f32[2,72,1280]{2,1,0:T(8,128)S(1)} %get-tuple-element.71.top, f32[4,72,1280]{2,1,0:T(8,128)S(1)} %inner_kernel.3.inner, f32[2,72,1280]{2,1,0:T(8,128)S(1)} %get-tuple-element.72.bottom, ...), custom_call_target="tpu_custom_call" | custom-call | flops 400000000 | bytes 400000 | tf_op jit(solution)/shard_map/inner_kernel/pallas_call | solution.py:516
  74.7 2.7 %top_kernel.4.top = f32[2,72,1280]{2,1,0:T(8,128)S(1)} custom-call(f32[2,72,1280]{2,1,0:T(8,128)S(1)} %collective-permute-done.12.up, f32[2,72,1280]{2,1,0:T(8,128)S(1)} %get-tuple-element.71.top, f32[4,72,1280]{2,1,0:T(8,128)S(1)} %inner_kernel.3.inner, f32[8,80,128]{2,1,0:T(8,128)S(1)} %get-tuple-element.66.sea, ...), custom_call_target="tpu_custom_call" | custom-call | flops 200000000 | bytes 200000 | tf_op jit(solution)/shard_map/top_kernel/pallas_call | solution.py:516
  77.8 2.8 %bottom_kernel.4.bottom = f32[2,72,1280]{2,1,0:T(8,128)S(1)} custom-call(f32[2,72,1280]{2,1,0:T(8,128)S(1)} %collective-permute-done.9.down, f32[2,72,1280]{2,1,0:T(8,128)S(1)} %get-tuple-element.72.bottom, f32[4,72,1280]{2,1,0:T(8,128)S(1)} %inner_kernel.3.inner, f32[8,80,128]{2,1,0:T(8,128)S(1)} %get-tuple-element.66.sea, ...), custom_call_target="tpu_custom_call" | custom-call | flops 200000000 | bytes 200000 | tf_op jit(solution)/shard_map/bottom_kernel/pallas_call | solution.py:516
  80.8 5.3 %inner_kernel.5 = (f32[4,64,1280]{2,1,0:T(8,128)S(1)}, f32[2,72,1152]{2,1,0:T(8,128)S(1)}, f32[2,72,1152]{2,1,0:T(8,128)S(1)}) custom-call(f32[2,72,1280]{2,1,0:T(8,128)S(1)} %top_kernel.4.top, f32[4,72,1280]{2,1,0:T(8,128)S(1)} %get-tuple-element.78.inner, f32[2,72,1280]{2,1,0:T(8,128)S(1)} %bottom_kernel.4.bottom, ...), custom_call_target="tpu_custom_call" | custom-call | flops 400000000 | bytes 400000 | tf_op jit(solution)/shard_map/inner_kernel/pallas_call | solution.py:516
  89.6 2.8 %collective-permute-done.13.down = f32[2,72,1280]{2,1,0:T(8,128)S(1)} collective-permute-done((f32[2,72,1280]{2,1,0:T(8,128)S(1)}, f32[2,72,1280]{2,1,0:T(8,128)S(1)}, u32[]{:S(2)}, u32[]{:S(2)}) %collective-permute-start.13) | collective-permute-done | bytes 737312 | tf_op jit(solution)/shard_map/ppermute | solution.py:536
  92.4 2.1 %collective-permute-start.21 = (f32[10,64,128]{2,1,0:T(8,128)S(1)}, f32[10,64,128]{2,1,0:T(8,128)S(1)}, u32[]{:S(2)}, u32[]{:S(2)}) collective-permute-start(f32[10,64,128]{2,1,0:T(8,128)S(1)} %get-tuple-element.89), channel_id=1, source_target_pairs={{6,0},{0,1},{4,2},{2,3},{3,4},{5,5},{1,6},{7,7},{14,8},{8,9},{12,1... | collective-permute-start | bytes 983048 | tf_op jit(solution)/shard_map/ppermute | solution.py:581
  94.5 2.7 %bottom_kernel.5.refs_1_ = f32[2,64,1280]{2,1,0:T(8,128)S(1)} custom-call(f32[2,72,1280]{2,1,0:T(8,128)S(1)} %collective-permute-done.13.down, f32[2,72,1280]{2,1,0:T(8,128)S(1)} %bottom_kernel.4.bottom, f32[4,72,1280]{2,1,0:T(8,128)S(1)} %get-tuple-element.78.inner, f32[8,80,128]{2,1,0:T(8,128)S(1)} %get-tuple-element.66.sea, ...), custom_call_target="tpu_custom_call" | custom-call | flops 200000000 | bytes 200000 | tf_op jit(solution)/shard_map/bottom_kernel/pallas_call | solution.py:516
  97.2 2.6 %top_kernel.5.refs_0_ = f32[2,64,1280]{2,1,0:T(8,128)S(1)} custom-call(f32[2,72,1280]{2,1,0:T(8,128)S(1)} %collective-permute-done.11.up, f32[2,72,1280]{2,1,0:T(8,128)S(1)} %top_kernel.4.top, f32[4,72,1280]{2,1,0:T(8,128)S(1)} %get-tuple-element.78.inner, f32[8,80,128]{2,1,0:T(8,128)S(1)} %get-tuple-element.66.sea, ...), custom_call_target="tpu_custom_call" | custom-call | flops 200000000 | bytes 200000 | tf_op jit(solution)/shard_map/top_kernel/pallas_call | solution.py:516
  102.1 3.4 %collective-permute-start.16 = (f32[10,64,128]{2,1,0:T(8,128)S(1)}, f32[10,64,128]{2,1,0:T(8,128)S(1)}, u32[]{:S(2)}, u32[]{:S(2)}) collective-permute-start(f32[10,64,128]{2,1,0:T(8,128)S(1)} %get-tuple-element.83), channel_id=1, source_target_pairs={{4,0},{2,1},{6,2},{0,3},{1,4},{7,5},{3,6},{5,7},{12,8},{10,9},{14,... | collective-permute-start | bytes 983048 | tf_op jit(solution)/shard_map/ppermute | solution.py:581
  105.5 2.1 %collective-permute-start.17 = (f32[10,64,128]{2,1,0:T(8,128)S(1)}, f32[10,64,128]{2,1,0:T(8,128)S(1)}, u32[]{:S(2)}, u32[]{:S(2)}) collective-permute-start(f32[10,64,128]{2,1,0:T(8,128)S(1)} %get-tuple-element.84), channel_id=1, source_target_pairs={{6,0},{0,1},{4,2},{2,3},{3,4},{5,5},{1,6},{7,7},{14,8},{8,9},{12,1... | collective-permute-start | bytes 983048 | tf_op jit(solution)/shard_map/ppermute | solution.py:581
  107.7 5.8 %collective-permute-done.15.refs_1_ = f32[10,64,128]{2,1,0:T(8,128)S(1)} collective-permute-done((f32[10,64,128]{2,1,0:T(8,128)S(1)}, f32[10,64,128]{2,1,0:T(8,128)S(1)}, u32[]{:S(2)}, u32[]{:S(2)}) %collective-permute-start.15) | collective-permute-done | bytes 327712 | tf_op jit(solution)/shard_map/ppermute | solution.py:581
  113.5 4.0 %collective-permute-done.16.refs_2_ = f32[10,64,128]{2,1,0:T(8,128)S(1)} collective-permute-done((f32[10,64,128]{2,1,0:T(8,128)S(1)}, f32[10,64,128]{2,1,0:T(8,128)S(1)}, u32[]{:S(2)}, u32[]{:S(2)}) %collective-permute-start.16) | collective-permute-done | bytes 327712 | tf_op jit(solution)/shard_map/ppermute | solution.py:581
  117.6 3.1 %collective-permute-done.17.refs_3_ = f32[10,64,128]{2,1,0:T(8,128)S(1)} collective-permute-done((f32[10,64,128]{2,1,0:T(8,128)S(1)}, f32[10,64,128]{2,1,0:T(8,128)S(1)}, u32[]{:S(2)}, u32[]{:S(2)}) %collective-permute-start.17) | collective-permute-done | bytes 327712 | tf_op jit(solution)/shard_map/ppermute | solution.py:581
  120.6 2.7 %restore.1 = (f32[2304,256]{1,0:T(8,128)}, f32[256,256]{1,0:T(8,128)}) custom-call(s32[1]{0:T(128)} %bitcast.odd, s32[1]{0:T(128)} %bitcast.1.part, f32[10,64,128]{2,1,0:T(8,128)S(1)} %collective-permute-done.14.refs_0_, f32[10,64,128]{2,1,0:T(8,128)S(1)} %collective-permute-done.15.refs_1_, f32[10,64,128]{2,1,0:T(8,128)S(1)} %collective-permute-done.16.refs_2_, ...), custom_call_target="tpu_custom_call" | custom-call | tf_op jit(solution)/shard_map/restore/pallas_call | solution.py:583
  (47 shorter events, 10.7 us)
Async XLA Ops:
  0.6 18.2 %copy-start = (bf16[1152,1152]{1,0:T(8,128)(2,1)S(1)}, bf16[1152,1152]{1,0:T(8,128)(2,1)}, u32[]{:S(2)}) copy-start(bf16[1152,1152]{1,0:T(8,128)(2,1)} %linear.1) | copy-start | bytes 7962628
  0.7 18.2 %copy-start.2 = (bf16[128,1152]{1,0:T(8,128)(2,1)S(1)}, bf16[128,1152]{1,0:T(8,128)(2,1)}, u32[]{:S(2)}) copy-start(bf16[128,1152]{1,0:T(8,128)(2,1)} %drift.1) | copy-start | bytes 884740
  4.0 18.2 %collective-permute-start.2 = (f32[808,128]{1,0:T(8,128)}, f32[808,128]{1,0:T(8,128)S(1)}, u32[]{:S(2)}, u32[]{:S(2)}) collective-permute-start(f32[808,128]{1,0:T(8,128)} %get-tuple-element.51), channel_id=1, source_target_pairs={{0,0},{1,6},{2,2},{3,4},{4,5},{5,3},{6,7},{7,1},{8,8},{9,14},{10,1... | collective-permute-start | bytes 1241096 | tf_op jit(solution)/shard_map/ppermute | solution.py:474
  5.7 18.9 %collective-permute-start.3 = (f32[808,128]{1,0:T(8,128)}, f32[808,128]{1,0:T(8,128)S(1)}, u32[]{:S(2)}, u32[]{:S(2)}) collective-permute-start(f32[808,128]{1,0:T(8,128)} %get-tuple-element.52), channel_id=1, source_target_pairs={{0,2},{1,4},{2,0},{3,6},{4,7},{5,1},{6,5},{7,3},{8,10},{9,12},{10,... | collective-permute-start | bytes 1241096 | tf_op jit(solution)/shard_map/ppermute | solution.py:474
  8.7 16.4 %collective-permute-start.4 = (f32[808,128]{1,0:T(8,128)}, f32[808,128]{1,0:T(8,128)S(1)}, u32[]{:S(2)}, u32[]{:S(2)}) collective-permute-start(f32[808,128]{1,0:T(8,128)} %get-tuple-element.53), channel_id=1, source_target_pairs={{0,4},{1,2},{2,6},{3,0},{4,1},{5,7},{6,3},{7,5},{8,12},{9,10},{10,... | collective-permute-start | bytes 1241096 | tf_op jit(solution)/shard_map/ppermute | solution.py:474
  9.9 19.1 %collective-permute-start.5 = (f32[808,128]{1,0:T(8,128)}, f32[808,128]{1,0:T(8,128)S(1)}, u32[]{:S(2)}, u32[]{:S(2)}) collective-permute-start(f32[808,128]{1,0:T(8,128)} %get-tuple-element.54), channel_id=1, source_target_pairs={{0,6},{1,0},{2,4},{3,2},{4,3},{5,5},{6,1},{7,7},{8,14},{9,8},{10,1... | collective-permute-start | bytes 1241096 | tf_op jit(solution)/shard_map/ppermute | solution.py:474
  16.8 19.6 %collective-permute-start = (f32[800,128]{1,0:T(8,128)}, f32[800,128]{1,0:T(8,128)S(1)}, u32[]{:S(2)}, u32[]{:S(2)}) collective-permute-start(f32[800,128]{1,0:T(8,128)} %get-tuple-element.47), channel_id=1, source_target_pairs={{0,0},{1,6},{2,2},{3,4},{4,5},{5,3},{6,7},{7,1},{8,8},{9,14},{10,1... | collective-permute-start | bytes 1228808 | tf_op jit(solution)/shard_map/ppermute | solution.py:509
  18.9 1.8 %copy-start.1 = (bf16[1152,1152]{1,0:T(8,128)(2,1)S(1)}, bf16[1152,1152]{1,0:T(8,128)(2,1)}, u32[]{:S(2)}) copy-start(bf16[1152,1152]{1,0:T(8,128)(2,1)} %square.1) | copy-start | bytes 7962628
  20.6 14.3 %copy-start.5 = (f32[800,128]{1,0:T(8,128)S(1)}, f32[800,128]{1,0:T(8,128)}, u32[]{:S(2)}) copy-start(f32[800,128]{1,0:T(8,128)} %get-tuple-element.48) | copy-start | bytes 1228804
  20.6 15.8 %copy-start.4 = (f32[800,128]{1,0:T(8,128)S(1)}, f32[800,128]{1,0:T(8,128)}, u32[]{:S(2)}) copy-start(f32[800,128]{1,0:T(8,128)} %get-tuple-element.62) | copy-start | bytes 1228804
  20.6 15.9 %copy-start.3 = (f32[800,128]{1,0:T(8,128)S(1)}, f32[800,128]{1,0:T(8,128)}, u32[]{:S(2)}) copy-start(f32[800,128]{1,0:T(8,128)} %get-tuple-element.63) | copy-start | bytes 1228804
  29.6 22.5 %collective-permute-start.10 = (f32[2,80,1280]{2,1,0:T(8,128)S(1)}, f32[2,80,1280]{2,1,0:T(8,128)S(1)}, u32[]{:S(2)}, u32[]{:S(2)}) collective-permute-start(f32[2,80,1280]{2,1,0:T(8,128)S(1)} %get-tuple-element.65.top), channel_id=1, source_target_pairs={{1,0},{3,2},{5,4},{7,6},{8,1},{10,3},{12,5},{14,7},{9,8},{11,10},{... | collective-permute-start | bytes 2457608 | tf_op jit(solution)/shard_map/ppermute | solution.py:536
  34.9 20.9 %collective-permute-start.8 = (f32[2,80,1280]{2,1,0:T(8,128)S(1)}, f32[2,80,1280]{2,1,0:T(8,128)S(1)}, u32[]{:S(2)}, u32[]{:S(2)}) collective-permute-start(f32[2,80,1280]{2,1,0:T(8,128)S(1)} %get-tuple-element.64.bottom), channel_id=1, source_target_pairs={{0,1},{2,3},{4,5},{6,7},{1,8},{3,10},{5,12},{7,14},{8,9},{10,11},{... | collective-permute-start | bytes 2457608 | tf_op jit(solution)/shard_map/ppermute | solution.py:537
  34.9 15.8 %collective-permute-start.1 = (f32[800,128]{1,0:T(8,128)S(1)}, f32[800,128]{1,0:T(8,128)S(1)}, u32[]{:S(2)}, u32[]{:S(2)}) collective-permute-start(f32[800,128]{1,0:T(8,128)S(1)} %copy-done.5), channel_id=1, source_target_pairs={{0,2},{1,4},{2,0},{3,6},{4,7},{5,1},{6,5},{7,3},{8,10},{9,12},{10,... | collective-permute-start | bytes 1228808 | tf_op jit(solution)/shard_map/ppermute | solution.py:509
  36.5 15.2 %collective-permute-start.6 = (f32[800,128]{1,0:T(8,128)S(1)}, f32[800,128]{1,0:T(8,128)S(1)}, u32[]{:S(2)}, u32[]{:S(2)}) collective-permute-start(f32[800,128]{1,0:T(8,128)S(1)} %copy-done.4), channel_id=1, source_target_pairs={{0,4},{1,2},{2,6},{3,0},{4,1},{5,7},{6,3},{7,5},{8,12},{9,10},{10,... | collective-permute-start | bytes 1228808 | tf_op jit(solution)/shard_map/ppermute | solution.py:509
  36.5 15.2 %collective-permute-start.7 = (f32[800,128]{1,0:T(8,128)S(1)}, f32[800,128]{1,0:T(8,128)S(1)}, u32[]{:S(2)}, u32[]{:S(2)}) collective-permute-start(f32[800,128]{1,0:T(8,128)S(1)} %copy-done.3), channel_id=1, source_target_pairs={{0,6},{1,0},{2,4},{3,2},{4,3},{5,5},{6,1},{7,7},{8,14},{9,8},{10,1... | collective-permute-start | bytes 1228808 | tf_op jit(solution)/shard_map/ppermute | solution.py:509
  55.8 18.9 %collective-permute-start.12 = (f32[2,72,1280]{2,1,0:T(8,128)S(1)}, f32[2,72,1280]{2,1,0:T(8,128)S(1)}, u32[]{:S(2)}, u32[]{:S(2)}) collective-permute-start(f32[2,72,1280]{2,1,0:T(8,128)S(1)} %get-tuple-element.72.bottom), channel_id=1, source_target_pairs={{0,1},{2,3},{4,5},{6,7},{1,8},{3,10},{5,12},{7,14},{8,9},{10,11},{... | collective-permute-start | bytes 2211848 | tf_op jit(solution)/shard_map/ppermute | solution.py:537
  59.5 18.3 %collective-permute-start.9 = (f32[2,72,1280]{2,1,0:T(8,128)S(1)}, f32[2,72,1280]{2,1,0:T(8,128)S(1)}, u32[]{:S(2)}, u32[]{:S(2)}) collective-permute-start(f32[2,72,1280]{2,1,0:T(8,128)S(1)} %get-tuple-element.71.top), channel_id=1, source_target_pairs={{1,0},{3,2},{5,4},{7,6},{8,1},{10,3},{12,5},{14,7},{9,8},{11,10},{... | collective-permute-start | bytes 2211848 | tf_op jit(solution)/shard_map/ppermute | solution.py:536
  77.4 14.9 %collective-permute-start.13 = (f32[2,72,1280]{2,1,0:T(8,128)S(1)}, f32[2,72,1280]{2,1,0:T(8,128)S(1)}, u32[]{:S(2)}, u32[]{:S(2)}) collective-permute-start(f32[2,72,1280]{2,1,0:T(8,128)S(1)} %top_kernel.4.top), channel_id=1, source_target_pairs={{1,0},{3,2},{5,4},{7,6},{8,1},{10,3},{12,5},{14,7},{9,8},{11,10},{... | collective-permute-start | bytes 2211848 | tf_op jit(solution)/shard_map/ppermute | solution.py:536
  80.6 16.6 %collective-permute-start.11 = (f32[2,72,1280]{2,1,0:T(8,128)S(1)}, f32[2,72,1280]{2,1,0:T(8,128)S(1)}, u32[]{:S(2)}, u32[]{:S(2)}) collective-permute-start(f32[2,72,1280]{2,1,0:T(8,128)S(1)} %bottom_kernel.4.bottom), channel_id=1, source_target_pairs={{0,1},{2,3},{4,5},{6,7},{1,8},{3,10},{5,12},{7,14},{8,9},{10,11},{... | collective-permute-start | bytes 2211848 | tf_op jit(solution)/shard_map/ppermute | solution.py:537
  86.4 14.5 %collective-permute-start.18 = (f32[10,64,128]{2,1,0:T(8,128)S(1)}, f32[10,64,128]{2,1,0:T(8,128)S(1)}, u32[]{:S(2)}, u32[]{:S(2)}) collective-permute-start(f32[10,64,128]{2,1,0:T(8,128)S(1)} %get-tuple-element.86), channel_id=1, source_target_pairs={{0,0},{6,1},{2,2},{4,3},{5,4},{3,5},{7,6},{1,7},{8,8},{14,9},{10,1... | collective-permute-start | bytes 983048 | tf_op jit(solution)/shard_map/ppermute | solution.py:581
  87.1 15.0 %collective-permute-start.19 = (f32[10,64,128]{2,1,0:T(8,128)S(1)}, f32[10,64,128]{2,1,0:T(8,128)S(1)}, u32[]{:S(2)}, u32[]{:S(2)}) collective-permute-start(f32[10,64,128]{2,1,0:T(8,128)S(1)} %get-tuple-element.87), channel_id=1, source_target_pairs={{2,0},{4,1},{0,2},{6,3},{7,4},{1,5},{5,6},{3,7},{10,8},{12,9},{8,1... | collective-permute-start | bytes 983048 | tf_op jit(solution)/shard_map/ppermute | solution.py:581
  88.7 16.9 %collective-permute-start.20 = (f32[10,64,128]{2,1,0:T(8,128)S(1)}, f32[10,64,128]{2,1,0:T(8,128)S(1)}, u32[]{:S(2)}, u32[]{:S(2)}) collective-permute-start(f32[10,64,128]{2,1,0:T(8,128)S(1)} %get-tuple-element.88), channel_id=1, source_target_pairs={{4,0},{2,1},{6,2},{0,3},{1,4},{7,5},{3,6},{5,7},{12,8},{10,9},{14,... | collective-permute-start | bytes 983048 | tf_op jit(solution)/shard_map/ppermute | solution.py:581
  92.4 15.3 %collective-permute-start.21 = (f32[10,64,128]{2,1,0:T(8,128)S(1)}, f32[10,64,128]{2,1,0:T(8,128)S(1)}, u32[]{:S(2)}, u32[]{:S(2)}) collective-permute-start(f32[10,64,128]{2,1,0:T(8,128)S(1)} %get-tuple-element.89), channel_id=1, source_target_pairs={{6,0},{0,1},{4,2},{2,3},{3,4},{5,5},{1,6},{7,7},{14,8},{8,9},{12,1... | collective-permute-start | bytes 983048 | tf_op jit(solution)/shard_map/ppermute | solution.py:581
  100.2 7.5 %collective-permute-start.14 = (f32[10,64,128]{2,1,0:T(8,128)S(1)}, f32[10,64,128]{2,1,0:T(8,128)S(1)}, u32[]{:S(2)}, u32[]{:S(2)}) collective-permute-start(f32[10,64,128]{2,1,0:T(8,128)S(1)} %get-tuple-element.81), channel_id=1, source_target_pairs={{0,0},{6,1},{2,2},{4,3},{5,4},{3,5},{7,6},{1,7},{8,8},{14,9},{10,1... | collective-permute-start | bytes 983048 | tf_op jit(solution)/shard_map/ppermute | solution.py:581
  100.9 12.6 %collective-permute-start.15 = (f32[10,64,128]{2,1,0:T(8,128)S(1)}, f32[10,64,128]{2,1,0:T(8,128)S(1)}, u32[]{:S(2)}, u32[]{:S(2)}) collective-permute-start(f32[10,64,128]{2,1,0:T(8,128)S(1)} %get-tuple-element.82), channel_id=1, source_target_pairs={{2,0},{4,1},{0,2},{6,3},{7,4},{1,5},{5,6},{3,7},{10,8},{12,9},{8,1... | collective-permute-start | bytes 983048 | tf_op jit(solution)/shard_map/ppermute | solution.py:581
  102.1 15.4 %collective-permute-start.16 = (f32[10,64,128]{2,1,0:T(8,128)S(1)}, f32[10,64,128]{2,1,0:T(8,128)S(1)}, u32[]{:S(2)}, u32[]{:S(2)}) collective-permute-start(f32[10,64,128]{2,1,0:T(8,128)S(1)} %get-tuple-element.83), channel_id=1, source_target_pairs={{4,0},{2,1},{6,2},{0,3},{1,4},{7,5},{3,6},{5,7},{12,8},{10,9},{14,... | collective-permute-start | bytes 983048 | tf_op jit(solution)/shard_map/ppermute | solution.py:581
  105.5 15.1 %collective-permute-start.17 = (f32[10,64,128]{2,1,0:T(8,128)S(1)}, f32[10,64,128]{2,1,0:T(8,128)S(1)}, u32[]{:S(2)}, u32[]{:S(2)}) collective-permute-start(f32[10,64,128]{2,1,0:T(8,128)S(1)} %get-tuple-element.84), channel_id=1, source_target_pairs={{6,0},{0,1},{4,2},{2,3},{3,4},{5,5},{1,6},{7,7},{14,8},{8,9},{12,1... | collective-permute-start | bytes 983048 | tf_op jit(solution)/shard_map/ppermute | solution.py:581

commit v7 on v6

--- a/solution.py
+++ b/solution.py
@@ -255,11 +255,20 @@
     def sea_row(place):
         return place[0][place[1], sea_cols]
 
-    for r in range(min(first[0] - 1, 1), max(first[-1] + 2, n - 1)):
+    needed = range(min(first[0] - 1, 1), max(first[-1] + 2, n - 1))
+    lane = lax.broadcasted_iota(jnp.int32, (1, LANES), 1)
+    currents = jnp.zeros((E, LANES), F32)
+    for r in needed:
         ref, i = rows[r]
         surface = ref[i, :, NB:CH]
-        moved[0, r] = DOPPLER * jnp.tanh(jnp.broadcast_to(surface[:, 0:1], (E, LANES)))
-        moved[1, r] = DOPPLER * jnp.tanh(jnp.broadcast_to(surface[:, L : L + 1], (E, LANES)))
+        for c in range(2):
+            brought = pltpu.roll(surface, (2 * r + c - c * L) % LANES, axis=1)
+            currents = jnp.where(lane == 2 * r + c, brought, currents)
+    currents = DOPPLER * jnp.tanh(currents)
+    for r in needed:
+        for c in range(2):
+            at = 2 * r + c
+            moved[c, r] = jnp.broadcast_to(currents[:, at : at + 1], (E, LANES))
 
     def advect(read, write, start, stop, speed_cx, speed_cy):
         plus_before, waiting = None, None
@@ -320,9 +329,8 @@
     own_sea = sea_rows[2 : n - 2]
     energy = moved_twice[...].reshape(count * N, NB)
     squares = energy * energy
-    interaction = jnp.dot(
-        energy.astype(BF16), weights[:NB], preferred_element_type=F32
-    ) + jnp.dot(squares.astype(BF16), weights[NB:], preferred_element_type=F32)
+    both = jnp.concatenate([energy.astype(BF16), squares.astype(BF16)], axis=1)
+    interaction = jnp.dot(both, weights[...], preferred_element_type=F32)
     total = jnp.sum(squares, axis=1, keepdims=True)
     sea_here = jnp.concatenate([sea_row(place)[keep] for place in own_sea], axis=0)
     scale = (DT_SOURCE * sea_here[:, 0:1]) / (1.0 + total / NB)

time: 124 us -> 124 us (level)
  no operation moved by 1% of the time
where the time goes in v7:
time: 124 us
  Pallas kernels  48.2 us (39%)
  starting transfers between devices  37 us (30%)
  waiting for transfers between devices  35.6 us (29%)
  local copies, waits for them, and re-layouts  1.92 us (2%)
    pallas_call x9, Pallas kernels, step_call(): pl.pallas_call(functools.partial(body, z, first, cut, sea_at), out_shape=...  35.5 us
    ppermute x4, waiting for transfers between devices, per_device(): got = [lax.ppermute(blocks[k], axes, forward[k]) for k in range(B)]  13.3 us
    ppermute x8, waiting for transfers between devices, per_device(): lax.ppermute(packed[i], axes, [(t, s) for s, t in forward[i % B]])  13 us
    ppermute x8, starting transfers between devices, per_device(): lax.ppermute(packed[i], axes, [(t, s) for s, t in forward[i % B]])  12.6 us
    ppermute x4, starting transfers between devices, per_device(): got = [lax.ppermute(packed[k], axes, forward[k]) for k in range(B)]  9.52 us
    ppermute x3, starting transfers between devices, per_device(): down = lax.ppermute(top, axes, to_prev_row)  9.41 us
    ppermute x4, waiting for transfers between devices, per_device(): got = [lax.ppermute(packed[k], axes, forward[k]) for k in range(B)]  6.76 us
    pallas_call x2, Pallas kernels, pack(): pl.pallas_call(functools.partial(pack_kernel, z, rows), out_shape=[jax.Sh...  6.62 us
  transfers between devices with their start and end apart: 22, of which 9 were waited for; matrix products, arithmetic and copies ran while one was open for 0% of the time, Pallas kernels for 34%

profile of v7, /device:TPU:0, one launch (start us, length us, event | category | flops | bytes accessed | tf_op | source)
XLA Modules:
  0.0 123.9 jit_solution(928537863640819162)
XLA Ops:
  0.7 3.4 %pack.3 = (f32[808,128]{1,0:T(8,128)}, f32[808,128]{1,0:T(8,128)}, f32[808,128]{1,0:T(8,128)}, f32[808,128]{1,0:T(8,128)}) custom-call(s32[1]{0:T(128)} %bitcast.odd, s32[1]{0:T(128)} %bitcast.1.part, f32[2304,256]{1,0:T(8,128)} %bitcast.6, f32[256,256]{1,0:T(8,128)} %bitcast.8, s32[8,256]{1,0:T(8,128)} %mask_in.3), custom_call_target="tpu_custom_call" | custom-call | tf_op jit(solution)/shard_map/pack/pallas_call | solution.py:466
  4.0 1.7 %collective-permute-start.2 = (f32[808,128]{1,0:T(8,128)}, f32[808,128]{1,0:T(8,128)S(1)}, u32[]{:S(2)}, u32[]{:S(2)}) collective-permute-start(f32[808,128]{1,0:T(8,128)} %get-tuple-element.51), channel_id=1, source_target_pairs={{0,0},{1,6},{2,2},{3,4},{4,5},{5,3},{6,7},{7,1},{8,8},{9,14},{10,1... | collective-permute-start | bytes 1241096 | tf_op jit(solution)/shard_map/ppermute | solution.py:482
  5.7 3.0 %collective-permute-start.3 = (f32[808,128]{1,0:T(8,128)}, f32[808,128]{1,0:T(8,128)S(1)}, u32[]{:S(2)}, u32[]{:S(2)}) collective-permute-start(f32[808,128]{1,0:T(8,128)} %get-tuple-element.52), channel_id=1, source_target_pairs={{0,2},{1,4},{2,0},{3,6},{4,7},{5,1},{6,5},{7,3},{8,10},{9,12},{10,... | collective-permute-start | bytes 1241096 | tf_op jit(solution)/shard_map/ppermute | solution.py:482
  9.9 3.6 %collective-permute-start.5 = (f32[808,128]{1,0:T(8,128)}, f32[808,128]{1,0:T(8,128)S(1)}, u32[]{:S(2)}, u32[]{:S(2)}) collective-permute-start(f32[808,128]{1,0:T(8,128)} %get-tuple-element.54), channel_id=1, source_target_pairs={{0,6},{1,0},{2,4},{3,2},{4,3},{5,5},{6,1},{7,7},{8,14},{9,8},{10,1... | collective-permute-start | bytes 1241096 | tf_op jit(solution)/shard_map/ppermute | solution.py:482
  13.6 3.3 %pack.2 = (f32[800,128]{1,0:T(8,128)}, f32[800,128]{1,0:T(8,128)}, f32[800,128]{1,0:T(8,128)}, f32[800,128]{1,0:T(8,128)}) custom-call(s32[1]{0:T(128)} %bitcast.odd, s32[1]{0:T(128)} %bitcast.1.part, f32[2304,256]{1,0:T(8,128)} %bitcast.7, f32[256,256]{1,0:T(8,128)} %bitcast.9, s32[8,256]{1,0:T(8,128)} %mask_in.3), custom_call_target="tpu_custom_call" | custom-call | tf_op jit(solution)/shard_map/pack/pallas_call | solution.py:466
  16.8 1.7 %collective-permute-start = (f32[800,128]{1,0:T(8,128)}, f32[800,128]{1,0:T(8,128)S(1)}, u32[]{:S(2)}, u32[]{:S(2)}) collective-permute-start(f32[800,128]{1,0:T(8,128)} %get-tuple-element.47), channel_id=1, source_target_pairs={{0,0},{1,6},{2,2},{3,4},{4,5},{5,3},{6,7},{7,1},{8,8},{9,14},{10,1... | collective-permute-start | bytes 1228808 | tf_op jit(solution)/shard_map/ppermute | solution.py:517
  18.9 1.7 %copy-done.1 = bf16[1152,1152]{1,0:T(8,128)(2,1)S(1)} copy-done((bf16[1152,1152]{1,0:T(8,128)(2,1)S(1)}, bf16[1152,1152]{1,0:T(8,128)(2,1)}, u32[]{:S(2)}) %copy-start.1) | copy-done | bytes 2654232
  20.6 1.5 %weights.1 = (bf16[2304,1152]{1,0:T(8,128)(2,1)S(1)}, bf16[1152,128]{1,0:T(8,128)(2,1)S(1)}) custom-call(bf16[1152,1152]{1,0:T(8,128)(2,1)S(1)} %copy-done, bf16[1152,1152]{1,0:T(8,128)(2,1)S(1)} %copy-done.1, bf16[128,1152]{1,0:T(8,128)(2,1)S(1)} %copy-done.2), custom_call_target="tpu_custom_call" | custom-call | flops 2000000000 | bytes 10616832 | tf_op jit(solution)/shard_map/weights/pallas_call | solution.py:485
  22.2 2.3 %collective-permute-done.3.refs_1_ = f32[808,128]{1,0:T(8,128)S(1)} collective-permute-done((f32[808,128]{1,0:T(8,128)}, f32[808,128]{1,0:T(8,128)S(1)}, u32[]{:S(2)}, u32[]{:S(2)}) %collective-permute-start.3) | collective-permute-done | bytes 413728 | tf_op jit(solution)/shard_map/ppermute | solution.py:482
  25.1 3.9 %collective-permute-done.5.refs_3_ = f32[808,128]{1,0:T(8,128)S(1)} collective-permute-done((f32[808,128]{1,0:T(8,128)}, f32[808,128]{1,0:T(8,128)S(1)}, u32[]{:S(2)}, u32[]{:S(2)}) %collective-permute-start.5) | collective-permute-done | bytes 413728 | tf_op jit(solution)/shard_map/ppermute | solution.py:482
  29.6 5.3 %collective-permute-start.10 = (f32[2,80,1280]{2,1,0:T(8,128)S(1)}, f32[2,80,1280]{2,1,0:T(8,128)S(1)}, u32[]{:S(2)}, u32[]{:S(2)}) collective-permute-start(f32[2,80,1280]{2,1,0:T(8,128)S(1)} %get-tuple-element.65.top), channel_id=1, source_target_pairs={{1,0},{3,2},{5,4},{7,6},{8,1},{10,3},{12,5},{14,7},{9,8},{11,10},{... | collective-permute-start | bytes 2457608 | tf_op jit(solution)/shard_map/ppermute | solution.py:544
  36.5 1.9 %collective-permute-start.7 = (f32[800,128]{1,0:T(8,128)S(1)}, f32[800,128]{1,0:T(8,128)S(1)}, u32[]{:S(2)}, u32[]{:S(2)}) collective-permute-start(f32[800,128]{1,0:T(8,128)S(1)} %copy-done.3), channel_id=1, source_target_pairs={{0,6},{1,0},{2,4},{3,2},{4,3},{5,5},{6,1},{7,7},{8,14},{9,8},{10,1... | collective-permute-start | bytes 1228808 | tf_op jit(solution)/shard_map/ppermute | solution.py:517
  38.4 12.3 %collective-permute-done.1.refs_1_ = f32[800,128]{1,0:T(8,128)S(1)} collective-permute-done((f32[800,128]{1,0:T(8,128)S(1)}, f32[800,128]{1,0:T(8,128)S(1)}, u32[]{:S(2)}, u32[]{:S(2)}) %collective-permute-start.1) | collective-permute-done | bytes 409632 | tf_op jit(solution)/shard_map/ppermute | solution.py:517
  52.1 3.7 %bottom_kernel.3 = (f32[2,72,1280]{2,1,0:T(8,128)S(1)}, f32[2,80,128]{2,1,0:T(8,128)S(1)}) custom-call(f32[2,80,1280]{2,1,0:T(8,128)S(1)} %collective-permute-done.10.down, f32[2,80,1280]{2,1,0:T(8,128)S(1)} %get-tuple-element.64.bottom, f32[4,80,1280]{2,1,0:T(8,128)S(1)} %unpack.3.inner, f32[8,80,128]{2,1,0:T(8,128)S(1)} %get-tuple-element.66.sea, ...), custom_call_target="tpu_custom_call" | custom-call | flops 200000000 | bytes 200000 | tf_op jit(solution)/shard_map/bottom_kernel/pallas_call | solution.py:524
  55.9 3.7 %top_kernel.3 = (f32[2,72,1280]{2,1,0:T(8,128)S(1)}, f32[2,80,128]{2,1,0:T(8,128)S(1)}) custom-call(f32[2,80,1280]{2,1,0:T(8,128)S(1)} %collective-permute-done.8.up, f32[2,80,1280]{2,1,0:T(8,128)S(1)} %get-tuple-element.65.top, f32[4,80,1280]{2,1,0:T(8,128)S(1)} %unpack.3.inner, f32[8,80,128]{2,1,0:T(8,128)S(1)} %get-tuple-element.66.sea, ...), custom_call_target="tpu_custom_call" | custom-call | flops 200000000 | bytes 200000 | tf_op jit(solution)/shard_map/top_kernel/pallas_call | solution.py:524
  59.6 3.8 %collective-permute-start.9 = (f32[2,72,1280]{2,1,0:T(8,128)S(1)}, f32[2,72,1280]{2,1,0:T(8,128)S(1)}, u32[]{:S(2)}, u32[]{:S(2)}) collective-permute-start(f32[2,72,1280]{2,1,0:T(8,128)S(1)} %get-tuple-element.71.top), channel_id=1, source_target_pairs={{1,0},{3,2},{5,4},{7,6},{8,1},{10,3},{12,5},{14,7},{9,8},{11,10},{... | collective-permute-start | bytes 2211848 | tf_op jit(solution)/shard_map/ppermute | solution.py:544
  63.4 6.0 %inner_kernel.3.inner = f32[4,72,1280]{2,1,0:T(8,128)S(1)} custom-call(f32[2,80,1280]{2,1,0:T(8,128)S(1)} %get-tuple-element.65.top, f32[4,80,1280]{2,1,0:T(8,128)S(1)} %unpack.3.inner, f32[2,80,1280]{2,1,0:T(8,128)S(1)} %get-tuple-element.64.bottom, f32[8,80,128]{2,1,0:T(8,128)S(1)} %get-tuple-element.66.sea, ...), custom_call_target="tpu_custom_call" | custom-call | flops 400000000 | bytes 400000 | tf_op jit(solution)/shard_map/inner_kernel/pallas_call | solution.py:524
  69.4 5.6 %inner_kernel.4 = (f32[4,72,1280]{2,1,0:T(8,128)S(1)}, f32[2,72,1152]{2,1,0:T(8,128)S(1)}, f32[2,72,1152]{2,1,0:T(8,128)S(1)}) custom-call(f32[2,72,1280]{2,1,0:T(8,128)S(1)} %get-tuple-element.71.top, f32[4,72,1280]{2,1,0:T(8,128)S(1)} %inner_kernel.3.inner, f32[2,72,1280]{2,1,0:T(8,128)S(1)} %get-tuple-element.72.bottom, ...), custom_call_target="tpu_custom_call" | custom-call | flops 400000000 | bytes 400000 | tf_op jit(solution)/shard_map/inner_kernel/pallas_call | solution.py:524
  75.1 2.8 %top_kernel.4.top = f32[2,72,1280]{2,1,0:T(8,128)S(1)} custom-call(f32[2,72,1280]{2,1,0:T(8,128)S(1)} %collective-permute-done.12.up, f32[2,72,1280]{2,1,0:T(8,128)S(1)} %get-tuple-element.71.top, f32[4,72,1280]{2,1,0:T(8,128)S(1)} %inner_kernel.3.inner, f32[8,80,128]{2,1,0:T(8,128)S(1)} %get-tuple-element.66.sea, ...), custom_call_target="tpu_custom_call" | custom-call | flops 200000000 | bytes 200000 | tf_op jit(solution)/shard_map/top_kernel/pallas_call | solution.py:524
  78.2 2.8 %bottom_kernel.4.bottom = f32[2,72,1280]{2,1,0:T(8,128)S(1)} custom-call(f32[2,72,1280]{2,1,0:T(8,128)S(1)} %collective-permute-done.9.down, f32[2,72,1280]{2,1,0:T(8,128)S(1)} %get-tuple-element.72.bottom, f32[4,72,1280]{2,1,0:T(8,128)S(1)} %inner_kernel.3.inner, f32[8,80,128]{2,1,0:T(8,128)S(1)} %get-tuple-element.66.sea, ...), custom_call_target="tpu_custom_call" | custom-call | flops 200000000 | bytes 200000 | tf_op jit(solution)/shard_map/bottom_kernel/pallas_call | solution.py:524
  81.3 5.3 %inner_kernel.5 = (f32[4,64,1280]{2,1,0:T(8,128)S(1)}, f32[2,72,1152]{2,1,0:T(8,128)S(1)}, f32[2,72,1152]{2,1,0:T(8,128)S(1)}) custom-call(f32[2,72,1280]{2,1,0:T(8,128)S(1)} %top_kernel.4.top, f32[4,72,1280]{2,1,0:T(8,128)S(1)} %get-tuple-element.78.inner, f32[2,72,1280]{2,1,0:T(8,128)S(1)} %bottom_kernel.4.bottom, ...), custom_call_target="tpu_custom_call" | custom-call | flops 400000000 | bytes 400000 | tf_op jit(solution)/shard_map/inner_kernel/pallas_call | solution.py:524
  87.7 1.5 %collective-permute-start.19 = (f32[10,64,128]{2,1,0:T(8,128)S(1)}, f32[10,64,128]{2,1,0:T(8,128)S(1)}, u32[]{:S(2)}, u32[]{:S(2)}) collective-permute-start(f32[10,64,128]{2,1,0:T(8,128)S(1)} %get-tuple-element.87), channel_id=1, source_target_pairs={{2,0},{4,1},{0,2},{6,3},{7,4},{1,5},{5,6},{3,7},{10,8},{12,9},{8,1... | collective-permute-start | bytes 983048 | tf_op jit(solution)/shard_map/ppermute | solution.py:589
  90.1 2.6 %collective-permute-done.13.down = f32[2,72,1280]{2,1,0:T(8,128)S(1)} collective-permute-done((f32[2,72,1280]{2,1,0:T(8,128)S(1)}, f32[2,72,1280]{2,1,0:T(8,128)S(1)}, u32[]{:S(2)}, u32[]{:S(2)}) %collective-permute-start.13) | collective-permute-done | bytes 737312 | tf_op jit(solution)/shard_map/ppermute | solution.py:544
  92.7 2.1 %collective-permute-start.21 = (f32[10,64,128]{2,1,0:T(8,128)S(1)}, f32[10,64,128]{2,1,0:T(8,128)S(1)}, u32[]{:S(2)}, u32[]{:S(2)}) collective-permute-start(f32[10,64,128]{2,1,0:T(8,128)S(1)} %get-tuple-element.89), channel_id=1, source_target_pairs={{6,0},{0,1},{4,2},{2,3},{3,4},{5,5},{1,6},{7,7},{14,8},{8,9},{12,1... | collective-permute-start | bytes 983048 | tf_op jit(solution)/shard_map/ppermute | solution.py:589
  94.8 2.8 %bottom_kernel.5.refs_1_ = f32[2,64,1280]{2,1,0:T(8,128)S(1)} custom-call(f32[2,72,1280]{2,1,0:T(8,128)S(1)} %collective-permute-done.13.down, f32[2,72,1280]{2,1,0:T(8,128)S(1)} %bottom_kernel.4.bottom, f32[4,72,1280]{2,1,0:T(8,128)S(1)} %get-tuple-element.78.inner, f32[8,80,128]{2,1,0:T(8,128)S(1)} %get-tuple-element.66.sea, ...), custom_call_target="tpu_custom_call" | custom-call | flops 200000000 | bytes 200000 | tf_op jit(solution)/shard_map/bottom_kernel/pallas_call | solution.py:524
  97.7 2.7 %top_kernel.5.refs_0_ = f32[2,64,1280]{2,1,0:T(8,128)S(1)} custom-call(f32[2,72,1280]{2,1,0:T(8,128)S(1)} %collective-permute-done.11.up, f32[2,72,1280]{2,1,0:T(8,128)S(1)} %top_kernel.4.top, f32[4,72,1280]{2,1,0:T(8,128)S(1)} %get-tuple-element.78.inner, f32[8,80,128]{2,1,0:T(8,128)S(1)} %get-tuple-element.66.sea, ...), custom_call_target="tpu_custom_call" | custom-call | flops 200000000 | bytes 200000 | tf_op jit(solution)/shard_map/top_kernel/pallas_call | solution.py:524
  102.7 3.4 %collective-permute-start.16 = (f32[10,64,128]{2,1,0:T(8,128)S(1)}, f32[10,64,128]{2,1,0:T(8,128)S(1)}, u32[]{:S(2)}, u32[]{:S(2)}) collective-permute-start(f32[10,64,128]{2,1,0:T(8,128)S(1)} %get-tuple-element.83), channel_id=1, source_target_pairs={{4,0},{2,1},{6,2},{0,3},{1,4},{7,5},{3,6},{5,7},{12,8},{10,9},{14,... | collective-permute-start | bytes 983048 | tf_op jit(solution)/shard_map/ppermute | solution.py:589
  106.1 2.1 %collective-permute-start.17 = (f32[10,64,128]{2,1,0:T(8,128)S(1)}, f32[10,64,128]{2,1,0:T(8,128)S(1)}, u32[]{:S(2)}, u32[]{:S(2)}) collective-permute-start(f32[10,64,128]{2,1,0:T(8,128)S(1)} %get-tuple-element.84), channel_id=1, source_target_pairs={{6,0},{0,1},{4,2},{2,3},{3,4},{5,5},{1,6},{7,7},{14,8},{8,9},{12,1... | collective-permute-start | bytes 983048 | tf_op jit(solution)/shard_map/ppermute | solution.py:589
  108.2 5.9 %collective-permute-done.15.refs_1_ = f32[10,64,128]{2,1,0:T(8,128)S(1)} collective-permute-done((f32[10,64,128]{2,1,0:T(8,128)S(1)}, f32[10,64,128]{2,1,0:T(8,128)S(1)}, u32[]{:S(2)}, u32[]{:S(2)}) %collective-permute-start.15) | collective-permute-done | bytes 327712 | tf_op jit(solution)/shard_map/ppermute | solution.py:589
  114.1 4.0 %collective-permute-done.16.refs_2_ = f32[10,64,128]{2,1,0:T(8,128)S(1)} collective-permute-done((f32[10,64,128]{2,1,0:T(8,128)S(1)}, f32[10,64,128]{2,1,0:T(8,128)S(1)}, u32[]{:S(2)}, u32[]{:S(2)}) %collective-permute-start.16) | collective-permute-done | bytes 327712 | tf_op jit(solution)/shard_map/ppermute | solution.py:589
  118.1 3.1 %collective-permute-done.17.refs_3_ = f32[10,64,128]{2,1,0:T(8,128)S(1)} collective-permute-done((f32[10,64,128]{2,1,0:T(8,128)S(1)}, f32[10,64,128]{2,1,0:T(8,128)S(1)}, u32[]{:S(2)}, u32[]{:S(2)}) %collective-permute-start.17) | collective-permute-done | bytes 327712 | tf_op jit(solution)/shard_map/ppermute | solution.py:589
  121.2 2.7 %restore.1 = (f32[2304,256]{1,0:T(8,128)}, f32[256,256]{1,0:T(8,128)}) custom-call(s32[1]{0:T(128)} %bitcast.odd, s32[1]{0:T(128)} %bitcast.1.part, f32[10,64,128]{2,1,0:T(8,128)S(1)} %collective-permute-done.14.refs_0_, f32[10,64,128]{2,1,0:T(8,128)S(1)} %collective-permute-done.15.refs_1_, f32[10,64,128]{2,1,0:T(8,128)S(1)} %collective-permute-done.16.refs_2_, ...), custom_call_target="tpu_custom_call" | custom-call | tf_op jit(solution)/shard_map/restore/pallas_call | solution.py:591
  (47 shorter events, 10.7 us)
Async XLA Ops:
  0.6 18.2 %copy-start = (bf16[1152,1152]{1,0:T(8,128)(2,1)S(1)}, bf16[1152,1152]{1,0:T(8,128)(2,1)}, u32[]{:S(2)}) copy-start(bf16[1152,1152]{1,0:T(8,128)(2,1)} %linear.1) | copy-start | bytes 7962628
  0.7 18.2 %copy-start.2 = (bf16[128,1152]{1,0:T(8,128)(2,1)S(1)}, bf16[128,1152]{1,0:T(8,128)(2,1)}, u32[]{:S(2)}) copy-start(bf16[128,1152]{1,0:T(8,128)(2,1)} %drift.1) | copy-start | bytes 884740
  4.0 18.2 %collective-permute-start.2 = (f32[808,128]{1,0:T(8,128)}, f32[808,128]{1,0:T(8,128)S(1)}, u32[]{:S(2)}, u32[]{:S(2)}) collective-permute-start(f32[808,128]{1,0:T(8,128)} %get-tuple-element.51), channel_id=1, source_target_pairs={{0,0},{1,6},{2,2},{3,4},{4,5},{5,3},{6,7},{7,1},{8,8},{9,14},{10,1... | collective-permute-start | bytes 1241096 | tf_op jit(solution)/shard_map/ppermute | solution.py:482
  5.7 18.9 %collective-permute-start.3 = (f32[808,128]{1,0:T(8,128)}, f32[808,128]{1,0:T(8,128)S(1)}, u32[]{:S(2)}, u32[]{:S(2)}) collective-permute-start(f32[808,128]{1,0:T(8,128)} %get-tuple-element.52), channel_id=1, source_target_pairs={{0,2},{1,4},{2,0},{3,6},{4,7},{5,1},{6,5},{7,3},{8,10},{9,12},{10,... | collective-permute-start | bytes 1241096 | tf_op jit(solution)/shard_map/ppermute | solution.py:482
  8.7 16.4 %collective-permute-start.4 = (f32[808,128]{1,0:T(8,128)}, f32[808,128]{1,0:T(8,128)S(1)}, u32[]{:S(2)}, u32[]{:S(2)}) collective-permute-start(f32[808,128]{1,0:T(8,128)} %get-tuple-element.53), channel_id=1, source_target_pairs={{0,4},{1,2},{2,6},{3,0},{4,1},{5,7},{6,3},{7,5},{8,12},{9,10},{10,... | collective-permute-start | bytes 1241096 | tf_op jit(solution)/shard_map/ppermute | solution.py:482
  9.9 19.1 %collective-permute-start.5 = (f32[808,128]{1,0:T(8,128)}, f32[808,128]{1,0:T(8,128)S(1)}, u32[]{:S(2)}, u32[]{:S(2)}) collective-permute-start(f32[808,128]{1,0:T(8,128)} %get-tuple-element.54), channel_id=1, source_target_pairs={{0,6},{1,0},{2,4},{3,2},{4,3},{5,5},{6,1},{7,7},{8,14},{9,8},{10,1... | collective-permute-start | bytes 1241096 | tf_op jit(solution)/shard_map/ppermute | solution.py:482
  16.8 19.6 %collective-permute-start = (f32[800,128]{1,0:T(8,128)}, f32[800,128]{1,0:T(8,128)S(1)}, u32[]{:S(2)}, u32[]{:S(2)}) collective-permute-start(f32[800,128]{1,0:T(8,128)} %get-tuple-element.47), channel_id=1, source_target_pairs={{0,0},{1,6},{2,2},{3,4},{4,5},{5,3},{6,7},{7,1},{8,8},{9,14},{10,1... | collective-permute-start | bytes 1228808 | tf_op jit(solution)/shard_map/ppermute | solution.py:517
  18.9 1.8 %copy-start.1 = (bf16[1152,1152]{1,0:T(8,128)(2,1)S(1)}, bf16[1152,1152]{1,0:T(8,128)(2,1)}, u32[]{:S(2)}) copy-start(bf16[1152,1152]{1,0:T(8,128)(2,1)} %square.1) | copy-start | bytes 7962628
  20.6 14.3 %copy-start.5 = (f32[800,128]{1,0:T(8,128)S(1)}, f32[800,128]{1,0:T(8,128)}, u32[]{:S(2)}) copy-start(f32[800,128]{1,0:T(8,128)} %get-tuple-element.48) | copy-start | bytes 1228804
  20.6 15.8 %copy-start.4 = (f32[800,128]{1,0:T(8,128)S(1)}, f32[800,128]{1,0:T(8,128)}, u32[]{:S(2)}) copy-start(f32[800,128]{1,0:T(8,128)} %get-tuple-element.62) | copy-start | bytes 1228804
  20.6 15.9 %copy-start.3 = (f32[800,128]{1,0:T(8,128)S(1)}, f32[800,128]{1,0:T(8,128)}, u32[]{:S(2)}) copy-start(f32[800,128]{1,0:T(8,128)} %get-tuple-element.63) | copy-start | bytes 1228804
  29.6 22.5 %collective-permute-start.10 = (f32[2,80,1280]{2,1,0:T(8,128)S(1)}, f32[2,80,1280]{2,1,0:T(8,128)S(1)}, u32[]{:S(2)}, u32[]{:S(2)}) collective-permute-start(f32[2,80,1280]{2,1,0:T(8,128)S(1)} %get-tuple-element.65.top), channel_id=1, source_target_pairs={{1,0},{3,2},{5,4},{7,6},{8,1},{10,3},{12,5},{14,7},{9,8},{11,10},{... | collective-permute-start | bytes 2457608 | tf_op jit(solution)/shard_map/ppermute | solution.py:544
  34.9 21.0 %collective-permute-start.8 = (f32[2,80,1280]{2,1,0:T(8,128)S(1)}, f32[2,80,1280]{2,1,0:T(8,128)S(1)}, u32[]{:S(2)}, u32[]{:S(2)}) collective-permute-start(f32[2,80,1280]{2,1,0:T(8,128)S(1)} %get-tuple-element.64.bottom), channel_id=1, source_target_pairs={{0,1},{2,3},{4,5},{6,7},{1,8},{3,10},{5,12},{7,14},{8,9},{10,11},{... | collective-permute-start | bytes 2457608 | tf_op jit(solution)/shard_map/ppermute | solution.py:545
  34.9 15.8 %collective-permute-start.1 = (f32[800,128]{1,0:T(8,128)S(1)}, f32[800,128]{1,0:T(8,128)S(1)}, u32[]{:S(2)}, u32[]{:S(2)}) collective-permute-start(f32[800,128]{1,0:T(8,128)S(1)} %copy-done.5), channel_id=1, source_target_pairs={{0,2},{1,4},{2,0},{3,6},{4,7},{5,1},{6,5},{7,3},{8,10},{9,12},{10,... | collective-permute-start | bytes 1228808 | tf_op jit(solution)/shard_map/ppermute | solution.py:517
  36.5 15.2 %collective-permute-start.6 = (f32[800,128]{1,0:T(8,128)S(1)}, f32[800,128]{1,0:T(8,128)S(1)}, u32[]{:S(2)}, u32[]{:S(2)}) collective-permute-start(f32[800,128]{1,0:T(8,128)S(1)} %copy-done.4), channel_id=1, source_target_pairs={{0,4},{1,2},{2,6},{3,0},{4,1},{5,7},{6,3},{7,5},{8,12},{9,10},{10,... | collective-permute-start | bytes 1228808 | tf_op jit(solution)/shard_map/ppermute | solution.py:517
  36.5 15.2 %collective-permute-start.7 = (f32[800,128]{1,0:T(8,128)S(1)}, f32[800,128]{1,0:T(8,128)S(1)}, u32[]{:S(2)}, u32[]{:S(2)}) collective-permute-start(f32[800,128]{1,0:T(8,128)S(1)} %copy-done.3), channel_id=1, source_target_pairs={{0,6},{1,0},{2,4},{3,2},{4,3},{5,5},{6,1},{7,7},{8,14},{9,8},{10,1... | collective-permute-start | bytes 1228808 | tf_op jit(solution)/shard_map/ppermute | solution.py:517
  55.9 19.2 %collective-permute-start.12 = (f32[2,72,1280]{2,1,0:T(8,128)S(1)}, f32[2,72,1280]{2,1,0:T(8,128)S(1)}, u32[]{:S(2)}, u32[]{:S(2)}) collective-permute-start(f32[2,72,1280]{2,1,0:T(8,128)S(1)} %get-tuple-element.72.bottom), channel_id=1, source_target_pairs={{0,1},{2,3},{4,5},{6,7},{1,8},{3,10},{5,12},{7,14},{8,9},{10,11},{... | collective-permute-start | bytes 2211848 | tf_op jit(solution)/shard_map/ppermute | solution.py:545
  59.6 18.6 %collective-permute-start.9 = (f32[2,72,1280]{2,1,0:T(8,128)S(1)}, f32[2,72,1280]{2,1,0:T(8,128)S(1)}, u32[]{:S(2)}, u32[]{:S(2)}) collective-permute-start(f32[2,72,1280]{2,1,0:T(8,128)S(1)} %get-tuple-element.71.top), channel_id=1, source_target_pairs={{1,0},{3,2},{5,4},{7,6},{8,1},{10,3},{12,5},{14,7},{9,8},{11,10},{... | collective-permute-start | bytes 2211848 | tf_op jit(solution)/shard_map/ppermute | solution.py:544
  77.8 14.9 %collective-permute-start.13 = (f32[2,72,1280]{2,1,0:T(8,128)S(1)}, f32[2,72,1280]{2,1,0:T(8,128)S(1)}, u32[]{:S(2)}, u32[]{:S(2)}) collective-permute-start(f32[2,72,1280]{2,1,0:T(8,128)S(1)} %top_kernel.4.top), channel_id=1, source_target_pairs={{1,0},{3,2},{5,4},{7,6},{8,1},{10,3},{12,5},{14,7},{9,8},{11,10},{... | collective-permute-start | bytes 2211848 | tf_op jit(solution)/shard_map/ppermute | solution.py:544
  81.0 16.6 %collective-permute-start.11 = (f32[2,72,1280]{2,1,0:T(8,128)S(1)}, f32[2,72,1280]{2,1,0:T(8,128)S(1)}, u32[]{:S(2)}, u32[]{:S(2)}) collective-permute-start(f32[2,72,1280]{2,1,0:T(8,128)S(1)} %bottom_kernel.4.bottom), channel_id=1, source_target_pairs={{0,1},{2,3},{4,5},{6,7},{1,8},{3,10},{5,12},{7,14},{8,9},{10,11},{... | collective-permute-start | bytes 2211848 | tf_op jit(solution)/shard_map/ppermute | solution.py:545
  87.0 14.5 %collective-permute-start.18 = (f32[10,64,128]{2,1,0:T(8,128)S(1)}, f32[10,64,128]{2,1,0:T(8,128)S(1)}, u32[]{:S(2)}, u32[]{:S(2)}) collective-permute-start(f32[10,64,128]{2,1,0:T(8,128)S(1)} %get-tuple-element.86), channel_id=1, source_target_pairs={{0,0},{6,1},{2,2},{4,3},{5,4},{3,5},{7,6},{1,7},{8,8},{14,9},{10,1... | collective-permute-start | bytes 983048 | tf_op jit(solution)/shard_map/ppermute | solution.py:589
  87.7 15.0 %collective-permute-start.19 = (f32[10,64,128]{2,1,0:T(8,128)S(1)}, f32[10,64,128]{2,1,0:T(8,128)S(1)}, u32[]{:S(2)}, u32[]{:S(2)}) collective-permute-start(f32[10,64,128]{2,1,0:T(8,128)S(1)} %get-tuple-element.87), channel_id=1, source_target_pairs={{2,0},{4,1},{0,2},{6,3},{7,4},{1,5},{5,6},{3,7},{10,8},{12,9},{8,1... | collective-permute-start | bytes 983048 | tf_op jit(solution)/shard_map/ppermute | solution.py:589
  89.2 16.9 %collective-permute-start.20 = (f32[10,64,128]{2,1,0:T(8,128)S(1)}, f32[10,64,128]{2,1,0:T(8,128)S(1)}, u32[]{:S(2)}, u32[]{:S(2)}) collective-permute-start(f32[10,64,128]{2,1,0:T(8,128)S(1)} %get-tuple-element.88), channel_id=1, source_target_pairs={{4,0},{2,1},{6,2},{0,3},{1,4},{7,5},{3,6},{5,7},{12,8},{10,9},{14,... | collective-permute-start | bytes 983048 | tf_op jit(solution)/shard_map/ppermute | solution.py:589
  92.7 15.5 %collective-permute-start.21 = (f32[10,64,128]{2,1,0:T(8,128)S(1)}, f32[10,64,128]{2,1,0:T(8,128)S(1)}, u32[]{:S(2)}, u32[]{:S(2)}) collective-permute-start(f32[10,64,128]{2,1,0:T(8,128)S(1)} %get-tuple-element.89), channel_id=1, source_target_pairs={{6,0},{0,1},{4,2},{2,3},{3,4},{5,5},{1,6},{7,7},{14,8},{8,9},{12,1... | collective-permute-start | bytes 983048 | tf_op jit(solution)/shard_map/ppermute | solution.py:589
  100.8 7.4 %collective-permute-start.14 = (f32[10,64,128]{2,1,0:T(8,128)S(1)}, f32[10,64,128]{2,1,0:T(8,128)S(1)}, u32[]{:S(2)}, u32[]{:S(2)}) collective-permute-start(f32[10,64,128]{2,1,0:T(8,128)S(1)} %get-tuple-element.81), channel_id=1, source_target_pairs={{0,0},{6,1},{2,2},{4,3},{5,4},{3,5},{7,6},{1,7},{8,8},{14,9},{10,1... | collective-permute-start | bytes 983048 | tf_op jit(solution)/shard_map/ppermute | solution.py:589
  101.5 12.6 %collective-permute-start.15 = (f32[10,64,128]{2,1,0:T(8,128)S(1)}, f32[10,64,128]{2,1,0:T(8,128)S(1)}, u32[]{:S(2)}, u32[]{:S(2)}) collective-permute-start(f32[10,64,128]{2,1,0:T(8,128)S(1)} %get-tuple-element.82), channel_id=1, source_target_pairs={{2,0},{4,1},{0,2},{6,3},{7,4},{1,5},{5,6},{3,7},{10,8},{12,9},{8,1... | collective-permute-start | bytes 983048 | tf_op jit(solution)/shard_map/ppermute | solution.py:589
  102.7 15.4 %collective-permute-start.16 = (f32[10,64,128]{2,1,0:T(8,128)S(1)}, f32[10,64,128]{2,1,0:T(8,128)S(1)}, u32[]{:S(2)}, u32[]{:S(2)}) collective-permute-start(f32[10,64,128]{2,1,0:T(8,128)S(1)} %get-tuple-element.83), channel_id=1, source_target_pairs={{4,0},{2,1},{6,2},{0,3},{1,4},{7,5},{3,6},{5,7},{12,8},{10,9},{14,... | collective-permute-start | bytes 983048 | tf_op jit(solution)/shard_map/ppermute | solution.py:589
  106.1 15.1 %collective-permute-start.17 = (f32[10,64,128]{2,1,0:T(8,128)S(1)}, f32[10,64,128]{2,1,0:T(8,128)S(1)}, u32[]{:S(2)}, u32[]{:S(2)}) collective-permute-start(f32[10,64,128]{2,1,0:T(8,128)S(1)} %get-tuple-element.84), channel_id=1, source_target_pairs={{6,0},{0,1},{4,2},{2,3},{3,4},{5,5},{1,6},{7,7},{14,8},{8,9},{12,1... | collective-permute-start | bytes 983048 | tf_op jit(solution)/shard_map/ppermute | solution.py:589

commit v8 on v6

--- a/solution.py
+++ b/solution.py
@@ -18,6 +18,7 @@
 DOPPLER = 0.1
 
 LANES = 128
+SUBLANES = 8
 PAD = 8
 EDGE = 2
 VMEM = pl.BlockSpec(memory_space=pltpu.VMEM)
@@ -49,11 +50,11 @@
 
     def folds(self, rows):
         out, base = [], len(rows) * self.mt
-        for count, lane in ((self.nr, self.B * self.main), (self.no, self.NB)):
+        for count, tile in ((self.nr, self.B * self.mt), (self.no, self.NB // LANES)):
             used = min(LANES // count, len(rows))
             deep = len(rows) // used
             assert deep * used == len(rows)
-            out.append((count, used, deep, base, lane))
+            out.append((count, used, deep, base, tile))
             base += deep
         return out, base
 
@@ -135,47 +136,45 @@
         lines = got[0][z.slabs(rows) * E : z.slabs(rows) * E + z.R]
         for r in range(z.R):
             sea[r] = spread_line(lines[r : r + 1])[:E]
-    places = [(ref, i) for ref in outs for i in range(ref.shape[0])]
+    places = listed(*outs)
     src = [exchange_part(z, k, odd[0], part[0]) for k in range(B)]
     for k in range(B):
         for t in range(mt):
-            lanes = pl.ds(pl.multiple_of(src[k] * z.main + t * LANES, LANES), LANES)
             for i, (ref, at) in enumerate(places):
-                ref[at, :, lanes] = got[k][(i * mt + t) * E : (i * mt + t + 1) * E]
-    for count, used, deep, base, lane in z.folds(rows)[0]:
+                ref[src[k] * mt + t, at] = got[k][(i * mt + t) * E : (i * mt + t + 1) * E]
+    for count, used, deep, base, home in z.folds(rows)[0]:
         group = lane_group(count)
         for i, (ref, at) in enumerate(places):
-            tile = jnp.zeros(ref.shape[1:2] + (LANES,), F32)
+            tile = jnp.zeros((E, LANES), F32)
             for k in range(B):
                 shift = lax.rem((src[k] - i // deep) * count + LANES, LANES)
                 slab = base + i % deep
                 moved = pltpu.roll(got[k][slab * E : (slab + 1) * E], shift, axis=1)
                 tile = jnp.where(group == src[k], moved, tile)
-            ref[at, :, lane : lane + LANES] = tile
+            ref[home, at] = tile
     if rows == z.edge_rows:
         for i, (ref, at) in enumerate(places):
             r = rows[i]
-            ref[at, 0:1, 0:LANES] = lines[r : r + 1]
+            ref[0, at, 0:1] = lines[r : r + 1]
 
 
 def send_back_kernel(z, rows, odd, part, *refs):
     B, mt = z.B, z.mt
     states, outs = refs[:-B], refs[-B:]
-    places = [(ref, i) for ref in states for i in range(ref.shape[0])]
+    places = listed(*states)
     for k in range(B):
         src = exchange_part(z, k, odd[0], part[0])
         for t in range(mt):
-            lanes = pl.ds(pl.multiple_of(src * z.main + t * LANES, LANES), LANES)
             for i, (ref, at) in enumerate(places):
-                outs[k][i * mt + t] = ref[at, :, lanes]
-        for count, used, deep, base, lane in z.folds(rows)[0]:
+                outs[k][i * mt + t] = ref[src * mt + t, at]
+        for count, used, deep, base, home in z.folds(rows)[0]:
             group = lane_group(count)
             for rr in range(deep):
                 tile = jnp.zeros((z.C, LANES), F32)
                 for i in range(used):
                     ref, at = places[rr + i * deep]
                     shift = lax.rem((i - src) * count + LANES, LANES)
-                    moved = pltpu.roll(ref[at, :, lane : lane + LANES], shift, axis=1)
+                    moved = pltpu.roll(ref[home, at], shift, axis=1)
                     tile = jnp.where(group == i, moved, tile)
                 outs[k][base + rr] = tile
 
@@ -241,23 +240,33 @@
     z, sea_rows, rows, outs, cut, sea_at, speed, weights, drift_weights, moved, moved_twice,
     known=None, kept=None,
 ):
-    NB, CH, L = z.NB, z.CH, z.L
+    NB, L, tiles = z.NB, z.L, z.NB // LANES
     known, kept = known or {}, kept or {}
     n = len(rows)
     first = [r for r in range(1, n - 1) if r not in known]
     assert first == list(range(first[0], first[-1] + 1))
-    E = rows[0][0].shape[1]
+    E = rows[0][0].shape[2]
     N = E - 2 * cut
     keep = slice(cut, cut + N)
-    sea_cols = pl.ds(sea_at, E)
-    places = [(ref, i) for ref in outs for i in range(ref.shape[0])]
+    places = listed(*outs)
+    T = E // SUBLANES
+    offset = -cut % SUBLANES
+
+    def apart(start):
+        return [pl.ds(start + t, SUBLANES, stride=T) for t in range(T)]
 
     def sea_row(place):
-        return place[0][place[1], sea_cols]
+        return place[0][place[1], pl.ds(sea_at, E)]
+
+    def shift_up(parts):
+        return [pltpu.roll(parts[-1], 1, axis=0)] + parts[:-1]
+
+    def shift_down(parts):
+        return parts[1:] + [pltpu.roll(parts[0], SUBLANES - 1, axis=0)]
 
     for r in range(min(first[0] - 1, 1), max(first[-1] + 2, n - 1)):
         ref, i = rows[r]
-        surface = ref[i, :, NB:CH]
+        surface = ref[tiles, i]
         moved[0, r] = DOPPLER * jnp.tanh(jnp.broadcast_to(surface[:, 0:1], (E, LANES)))
         moved[1, r] = DOPPLER * jnp.tanh(jnp.broadcast_to(surface[:, L : L + 1], (E, LANES)))
 
@@ -265,25 +274,26 @@
         plus_before, waiting = None, None
         for r in range(start - 1, stop + 1):
             energy = read(r)
-            speed_x = speed_cx + moved[0, r]
+            speed_x = [speed_cx + moved[0, r, at, :] for at in apart(0)]
             if r >= start:
-                minus = jnp.minimum(speed_x, 0.0) * energy
+                minus = [jnp.minimum(v, 0.0) * e for v, e in zip(speed_x, energy)]
             if r > start:
-                write(r - 1, (waiting - minus) * sea_row(sea_rows[r - 1]))
+                ref, i = sea_rows[r - 1]
+                sea = [ref[i, at, :] for at in apart(sea_at)]
+                write(r - 1, [(w - m) * s for w, m, s in zip(waiting, minus, sea)])
             if r < stop:
-                plus = jnp.maximum(speed_x, 0.0) * energy
+                plus = [jnp.maximum(v, 0.0) * e for v, e in zip(speed_x, energy)]
             if start <= r < stop:
-                speed_y = speed_cy + moved[1, r]
-                plus_y = jnp.maximum(speed_y, 0.0) * energy
-                minus_y = jnp.minimum(speed_y, 0.0) * energy
-                waiting = (
-                    energy
-                    - ((plus - plus_before) - minus)
-                    - (
-                        (plus_y - pltpu.roll(plus_y, 1, axis=0))
-                        + (pltpu.roll(minus_y, E - 1, axis=0) - minus_y)
+                speed_y = [speed_cy + moved[1, r, at, :] for at in apart(0)]
+                plus_y = [jnp.maximum(v, 0.0) * e for v, e in zip(speed_y, energy)]
+                minus_y = [jnp.minimum(v, 0.0) * e for v, e in zip(speed_y, energy)]
+                waiting = [
+                    e - ((p - before) - m) - ((py - south) + (north - my))
+                    for e, p, before, m, py, south, north, my in zip(
+                        energy, plus, plus_before, minus,
+                        plus_y, shift_up(plus_y), shift_down(minus_y), minus_y,
                     )
-                )
+                ]
             plus_before = plus
 
     def one_tile(j, carry):
@@ -291,34 +301,42 @@
         speed_cx = speed[0:1, lanes]
         speed_cy = speed[1:2, lanes]
 
+        def in_order(t):
+            return slice(t * SUBLANES, (t + 1) * SUBLANES)
+
         def read_first(r):
             ref, i = rows[r]
-            return ref[i, :, lanes]
-
-        def write_first(r, value):
-            moved[2, r] = value
-            if r in kept:
-                ref, i = kept[r]
-                ref[i, :, lanes] = value
+            return [ref[j, i, at, :] for at in apart(0)]
+
+        def write_first(r, parts):
+            for t, part in enumerate(parts):
+                moved[2, r, in_order(t)] = part
+                if r in kept:
+                    ref, i = kept[r]
+                    ref[j, i, in_order(t)] = part
 
         def read_second(r):
             if r in known:
                 ref, i = known[r]
-                return ref[i, :, lanes]
-            return moved[2, r]
-
-        def write_second(r, value):
-            moved_twice[r - 2, :, lanes] = value[keep]
+                return [ref[j, i, in_order(t)] for t in range(T)]
+            return [moved[2, r, in_order(t)] for t in range(T)]
+
+        def write_second(r, parts):
+            for at, part in zip(apart(offset), parts):
+                moved_twice[j, r - 2, at, :] = part
 
         advect(read_first, write_first, first[0], first[-1] + 1, speed_cx, speed_cy)
         advect(read_second, write_second, 2, n - 2, speed_cx, speed_cy)
         return carry
 
-    lax.fori_loop(0, NB // LANES, one_tile, 0)
+    lax.fori_loop(0, tiles, one_tile, 0)
 
     count = len(places)
     own_sea = sea_rows[2 : n - 2]
-    energy = moved_twice[...].reshape(count * N, NB)
+    own = slice(cut + offset, cut + offset + N)
+    energy = jnp.concatenate(
+        [moved_twice[j, :, own].reshape(count * N, LANES) for j in range(tiles)], axis=1
+    )
     squares = energy * energy
     interaction = jnp.dot(
         energy.astype(BF16), weights[:NB], preferred_element_type=F32
@@ -328,14 +346,15 @@
     scale = (DT_SOURCE * sea_here[:, 0:1]) / (1.0 + total / NB)
     fresh = energy + scale * (interaction * energy)
     for i, (ref, at) in enumerate(places):
-        ref[at, :, 0:NB] = fresh[i * N : (i + 1) * N]
+        for j in range(tiles):
+            ref[j, at] = fresh[i * N : (i + 1) * N, j * LANES : (j + 1) * LANES]
     drift = jnp.dot(fresh.astype(BF16), drift_weights[...], preferred_element_type=F32)
 
     comp = (lax.broadcasted_iota(jnp.int32, (1, LANES), 1) // L) % 2
     sign = jnp.where(comp == 0, 1.0, -1.0).astype(F32)
     for i, (out, at) in enumerate(places):
         here, before, after = [
-            ref[row, :, NB:CH] for ref, row in (rows[i + 2], rows[i + 1], rows[i + 3])
+            ref[tiles, row] for ref, row in (rows[i + 2], rows[i + 1], rows[i + 3])
         ]
         lap = (
             (after + before)
@@ -347,13 +366,13 @@
             comp == 0, pltpu.roll(centre, LANES - L, axis=1), pltpu.roll(centre, L, axis=1)
         )
         turn = sign * (CORIOLIS * (other + drift[i * N : (i + 1) * N]))
-        out[at, :, NB:CH] = (
+        out[tiles, at] = (
             centre + DT_OCEAN * (turn + VISCOSITY * lap)
         ) * sea_row(own_sea[i])[keep]
 
 
 def listed(*refs):
-    return [(ref, i) for ref in refs for i in range(ref.shape[0])]
+    return [(ref, i) for ref in refs for i in range(ref.shape[-3])]
 
 
 def inner_kernel(z, first, cut, sea_at, top, inner, bottom, sea, speed, weights, drift_weights, *refs):
@@ -370,7 +389,7 @@
 
 def read_sea(halo, sea):
     for i in range(EDGE):
-        sea[i] = spread_line(halo[i, 0:1, 0:LANES])[: halo.shape[1]]
+        sea[i] = spread_line(halo[0, i, 0:1])[: halo.shape[2]]
     return sea
 
 
@@ -491,10 +510,13 @@
         (*got, weights, drift_weights, speed)
     )
 
+    def state(rows, columns):
+        return (CH // LANES, rows, columns, LANES)
+
     def unpack(rows, received, shapes):
         return pl.pallas_call(
             functools.partial(unpack_kernel, z, rows),
-            out_shape=[jax.ShapeDtypeStruct((n, width, lanes), F32) for n, lanes in shapes],
+            out_shape=[jax.ShapeDtypeStruct(shape, F32) for shape in shapes],
             in_specs=[SMEM] * 2 + [VMEM] * B,
             out_specs=[VMEM] * len(shapes),
             compiler_params=params(16),
@@ -502,17 +524,17 @@
         )(*who, *received)
 
     top, bottom, sea = unpack(
-        z.edge_rows, got[:B], [(EDGE, CH), (EDGE, CH), (R, LANES)]
+        z.edge_rows, got[:B], [state(EDGE, width), state(EDGE, width), (R, width, LANES)]
     )
     *blocks, top = lax.optimization_barrier((*packed[half:], top))
     blocks = list(packed[:half]) + blocks
     got = [lax.ppermute(blocks[k], axes, forward[k]) for k in range(B)]
-    (inner,) = unpack(z.inner_rows, got, [(R - 2 * EDGE, CH)])
+    (inner,) = unpack(z.inner_rows, got, [state(R - 2 * EDGE, width)])
 
     def step_call(body, first, cut, sea_at, count, deepest, inputs, more=()):
-        width = inputs[0].shape[1]
+        width = inputs[0].shape[2]
         n = width - 2 * cut
-        shapes = [(count, n, CH)] + [(EDGE, width, lanes) for lanes in more]
+        shapes = [state(count, n)] + [before + (EDGE, width, LANES) for before in more]
         return pl.pallas_call(
             functools.partial(body, z, first, cut, sea_at),
             out_shape=[jax.ShapeDtypeStruct(shape, F32) for shape in shapes],
@@ -520,7 +542,7 @@
             out_specs=[VMEM] * len(shapes),
             scratch_shapes=[
                 pltpu.VMEM((3, deepest, width, LANES), F32),
-                pltpu.VMEM((count, n, NB), F32),
+                pltpu.VMEM((NB // LANES, count, width + PAD, LANES), F32),
             ],
             compiler_params=params(24),
             cost_estimate=cost(count * 1e8, count * 1e5),
@@ -540,7 +562,7 @@
         def advance_inner():
             return step_call(
                 inner_kernel, first, cut, sea_at, R - 2 * EDGE, R, (top, inner, bottom, sea),
-                () if first else (NB, NB),
+                () if first else ((NB // LANES,),) * 2,
             )
 
         given = ()
@@ -549,13 +571,13 @@
         new_bottom, *found = step_call(
             bottom_kernel, first, cut, sea_at, EDGE, 3 * EDGE,
             (down, bottom, inner, sea, *sea_down, *given[1:]),
-            (LANES,) if first else (),
+            ((),) if first else (),
         )
         sea_down = sea_down or found
         new_top, *found = step_call(
             top_kernel, first, cut, sea_at, EDGE, 3 * EDGE,
             (up, top, inner, sea, *sea_up, *given[:1]),
-            (LANES,) if first else (),
+            ((),) if first else (),
         )
         sea_up = sea_up or found
         if first:

time: 124 us -> 121 us (0.976)
  Pallas kernels: 47.4 us -> 44.3 us
    pallas_call x9, Pallas kernels: 34.7 us -> 31.6 us  [step_call(): pl.pallas_call(functools.partial(body, z, first, cut, sea_at), out_shape=...]
  transfers between devices with their start and end apart: 22 -> 22, of which waited for: 9 -> 9; matrix products, arithmetic and copies ran while one was open for 0% -> 0% of each run, Pallas kernels for 34% -> 32%
where the time goes in v8:
time: 121 us
  Pallas kernels  44.3 us (37%)
  starting transfers between devices  37.1 us (31%)
  waiting for transfers between devices  36.4 us (30%)
  local copies, waits for them, and re-layouts  1.92 us (2%)
    pallas_call x9, Pallas kernels, step_call(): pl.pallas_call(functools.partial(body, z, first, cut, sea_at), out_shape=...  31.6 us
    ppermute x4, waiting for transfers between devices, per_device(): got = [lax.ppermute(blocks[k], axes, forward[k]) for k in range(B)]  13.3 us
    ppermute x8, waiting for transfers between devices, per_device(): lax.ppermute(packed[i], axes, [(t, s) for s, t in forward[i % B]])  12.8 us
    ppermute x8, starting transfers between devices, per_device(): lax.ppermute(packed[i], axes, [(t, s) for s, t in forward[i % B]])  12.8 us
    ppermute x4, starting transfers between devices, per_device(): got = [lax.ppermute(packed[k], axes, forward[k]) for k in range(B)]  9.52 us
    ppermute x3, starting transfers between devices, per_device(): down = lax.ppermute(top, axes, to_prev_row)  9.41 us
    ppermute x4, waiting for transfers between devices, per_device(): got = [lax.ppermute(packed[k], axes, forward[k]) for k in range(B)]  6.76 us
    pallas_call x2, Pallas kernels, pack(): pl.pallas_call(functools.partial(pack_kernel, z, rows), out_shape=[jax.Sh...  6.62 us
  transfers between devices with their start and end apart: 22, of which 9 were waited for; matrix products, arithmetic and copies ran while one was open for 0% of the time, Pallas kernels for 32%

profile of v8, /device:TPU:0, one launch (start us, length us, event | category | flops | bytes accessed | tf_op | source)
XLA Modules:
  0.0 121.0 jit_solution(11907221849109771620)
XLA Ops:
  0.7 3.4 %pack.3 = (f32[808,128]{1,0:T(8,128)}, f32[808,128]{1,0:T(8,128)}, f32[808,128]{1,0:T(8,128)}, f32[808,128]{1,0:T(8,128)}) custom-call(s32[1]{0:T(128)} %bitcast.odd, s32[1]{0:T(128)} %bitcast.1.part, f32[2304,256]{1,0:T(8,128)} %bitcast.6, f32[256,256]{1,0:T(8,128)} %bitcast.8, s32[8,256]{1,0:T(8,128)} %mask_in.3), custom_call_target="tpu_custom_call" | custom-call | tf_op jit(solution)/shard_map/pack/pallas_call | solution.py:477
  4.0 1.7 %collective-permute-start.2 = (f32[808,128]{1,0:T(8,128)}, f32[808,128]{1,0:T(8,128)S(1)}, u32[]{:S(2)}, u32[]{:S(2)}) collective-permute-start(f32[808,128]{1,0:T(8,128)} %get-tuple-element.51), channel_id=1, source_target_pairs={{0,0},{1,6},{2,2},{3,4},{4,5},{5,3},{6,7},{7,1},{8,8},{9,14},{10,1... | collective-permute-start | bytes 1241096 | tf_op jit(solution)/shard_map/ppermute | solution.py:493
  5.7 3.0 %collective-permute-start.3 = (f32[808,128]{1,0:T(8,128)}, f32[808,128]{1,0:T(8,128)S(1)}, u32[]{:S(2)}, u32[]{:S(2)}) collective-permute-start(f32[808,128]{1,0:T(8,128)} %get-tuple-element.52), channel_id=1, source_target_pairs={{0,2},{1,4},{2,0},{3,6},{4,7},{5,1},{6,5},{7,3},{8,10},{9,12},{10,... | collective-permute-start | bytes 1241096 | tf_op jit(solution)/shard_map/ppermute | solution.py:493
  9.9 3.6 %collective-permute-start.5 = (f32[808,128]{1,0:T(8,128)}, f32[808,128]{1,0:T(8,128)S(1)}, u32[]{:S(2)}, u32[]{:S(2)}) collective-permute-start(f32[808,128]{1,0:T(8,128)} %get-tuple-element.54), channel_id=1, source_target_pairs={{0,6},{1,0},{2,4},{3,2},{4,3},{5,5},{6,1},{7,7},{8,14},{9,8},{10,1... | collective-permute-start | bytes 1241096 | tf_op jit(solution)/shard_map/ppermute | solution.py:493
  13.6 3.3 %pack.2 = (f32[800,128]{1,0:T(8,128)}, f32[800,128]{1,0:T(8,128)}, f32[800,128]{1,0:T(8,128)}, f32[800,128]{1,0:T(8,128)}) custom-call(s32[1]{0:T(128)} %bitcast.odd, s32[1]{0:T(128)} %bitcast.1.part, f32[2304,256]{1,0:T(8,128)} %bitcast.7, f32[256,256]{1,0:T(8,128)} %bitcast.9, s32[8,256]{1,0:T(8,128)} %mask_in.3), custom_call_target="tpu_custom_call" | custom-call | tf_op jit(solution)/shard_map/pack/pallas_call | solution.py:477
  16.8 1.7 %collective-permute-start = (f32[800,128]{1,0:T(8,128)}, f32[800,128]{1,0:T(8,128)S(1)}, u32[]{:S(2)}, u32[]{:S(2)}) collective-permute-start(f32[800,128]{1,0:T(8,128)} %get-tuple-element.47), channel_id=1, source_target_pairs={{0,0},{1,6},{2,2},{3,4},{4,5},{5,3},{6,7},{7,1},{8,8},{9,14},{10,1... | collective-permute-start | bytes 1228808 | tf_op jit(solution)/shard_map/ppermute | solution.py:531
  18.9 1.7 %copy-done.1 = bf16[1152,1152]{1,0:T(8,128)(2,1)S(1)} copy-done((bf16[1152,1152]{1,0:T(8,128)(2,1)S(1)}, bf16[1152,1152]{1,0:T(8,128)(2,1)}, u32[]{:S(2)}) %copy-start.1) | copy-done | bytes 2654232
  20.6 1.5 %weights.1 = (bf16[2304,1152]{1,0:T(8,128)(2,1)S(1)}, bf16[1152,128]{1,0:T(8,128)(2,1)S(1)}) custom-call(bf16[1152,1152]{1,0:T(8,128)(2,1)S(1)} %copy-done, bf16[1152,1152]{1,0:T(8,128)(2,1)S(1)} %copy-done.1, bf16[128,1152]{1,0:T(8,128)(2,1)S(1)} %copy-done.2), custom_call_target="tpu_custom_call" | custom-call | flops 2000000000 | bytes 10616832 | tf_op jit(solution)/shard_map/weights/pallas_call | solution.py:496
  22.2 2.3 %collective-permute-done.3.refs_1_ = f32[808,128]{1,0:T(8,128)S(1)} collective-permute-done((f32[808,128]{1,0:T(8,128)}, f32[808,128]{1,0:T(8,128)S(1)}, u32[]{:S(2)}, u32[]{:S(2)}) %collective-permute-start.3) | collective-permute-done | bytes 413728 | tf_op jit(solution)/shard_map/ppermute | solution.py:493
  25.1 3.9 %collective-permute-done.5.refs_3_ = f32[808,128]{1,0:T(8,128)S(1)} collective-permute-done((f32[808,128]{1,0:T(8,128)}, f32[808,128]{1,0:T(8,128)S(1)}, u32[]{:S(2)}, u32[]{:S(2)}) %collective-permute-start.5) | collective-permute-done | bytes 413728 | tf_op jit(solution)/shard_map/ppermute | solution.py:493
  29.6 5.3 %collective-permute-start.10 = (f32[10,2,80,128]{3,2,1,0:T(8,128)S(1)}, f32[10,2,80,128]{3,2,1,0:T(8,128)S(1)}, u32[]{:S(2)}, u32[]{:S(2)}) collective-permute-start(f32[10,2,80,128]{3,2,1,0:T(8,128)S(1)} %get-tuple-element.65.top), channel_id=1, source_target_pairs={{1,0},{3,2},{5,4},{7,6},{8,1},{10,3},{12,5},{14,7},{9,8},{11,10},{... | collective-permute-start | bytes 2457608 | tf_op jit(solution)/shard_map/ppermute | solution.py:558
  34.9 1.5 %collective-permute-start.1 = (f32[800,128]{1,0:T(8,128)S(1)}, f32[800,128]{1,0:T(8,128)S(1)}, u32[]{:S(2)}, u32[]{:S(2)}) collective-permute-start(f32[800,128]{1,0:T(8,128)S(1)} %copy-done.5), channel_id=1, source_target_pairs={{0,2},{1,4},{2,0},{3,6},{4,7},{5,1},{6,5},{7,3},{8,10},{9,12},{10,... | collective-permute-start | bytes 1228808 | tf_op jit(solution)/shard_map/ppermute | solution.py:531
  36.5 1.9 %collective-permute-start.7 = (f32[800,128]{1,0:T(8,128)S(1)}, f32[800,128]{1,0:T(8,128)S(1)}, u32[]{:S(2)}, u32[]{:S(2)}) collective-permute-start(f32[800,128]{1,0:T(8,128)S(1)} %copy-done.3), channel_id=1, source_target_pairs={{0,6},{1,0},{2,4},{3,2},{4,3},{5,5},{6,1},{7,7},{8,14},{9,8},{10,1... | collective-permute-start | bytes 1228808 | tf_op jit(solution)/shard_map/ppermute | solution.py:531
  38.4 12.3 %collective-permute-done.1.refs_1_ = f32[800,128]{1,0:T(8,128)S(1)} collective-permute-done((f32[800,128]{1,0:T(8,128)S(1)}, f32[800,128]{1,0:T(8,128)S(1)}, u32[]{:S(2)}, u32[]{:S(2)}) %collective-permute-start.1) | collective-permute-done | bytes 409632 | tf_op jit(solution)/shard_map/ppermute | solution.py:531
  52.1 3.2 %bottom_kernel.3 = (f32[10,2,72,128]{3,2,1,0:T(8,128)S(1)}, f32[2,80,128]{2,1,0:T(8,128)S(1)}) custom-call(f32[10,2,80,128]{3,2,1,0:T(8,128)S(1)} %collective-permute-done.10.down, f32[10,2,80,128]{3,2,1,0:T(8,128)S(1)} %get-tuple-element.64.bottom, f32[10,4,80,128]{3,2,1,0:T(8,128)S(1)} %unpack.3.inner, f32[8,80,128]{2,1,0:T(8,128)S(1)} %get-tuple-element.66.sea, ...), custom_call_target="tpu_custom_call" | custom-call | flops 200000000 | bytes 200000 | tf_op jit(solution)/shard_map/bottom_kernel/pallas_call | solution.py:538
  55.5 3.3 %top_kernel.3 = (f32[10,2,72,128]{3,2,1,0:T(8,128)S(1)}, f32[2,80,128]{2,1,0:T(8,128)S(1)}) custom-call(f32[10,2,80,128]{3,2,1,0:T(8,128)S(1)} %collective-permute-done.8.up, f32[10,2,80,128]{3,2,1,0:T(8,128)S(1)} %get-tuple-element.65.top, f32[10,4,80,128]{3,2,1,0:T(8,128)S(1)} %unpack.3.inner, f32[8,80,128]{2,1,0:T(8,128)S(1)} %get-tuple-element.66.sea, ...), custom_call_target="tpu_custom_call" | custom-call | flops 200000000 | bytes 200000 | tf_op jit(solution)/shard_map/top_kernel/pallas_call | solution.py:538
  58.7 3.8 %collective-permute-start.9 = (f32[10,2,72,128]{3,2,1,0:T(8,128)S(1)}, f32[10,2,72,128]{3,2,1,0:T(8,128)S(1)}, u32[]{:S(2)}, u32[]{:S(2)}) collective-permute-start(f32[10,2,72,128]{3,2,1,0:T(8,128)S(1)} %get-tuple-element.71.top), channel_id=1, source_target_pairs={{1,0},{3,2},{5,4},{7,6},{8,1},{10,3},{12,5},{14,7},{9,8},{11,10},{... | collective-permute-start | bytes 2211848 | tf_op jit(solution)/shard_map/ppermute | solution.py:558
  62.5 5.3 %inner_kernel.3.inner = f32[10,4,72,128]{3,2,1,0:T(8,128)S(1)} custom-call(f32[10,2,80,128]{3,2,1,0:T(8,128)S(1)} %get-tuple-element.65.top, f32[10,4,80,128]{3,2,1,0:T(8,128)S(1)} %unpack.3.inner, f32[10,2,80,128]{3,2,1,0:T(8,128)S(1)} %get-tuple-element.64.bottom, f32[8,80,128]{2,1,0:T(8,128)S(1)} %get-tuple-element.66.sea, ...), custom_call_target="tpu_custom_call" | custom-call | flops 400000000 | bytes 400000 | tf_op jit(solution)/shard_map/inner_kernel/pallas_call | solution.py:538
  67.8 5.0 %inner_kernel.4 = (f32[10,4,72,128]{3,2,1,0:T(8,128)S(1)}, f32[9,2,72,128]{3,2,1,0:T(8,128)S(1)}, f32[9,2,72,128]{3,2,1,0:T(8,128)S(1)}) custom-call(f32[10,2,72,128]{3,2,1,0:T(8,128)S(1)} %get-tuple-element.71.top, f32[10,4,72,128]{3,2,1,0:T(8,128)S(1)} %inner_kernel.3.inner, f32[10,2,72,128]{3,2,1,0:T(8,128)S(1)} %get-tuple-element.72.bottom, ...), custom_call_target="tpu_custom_call" | custom-call | flops 400000000 | bytes 400000 | tf_op jit(solution)/shard_map/inner_kernel/pallas_call | solution.py:538
  72.8 2.6 %top_kernel.4.top = f32[10,2,72,128]{3,2,1,0:T(8,128)S(1)} custom-call(f32[10,2,72,128]{3,2,1,0:T(8,128)S(1)} %collective-permute-done.12.up, f32[10,2,72,128]{3,2,1,0:T(8,128)S(1)} %get-tuple-element.71.top, f32[10,4,72,128]{3,2,1,0:T(8,128)S(1)} %inner_kernel.3.inner, f32[8,80,128]{2,1,0:T(8,128)S(1)} %get-tuple-element.66.sea, ...), custom_call_target="tpu_custom_call" | custom-call | flops 200000000 | bytes 200000 | tf_op jit(solution)/shard_map/top_kernel/pallas_call | solution.py:538
  75.8 2.6 %bottom_kernel.4.bottom = f32[10,2,72,128]{3,2,1,0:T(8,128)S(1)} custom-call(f32[10,2,72,128]{3,2,1,0:T(8,128)S(1)} %collective-permute-done.9.down, f32[10,2,72,128]{3,2,1,0:T(8,128)S(1)} %get-tuple-element.72.bottom, f32[10,4,72,128]{3,2,1,0:T(8,128)S(1)} %inner_kernel.3.inner, f32[8,80,128]{2,1,0:T(8,128)S(1)} %get-tuple-element.66.sea, ...), custom_call_target="tpu_custom_call" | custom-call | flops 200000000 | bytes 200000 | tf_op jit(solution)/shard_map/bottom_kernel/pallas_call | solution.py:538
  78.7 4.7 %inner_kernel.5 = (f32[10,4,64,128]{3,2,1,0:T(8,128)S(1)}, f32[9,2,72,128]{3,2,1,0:T(8,128)S(1)}, f32[9,2,72,128]{3,2,1,0:T(8,128)S(1)}) custom-call(f32[10,2,72,128]{3,2,1,0:T(8,128)S(1)} %top_kernel.4.top, f32[10,4,72,128]{3,2,1,0:T(8,128)S(1)} %get-tuple-element.78.inner, f32[10,2,72,128]{3,2,1,0:T(8,128)S(1)} %bottom_kernel.4.bottom, ...), custom_call_target="tpu_custom_call" | custom-call | flops 400000000 | bytes 400000 | tf_op jit(solution)/shard_map/inner_kernel/pallas_call | solution.py:538
  86.8 3.6 %collective-permute-done.13.down = f32[10,2,72,128]{3,2,1,0:T(8,128)S(1)} collective-permute-done((f32[10,2,72,128]{3,2,1,0:T(8,128)S(1)}, f32[10,2,72,128]{3,2,1,0:T(8,128)S(1)}, u32[]{:S(2)}, u32[]{:S(2)}) %collective-permute-start.13) | collective-permute-done | bytes 737312 | tf_op jit(solution)/shard_map/ppermute | solution.py:558
  90.4 2.1 %collective-permute-start.21 = (f32[10,64,128]{2,1,0:T(8,128)S(1)}, f32[10,64,128]{2,1,0:T(8,128)S(1)}, u32[]{:S(2)}, u32[]{:S(2)}) collective-permute-start(f32[10,64,128]{2,1,0:T(8,128)S(1)} %get-tuple-element.89), channel_id=1, source_target_pairs={{6,0},{0,1},{4,2},{2,3},{3,4},{5,5},{1,6},{7,7},{14,8},{8,9},{12,1... | collective-permute-start | bytes 983048 | tf_op jit(solution)/shard_map/ppermute | solution.py:603
  92.5 2.5 %bottom_kernel.5.refs_1_ = f32[10,2,64,128]{3,2,1,0:T(8,128)S(1)} custom-call(f32[10,2,72,128]{3,2,1,0:T(8,128)S(1)} %collective-permute-done.13.down, f32[10,2,72,128]{3,2,1,0:T(8,128)S(1)} %bottom_kernel.4.bottom, f32[10,4,72,128]{3,2,1,0:T(8,128)S(1)} %get-tuple-element.78.inner, f32[8,80,128]{2,1,0:T(8,128)S(1)} %get-tuple-element.66.sea, ...), custom_call_target="tpu_custom_call" | custom-call | flops 200000000 | bytes 200000 | tf_op jit(solution)/shard_map/bottom_kernel/pallas_call | solution.py:538
  95.0 2.4 %top_kernel.5.refs_0_ = f32[10,2,64,128]{3,2,1,0:T(8,128)S(1)} custom-call(f32[10,2,72,128]{3,2,1,0:T(8,128)S(1)} %collective-permute-done.11.up, f32[10,2,72,128]{3,2,1,0:T(8,128)S(1)} %top_kernel.4.top, f32[10,4,72,128]{3,2,1,0:T(8,128)S(1)} %get-tuple-element.78.inner, f32[8,80,128]{2,1,0:T(8,128)S(1)} %get-tuple-element.66.sea, ...), custom_call_target="tpu_custom_call" | custom-call | flops 200000000 | bytes 200000 | tf_op jit(solution)/shard_map/top_kernel/pallas_call | solution.py:538
  99.7 3.4 %collective-permute-start.16 = (f32[10,64,128]{2,1,0:T(8,128)S(1)}, f32[10,64,128]{2,1,0:T(8,128)S(1)}, u32[]{:S(2)}, u32[]{:S(2)}) collective-permute-start(f32[10,64,128]{2,1,0:T(8,128)S(1)} %get-tuple-element.83), channel_id=1, source_target_pairs={{4,0},{2,1},{6,2},{0,3},{1,4},{7,5},{3,6},{5,7},{12,8},{10,9},{14,... | collective-permute-start | bytes 983048 | tf_op jit(solution)/shard_map/ppermute | solution.py:603
  103.2 2.3 %collective-permute-start.17 = (f32[10,64,128]{2,1,0:T(8,128)S(1)}, f32[10,64,128]{2,1,0:T(8,128)S(1)}, u32[]{:S(2)}, u32[]{:S(2)}) collective-permute-start(f32[10,64,128]{2,1,0:T(8,128)S(1)} %get-tuple-element.84), channel_id=1, source_target_pairs={{6,0},{0,1},{4,2},{2,3},{3,4},{5,5},{1,6},{7,7},{14,8},{8,9},{12,1... | collective-permute-start | bytes 983048 | tf_op jit(solution)/shard_map/ppermute | solution.py:603
  105.5 5.3 %collective-permute-done.15.refs_1_ = f32[10,64,128]{2,1,0:T(8,128)S(1)} collective-permute-done((f32[10,64,128]{2,1,0:T(8,128)S(1)}, f32[10,64,128]{2,1,0:T(8,128)S(1)}, u32[]{:S(2)}, u32[]{:S(2)}) %collective-permute-start.15) | collective-permute-done | bytes 327712 | tf_op jit(solution)/shard_map/ppermute | solution.py:603
  110.8 4.6 %collective-permute-done.16.refs_2_ = f32[10,64,128]{2,1,0:T(8,128)S(1)} collective-permute-done((f32[10,64,128]{2,1,0:T(8,128)S(1)}, f32[10,64,128]{2,1,0:T(8,128)S(1)}, u32[]{:S(2)}, u32[]{:S(2)}) %collective-permute-start.16) | collective-permute-done | bytes 327712 | tf_op jit(solution)/shard_map/ppermute | solution.py:603
  115.3 2.9 %collective-permute-done.17.refs_3_ = f32[10,64,128]{2,1,0:T(8,128)S(1)} collective-permute-done((f32[10,64,128]{2,1,0:T(8,128)S(1)}, f32[10,64,128]{2,1,0:T(8,128)S(1)}, u32[]{:S(2)}, u32[]{:S(2)}) %collective-permute-start.17) | collective-permute-done | bytes 327712 | tf_op jit(solution)/shard_map/ppermute | solution.py:603
  118.3 2.7 %restore.1 = (f32[2304,256]{1,0:T(8,128)}, f32[256,256]{1,0:T(8,128)}) custom-call(s32[1]{0:T(128)} %bitcast.odd, s32[1]{0:T(128)} %bitcast.1.part, f32[10,64,128]{2,1,0:T(8,128)S(1)} %collective-permute-done.14.refs_0_, f32[10,64,128]{2,1,0:T(8,128)S(1)} %collective-permute-done.15.refs_1_, f32[10,64,128]{2,1,0:T(8,128)S(1)} %collective-permute-done.16.refs_2_, ...), custom_call_target="tpu_custom_call" | custom-call | tf_op jit(solution)/shard_map/restore/pallas_call | solution.py:605
  (47 shorter events, 10.7 us)
Async XLA Ops:
  0.6 18.2 %copy-start = (bf16[1152,1152]{1,0:T(8,128)(2,1)S(1)}, bf16[1152,1152]{1,0:T(8,128)(2,1)}, u32[]{:S(2)}) copy-start(bf16[1152,1152]{1,0:T(8,128)(2,1)} %linear.1) | copy-start | bytes 7962628
  0.7 18.2 %copy-start.2 = (bf16[128,1152]{1,0:T(8,128)(2,1)S(1)}, bf16[128,1152]{1,0:T(8,128)(2,1)}, u32[]{:S(2)}) copy-start(bf16[128,1152]{1,0:T(8,128)(2,1)} %drift.1) | copy-start | bytes 884740
  4.0 18.2 %collective-permute-start.2 = (f32[808,128]{1,0:T(8,128)}, f32[808,128]{1,0:T(8,128)S(1)}, u32[]{:S(2)}, u32[]{:S(2)}) collective-permute-start(f32[808,128]{1,0:T(8,128)} %get-tuple-element.51), channel_id=1, source_target_pairs={{0,0},{1,6},{2,2},{3,4},{4,5},{5,3},{6,7},{7,1},{8,8},{9,14},{10,1... | collective-permute-start | bytes 1241096 | tf_op jit(solution)/shard_map/ppermute | solution.py:493
  5.7 18.9 %collective-permute-start.3 = (f32[808,128]{1,0:T(8,128)}, f32[808,128]{1,0:T(8,128)S(1)}, u32[]{:S(2)}, u32[]{:S(2)}) collective-permute-start(f32[808,128]{1,0:T(8,128)} %get-tuple-element.52), channel_id=1, source_target_pairs={{0,2},{1,4},{2,0},{3,6},{4,7},{5,1},{6,5},{7,3},{8,10},{9,12},{10,... | collective-permute-start | bytes 1241096 | tf_op jit(solution)/shard_map/ppermute | solution.py:493
  8.7 16.4 %collective-permute-start.4 = (f32[808,128]{1,0:T(8,128)}, f32[808,128]{1,0:T(8,128)S(1)}, u32[]{:S(2)}, u32[]{:S(2)}) collective-permute-start(f32[808,128]{1,0:T(8,128)} %get-tuple-element.53), channel_id=1, source_target_pairs={{0,4},{1,2},{2,6},{3,0},{4,1},{5,7},{6,3},{7,5},{8,12},{9,10},{10,... | collective-permute-start | bytes 1241096 | tf_op jit(solution)/shard_map/ppermute | solution.py:493
  9.9 19.1 %collective-permute-start.5 = (f32[808,128]{1,0:T(8,128)}, f32[808,128]{1,0:T(8,128)S(1)}, u32[]{:S(2)}, u32[]{:S(2)}) collective-permute-start(f32[808,128]{1,0:T(8,128)} %get-tuple-element.54), channel_id=1, source_target_pairs={{0,6},{1,0},{2,4},{3,2},{4,3},{5,5},{6,1},{7,7},{8,14},{9,8},{10,1... | collective-permute-start | bytes 1241096 | tf_op jit(solution)/shard_map/ppermute | solution.py:493
  16.8 19.6 %collective-permute-start = (f32[800,128]{1,0:T(8,128)}, f32[800,128]{1,0:T(8,128)S(1)}, u32[]{:S(2)}, u32[]{:S(2)}) collective-permute-start(f32[800,128]{1,0:T(8,128)} %get-tuple-element.47), channel_id=1, source_target_pairs={{0,0},{1,6},{2,2},{3,4},{4,5},{5,3},{6,7},{7,1},{8,8},{9,14},{10,1... | collective-permute-start | bytes 1228808 | tf_op jit(solution)/shard_map/ppermute | solution.py:531
  18.9 1.8 %copy-start.1 = (bf16[1152,1152]{1,0:T(8,128)(2,1)S(1)}, bf16[1152,1152]{1,0:T(8,128)(2,1)}, u32[]{:S(2)}) copy-start(bf16[1152,1152]{1,0:T(8,128)(2,1)} %square.1) | copy-start | bytes 7962628
  20.6 14.3 %copy-start.5 = (f32[800,128]{1,0:T(8,128)S(1)}, f32[800,128]{1,0:T(8,128)}, u32[]{:S(2)}) copy-start(f32[800,128]{1,0:T(8,128)} %get-tuple-element.48) | copy-start | bytes 1228804
  20.6 15.8 %copy-start.4 = (f32[800,128]{1,0:T(8,128)S(1)}, f32[800,128]{1,0:T(8,128)}, u32[]{:S(2)}) copy-start(f32[800,128]{1,0:T(8,128)} %get-tuple-element.62) | copy-start | bytes 1228804
  20.6 15.8 %copy-start.3 = (f32[800,128]{1,0:T(8,128)S(1)}, f32[800,128]{1,0:T(8,128)}, u32[]{:S(2)}) copy-start(f32[800,128]{1,0:T(8,128)} %get-tuple-element.63) | copy-start | bytes 1228804
  29.6 22.5 %collective-permute-start.10 = (f32[10,2,80,128]{3,2,1,0:T(8,128)S(1)}, f32[10,2,80,128]{3,2,1,0:T(8,128)S(1)}, u32[]{:S(2)}, u32[]{:S(2)}) collective-permute-start(f32[10,2,80,128]{3,2,1,0:T(8,128)S(1)} %get-tuple-element.65.top), channel_id=1, source_target_pairs={{1,0},{3,2},{5,4},{7,6},{8,1},{10,3},{12,5},{14,7},{9,8},{11,10},{... | collective-permute-start | bytes 2457608 | tf_op jit(solution)/shard_map/ppermute | solution.py:558
  34.9 20.5 %collective-permute-start.8 = (f32[10,2,80,128]{3,2,1,0:T(8,128)S(1)}, f32[10,2,80,128]{3,2,1,0:T(8,128)S(1)}, u32[]{:S(2)}, u32[]{:S(2)}) collective-permute-start(f32[10,2,80,128]{3,2,1,0:T(8,128)S(1)} %get-tuple-element.64.bottom), channel_id=1, source_target_pairs={{0,1},{2,3},{4,5},{6,7},{1,8},{3,10},{5,12},{7,14},{8,9},{10,11},{... | collective-permute-start | bytes 2457608 | tf_op jit(solution)/shard_map/ppermute | solution.py:559
  34.9 15.8 %collective-permute-start.1 = (f32[800,128]{1,0:T(8,128)S(1)}, f32[800,128]{1,0:T(8,128)S(1)}, u32[]{:S(2)}, u32[]{:S(2)}) collective-permute-start(f32[800,128]{1,0:T(8,128)S(1)} %copy-done.5), channel_id=1, source_target_pairs={{0,2},{1,4},{2,0},{3,6},{4,7},{5,1},{6,5},{7,3},{8,10},{9,12},{10,... | collective-permute-start | bytes 1228808 | tf_op jit(solution)/shard_map/ppermute | solution.py:531
  36.4 15.2 %collective-permute-start.6 = (f32[800,128]{1,0:T(8,128)S(1)}, f32[800,128]{1,0:T(8,128)S(1)}, u32[]{:S(2)}, u32[]{:S(2)}) collective-permute-start(f32[800,128]{1,0:T(8,128)S(1)} %copy-done.4), channel_id=1, source_target_pairs={{0,4},{1,2},{2,6},{3,0},{4,1},{5,7},{6,3},{7,5},{8,12},{9,10},{10,... | collective-permute-start | bytes 1228808 | tf_op jit(solution)/shard_map/ppermute | solution.py:531
  36.5 15.2 %collective-permute-start.7 = (f32[800,128]{1,0:T(8,128)S(1)}, f32[800,128]{1,0:T(8,128)S(1)}, u32[]{:S(2)}, u32[]{:S(2)}) collective-permute-start(f32[800,128]{1,0:T(8,128)S(1)} %copy-done.3), channel_id=1, source_target_pairs={{0,6},{1,0},{2,4},{3,2},{4,3},{5,5},{6,1},{7,7},{8,14},{9,8},{10,1... | collective-permute-start | bytes 1228808 | tf_op jit(solution)/shard_map/ppermute | solution.py:531
  55.4 17.4 %collective-permute-start.12 = (f32[10,2,72,128]{3,2,1,0:T(8,128)S(1)}, f32[10,2,72,128]{3,2,1,0:T(8,128)S(1)}, u32[]{:S(2)}, u32[]{:S(2)}) collective-permute-start(f32[10,2,72,128]{3,2,1,0:T(8,128)S(1)} %get-tuple-element.72.bottom), channel_id=1, source_target_pairs={{0,1},{2,3},{4,5},{6,7},{1,8},{3,10},{5,12},{7,14},{8,9},{10,11},{... | collective-permute-start | bytes 2211848 | tf_op jit(solution)/shard_map/ppermute | solution.py:559
  58.7 17.0 %collective-permute-start.9 = (f32[10,2,72,128]{3,2,1,0:T(8,128)S(1)}, f32[10,2,72,128]{3,2,1,0:T(8,128)S(1)}, u32[]{:S(2)}, u32[]{:S(2)}) collective-permute-start(f32[10,2,72,128]{3,2,1,0:T(8,128)S(1)} %get-tuple-element.71.top), channel_id=1, source_target_pairs={{1,0},{3,2},{5,4},{7,6},{8,1},{10,3},{12,5},{14,7},{9,8},{11,10},{... | collective-permute-start | bytes 2211848 | tf_op jit(solution)/shard_map/ppermute | solution.py:558
  75.4 15.0 %collective-permute-start.13 = (f32[10,2,72,128]{3,2,1,0:T(8,128)S(1)}, f32[10,2,72,128]{3,2,1,0:T(8,128)S(1)}, u32[]{:S(2)}, u32[]{:S(2)}) collective-permute-start(f32[10,2,72,128]{3,2,1,0:T(8,128)S(1)} %top_kernel.4.top), channel_id=1, source_target_pairs={{1,0},{3,2},{5,4},{7,6},{8,1},{10,3},{12,5},{14,7},{9,8},{11,10},{... | collective-permute-start | bytes 2211848 | tf_op jit(solution)/shard_map/ppermute | solution.py:558
  78.4 16.6 %collective-permute-start.11 = (f32[10,2,72,128]{3,2,1,0:T(8,128)S(1)}, f32[10,2,72,128]{3,2,1,0:T(8,128)S(1)}, u32[]{:S(2)}, u32[]{:S(2)}) collective-permute-start(f32[10,2,72,128]{3,2,1,0:T(8,128)S(1)} %bottom_kernel.4.bottom), channel_id=1, source_target_pairs={{0,1},{2,3},{4,5},{6,7},{1,8},{3,10},{5,12},{7,14},{8,9},{10,11},{... | collective-permute-start | bytes 2211848 | tf_op jit(solution)/shard_map/ppermute | solution.py:559
  83.7 14.8 %collective-permute-start.18 = (f32[10,64,128]{2,1,0:T(8,128)S(1)}, f32[10,64,128]{2,1,0:T(8,128)S(1)}, u32[]{:S(2)}, u32[]{:S(2)}) collective-permute-start(f32[10,64,128]{2,1,0:T(8,128)S(1)} %get-tuple-element.86), channel_id=1, source_target_pairs={{0,0},{6,1},{2,2},{4,3},{5,4},{3,5},{7,6},{1,7},{8,8},{14,9},{10,1... | collective-permute-start | bytes 983048 | tf_op jit(solution)/shard_map/ppermute | solution.py:603
  84.4 15.4 %collective-permute-start.19 = (f32[10,64,128]{2,1,0:T(8,128)S(1)}, f32[10,64,128]{2,1,0:T(8,128)S(1)}, u32[]{:S(2)}, u32[]{:S(2)}) collective-permute-start(f32[10,64,128]{2,1,0:T(8,128)S(1)} %get-tuple-element.87), channel_id=1, source_target_pairs={{2,0},{4,1},{0,2},{6,3},{7,4},{1,5},{5,6},{3,7},{10,8},{12,9},{8,1... | collective-permute-start | bytes 983048 | tf_op jit(solution)/shard_map/ppermute | solution.py:603
  85.9 17.3 %collective-permute-start.20 = (f32[10,64,128]{2,1,0:T(8,128)S(1)}, f32[10,64,128]{2,1,0:T(8,128)S(1)}, u32[]{:S(2)}, u32[]{:S(2)}) collective-permute-start(f32[10,64,128]{2,1,0:T(8,128)S(1)} %get-tuple-element.88), channel_id=1, source_target_pairs={{4,0},{2,1},{6,2},{0,3},{1,4},{7,5},{3,6},{5,7},{12,8},{10,9},{14,... | collective-permute-start | bytes 983048 | tf_op jit(solution)/shard_map/ppermute | solution.py:603
  90.4 15.0 %collective-permute-start.21 = (f32[10,64,128]{2,1,0:T(8,128)S(1)}, f32[10,64,128]{2,1,0:T(8,128)S(1)}, u32[]{:S(2)}, u32[]{:S(2)}) collective-permute-start(f32[10,64,128]{2,1,0:T(8,128)S(1)} %get-tuple-element.89), channel_id=1, source_target_pairs={{6,0},{0,1},{4,2},{2,3},{3,4},{5,5},{1,6},{7,7},{14,8},{8,9},{12,1... | collective-permute-start | bytes 983048 | tf_op jit(solution)/shard_map/ppermute | solution.py:603
  97.9 7.6 %collective-permute-start.14 = (f32[10,64,128]{2,1,0:T(8,128)S(1)}, f32[10,64,128]{2,1,0:T(8,128)S(1)}, u32[]{:S(2)}, u32[]{:S(2)}) collective-permute-start(f32[10,64,128]{2,1,0:T(8,128)S(1)} %get-tuple-element.81), channel_id=1, source_target_pairs={{0,0},{6,1},{2,2},{4,3},{5,4},{3,5},{7,6},{1,7},{8,8},{14,9},{10,1... | collective-permute-start | bytes 983048 | tf_op jit(solution)/shard_map/ppermute | solution.py:603
  98.6 12.2 %collective-permute-start.15 = (f32[10,64,128]{2,1,0:T(8,128)S(1)}, f32[10,64,128]{2,1,0:T(8,128)S(1)}, u32[]{:S(2)}, u32[]{:S(2)}) collective-permute-start(f32[10,64,128]{2,1,0:T(8,128)S(1)} %get-tuple-element.82), channel_id=1, source_target_pairs={{2,0},{4,1},{0,2},{6,3},{7,4},{1,5},{5,6},{3,7},{10,8},{12,9},{8,1... | collective-permute-start | bytes 983048 | tf_op jit(solution)/shard_map/ppermute | solution.py:603
  99.7 15.6 %collective-permute-start.16 = (f32[10,64,128]{2,1,0:T(8,128)S(1)}, f32[10,64,128]{2,1,0:T(8,128)S(1)}, u32[]{:S(2)}, u32[]{:S(2)}) collective-permute-start(f32[10,64,128]{2,1,0:T(8,128)S(1)} %get-tuple-element.83), channel_id=1, source_target_pairs={{4,0},{2,1},{6,2},{0,3},{1,4},{7,5},{3,6},{5,7},{12,8},{10,9},{14,... | collective-permute-start | bytes 983048 | tf_op jit(solution)/shard_map/ppermute | solution.py:603
  103.2 15.1 %collective-permute-start.17 = (f32[10,64,128]{2,1,0:T(8,128)S(1)}, f32[10,64,128]{2,1,0:T(8,128)S(1)}, u32[]{:S(2)}, u32[]{:S(2)}) collective-permute-start(f32[10,64,128]{2,1,0:T(8,128)S(1)} %get-tuple-element.84), channel_id=1, source_target_pairs={{6,0},{0,1},{4,2},{2,3},{3,4},{5,5},{1,6},{7,7},{14,8},{8,9},{12,1... | collective-permute-start | bytes 983048 | tf_op jit(solution)/shard_map/ppermute | solution.py:603

commit v9 on v8

--- a/solution.py
+++ b/solution.py
@@ -20,6 +20,7 @@
 LANES = 128
 SUBLANES = 8
 PAD = 8
+HALO = SUB * STEPS
 EDGE = 2
 VMEM = pl.BlockSpec(memory_space=pltpu.VMEM)
 SMEM = pl.BlockSpec(memory_space=pltpu.SMEM)
@@ -81,7 +82,7 @@
 def pack_kernel(z, rows, odd, part, spec_in, ocean_in, mask_in, *refs):
     B, R, C, W, mt = z.B, z.R, z.C, z.W, z.mt
     outs, (spec, ocean, mask, wide, sems) = refs[:B], refs[B:]
-    E = C + 2 * PAD
+    E, H = C + 2 * PAD, C + 2 * HALO
     copies = []
     for half in range(W // LANES):
         cols = pl.ds(half * LANES, LANES)
@@ -115,11 +116,12 @@
     for k, out in enumerate(outs):
         share = exchange_share(z, k, odd[0], part[0])
         start = pl.multiple_of(share * C, PAD)
-        block = wide[:, pl.ds(start, E), :]
-        out[0 : slabs * E] = block.reshape(slabs * E, LANES)
+        for i in range(slabs):
+            block = wide[i, pl.ds(start, E), :]
+            out[i * H : (i + 1) * H] = block[PAD - HALO : PAD - HALO + H]
         if rows == z.edge_rows:
             shift = lax.rem(W + LANES + PAD - start, W + LANES)
-            out[slabs * E : slabs * E + R] = pltpu.roll(sea, shift, axis=1)[:, :LANES]
+            out[slabs * H : slabs * H + R] = pltpu.roll(sea, shift, axis=1)[:, :LANES]
 
 
 def spread_line(line):
@@ -129,29 +131,34 @@
 def unpack_kernel(z, rows, odd, part, *refs):
     B, mt = z.B, z.mt
     got, outs = refs[:B], refs[B:]
-    E = z.C + 2 * PAD
+    E, H = z.C + 2 * PAD, z.C + 2 * HALO
+    brought = slice(PAD - HALO, PAD - HALO + H)
     if rows == z.edge_rows:
         sea = outs[-1]
         outs = outs[:-1]
-        lines = got[0][z.slabs(rows) * E : z.slabs(rows) * E + z.R]
+        lines = got[0][z.slabs(rows) * H : z.slabs(rows) * H + z.R]
         for r in range(z.R):
             sea[r] = spread_line(lines[r : r + 1])[:E]
     places = listed(*outs)
+    for ref in outs:
+        for columns in (slice(0, PAD), slice(E - PAD, E)):
+            ref[:, :, columns] = jnp.zeros(ref.shape[:2] + (PAD, LANES), F32)
     src = [exchange_part(z, k, odd[0], part[0]) for k in range(B)]
     for k in range(B):
         for t in range(mt):
             for i, (ref, at) in enumerate(places):
-                ref[src[k] * mt + t, at] = got[k][(i * mt + t) * E : (i * mt + t + 1) * E]
+                slab = i * mt + t
+                ref[src[k] * mt + t, at, brought] = got[k][slab * H : (slab + 1) * H]
     for count, used, deep, base, home in z.folds(rows)[0]:
         group = lane_group(count)
         for i, (ref, at) in enumerate(places):
-            tile = jnp.zeros((E, LANES), F32)
+            tile = jnp.zeros((H, LANES), F32)
             for k in range(B):
                 shift = lax.rem((src[k] - i // deep) * count + LANES, LANES)
                 slab = base + i % deep
-                moved = pltpu.roll(got[k][slab * E : (slab + 1) * E], shift, axis=1)
+                moved = pltpu.roll(got[k][slab * H : (slab + 1) * H], shift, axis=1)
                 tile = jnp.where(group == src[k], moved, tile)
-            ref[home, at] = tile
+            ref[home, at, brought] = tile
     if rows == z.edge_rows:
         for i, (ref, at) in enumerate(places):
             r = rows[i]
@@ -179,32 +186,43 @@
                 outs[k][base + rr] = tile
 
 
-def restore_kernel(z, odd, part, *refs):
-    B, R, C, mt = z.B, z.R, z.C, z.mt
-    got, (spec_out, ocean_out, wide, spec, ocean) = refs[: 2 * B], refs[2 * B :]
-    at = 0
-    for which, rows in enumerate((z.edge_rows, z.inner_rows)):
-        folds, slabs = z.folds(rows)
-        for k in range(B):
-            c = exchange_share(z, k, odd[0], part[0])
-            wide[at : at + slabs, pl.ds(pl.multiple_of(c * C, PAD), C), :] = got[which * B + k][...]
-        for half in range(z.W // LANES):
-            cols = slice(half * LANES, (half + 1) * LANES)
-            for i, r in enumerate(rows):
-                for t in range(mt):
-                    place = pl.ds(t * LANES * R + r, LANES, stride=R)
-                    spec[half, place, :] = wide[at + i * mt + t, cols].T
-            for (count, used, deep, base, _), dst, first in zip(folds, (spec, ocean), (z.main, 0)):
-                for rr in range(deep):
-                    turned = wide[at + base + rr, cols].T
-                    for i in range(used):
-                        place = pl.ds(first * R + rows[rr + i * deep], count, stride=R)
-                        dst[half, place, :] = turned[i * count : (i + 1) * count]
-        at += slabs
+def restore_rows(z, rows, odd, part, got, wide, spec, ocean):
+    R, C, mt = z.R, z.C, z.mt
+    folds, slabs = z.folds(rows)
+    for k, block in enumerate(got):
+        share = exchange_share(z, k, odd[0], part[0])
+        wide[:, pl.ds(pl.multiple_of(share * C, PAD), C), :] = block[...]
     for half in range(z.W // LANES):
         cols = slice(half * LANES, (half + 1) * LANES)
-        spec_out[:, cols] = spec[half]
-        ocean_out[:, cols] = ocean[half]
+        for i, r in enumerate(rows):
+            for t in range(mt):
+                place = pl.ds(t * LANES * R + r, LANES, stride=R)
+                spec[half, place, :] = wide[i * mt + t, cols].T
+        for (count, used, deep, base, _), dst, first in zip(folds, (spec, ocean), (z.main, 0)):
+            for rr in range(deep):
+                turned = wide[base + rr, cols].T
+                for i in range(used):
+                    place = pl.ds(first * R + rows[rr + i * deep], count, stride=R)
+                    dst[half, place, :] = turned[i * count : (i + 1) * count]
+        yield half
+
+
+def restore_inner_kernel(z, odd, part, *refs):
+    got, (spec, ocean, wide) = refs[: z.B], refs[z.B :]
+    for _ in restore_rows(z, z.inner_rows, odd, part, got, wide, spec, ocean):
+        pass
+
+
+def restore_kernel(z, odd, part, *refs):
+    got, (_, _, spec_out, ocean_out, spec, ocean, wide, sems) = refs[: z.B], refs[z.B :]
+    copies = []
+    for half in restore_rows(z, z.edge_rows, odd, part, got, wide, spec, ocean):
+        cols = pl.ds(half * LANES, LANES)
+        for n, (src, dst) in enumerate(((spec, spec_out), (ocean, ocean_out))):
+            copies.append(pltpu.make_async_copy(src.at[half], dst.at[:, cols], sems.at[n, half]))
+            copies[-1].start()
+    for copy in copies:
+        copy.wait()
 
 
 def weights_kernel(z, linear, square, drift, weights, drift_weights):
@@ -466,14 +484,13 @@
     who = ((geo % 2).astype(jnp.int32).reshape(1), part.astype(jnp.int32).reshape(1))
 
     width = C + 2 * PAD
-    all_slabs = z.slabs(z.edge_rows) + z.slabs(z.inner_rows)
     columns_scratch = [
         pltpu.VMEM((W // LANES, nb * R, LANES), F32),
         pltpu.VMEM((W // LANES, 2 * L * R, LANES), F32),
     ]
     def pack(rows):
         slabs = z.slabs(rows)
-        lines = slabs * width + (R if rows == z.edge_rows else 0)
+        lines = slabs * (C + 2 * HALO) + (R if rows == z.edge_rows else 0)
         return pl.pallas_call(
             functools.partial(pack_kernel, z, rows),
             out_shape=[jax.ShapeDtypeStruct((lines, LANES), F32)] * B,
@@ -506,8 +523,9 @@
         name="weights",
     )(kernel_linear, kernel_square, drift_kernel)
     speed = speeds(z)
-    *got, weights, drift_weights, speed = lax.optimization_barrier(
-        (*got, weights, drift_weights, speed)
+    held_back = packed[half:]
+    got, weights, drift_weights, speed, held_back = lax.optimization_barrier(
+        (got, weights, drift_weights, speed, held_back)
     )
 
     def state(rows, columns):
@@ -526,9 +544,9 @@
     top, bottom, sea = unpack(
         z.edge_rows, got[:B], [state(EDGE, width), state(EDGE, width), (R, width, LANES)]
     )
-    *blocks, top = lax.optimization_barrier((*packed[half:], top))
-    blocks = list(packed[:half]) + blocks
-    got = [lax.ppermute(blocks[k], axes, forward[k]) for k in range(B)]
+    got = [lax.ppermute(packed[k], axes, forward[k]) for k in range(half)]
+    held_back, got[0], _ = lax.optimization_barrier((held_back, got[0], top))
+    got += [lax.ppermute(held_back[k], axes, forward[half + k]) for k in range(B - half)]
     (inner,) = unpack(z.inner_rows, got, [state(R - 2 * EDGE, width)])
 
     def step_call(body, first, cut, sea_at, count, deepest, inputs, more=()):
@@ -602,18 +620,36 @@
     back = [
         lax.ppermute(packed[i], axes, [(t, s) for s, t in forward[i % B]]) for i in range(2 * B)
     ]
-    spectrum_out, ocean_out = pl.pallas_call(
+    halves = [
+        jax.ShapeDtypeStruct((W // LANES, nb * R, LANES), F32),
+        jax.ShapeDtypeStruct((W // LANES, 2 * L * R, LANES), F32),
+    ]
+    held = pl.pallas_call(
+        functools.partial(restore_inner_kernel, z),
+        out_shape=halves,
+        in_specs=[SMEM] * 2 + [VMEM] * B,
+        out_specs=[VMEM] * 2,
+        scratch_shapes=[pltpu.VMEM((z.slabs(z.inner_rows), W, LANES), F32)],
+        compiler_params=params(16),
+        name="restore_inner",
+    )(*who, *back[B:])
+    spectrum_out, ocean_out, *_ = pl.pallas_call(
         functools.partial(restore_kernel, z),
-        out_shape=(
+        out_shape=[
             jax.ShapeDtypeStruct((nb * R, W), F32),
             jax.ShapeDtypeStruct((2 * L * R, W), F32),
-        ),
-        in_specs=[SMEM] * 2 + [VMEM] * (2 * B),
-        out_specs=(VMEM,) * 2,
-        scratch_shapes=[pltpu.VMEM((all_slabs, W, LANES), F32)] + columns_scratch,
-        compiler_params=params(24),
+        ]
+        + halves,
+        in_specs=[SMEM] * 2 + [VMEM] * (B + 2),
+        out_specs=[HBM] * 2 + [VMEM] * 2,
+        scratch_shapes=[
+            pltpu.VMEM((z.slabs(z.edge_rows), W, LANES), F32),
+            pltpu.SemaphoreType.DMA((2, W // LANES)),
+        ],
+        input_output_aliases={B + 2: 2, B + 3: 3},
+        compiler_params=params(16),
         name="restore",
-    )(*who, *back)
+    )(*who, *back[:B], *held)
     return spectrum_out.reshape(nb, R, W), ocean_out.reshape(2, L, R, W)
 
 

time: 121 us -> 125 us (1.033)
  starting transfers between devices: 37.1 us -> 48.1 us
  waiting for transfers between devices: 36.4 us -> 29.6 us
    ppermute x4, starting transfers between devices: 5.1 us -> 15.2 us  [the longest x2 13.1 us: per_device(): lax.ppermute(held_back[k], axes, forward[half + k])]
    ppermute x4, waiting for transfers between devices: 13.3 us -> 7.13 us  [the longest x2 7.13 us: per_device(): lax.ppermute(held_back[k], axes, forward[half + k])]
    ppermute x3, waiting for transfers between devices: 3.56 us -> 0.01 us  [per_device(): down = lax.ppermute(top, axes, to_prev_row)]
    ppermute x3, waiting for transfers between devices: 0.01 us -> 2.03 us  [per_device(): up = lax.ppermute(bottom, axes, to_next_row)]
    ppermute x8, starting transfers between devices: 12.8 us -> 14.6 us  [per_device(): lax.ppermute(packed[i], axes, [(t, s) for s, t in forward[i % B]])]
    ppermute x3, starting transfers between devices: 9.41 us -> 8.04 us  [per_device(): down = lax.ppermute(top, axes, to_prev_row)]
    pallas_call x1 -> x2, Pallas kernels: 2.71 us -> 2.41 us  [the longest x1 1.87 us: per_device(): pl.pallas_call(functools.partial(restore_kernel, z), out_shape=[jax.Shape...]
  transfers between devices with their start and end apart: 22 -> 22, of which waited for: 9 -> 10; matrix products, arithmetic and copies ran while one was open for 0% -> 0% of each run, Pallas kernels for 32% -> 31%
where the time goes in v9:
time: 125 us
  starting transfers between devices  48.1 us (38%)
  Pallas kernels  44 us (35%)
  waiting for transfers between devices  29.6 us (24%)
  local copies, waits for them, and re-layouts  1.93 us (2%)
    pallas_call x9, Pallas kernels, step_call(): pl.pallas_call(functools.partial(body, z, first, cut, sea_at), out_shape=...  31.7 us
    ppermute x8, starting transfers between devices, per_device(): lax.ppermute(packed[i], axes, [(t, s) for s, t in forward[i % B]])  14.6 us
    ppermute x8, waiting for transfers between devices, per_device(): lax.ppermute(packed[i], axes, [(t, s) for s, t in forward[i % B]])  13.4 us
    ppermute x2, starting transfers between devices, per_device(): lax.ppermute(held_back[k], axes, forward[half + k])  13.1 us
    ppermute x4, starting transfers between devices, per_device(): got = [lax.ppermute(packed[k], axes, forward[k]) for k in range(B)]  9.52 us
    ppermute x3, starting transfers between devices, per_device(): down = lax.ppermute(top, axes, to_prev_row)  8.04 us
    ppermute x2, waiting for transfers between devices, per_device(): lax.ppermute(held_back[k], axes, forward[half + k])  7.13 us
    ppermute x4, waiting for transfers between devices, per_device(): got = [lax.ppermute(packed[k], axes, forward[k]) for k in range(B)]  6.96 us
  transfers between devices with their start and end apart: 22, of which 10 were waited for; matrix products, arithmetic and copies ran while one was open for 0% of the time, Pallas kernels for 31%

profile of v9, /device:TPU:0, one launch (start us, length us, event | category | flops | bytes accessed | tf_op | source)
XLA Modules:
  0.0 125.0 jit_solution(16941276059166222805)
XLA Ops:
  0.7 3.3 %pack.2 = (f32[768,128]{1,0:T(8,128)}, f32[768,128]{1,0:T(8,128)}, f32[768,128]{1,0:T(8,128)}, f32[768,128]{1,0:T(8,128)}) custom-call(s32[1]{0:T(128)} %bitcast.odd, s32[1]{0:T(128)} %bitcast.1.part, f32[2304,256]{1,0:T(8,128)} %bitcast.6, f32[256,256]{1,0:T(8,128)} %bitcast.8, s32[8,256]{1,0:T(8,128)} %mask_in.3), custom_call_target="tpu_custom_call" | custom-call | tf_op jit(solution)/shard_map/pack/pallas_call | solution.py:494
  4.0 1.7 %collective-permute-start = (f32[768,128]{1,0:T(8,128)}, f32[768,128]{1,0:T(8,128)S(1)}, u32[]{:S(2)}, u32[]{:S(2)}) collective-permute-start(f32[768,128]{1,0:T(8,128)} %get-tuple-element.51), channel_id=1, source_target_pairs={{0,0},{1,6},{2,2},{3,4},{4,5},{5,3},{6,7},{7,1},{8,8},{9,14},{10,1... | collective-permute-start | bytes 1179656 | tf_op jit(solution)/shard_map/ppermute | solution.py:510
  5.7 3.0 %collective-permute-start.1 = (f32[768,128]{1,0:T(8,128)}, f32[768,128]{1,0:T(8,128)S(1)}, u32[]{:S(2)}, u32[]{:S(2)}) collective-permute-start(f32[768,128]{1,0:T(8,128)} %get-tuple-element.52), channel_id=1, source_target_pairs={{0,2},{1,4},{2,0},{3,6},{4,7},{5,1},{6,5},{7,3},{8,10},{9,12},{10,... | collective-permute-start | bytes 1179656 | tf_op jit(solution)/shard_map/ppermute | solution.py:510
  9.9 3.6 %collective-permute-start.3 = (f32[768,128]{1,0:T(8,128)}, f32[768,128]{1,0:T(8,128)S(1)}, u32[]{:S(2)}, u32[]{:S(2)}) collective-permute-start(f32[768,128]{1,0:T(8,128)} %get-tuple-element.54), channel_id=1, source_target_pairs={{0,6},{1,0},{2,4},{3,2},{4,3},{5,5},{6,1},{7,7},{8,14},{9,8},{10,1... | collective-permute-start | bytes 1179656 | tf_op jit(solution)/shard_map/ppermute | solution.py:510
  13.7 3.2 %pack.3 = (f32[760,128]{1,0:T(8,128)}, f32[760,128]{1,0:T(8,128)}, f32[760,128]{1,0:T(8,128)}, f32[760,128]{1,0:T(8,128)}) custom-call(s32[1]{0:T(128)} %bitcast.odd, s32[1]{0:T(128)} %bitcast.1.part, f32[2304,256]{1,0:T(8,128)} %bitcast.7, f32[256,256]{1,0:T(8,128)} %bitcast.9, s32[8,256]{1,0:T(8,128)} %mask_in.3), custom_call_target="tpu_custom_call" | custom-call | tf_op jit(solution)/shard_map/pack/pallas_call | solution.py:494
  17.1 1.7 %copy-done.1 = bf16[1152,1152]{1,0:T(8,128)(2,1)S(1)} copy-done((bf16[1152,1152]{1,0:T(8,128)(2,1)S(1)}, bf16[1152,1152]{1,0:T(8,128)(2,1)}, u32[]{:S(2)}) %copy-start.1) | copy-done | bytes 2654232
  20.5 3.1 %collective-permute-done.1.refs_1_ = f32[768,128]{1,0:T(8,128)S(1)} collective-permute-done((f32[768,128]{1,0:T(8,128)}, f32[768,128]{1,0:T(8,128)S(1)}, u32[]{:S(2)}, u32[]{:S(2)}) %collective-permute-start.1) | collective-permute-done | bytes 393248 | tf_op jit(solution)/shard_map/ppermute | solution.py:510
  24.2 3.3 %collective-permute-done.3.refs_3_ = f32[768,128]{1,0:T(8,128)S(1)} collective-permute-done((f32[768,128]{1,0:T(8,128)}, f32[768,128]{1,0:T(8,128)S(1)}, u32[]{:S(2)}, u32[]{:S(2)}) %collective-permute-start.3) | collective-permute-done | bytes 393248 | tf_op jit(solution)/shard_map/ppermute | solution.py:510
  28.2 3.5 %collective-permute-start.10 = (f32[10,2,80,128]{3,2,1,0:T(8,128)S(1)}, f32[10,2,80,128]{3,2,1,0:T(8,128)S(1)}, u32[]{:S(2)}, u32[]{:S(2)}) collective-permute-start(f32[10,2,80,128]{3,2,1,0:T(8,128)S(1)} %get-tuple-element.66.top), channel_id=1, source_target_pairs={{1,0},{3,2},{5,4},{7,6},{8,1},{10,3},{12,5},{14,7},{9,8},{11,10},{... | collective-permute-start | bytes 2457608 | tf_op jit(solution)/shard_map/ppermute | solution.py:576
  33.9 10.2 %collective-permute-start.6 = (f32[760,128]{1,0:T(8,128)S(1)}, f32[760,128]{1,0:T(8,128)S(1)}, u32[]{:S(2)}, u32[]{:S(2)}) collective-permute-start(f32[760,128]{1,0:T(8,128)S(1)} %copy-done.4), channel_id=1, source_target_pairs={{0,4},{1,2},{2,6},{3,0},{4,1},{5,7},{6,3},{7,5},{8,12},{9,10},{10,... | collective-permute-start | bytes 1167368 | tf_op jit(solution)/shard_map/ppermute | solution.py:549
  44.1 2.9 %collective-permute-start.7 = (f32[760,128]{1,0:T(8,128)S(1)}, f32[760,128]{1,0:T(8,128)S(1)}, u32[]{:S(2)}, u32[]{:S(2)}) collective-permute-start(f32[760,128]{1,0:T(8,128)S(1)} %copy-done.3), channel_id=1, source_target_pairs={{0,6},{1,0},{2,4},{3,2},{4,3},{5,5},{6,1},{7,7},{8,14},{9,8},{10,1... | collective-permute-start | bytes 1167368 | tf_op jit(solution)/shard_map/ppermute | solution.py:549
  47.0 3.0 %collective-permute-done.6.refs_2_ = f32[760,128]{1,0:T(8,128)S(1)} collective-permute-done((f32[760,128]{1,0:T(8,128)S(1)}, f32[760,128]{1,0:T(8,128)S(1)}, u32[]{:S(2)}, u32[]{:S(2)}) %collective-permute-start.6) | collective-permute-done | bytes 389152 | tf_op jit(solution)/shard_map/ppermute | solution.py:549
  49.9 4.2 %collective-permute-done.7.refs_3_ = f32[760,128]{1,0:T(8,128)S(1)} collective-permute-done((f32[760,128]{1,0:T(8,128)S(1)}, f32[760,128]{1,0:T(8,128)S(1)}, u32[]{:S(2)}, u32[]{:S(2)}) %collective-permute-start.7) | collective-permute-done | bytes 389152 | tf_op jit(solution)/shard_map/ppermute | solution.py:549
  54.6 3.3 %top_kernel.3 = (f32[10,2,72,128]{3,2,1,0:T(8,128)S(1)}, f32[2,80,128]{2,1,0:T(8,128)S(1)}) custom-call(f32[10,2,80,128]{3,2,1,0:T(8,128)S(1)} %collective-permute-done.8.up, f32[10,2,80,128]{3,2,1,0:T(8,128)S(1)} %get-tuple-element.66.top, f32[10,4,80,128]{3,2,1,0:T(8,128)S(1)} %unpack.3.inner, f32[8,80,128]{2,1,0:T(8,128)S(1)} %get-tuple-element.72.sea, ...), custom_call_target="tpu_custom_call" | custom-call | flops 200000000 | bytes 200000 | tf_op jit(solution)/shard_map/top_kernel/pallas_call | solution.py:556
  57.9 2.1 %collective-permute-start.9 = (f32[10,2,72,128]{3,2,1,0:T(8,128)S(1)}, f32[10,2,72,128]{3,2,1,0:T(8,128)S(1)}, u32[]{:S(2)}, u32[]{:S(2)}) collective-permute-start(f32[10,2,72,128]{3,2,1,0:T(8,128)S(1)} %get-tuple-element.77.top), channel_id=1, source_target_pairs={{1,0},{3,2},{5,4},{7,6},{8,1},{10,3},{12,5},{14,7},{9,8},{11,10},{... | collective-permute-start | bytes 2211848 | tf_op jit(solution)/shard_map/ppermute | solution.py:576
  60.0 3.3 %bottom_kernel.3 = (f32[10,2,72,128]{3,2,1,0:T(8,128)S(1)}, f32[2,80,128]{2,1,0:T(8,128)S(1)}) custom-call(f32[10,2,80,128]{3,2,1,0:T(8,128)S(1)} %collective-permute-done.10.down, f32[10,2,80,128]{3,2,1,0:T(8,128)S(1)} %get-tuple-element.71.bottom, f32[10,4,80,128]{3,2,1,0:T(8,128)S(1)} %unpack.3.inner, f32[8,80,128]{2,1,0:T(8,128)S(1)} %get-tuple-element.72.sea, ...), custom_call_target="tpu_custom_call" | custom-call | flops 200000000 | bytes 200000 | tf_op jit(solution)/shard_map/bottom_kernel/pallas_call | solution.py:556
  63.5 5.3 %inner_kernel.3.inner = f32[10,4,72,128]{3,2,1,0:T(8,128)S(1)} custom-call(f32[10,2,80,128]{3,2,1,0:T(8,128)S(1)} %get-tuple-element.66.top, f32[10,4,80,128]{3,2,1,0:T(8,128)S(1)} %unpack.3.inner, f32[10,2,80,128]{3,2,1,0:T(8,128)S(1)} %get-tuple-element.71.bottom, f32[8,80,128]{2,1,0:T(8,128)S(1)} %get-tuple-element.72.sea, ...), custom_call_target="tpu_custom_call" | custom-call | flops 400000000 | bytes 400000 | tf_op jit(solution)/shard_map/inner_kernel/pallas_call | solution.py:556
  68.8 5.0 %inner_kernel.4 = (f32[10,4,72,128]{3,2,1,0:T(8,128)S(1)}, f32[9,2,72,128]{3,2,1,0:T(8,128)S(1)}, f32[9,2,72,128]{3,2,1,0:T(8,128)S(1)}) custom-call(f32[10,2,72,128]{3,2,1,0:T(8,128)S(1)} %get-tuple-element.77.top, f32[10,4,72,128]{3,2,1,0:T(8,128)S(1)} %inner_kernel.3.inner, f32[10,2,72,128]{3,2,1,0:T(8,128)S(1)} %get-tuple-element.78.bottom, ...), custom_call_target="tpu_custom_call" | custom-call | flops 400000000 | bytes 400000 | tf_op jit(solution)/shard_map/inner_kernel/pallas_call | solution.py:556
  73.8 2.6 %bottom_kernel.4.bottom = f32[10,2,72,128]{3,2,1,0:T(8,128)S(1)} custom-call(f32[10,2,72,128]{3,2,1,0:T(8,128)S(1)} %collective-permute-done.9.down, f32[10,2,72,128]{3,2,1,0:T(8,128)S(1)} %get-tuple-element.78.bottom, f32[10,4,72,128]{3,2,1,0:T(8,128)S(1)} %inner_kernel.3.inner, f32[8,80,128]{2,1,0:T(8,128)S(1)} %get-tuple-element.72.sea, ...), custom_call_target="tpu_custom_call" | custom-call | flops 200000000 | bytes 200000 | tf_op jit(solution)/shard_map/bottom_kernel/pallas_call | solution.py:556
  77.8 2.6 %top_kernel.4.top = f32[10,2,72,128]{3,2,1,0:T(8,128)S(1)} custom-call(f32[10,2,72,128]{3,2,1,0:T(8,128)S(1)} %collective-permute-done.12.up, f32[10,2,72,128]{3,2,1,0:T(8,128)S(1)} %get-tuple-element.77.top, f32[10,4,72,128]{3,2,1,0:T(8,128)S(1)} %inner_kernel.3.inner, f32[8,80,128]{2,1,0:T(8,128)S(1)} %get-tuple-element.72.sea, ...), custom_call_target="tpu_custom_call" | custom-call | flops 200000000 | bytes 200000 | tf_op jit(solution)/shard_map/top_kernel/pallas_call | solution.py:556
  80.3 2.4 %collective-permute-start.13 = (f32[10,2,72,128]{3,2,1,0:T(8,128)S(1)}, f32[10,2,72,128]{3,2,1,0:T(8,128)S(1)}, u32[]{:S(2)}, u32[]{:S(2)}) collective-permute-start(f32[10,2,72,128]{3,2,1,0:T(8,128)S(1)} %top_kernel.4.top), channel_id=1, source_target_pairs={{1,0},{3,2},{5,4},{7,6},{8,1},{10,3},{12,5},{14,7},{9,8},{11,10},{... | collective-permute-start | bytes 2211848 | tf_op jit(solution)/shard_map/ppermute | solution.py:576
  82.7 4.7 %inner_kernel.5 = (f32[10,4,64,128]{3,2,1,0:T(8,128)S(1)}, f32[9,2,72,128]{3,2,1,0:T(8,128)S(1)}, f32[9,2,72,128]{3,2,1,0:T(8,128)S(1)}) custom-call(f32[10,2,72,128]{3,2,1,0:T(8,128)S(1)} %top_kernel.4.top, f32[10,4,72,128]{3,2,1,0:T(8,128)S(1)} %get-tuple-element.84.inner, f32[10,2,72,128]{3,2,1,0:T(8,128)S(1)} %bottom_kernel.4.bottom, ...), custom_call_target="tpu_custom_call" | custom-call | flops 400000000 | bytes 400000 | tf_op jit(solution)/shard_map/inner_kernel/pallas_call | solution.py:556
  89.1 2.9 %collective-permute-start.20 = (f32[10,64,128]{2,1,0:T(8,128)S(1)}, f32[10,64,128]{2,1,0:T(8,128)S(1)}, u32[]{:S(2)}, u32[]{:S(2)}) collective-permute-start(f32[10,64,128]{2,1,0:T(8,128)S(1)} %get-tuple-element.94), channel_id=1, source_target_pairs={{4,0},{2,1},{6,2},{0,3},{1,4},{7,5},{3,6},{5,7},{12,8},{10,9},{14,... | collective-permute-start | bytes 983048 | tf_op jit(solution)/shard_map/ppermute | solution.py:621
  93.1 2.1 %collective-permute-start.21 = (f32[10,64,128]{2,1,0:T(8,128)S(1)}, f32[10,64,128]{2,1,0:T(8,128)S(1)}, u32[]{:S(2)}, u32[]{:S(2)}) collective-permute-start(f32[10,64,128]{2,1,0:T(8,128)S(1)} %get-tuple-element.95), channel_id=1, source_target_pairs={{6,0},{0,1},{4,2},{2,3},{3,4},{5,5},{1,6},{7,7},{14,8},{8,9},{12,1... | collective-permute-start | bytes 983048 | tf_op jit(solution)/shard_map/ppermute | solution.py:621
  95.2 2.5 %top_kernel.5.refs_0_ = f32[10,2,64,128]{3,2,1,0:T(8,128)S(1)} custom-call(f32[10,2,72,128]{3,2,1,0:T(8,128)S(1)} %collective-permute-done.11.up, f32[10,2,72,128]{3,2,1,0:T(8,128)S(1)} %top_kernel.4.top, f32[10,4,72,128]{3,2,1,0:T(8,128)S(1)} %get-tuple-element.84.inner, f32[8,80,128]{2,1,0:T(8,128)S(1)} %get-tuple-element.72.sea, ...), custom_call_target="tpu_custom_call" | custom-call | flops 200000000 | bytes 200000 | tf_op jit(solution)/shard_map/top_kernel/pallas_call | solution.py:556
  97.7 2.5 %bottom_kernel.5.refs_1_ = f32[10,2,64,128]{3,2,1,0:T(8,128)S(1)} custom-call(f32[10,2,72,128]{3,2,1,0:T(8,128)S(1)} %collective-permute-done.13.down, f32[10,2,72,128]{3,2,1,0:T(8,128)S(1)} %bottom_kernel.4.bottom, f32[10,4,72,128]{3,2,1,0:T(8,128)S(1)} %get-tuple-element.84.inner, f32[8,80,128]{2,1,0:T(8,128)S(1)} %get-tuple-element.72.sea, ...), custom_call_target="tpu_custom_call" | custom-call | flops 200000000 | bytes 200000 | tf_op jit(solution)/shard_map/bottom_kernel/pallas_call | solution.py:556
  101.9 4.0 %collective-permute-start.16 = (f32[10,64,128]{2,1,0:T(8,128)S(1)}, f32[10,64,128]{2,1,0:T(8,128)S(1)}, u32[]{:S(2)}, u32[]{:S(2)}) collective-permute-start(f32[10,64,128]{2,1,0:T(8,128)S(1)} %get-tuple-element.89), channel_id=1, source_target_pairs={{4,0},{2,1},{6,2},{0,3},{1,4},{7,5},{3,6},{5,7},{12,8},{10,9},{14,... | collective-permute-start | bytes 983048 | tf_op jit(solution)/shard_map/ppermute | solution.py:621
  105.9 3.1 %collective-permute-start.17 = (f32[10,64,128]{2,1,0:T(8,128)S(1)}, f32[10,64,128]{2,1,0:T(8,128)S(1)}, u32[]{:S(2)}, u32[]{:S(2)}) collective-permute-start(f32[10,64,128]{2,1,0:T(8,128)S(1)} %get-tuple-element.90), channel_id=1, source_target_pairs={{6,0},{0,1},{4,2},{2,3},{3,4},{5,5},{1,6},{7,7},{14,8},{8,9},{12,1... | collective-permute-start | bytes 983048 | tf_op jit(solution)/shard_map/ppermute | solution.py:621
  109.5 4.6 %collective-permute-done.15.refs_1_ = f32[10,64,128]{2,1,0:T(8,128)S(1)} collective-permute-done((f32[10,64,128]{2,1,0:T(8,128)S(1)}, f32[10,64,128]{2,1,0:T(8,128)S(1)}, u32[]{:S(2)}, u32[]{:S(2)}) %collective-permute-start.15) | collective-permute-done | bytes 327712 | tf_op jit(solution)/shard_map/ppermute | solution.py:621
  114.1 4.7 %collective-permute-done.16.refs_2_ = f32[10,64,128]{2,1,0:T(8,128)S(1)} collective-permute-done((f32[10,64,128]{2,1,0:T(8,128)S(1)}, f32[10,64,128]{2,1,0:T(8,128)S(1)}, u32[]{:S(2)}, u32[]{:S(2)}) %collective-permute-start.16) | collective-permute-done | bytes 327712 | tf_op jit(solution)/shard_map/ppermute | solution.py:621
  118.9 4.1 %collective-permute-done.17.refs_3_ = f32[10,64,128]{2,1,0:T(8,128)S(1)} collective-permute-done((f32[10,64,128]{2,1,0:T(8,128)S(1)}, f32[10,64,128]{2,1,0:T(8,128)S(1)}, u32[]{:S(2)}, u32[]{:S(2)}) %collective-permute-start.17) | collective-permute-done | bytes 327712 | tf_op jit(solution)/shard_map/ppermute | solution.py:621
  123.0 1.9 %restore.1 = (f32[2304,256]{1,0:T(8,128)}, f32[256,256]{1,0:T(8,128)}, f32[2,2304,128]{2,1,0:T(8,128)S(1)}, f32[2,256,128]{2,1,0:T(8,128)S(1)}) custom-call(s32[1]{0:T(128)} %bitcast.odd, s32[1]{0:T(128)} %bitcast.1.part, f32[10,64,128]{2,1,0:T(8,128)S(1)} %collective-permute-done.14.refs_0_, ...), custom_call_target="tpu_custom_call", output_to_operand_aliasing={{2}: (6, {}), {3}: (7, {})} | custom-call | tf_op jit(solution)/shard_map/restore/pallas_call | solution.py:636
  (50 shorter events, 13.6 us)
Async XLA Ops:
  0.6 16.5 %copy-start = (bf16[1152,1152]{1,0:T(8,128)(2,1)S(1)}, bf16[1152,1152]{1,0:T(8,128)(2,1)}, u32[]{:S(2)}) copy-start(bf16[1152,1152]{1,0:T(8,128)(2,1)} %linear.1) | copy-start | bytes 7962628
  0.7 16.5 %copy-start.2 = (bf16[128,1152]{1,0:T(8,128)(2,1)S(1)}, bf16[128,1152]{1,0:T(8,128)(2,1)}, u32[]{:S(2)}) copy-start(bf16[128,1152]{1,0:T(8,128)(2,1)} %drift.1) | copy-start | bytes 884740
  4.0 16.5 %collective-permute-start = (f32[768,128]{1,0:T(8,128)}, f32[768,128]{1,0:T(8,128)S(1)}, u32[]{:S(2)}, u32[]{:S(2)}) collective-permute-start(f32[768,128]{1,0:T(8,128)} %get-tuple-element.51), channel_id=1, source_target_pairs={{0,0},{1,6},{2,2},{3,4},{4,5},{5,3},{6,7},{7,1},{8,8},{9,14},{10,1... | collective-permute-start | bytes 1179656 | tf_op jit(solution)/shard_map/ppermute | solution.py:510
  5.7 17.9 %collective-permute-start.1 = (f32[768,128]{1,0:T(8,128)}, f32[768,128]{1,0:T(8,128)S(1)}, u32[]{:S(2)}, u32[]{:S(2)}) collective-permute-start(f32[768,128]{1,0:T(8,128)} %get-tuple-element.52), channel_id=1, source_target_pairs={{0,2},{1,4},{2,0},{3,6},{4,7},{5,1},{6,5},{7,3},{8,10},{9,12},{10,... | collective-permute-start | bytes 1179656 | tf_op jit(solution)/shard_map/ppermute | solution.py:510
  8.6 15.5 %collective-permute-start.2 = (f32[768,128]{1,0:T(8,128)}, f32[768,128]{1,0:T(8,128)S(1)}, u32[]{:S(2)}, u32[]{:S(2)}) collective-permute-start(f32[768,128]{1,0:T(8,128)} %get-tuple-element.53), channel_id=1, source_target_pairs={{0,4},{1,2},{2,6},{3,0},{4,1},{5,7},{6,3},{7,5},{8,12},{9,10},{10,... | collective-permute-start | bytes 1179656 | tf_op jit(solution)/shard_map/ppermute | solution.py:510
  9.9 17.6 %collective-permute-start.3 = (f32[768,128]{1,0:T(8,128)}, f32[768,128]{1,0:T(8,128)S(1)}, u32[]{:S(2)}, u32[]{:S(2)}) collective-permute-start(f32[768,128]{1,0:T(8,128)} %get-tuple-element.54), channel_id=1, source_target_pairs={{0,6},{1,0},{2,4},{3,2},{4,3},{5,5},{6,1},{7,7},{8,14},{9,8},{10,1... | collective-permute-start | bytes 1179656 | tf_op jit(solution)/shard_map/ppermute | solution.py:510
  17.1 1.8 %copy-start.1 = (bf16[1152,1152]{1,0:T(8,128)(2,1)S(1)}, bf16[1152,1152]{1,0:T(8,128)(2,1)}, u32[]{:S(2)}) copy-start(bf16[1152,1152]{1,0:T(8,128)(2,1)} %square.1) | copy-start | bytes 7962628
  18.9 12.8 %copy-start.6 = (f32[760,128]{1,0:T(8,128)S(1)}, f32[760,128]{1,0:T(8,128)}, u32[]{:S(2)}) copy-start(f32[760,128]{1,0:T(8,128)} %get-tuple-element.61) | copy-start | bytes 1167364
  18.9 13.5 %copy-start.5 = (f32[760,128]{1,0:T(8,128)S(1)}, f32[760,128]{1,0:T(8,128)}, u32[]{:S(2)}) copy-start(f32[760,128]{1,0:T(8,128)} %get-tuple-element.68) | copy-start | bytes 1167364
  18.9 15.0 %copy-start.4 = (f32[760,128]{1,0:T(8,128)S(1)}, f32[760,128]{1,0:T(8,128)}, u32[]{:S(2)}) copy-start(f32[760,128]{1,0:T(8,128)} %get-tuple-element.69) | copy-start | bytes 1167364
  18.9 25.2 %copy-start.3 = (f32[760,128]{1,0:T(8,128)S(1)}, f32[760,128]{1,0:T(8,128)}, u32[]{:S(2)}) copy-start(f32[760,128]{1,0:T(8,128)} %get-tuple-element.70) | copy-start | bytes 1167364
  28.1 26.5 %collective-permute-start.8 = (f32[10,2,80,128]{3,2,1,0:T(8,128)S(1)}, f32[10,2,80,128]{3,2,1,0:T(8,128)S(1)}, u32[]{:S(2)}, u32[]{:S(2)}) collective-permute-start(f32[10,2,80,128]{3,2,1,0:T(8,128)S(1)} %get-tuple-element.71.bottom), channel_id=1, source_target_pairs={{0,1},{2,3},{4,5},{6,7},{1,8},{3,10},{5,12},{7,14},{8,9},{10,11},{... | collective-permute-start | bytes 2457608 | tf_op jit(solution)/shard_map/ppermute | solution.py:577
  28.2 31.8 %collective-permute-start.10 = (f32[10,2,80,128]{3,2,1,0:T(8,128)S(1)}, f32[10,2,80,128]{3,2,1,0:T(8,128)S(1)}, u32[]{:S(2)}, u32[]{:S(2)}) collective-permute-start(f32[10,2,80,128]{3,2,1,0:T(8,128)S(1)} %get-tuple-element.66.top), channel_id=1, source_target_pairs={{1,0},{3,2},{5,4},{7,6},{8,1},{10,3},{12,5},{14,7},{9,8},{11,10},{... | collective-permute-start | bytes 2457608 | tf_op jit(solution)/shard_map/ppermute | solution.py:576
  31.7 2.1 %collective-permute-start.4 = (f32[760,128]{1,0:T(8,128)S(1)}, f32[760,128]{1,0:T(8,128)S(1)}, u32[]{:S(2)}, u32[]{:S(2)}) collective-permute-start(f32[760,128]{1,0:T(8,128)S(1)} %copy-done.6), channel_id=1, source_target_pairs={{0,0},{1,6},{2,2},{3,4},{4,5},{5,3},{6,7},{7,1},{8,8},{9,14},{10,1... | collective-permute-start | bytes 1167368 | tf_op jit(solution)/shard_map/ppermute | solution.py:547
  32.4 14.6 %collective-permute-start.5 = (f32[760,128]{1,0:T(8,128)S(1)}, f32[760,128]{1,0:T(8,128)S(1)}, u32[]{:S(2)}, u32[]{:S(2)}) collective-permute-start(f32[760,128]{1,0:T(8,128)S(1)} %copy-done.5), channel_id=1, source_target_pairs={{0,2},{1,4},{2,0},{3,6},{4,7},{5,1},{6,5},{7,3},{8,10},{9,12},{10,... | collective-permute-start | bytes 1167368 | tf_op jit(solution)/shard_map/ppermute | solution.py:547
  33.9 16.1 %collective-permute-start.6 = (f32[760,128]{1,0:T(8,128)S(1)}, f32[760,128]{1,0:T(8,128)S(1)}, u32[]{:S(2)}, u32[]{:S(2)}) collective-permute-start(f32[760,128]{1,0:T(8,128)S(1)} %copy-done.4), channel_id=1, source_target_pairs={{0,4},{1,2},{2,6},{3,0},{4,1},{5,7},{6,3},{7,5},{8,12},{9,10},{10,... | collective-permute-start | bytes 1167368 | tf_op jit(solution)/shard_map/ppermute | solution.py:549
  44.1 10.0 %collective-permute-start.7 = (f32[760,128]{1,0:T(8,128)S(1)}, f32[760,128]{1,0:T(8,128)S(1)}, u32[]{:S(2)}, u32[]{:S(2)}) collective-permute-start(f32[760,128]{1,0:T(8,128)S(1)} %copy-done.3), channel_id=1, source_target_pairs={{0,6},{1,0},{2,4},{3,2},{4,3},{5,5},{6,1},{7,7},{8,14},{9,8},{10,1... | collective-permute-start | bytes 1167368 | tf_op jit(solution)/shard_map/ppermute | solution.py:549
  57.9 15.9 %collective-permute-start.9 = (f32[10,2,72,128]{3,2,1,0:T(8,128)S(1)}, f32[10,2,72,128]{3,2,1,0:T(8,128)S(1)}, u32[]{:S(2)}, u32[]{:S(2)}) collective-permute-start(f32[10,2,72,128]{3,2,1,0:T(8,128)S(1)} %get-tuple-element.77.top), channel_id=1, source_target_pairs={{1,0},{3,2},{5,4},{7,6},{8,1},{10,3},{12,5},{14,7},{9,8},{11,10},{... | collective-permute-start | bytes 2211848 | tf_op jit(solution)/shard_map/ppermute | solution.py:576
  63.2 14.5 %collective-permute-start.12 = (f32[10,2,72,128]{3,2,1,0:T(8,128)S(1)}, f32[10,2,72,128]{3,2,1,0:T(8,128)S(1)}, u32[]{:S(2)}, u32[]{:S(2)}) collective-permute-start(f32[10,2,72,128]{3,2,1,0:T(8,128)S(1)} %get-tuple-element.78.bottom), channel_id=1, source_target_pairs={{0,1},{2,3},{4,5},{6,7},{1,8},{3,10},{5,12},{7,14},{8,9},{10,11},{... | collective-permute-start | bytes 2211848 | tf_op jit(solution)/shard_map/ppermute | solution.py:577
  76.5 16.6 %collective-permute-start.11 = (f32[10,2,72,128]{3,2,1,0:T(8,128)S(1)}, f32[10,2,72,128]{3,2,1,0:T(8,128)S(1)}, u32[]{:S(2)}, u32[]{:S(2)}) collective-permute-start(f32[10,2,72,128]{3,2,1,0:T(8,128)S(1)} %bottom_kernel.4.bottom), channel_id=1, source_target_pairs={{0,1},{2,3},{4,5},{6,7},{1,8},{3,10},{5,12},{7,14},{8,9},{10,11},{... | collective-permute-start | bytes 2211848 | tf_op jit(solution)/shard_map/ppermute | solution.py:577
  80.3 17.3 %collective-permute-start.13 = (f32[10,2,72,128]{3,2,1,0:T(8,128)S(1)}, f32[10,2,72,128]{3,2,1,0:T(8,128)S(1)}, u32[]{:S(2)}, u32[]{:S(2)}) collective-permute-start(f32[10,2,72,128]{3,2,1,0:T(8,128)S(1)} %top_kernel.4.top), channel_id=1, source_target_pairs={{1,0},{3,2},{5,4},{7,6},{8,1},{10,3},{12,5},{14,7},{9,8},{11,10},{... | collective-permute-start | bytes 2211848 | tf_op jit(solution)/shard_map/ppermute | solution.py:576
  87.8 13.5 %collective-permute-start.18 = (f32[10,64,128]{2,1,0:T(8,128)S(1)}, f32[10,64,128]{2,1,0:T(8,128)S(1)}, u32[]{:S(2)}, u32[]{:S(2)}) collective-permute-start(f32[10,64,128]{2,1,0:T(8,128)S(1)} %get-tuple-element.92), channel_id=1, source_target_pairs={{0,0},{6,1},{2,2},{4,3},{5,4},{3,5},{7,6},{1,7},{8,8},{14,9},{10,1... | collective-permute-start | bytes 983048 | tf_op jit(solution)/shard_map/ppermute | solution.py:621
  88.5 13.4 %collective-permute-start.19 = (f32[10,64,128]{2,1,0:T(8,128)S(1)}, f32[10,64,128]{2,1,0:T(8,128)S(1)}, u32[]{:S(2)}, u32[]{:S(2)}) collective-permute-start(f32[10,64,128]{2,1,0:T(8,128)S(1)} %get-tuple-element.93), channel_id=1, source_target_pairs={{2,0},{4,1},{0,2},{6,3},{7,4},{1,5},{5,6},{3,7},{10,8},{12,9},{8,1... | collective-permute-start | bytes 983048 | tf_op jit(solution)/shard_map/ppermute | solution.py:621
  89.1 16.8 %collective-permute-start.20 = (f32[10,64,128]{2,1,0:T(8,128)S(1)}, f32[10,64,128]{2,1,0:T(8,128)S(1)}, u32[]{:S(2)}, u32[]{:S(2)}) collective-permute-start(f32[10,64,128]{2,1,0:T(8,128)S(1)} %get-tuple-element.94), channel_id=1, source_target_pairs={{4,0},{2,1},{6,2},{0,3},{1,4},{7,5},{3,6},{5,7},{12,8},{10,9},{14,... | collective-permute-start | bytes 983048 | tf_op jit(solution)/shard_map/ppermute | solution.py:621
  93.1 15.9 %collective-permute-start.21 = (f32[10,64,128]{2,1,0:T(8,128)S(1)}, f32[10,64,128]{2,1,0:T(8,128)S(1)}, u32[]{:S(2)}, u32[]{:S(2)}) collective-permute-start(f32[10,64,128]{2,1,0:T(8,128)S(1)} %get-tuple-element.95), channel_id=1, source_target_pairs={{6,0},{0,1},{4,2},{2,3},{3,4},{5,5},{1,6},{7,7},{14,8},{8,9},{12,1... | collective-permute-start | bytes 983048 | tf_op jit(solution)/shard_map/ppermute | solution.py:621
  100.6 9.0 %collective-permute-start.14 = (f32[10,64,128]{2,1,0:T(8,128)S(1)}, f32[10,64,128]{2,1,0:T(8,128)S(1)}, u32[]{:S(2)}, u32[]{:S(2)}) collective-permute-start(f32[10,64,128]{2,1,0:T(8,128)S(1)} %get-tuple-element.87), channel_id=1, source_target_pairs={{0,0},{6,1},{2,2},{4,3},{5,4},{3,5},{7,6},{1,7},{8,8},{14,9},{10,1... | collective-permute-start | bytes 983048 | tf_op jit(solution)/shard_map/ppermute | solution.py:621
  101.3 12.9 %collective-permute-start.15 = (f32[10,64,128]{2,1,0:T(8,128)S(1)}, f32[10,64,128]{2,1,0:T(8,128)S(1)}, u32[]{:S(2)}, u32[]{:S(2)}) collective-permute-start(f32[10,64,128]{2,1,0:T(8,128)S(1)} %get-tuple-element.88), channel_id=1, source_target_pairs={{2,0},{4,1},{0,2},{6,3},{7,4},{1,5},{5,6},{3,7},{10,8},{12,9},{8,1... | collective-permute-start | bytes 983048 | tf_op jit(solution)/shard_map/ppermute | solution.py:621
  101.9 17.0 %collective-permute-start.16 = (f32[10,64,128]{2,1,0:T(8,128)S(1)}, f32[10,64,128]{2,1,0:T(8,128)S(1)}, u32[]{:S(2)}, u32[]{:S(2)}) collective-permute-start(f32[10,64,128]{2,1,0:T(8,128)S(1)} %get-tuple-element.89), channel_id=1, source_target_pairs={{4,0},{2,1},{6,2},{0,3},{1,4},{7,5},{3,6},{5,7},{12,8},{10,9},{14,... | collective-permute-start | bytes 983048 | tf_op jit(solution)/shard_map/ppermute | solution.py:621
  105.9 17.1 %collective-permute-start.17 = (f32[10,64,128]{2,1,0:T(8,128)S(1)}, f32[10,64,128]{2,1,0:T(8,128)S(1)}, u32[]{:S(2)}, u32[]{:S(2)}) collective-permute-start(f32[10,64,128]{2,1,0:T(8,128)S(1)} %get-tuple-element.90), channel_id=1, source_target_pairs={{6,0},{0,1},{4,2},{2,3},{3,4},{5,5},{1,6},{7,7},{14,8},{8,9},{12,1... | collective-permute-start | bytes 983048 | tf_op jit(solution)/shard_map/ppermute | solution.py:621

commit v10 on v9

--- a/solution.py
+++ b/solution.py
@@ -43,7 +43,7 @@
         self.no = 2 * levels_here
         self.NB = parts * bins_here
         self.CH = self.NB + LANES
-        self.edge_rows = (0, 1, rows - 2, rows - 1)
+        self.edge_rows = (rows - 2, rows - 1, 0, 1)
         self.inner_rows = tuple(range(2, rows - 2))
         self.half = parts // 2
         assert self.half & (self.half - 1) == 0 and self.half > 1
@@ -59,6 +59,9 @@
             base += deep
         return out, base
 
+    def halo(self, rows):
+        return HALO if rows == self.edge_rows else PAD
+
     def slabs(self, rows):
         return self.folds(rows)[1]
 
@@ -82,7 +85,8 @@
 def pack_kernel(z, rows, odd, part, spec_in, ocean_in, mask_in, *refs):
     B, R, C, W, mt = z.B, z.R, z.C, z.W, z.mt
     outs, (spec, ocean, mask, wide, sems) = refs[:B], refs[B:]
-    E, H = C + 2 * PAD, C + 2 * HALO
+    E, H = C + 2 * PAD, C + 2 * z.halo(rows)
+    brought = slice((E - H) // 2, (E + H) // 2)
     copies = []
     for half in range(W // LANES):
         cols = pl.ds(half * LANES, LANES)
@@ -118,7 +122,7 @@
         start = pl.multiple_of(share * C, PAD)
         for i in range(slabs):
             block = wide[i, pl.ds(start, E), :]
-            out[i * H : (i + 1) * H] = block[PAD - HALO : PAD - HALO + H]
+            out[i * H : (i + 1) * H] = block[brought]
         if rows == z.edge_rows:
             shift = lax.rem(W + LANES + PAD - start, W + LANES)
             out[slabs * H : slabs * H + R] = pltpu.roll(sea, shift, axis=1)[:, :LANES]
@@ -131,8 +135,8 @@
 def unpack_kernel(z, rows, odd, part, *refs):
     B, mt = z.B, z.mt
     got, outs = refs[:B], refs[B:]
-    E, H = z.C + 2 * PAD, z.C + 2 * HALO
-    brought = slice(PAD - HALO, PAD - HALO + H)
+    E, H = z.C + 2 * PAD, z.C + 2 * z.halo(rows)
+    brought = slice((E - H) // 2, (E + H) // 2)
     if rows == z.edge_rows:
         sea = outs[-1]
         outs = outs[:-1]
@@ -488,9 +492,9 @@
         pltpu.VMEM((W // LANES, nb * R, LANES), F32),
         pltpu.VMEM((W // LANES, 2 * L * R, LANES), F32),
     ]
-    def pack(rows):
+    def pack(rows, who):
         slabs = z.slabs(rows)
-        lines = slabs * (C + 2 * HALO) + (R if rows == z.edge_rows else 0)
+        lines = slabs * (C + 2 * z.halo(rows)) + (R if rows == z.edge_rows else 0)
         return pl.pallas_call(
             functools.partial(pack_kernel, z, rows),
             out_shape=[jax.ShapeDtypeStruct((lines, LANES), F32)] * B,
@@ -506,9 +510,10 @@
             name="pack",
         )(*who, spectrum.reshape(nb * R, W), ocean.reshape(2 * L * R, W), sea_mask)
 
-    packed = pack(z.edge_rows)
+    packed = pack(z.edge_rows, who)
     got = [lax.ppermute(packed[k], axes, forward[k]) for k in range(B)]
-    packed = pack(z.inner_rows)
+    later, _ = lax.optimization_barrier((who, packed[0]))
+    packed = pack(z.inner_rows, later)
 
     weights, drift_weights = pl.pallas_call(
         functools.partial(weights_kernel, z),
@@ -523,9 +528,8 @@
         name="weights",
     )(kernel_linear, kernel_square, drift_kernel)
     speed = speeds(z)
-    held_back = packed[half:]
-    got, weights, drift_weights, speed, held_back = lax.optimization_barrier(
-        (got, weights, drift_weights, speed, held_back)
+    *got, weights, drift_weights, speed = lax.optimization_barrier(
+        (*got, weights, drift_weights, speed)
     )
 
     def state(rows, columns):
@@ -541,12 +545,12 @@
             name="unpack",
         )(*who, *received)
 
-    top, bottom, sea = unpack(
+    bottom, top, sea = unpack(
         z.edge_rows, got[:B], [state(EDGE, width), state(EDGE, width), (R, width, LANES)]
     )
-    got = [lax.ppermute(packed[k], axes, forward[k]) for k in range(half)]
-    held_back, got[0], _ = lax.optimization_barrier((held_back, got[0], top))
-    got += [lax.ppermute(held_back[k], axes, forward[half + k]) for k in range(B - half)]
+    *blocks, top = lax.optimization_barrier((*packed[half:], top))
+    blocks = list(packed[:half]) + blocks
+    got = [lax.ppermute(blocks[k], axes, forward[k]) for k in range(B)]
     (inner,) = unpack(z.inner_rows, got, [state(R - 2 * EDGE, width)])
 
     def step_call(body, first, cut, sea_at, count, deepest, inputs, more=()):
@@ -615,7 +619,7 @@
             name="send_back",
         )(*who, *states)
 
-    packed = send_back(z.inner_rows, [inner]), send_back(z.edge_rows, [top, bottom])
+    packed = send_back(z.inner_rows, [inner]), send_back(z.edge_rows, [bottom, top])
     packed = list(packed[1]) + list(packed[0])
     back = [
         lax.ppermute(packed[i], axes, [(t, s) for s, t in forward[i % B]]) for i in range(2 * B)

time: 125 us -> 120 us (0.960)
  starting transfers between devices: 48.1 us -> 37.1 us
  waiting for transfers between devices: 29.6 us -> 35 us
    ppermute x4, starting transfers between devices: 15.2 us -> 5.1 us  [per_device(): got = [lax.ppermute(blocks[k], axes, forward[k]) for k in range(B)]]
    ppermute x4, waiting for transfers between devices: 7.13 us -> 13.3 us  [per_device(): got = [lax.ppermute(blocks[k], axes, forward[k]) for k in range(B)]]
    ppermute x3, waiting for transfers between devices: 0.01 us -> 3.52 us  [per_device(): down = lax.ppermute(top, axes, to_prev_row)]
    ppermute x3, waiting for transfers between devices: 2.03 us -> 0.01 us  [per_device(): up = lax.ppermute(bottom, axes, to_next_row)]
    ppermute x8, starting transfers between devices: 14.6 us -> 12.8 us  [per_device(): lax.ppermute(packed[i], axes, [(t, s) for s, t in forward[i % B]])]
    ppermute x3, starting transfers between devices: 8.04 us -> 9.41 us  [per_device(): down = lax.ppermute(top, axes, to_prev_row)]
  transfers between devices with their start and end apart: 22 -> 22, of which waited for: 10 -> 9; matrix products, arithmetic and copies ran while one was open for 0% -> 0% of each run, Pallas kernels for 31% -> 33%
where the time goes in v10:
time: 120 us
  Pallas kernels  44.1 us (37%)
  starting transfers between devices  37.1 us (31%)
  waiting for transfers between devices  35 us (29%)
  local copies, waits for them, and re-layouts  1.92 us (2%)
    pallas_call x9, Pallas kernels, step_call(): pl.pallas_call(functools.partial(body, z, first, cut, sea_at), out_shape=...  31.7 us
    ppermute x4, waiting for transfers between devices, per_device(): got = [lax.ppermute(blocks[k], axes, forward[k]) for k in range(B)]  13.3 us
    ppermute x8, starting transfers between devices, per_device(): lax.ppermute(packed[i], axes, [(t, s) for s, t in forward[i % B]])  12.8 us
    ppermute x8, waiting for transfers between devices, per_device(): lax.ppermute(packed[i], axes, [(t, s) for s, t in forward[i % B]])  12.3 us
    ppermute x4, starting transfers between devices, per_device(): got = [lax.ppermute(packed[k], axes, forward[k]) for k in range(B)]  9.52 us
    ppermute x3, starting transfers between devices, per_device(): down = lax.ppermute(top, axes, to_prev_row)  9.41 us
    pallas_call x2, Pallas kernels, pack(): pl.pallas_call(functools.partial(pack_kernel, z, rows), out_shape=[jax.Sh...  6.6 us
    ppermute x4, waiting for transfers between devices, per_device(): got = [lax.ppermute(packed[k], axes, forward[k]) for k in range(B)]  5.92 us
  transfers between devices with their start and end apart: 22, of which 9 were waited for; matrix products, arithmetic and copies ran while one was open for 0% of the time, Pallas kernels for 33%

profile of v10, /device:TPU:0, one launch (start us, length us, event | category | flops | bytes accessed | tf_op | source)
XLA Modules:
  0.0 119.5 jit_solution(12671207706950905279)
XLA Ops:
  0.7 3.4 %pack.2 = (f32[768,128]{1,0:T(8,128)}, f32[768,128]{1,0:T(8,128)}, f32[768,128]{1,0:T(8,128)}, f32[768,128]{1,0:T(8,128)}) custom-call(s32[1]{0:T(128)} %bitcast.odd, s32[1]{0:T(128)} %bitcast.1.part, f32[2304,256]{1,0:T(8,128)} %bitcast.6, f32[256,256]{1,0:T(8,128)} %bitcast.8, s32[8,256]{1,0:T(8,128)} %mask_in.3), custom_call_target="tpu_custom_call" | custom-call | tf_op jit(solution)/shard_map/pack/pallas_call | solution.py:498
  4.0 1.7 %collective-permute-start = (f32[768,128]{1,0:T(8,128)}, f32[768,128]{1,0:T(8,128)S(1)}, u32[]{:S(2)}, u32[]{:S(2)}) collective-permute-start(f32[768,128]{1,0:T(8,128)} %get-tuple-element.51), channel_id=1, source_target_pairs={{0,0},{1,6},{2,2},{3,4},{4,5},{5,3},{6,7},{7,1},{8,8},{9,14},{10,1... | collective-permute-start | bytes 1179656 | tf_op jit(solution)/shard_map/ppermute | solution.py:514
  5.7 3.0 %collective-permute-start.1 = (f32[768,128]{1,0:T(8,128)}, f32[768,128]{1,0:T(8,128)S(1)}, u32[]{:S(2)}, u32[]{:S(2)}) collective-permute-start(f32[768,128]{1,0:T(8,128)} %get-tuple-element.56), channel_id=1, source_target_pairs={{0,2},{1,4},{2,0},{3,6},{4,7},{5,1},{6,5},{7,3},{8,10},{9,12},{10,... | collective-permute-start | bytes 1179656 | tf_op jit(solution)/shard_map/ppermute | solution.py:514
  9.9 3.6 %collective-permute-start.3 = (f32[768,128]{1,0:T(8,128)}, f32[768,128]{1,0:T(8,128)S(1)}, u32[]{:S(2)}, u32[]{:S(2)}) collective-permute-start(f32[768,128]{1,0:T(8,128)} %get-tuple-element.58), channel_id=1, source_target_pairs={{0,6},{1,0},{2,4},{3,2},{4,3},{5,5},{6,1},{7,7},{8,14},{9,8},{10,1... | collective-permute-start | bytes 1179656 | tf_op jit(solution)/shard_map/ppermute | solution.py:514
  13.6 3.2 %pack.3 = (f32[800,128]{1,0:T(8,128)}, f32[800,128]{1,0:T(8,128)}, f32[800,128]{1,0:T(8,128)}, f32[800,128]{1,0:T(8,128)}) custom-call(s32[1]{0:T(128)} %bitcast.odd, s32[1]{0:T(128)} %bitcast.1.part, f32[2304,256]{1,0:T(8,128)} %bitcast.7, f32[256,256]{1,0:T(8,128)} %bitcast.9, s32[8,256]{1,0:T(8,128)} %mask_in.3), custom_call_target="tpu_custom_call" | custom-call | tf_op jit(solution)/shard_map/pack/pallas_call | solution.py:498
  16.8 1.7 %collective-permute-start.5 = (f32[800,128]{1,0:T(8,128)}, f32[800,128]{1,0:T(8,128)S(1)}, u32[]{:S(2)}, u32[]{:S(2)}) collective-permute-start(f32[800,128]{1,0:T(8,128)} %get-tuple-element.68), channel_id=1, source_target_pairs={{0,0},{1,6},{2,2},{3,4},{4,5},{5,3},{6,7},{7,1},{8,8},{9,14},{10,1... | collective-permute-start | bytes 1228808 | tf_op jit(solution)/shard_map/ppermute | solution.py:553
  18.8 1.7 %copy-done.1 = bf16[1152,1152]{1,0:T(8,128)(2,1)S(1)} copy-done((bf16[1152,1152]{1,0:T(8,128)(2,1)S(1)}, bf16[1152,1152]{1,0:T(8,128)(2,1)}, u32[]{:S(2)}) %copy-start.1) | copy-done | bytes 2654232
  20.6 1.5 %weights.1 = (bf16[2304,1152]{1,0:T(8,128)(2,1)S(1)}, bf16[1152,128]{1,0:T(8,128)(2,1)S(1)}) custom-call(bf16[1152,1152]{1,0:T(8,128)(2,1)S(1)} %copy-done, bf16[1152,1152]{1,0:T(8,128)(2,1)S(1)} %copy-done.1, bf16[128,1152]{1,0:T(8,128)(2,1)S(1)} %copy-done.2), custom_call_target="tpu_custom_call" | custom-call | flops 2000000000 | bytes 10616832 | tf_op jit(solution)/shard_map/weights/pallas_call | solution.py:518
  24.2 3.9 %collective-permute-done.3.refs_3_ = f32[768,128]{1,0:T(8,128)S(1)} collective-permute-done((f32[768,128]{1,0:T(8,128)}, f32[768,128]{1,0:T(8,128)S(1)}, u32[]{:S(2)}, u32[]{:S(2)}) %collective-permute-start.3) | collective-permute-done | bytes 393248 | tf_op jit(solution)/shard_map/ppermute | solution.py:514
  28.8 5.3 %collective-permute-start.4 = (f32[10,2,80,128]{3,2,1,0:T(8,128)S(1)}, f32[10,2,80,128]{3,2,1,0:T(8,128)S(1)}, u32[]{:S(2)}, u32[]{:S(2)}) collective-permute-start(f32[10,2,80,128]{3,2,1,0:T(8,128)S(1)} %get-tuple-element.66.top), channel_id=1, source_target_pairs={{1,0},{3,2},{5,4},{7,6},{8,1},{10,3},{12,5},{14,7},{9,8},{11,10},{... | collective-permute-start | bytes 2457608 | tf_op jit(solution)/shard_map/ppermute | solution.py:580
  34.1 1.5 %collective-permute-start.6 = (f32[800,128]{1,0:T(8,128)S(1)}, f32[800,128]{1,0:T(8,128)S(1)}, u32[]{:S(2)}, u32[]{:S(2)}) collective-permute-start(f32[800,128]{1,0:T(8,128)S(1)} %copy-done.5), channel_id=1, source_target_pairs={{0,2},{1,4},{2,0},{3,6},{4,7},{5,1},{6,5},{7,3},{8,10},{9,12},{10,... | collective-permute-start | bytes 1228808 | tf_op jit(solution)/shard_map/ppermute | solution.py:553
  35.6 1.9 %collective-permute-start.8 = (f32[800,128]{1,0:T(8,128)S(1)}, f32[800,128]{1,0:T(8,128)S(1)}, u32[]{:S(2)}, u32[]{:S(2)}) collective-permute-start(f32[800,128]{1,0:T(8,128)S(1)} %copy-done.3), channel_id=1, source_target_pairs={{0,6},{1,0},{2,4},{3,2},{4,3},{5,5},{6,1},{7,7},{8,14},{9,8},{10,1... | collective-permute-start | bytes 1228808 | tf_op jit(solution)/shard_map/ppermute | solution.py:553
  37.5 12.3 %collective-permute-done.6.refs_1_ = f32[800,128]{1,0:T(8,128)S(1)} collective-permute-done((f32[800,128]{1,0:T(8,128)S(1)}, f32[800,128]{1,0:T(8,128)S(1)}, u32[]{:S(2)}, u32[]{:S(2)}) %collective-permute-start.6) | collective-permute-done | bytes 409632 | tf_op jit(solution)/shard_map/ppermute | solution.py:553
  51.3 3.3 %bottom_kernel.3 = (f32[10,2,72,128]{3,2,1,0:T(8,128)S(1)}, f32[2,80,128]{2,1,0:T(8,128)S(1)}) custom-call(f32[10,2,80,128]{3,2,1,0:T(8,128)S(1)} %collective-permute-done.4.down, f32[10,2,80,128]{3,2,1,0:T(8,128)S(1)} %get-tuple-element.67.bottom, f32[10,4,80,128]{3,2,1,0:T(8,128)S(1)} %unpack.3.inner, f32[8,80,128]{2,1,0:T(8,128)S(1)} %get-tuple-element.72.sea, ...), custom_call_target="tpu_custom_call" | custom-call | flops 200000000 | bytes 200000 | tf_op jit(solution)/shard_map/bottom_kernel/pallas_call | solution.py:560
  54.7 3.3 %top_kernel.3 = (f32[10,2,72,128]{3,2,1,0:T(8,128)S(1)}, f32[2,80,128]{2,1,0:T(8,128)S(1)}) custom-call(f32[10,2,80,128]{3,2,1,0:T(8,128)S(1)} %collective-permute-done.10.up, f32[10,2,80,128]{3,2,1,0:T(8,128)S(1)} %get-tuple-element.66.top, f32[10,4,80,128]{3,2,1,0:T(8,128)S(1)} %unpack.3.inner, f32[8,80,128]{2,1,0:T(8,128)S(1)} %get-tuple-element.72.sea, ...), custom_call_target="tpu_custom_call" | custom-call | flops 200000000 | bytes 200000 | tf_op jit(solution)/shard_map/top_kernel/pallas_call | solution.py:560
  57.9 3.8 %collective-permute-start.12 = (f32[10,2,72,128]{3,2,1,0:T(8,128)S(1)}, f32[10,2,72,128]{3,2,1,0:T(8,128)S(1)}, u32[]{:S(2)}, u32[]{:S(2)}) collective-permute-start(f32[10,2,72,128]{3,2,1,0:T(8,128)S(1)} %get-tuple-element.78.top), channel_id=1, source_target_pairs={{1,0},{3,2},{5,4},{7,6},{8,1},{10,3},{12,5},{14,7},{9,8},{11,10},{... | collective-permute-start | bytes 2211848 | tf_op jit(solution)/shard_map/ppermute | solution.py:580
  61.7 5.3 %inner_kernel.3.inner = f32[10,4,72,128]{3,2,1,0:T(8,128)S(1)} custom-call(f32[10,2,80,128]{3,2,1,0:T(8,128)S(1)} %get-tuple-element.66.top, f32[10,4,80,128]{3,2,1,0:T(8,128)S(1)} %unpack.3.inner, f32[10,2,80,128]{3,2,1,0:T(8,128)S(1)} %get-tuple-element.67.bottom, f32[8,80,128]{2,1,0:T(8,128)S(1)} %get-tuple-element.72.sea, ...), custom_call_target="tpu_custom_call" | custom-call | flops 400000000 | bytes 400000 | tf_op jit(solution)/shard_map/inner_kernel/pallas_call | solution.py:560
  67.0 5.0 %inner_kernel.4 = (f32[10,4,72,128]{3,2,1,0:T(8,128)S(1)}, f32[9,2,72,128]{3,2,1,0:T(8,128)S(1)}, f32[9,2,72,128]{3,2,1,0:T(8,128)S(1)}) custom-call(f32[10,2,72,128]{3,2,1,0:T(8,128)S(1)} %get-tuple-element.78.top, f32[10,4,72,128]{3,2,1,0:T(8,128)S(1)} %inner_kernel.3.inner, f32[10,2,72,128]{3,2,1,0:T(8,128)S(1)} %get-tuple-element.76.bottom, ...), custom_call_target="tpu_custom_call" | custom-call | flops 400000000 | bytes 400000 | tf_op jit(solution)/shard_map/inner_kernel/pallas_call | solution.py:560
  72.0 2.6 %top_kernel.4.top = f32[10,2,72,128]{3,2,1,0:T(8,128)S(1)} custom-call(f32[10,2,72,128]{3,2,1,0:T(8,128)S(1)} %collective-permute-done.9.up, f32[10,2,72,128]{3,2,1,0:T(8,128)S(1)} %get-tuple-element.78.top, f32[10,4,72,128]{3,2,1,0:T(8,128)S(1)} %inner_kernel.3.inner, f32[8,80,128]{2,1,0:T(8,128)S(1)} %get-tuple-element.72.sea, ...), custom_call_target="tpu_custom_call" | custom-call | flops 200000000 | bytes 200000 | tf_op jit(solution)/shard_map/top_kernel/pallas_call | solution.py:560
  75.0 2.6 %bottom_kernel.4.bottom = f32[10,2,72,128]{3,2,1,0:T(8,128)S(1)} custom-call(f32[10,2,72,128]{3,2,1,0:T(8,128)S(1)} %collective-permute-done.12.down, f32[10,2,72,128]{3,2,1,0:T(8,128)S(1)} %get-tuple-element.76.bottom, f32[10,4,72,128]{3,2,1,0:T(8,128)S(1)} %inner_kernel.3.inner, f32[8,80,128]{2,1,0:T(8,128)S(1)} %get-tuple-element.72.sea, ...), custom_call_target="tpu_custom_call" | custom-call | flops 200000000 | bytes 200000 | tf_op jit(solution)/shard_map/bottom_kernel/pallas_call | solution.py:560
  77.8 4.7 %inner_kernel.5 = (f32[10,4,64,128]{3,2,1,0:T(8,128)S(1)}, f32[9,2,72,128]{3,2,1,0:T(8,128)S(1)}, f32[9,2,72,128]{3,2,1,0:T(8,128)S(1)}) custom-call(f32[10,2,72,128]{3,2,1,0:T(8,128)S(1)} %top_kernel.4.top, f32[10,4,72,128]{3,2,1,0:T(8,128)S(1)} %get-tuple-element.84.inner, f32[10,2,72,128]{3,2,1,0:T(8,128)S(1)} %bottom_kernel.4.bottom, ...), custom_call_target="tpu_custom_call" | custom-call | flops 400000000 | bytes 400000 | tf_op jit(solution)/shard_map/inner_kernel/pallas_call | solution.py:560
  83.6 1.5 %collective-permute-start.19 = (f32[10,64,128]{2,1,0:T(8,128)S(1)}, f32[10,64,128]{2,1,0:T(8,128)S(1)}, u32[]{:S(2)}, u32[]{:S(2)}) collective-permute-start(f32[10,64,128]{2,1,0:T(8,128)S(1)} %get-tuple-element.93), channel_id=1, source_target_pairs={{2,0},{4,1},{0,2},{6,3},{7,4},{1,5},{5,6},{3,7},{10,8},{12,9},{8,1... | collective-permute-start | bytes 983048 | tf_op jit(solution)/shard_map/ppermute | solution.py:625
  86.0 3.5 %collective-permute-done.11.down = f32[10,2,72,128]{3,2,1,0:T(8,128)S(1)} collective-permute-done((f32[10,2,72,128]{3,2,1,0:T(8,128)S(1)}, f32[10,2,72,128]{3,2,1,0:T(8,128)S(1)}, u32[]{:S(2)}, u32[]{:S(2)}) %collective-permute-start.11) | collective-permute-done | bytes 737312 | tf_op jit(solution)/shard_map/ppermute | solution.py:580
  89.6 2.1 %collective-permute-start.21 = (f32[10,64,128]{2,1,0:T(8,128)S(1)}, f32[10,64,128]{2,1,0:T(8,128)S(1)}, u32[]{:S(2)}, u32[]{:S(2)}) collective-permute-start(f32[10,64,128]{2,1,0:T(8,128)S(1)} %get-tuple-element.95), channel_id=1, source_target_pairs={{6,0},{0,1},{4,2},{2,3},{3,4},{5,5},{1,6},{7,7},{14,8},{8,9},{12,1... | collective-permute-start | bytes 983048 | tf_op jit(solution)/shard_map/ppermute | solution.py:625
  91.7 2.5 %bottom_kernel.5.refs_0_ = f32[10,2,64,128]{3,2,1,0:T(8,128)S(1)} custom-call(f32[10,2,72,128]{3,2,1,0:T(8,128)S(1)} %collective-permute-done.11.down, f32[10,2,72,128]{3,2,1,0:T(8,128)S(1)} %bottom_kernel.4.bottom, f32[10,4,72,128]{3,2,1,0:T(8,128)S(1)} %get-tuple-element.84.inner, f32[8,80,128]{2,1,0:T(8,128)S(1)} %get-tuple-element.72.sea, ...), custom_call_target="tpu_custom_call" | custom-call | flops 200000000 | bytes 200000 | tf_op jit(solution)/shard_map/bottom_kernel/pallas_call | solution.py:560
  94.2 2.5 %top_kernel.5.refs_1_ = f32[10,2,64,128]{3,2,1,0:T(8,128)S(1)} custom-call(f32[10,2,72,128]{3,2,1,0:T(8,128)S(1)} %collective-permute-done.13.up, f32[10,2,72,128]{3,2,1,0:T(8,128)S(1)} %top_kernel.4.top, f32[10,4,72,128]{3,2,1,0:T(8,128)S(1)} %get-tuple-element.84.inner, f32[8,80,128]{2,1,0:T(8,128)S(1)} %get-tuple-element.72.sea, ...), custom_call_target="tpu_custom_call" | custom-call | flops 200000000 | bytes 200000 | tf_op jit(solution)/shard_map/top_kernel/pallas_call | solution.py:560
  98.9 3.4 %collective-permute-start.16 = (f32[10,64,128]{2,1,0:T(8,128)S(1)}, f32[10,64,128]{2,1,0:T(8,128)S(1)}, u32[]{:S(2)}, u32[]{:S(2)}) collective-permute-start(f32[10,64,128]{2,1,0:T(8,128)S(1)} %get-tuple-element.89), channel_id=1, source_target_pairs={{4,0},{2,1},{6,2},{0,3},{1,4},{7,5},{3,6},{5,7},{12,8},{10,9},{14,... | collective-permute-start | bytes 983048 | tf_op jit(solution)/shard_map/ppermute | solution.py:625
  102.4 2.2 %collective-permute-start.17 = (f32[10,64,128]{2,1,0:T(8,128)S(1)}, f32[10,64,128]{2,1,0:T(8,128)S(1)}, u32[]{:S(2)}, u32[]{:S(2)}) collective-permute-start(f32[10,64,128]{2,1,0:T(8,128)S(1)} %get-tuple-element.90), channel_id=1, source_target_pairs={{6,0},{0,1},{4,2},{2,3},{3,4},{5,5},{1,6},{7,7},{14,8},{8,9},{12,1... | collective-permute-start | bytes 983048 | tf_op jit(solution)/shard_map/ppermute | solution.py:625
  105.2 4.8 %collective-permute-done.15.refs_1_ = f32[10,64,128]{2,1,0:T(8,128)S(1)} collective-permute-done((f32[10,64,128]{2,1,0:T(8,128)S(1)}, f32[10,64,128]{2,1,0:T(8,128)S(1)}, u32[]{:S(2)}, u32[]{:S(2)}) %collective-permute-start.15) | collective-permute-done | bytes 327712 | tf_op jit(solution)/shard_map/ppermute | solution.py:625
  110.0 4.5 %collective-permute-done.16.refs_2_ = f32[10,64,128]{2,1,0:T(8,128)S(1)} collective-permute-done((f32[10,64,128]{2,1,0:T(8,128)S(1)}, f32[10,64,128]{2,1,0:T(8,128)S(1)}, u32[]{:S(2)}, u32[]{:S(2)}) %collective-permute-start.16) | collective-permute-done | bytes 327712 | tf_op jit(solution)/shard_map/ppermute | solution.py:625
  114.5 2.9 %collective-permute-done.17.refs_3_ = f32[10,64,128]{2,1,0:T(8,128)S(1)} collective-permute-done((f32[10,64,128]{2,1,0:T(8,128)S(1)}, f32[10,64,128]{2,1,0:T(8,128)S(1)}, u32[]{:S(2)}, u32[]{:S(2)}) %collective-permute-start.17) | collective-permute-done | bytes 327712 | tf_op jit(solution)/shard_map/ppermute | solution.py:625
  117.5 1.9 %restore.1 = (f32[2304,256]{1,0:T(8,128)}, f32[256,256]{1,0:T(8,128)}, f32[2,2304,128]{2,1,0:T(8,128)S(1)}, f32[2,256,128]{2,1,0:T(8,128)S(1)}) custom-call(s32[1]{0:T(128)} %bitcast.odd, s32[1]{0:T(128)} %bitcast.1.part, f32[10,64,128]{2,1,0:T(8,128)S(1)} %collective-permute-done.14.refs_0_, ...), custom_call_target="tpu_custom_call", output_to_operand_aliasing={{2}: (6, {}), {3}: (7, {})} | custom-call | tf_op jit(solution)/shard_map/restore/pallas_call | solution.py:640
  (48 shorter events, 11.2 us)
Async XLA Ops:
  0.6 18.2 %copy-start = (bf16[1152,1152]{1,0:T(8,128)(2,1)S(1)}, bf16[1152,1152]{1,0:T(8,128)(2,1)}, u32[]{:S(2)}) copy-start(bf16[1152,1152]{1,0:T(8,128)(2,1)} %linear.1) | copy-start | bytes 7962628
  0.7 18.2 %copy-start.2 = (bf16[128,1152]{1,0:T(8,128)(2,1)S(1)}, bf16[128,1152]{1,0:T(8,128)(2,1)}, u32[]{:S(2)}) copy-start(bf16[128,1152]{1,0:T(8,128)(2,1)} %drift.1) | copy-start | bytes 884740
  4.0 18.2 %collective-permute-start = (f32[768,128]{1,0:T(8,128)}, f32[768,128]{1,0:T(8,128)S(1)}, u32[]{:S(2)}, u32[]{:S(2)}) collective-permute-start(f32[768,128]{1,0:T(8,128)} %get-tuple-element.51), channel_id=1, source_target_pairs={{0,0},{1,6},{2,2},{3,4},{4,5},{5,3},{6,7},{7,1},{8,8},{9,14},{10,1... | collective-permute-start | bytes 1179656 | tf_op jit(solution)/shard_map/ppermute | solution.py:514
  5.7 17.9 %collective-permute-start.1 = (f32[768,128]{1,0:T(8,128)}, f32[768,128]{1,0:T(8,128)S(1)}, u32[]{:S(2)}, u32[]{:S(2)}) collective-permute-start(f32[768,128]{1,0:T(8,128)} %get-tuple-element.56), channel_id=1, source_target_pairs={{0,2},{1,4},{2,0},{3,6},{4,7},{5,1},{6,5},{7,3},{8,10},{9,12},{10,... | collective-permute-start | bytes 1179656 | tf_op jit(solution)/shard_map/ppermute | solution.py:514
  8.7 15.5 %collective-permute-start.2 = (f32[768,128]{1,0:T(8,128)}, f32[768,128]{1,0:T(8,128)S(1)}, u32[]{:S(2)}, u32[]{:S(2)}) collective-permute-start(f32[768,128]{1,0:T(8,128)} %get-tuple-element.57), channel_id=1, source_target_pairs={{0,4},{1,2},{2,6},{3,0},{4,1},{5,7},{6,3},{7,5},{8,12},{9,10},{10,... | collective-permute-start | bytes 1179656 | tf_op jit(solution)/shard_map/ppermute | solution.py:514
  9.9 18.2 %collective-permute-start.3 = (f32[768,128]{1,0:T(8,128)}, f32[768,128]{1,0:T(8,128)S(1)}, u32[]{:S(2)}, u32[]{:S(2)}) collective-permute-start(f32[768,128]{1,0:T(8,128)} %get-tuple-element.58), channel_id=1, source_target_pairs={{0,6},{1,0},{2,4},{3,2},{4,3},{5,5},{6,1},{7,7},{8,14},{9,8},{10,1... | collective-permute-start | bytes 1179656 | tf_op jit(solution)/shard_map/ppermute | solution.py:514
  16.8 18.8 %collective-permute-start.5 = (f32[800,128]{1,0:T(8,128)}, f32[800,128]{1,0:T(8,128)S(1)}, u32[]{:S(2)}, u32[]{:S(2)}) collective-permute-start(f32[800,128]{1,0:T(8,128)} %get-tuple-element.68), channel_id=1, source_target_pairs={{0,0},{1,6},{2,2},{3,4},{4,5},{5,3},{6,7},{7,1},{8,8},{9,14},{10,1... | collective-permute-start | bytes 1228808 | tf_op jit(solution)/shard_map/ppermute | solution.py:553
  18.8 1.8 %copy-start.1 = (bf16[1152,1152]{1,0:T(8,128)(2,1)S(1)}, bf16[1152,1152]{1,0:T(8,128)(2,1)}, u32[]{:S(2)}) copy-start(bf16[1152,1152]{1,0:T(8,128)(2,1)} %square.1) | copy-start | bytes 7962628
  20.6 13.5 %copy-start.5 = (f32[800,128]{1,0:T(8,128)S(1)}, f32[800,128]{1,0:T(8,128)}, u32[]{:S(2)}) copy-start(f32[800,128]{1,0:T(8,128)} %get-tuple-element.69) | copy-start | bytes 1228804
  20.6 15.0 %copy-start.4 = (f32[800,128]{1,0:T(8,128)S(1)}, f32[800,128]{1,0:T(8,128)}, u32[]{:S(2)}) copy-start(f32[800,128]{1,0:T(8,128)} %get-tuple-element.70) | copy-start | bytes 1228804
  20.6 15.0 %copy-start.3 = (f32[800,128]{1,0:T(8,128)S(1)}, f32[800,128]{1,0:T(8,128)}, u32[]{:S(2)}) copy-start(f32[800,128]{1,0:T(8,128)} %get-tuple-element.71) | copy-start | bytes 1228804
  28.8 22.5 %collective-permute-start.4 = (f32[10,2,80,128]{3,2,1,0:T(8,128)S(1)}, f32[10,2,80,128]{3,2,1,0:T(8,128)S(1)}, u32[]{:S(2)}, u32[]{:S(2)}) collective-permute-start(f32[10,2,80,128]{3,2,1,0:T(8,128)S(1)} %get-tuple-element.66.top), channel_id=1, source_target_pairs={{1,0},{3,2},{5,4},{7,6},{8,1},{10,3},{12,5},{14,7},{9,8},{11,10},{... | collective-permute-start | bytes 2457608 | tf_op jit(solution)/shard_map/ppermute | solution.py:580
  34.1 20.6 %collective-permute-start.10 = (f32[10,2,80,128]{3,2,1,0:T(8,128)S(1)}, f32[10,2,80,128]{3,2,1,0:T(8,128)S(1)}, u32[]{:S(2)}, u32[]{:S(2)}) collective-permute-start(f32[10,2,80,128]{3,2,1,0:T(8,128)S(1)} %get-tuple-element.67.bottom), channel_id=1, source_target_pairs={{0,1},{2,3},{4,5},{6,7},{1,8},{3,10},{5,12},{7,14},{8,9},{10,11},{... | collective-permute-start | bytes 2457608 | tf_op jit(solution)/shard_map/ppermute | solution.py:581
  34.1 15.8 %collective-permute-start.6 = (f32[800,128]{1,0:T(8,128)S(1)}, f32[800,128]{1,0:T(8,128)S(1)}, u32[]{:S(2)}, u32[]{:S(2)}) collective-permute-start(f32[800,128]{1,0:T(8,128)S(1)} %copy-done.5), channel_id=1, source_target_pairs={{0,2},{1,4},{2,0},{3,6},{4,7},{5,1},{6,5},{7,3},{8,10},{9,12},{10,... | collective-permute-start | bytes 1228808 | tf_op jit(solution)/shard_map/ppermute | solution.py:553
  35.6 15.2 %collective-permute-start.7 = (f32[800,128]{1,0:T(8,128)S(1)}, f32[800,128]{1,0:T(8,128)S(1)}, u32[]{:S(2)}, u32[]{:S(2)}) collective-permute-start(f32[800,128]{1,0:T(8,128)S(1)} %copy-done.4), channel_id=1, source_target_pairs={{0,4},{1,2},{2,6},{3,0},{4,1},{5,7},{6,3},{7,5},{8,12},{9,10},{10,... | collective-permute-start | bytes 1228808 | tf_op jit(solution)/shard_map/ppermute | solution.py:553
  35.6 15.2 %collective-permute-start.8 = (f32[800,128]{1,0:T(8,128)S(1)}, f32[800,128]{1,0:T(8,128)S(1)}, u32[]{:S(2)}, u32[]{:S(2)}) collective-permute-start(f32[800,128]{1,0:T(8,128)S(1)} %copy-done.3), channel_id=1, source_target_pairs={{0,6},{1,0},{2,4},{3,2},{4,3},{5,5},{6,1},{7,7},{8,14},{9,8},{10,1... | collective-permute-start | bytes 1228808 | tf_op jit(solution)/shard_map/ppermute | solution.py:553
  54.6 17.4 %collective-permute-start.9 = (f32[10,2,72,128]{3,2,1,0:T(8,128)S(1)}, f32[10,2,72,128]{3,2,1,0:T(8,128)S(1)}, u32[]{:S(2)}, u32[]{:S(2)}) collective-permute-start(f32[10,2,72,128]{3,2,1,0:T(8,128)S(1)} %get-tuple-element.76.bottom), channel_id=1, source_target_pairs={{0,1},{2,3},{4,5},{6,7},{1,8},{3,10},{5,12},{7,14},{8,9},{10,11},{... | collective-permute-start | bytes 2211848 | tf_op jit(solution)/shard_map/ppermute | solution.py:581
  57.9 17.0 %collective-permute-start.12 = (f32[10,2,72,128]{3,2,1,0:T(8,128)S(1)}, f32[10,2,72,128]{3,2,1,0:T(8,128)S(1)}, u32[]{:S(2)}, u32[]{:S(2)}) collective-permute-start(f32[10,2,72,128]{3,2,1,0:T(8,128)S(1)} %get-tuple-element.78.top), channel_id=1, source_target_pairs={{1,0},{3,2},{5,4},{7,6},{8,1},{10,3},{12,5},{14,7},{9,8},{11,10},{... | collective-permute-start | bytes 2211848 | tf_op jit(solution)/shard_map/ppermute | solution.py:580
  74.6 15.0 %collective-permute-start.11 = (f32[10,2,72,128]{3,2,1,0:T(8,128)S(1)}, f32[10,2,72,128]{3,2,1,0:T(8,128)S(1)}, u32[]{:S(2)}, u32[]{:S(2)}) collective-permute-start(f32[10,2,72,128]{3,2,1,0:T(8,128)S(1)} %top_kernel.4.top), channel_id=1, source_target_pairs={{1,0},{3,2},{5,4},{7,6},{8,1},{10,3},{12,5},{14,7},{9,8},{11,10},{... | collective-permute-start | bytes 2211848 | tf_op jit(solution)/shard_map/ppermute | solution.py:580
  77.6 16.6 %collective-permute-start.13 = (f32[10,2,72,128]{3,2,1,0:T(8,128)S(1)}, f32[10,2,72,128]{3,2,1,0:T(8,128)S(1)}, u32[]{:S(2)}, u32[]{:S(2)}) collective-permute-start(f32[10,2,72,128]{3,2,1,0:T(8,128)S(1)} %bottom_kernel.4.bottom), channel_id=1, source_target_pairs={{0,1},{2,3},{4,5},{6,7},{1,8},{3,10},{5,12},{7,14},{8,9},{10,11},{... | collective-permute-start | bytes 2211848 | tf_op jit(solution)/shard_map/ppermute | solution.py:581
  82.9 14.8 %collective-permute-start.18 = (f32[10,64,128]{2,1,0:T(8,128)S(1)}, f32[10,64,128]{2,1,0:T(8,128)S(1)}, u32[]{:S(2)}, u32[]{:S(2)}) collective-permute-start(f32[10,64,128]{2,1,0:T(8,128)S(1)} %get-tuple-element.92), channel_id=1, source_target_pairs={{0,0},{6,1},{2,2},{4,3},{5,4},{3,5},{7,6},{1,7},{8,8},{14,9},{10,1... | collective-permute-start | bytes 983048 | tf_op jit(solution)/shard_map/ppermute | solution.py:625
  83.6 15.3 %collective-permute-start.19 = (f32[10,64,128]{2,1,0:T(8,128)S(1)}, f32[10,64,128]{2,1,0:T(8,128)S(1)}, u32[]{:S(2)}, u32[]{:S(2)}) collective-permute-start(f32[10,64,128]{2,1,0:T(8,128)S(1)} %get-tuple-element.93), channel_id=1, source_target_pairs={{2,0},{4,1},{0,2},{6,3},{7,4},{1,5},{5,6},{3,7},{10,8},{12,9},{8,1... | collective-permute-start | bytes 983048 | tf_op jit(solution)/shard_map/ppermute | solution.py:625
  85.1 17.3 %collective-permute-start.20 = (f32[10,64,128]{2,1,0:T(8,128)S(1)}, f32[10,64,128]{2,1,0:T(8,128)S(1)}, u32[]{:S(2)}, u32[]{:S(2)}) collective-permute-start(f32[10,64,128]{2,1,0:T(8,128)S(1)} %get-tuple-element.94), channel_id=1, source_target_pairs={{4,0},{2,1},{6,2},{0,3},{1,4},{7,5},{3,6},{5,7},{12,8},{10,9},{14,... | collective-permute-start | bytes 983048 | tf_op jit(solution)/shard_map/ppermute | solution.py:625
  89.6 15.1 %collective-permute-start.21 = (f32[10,64,128]{2,1,0:T(8,128)S(1)}, f32[10,64,128]{2,1,0:T(8,128)S(1)}, u32[]{:S(2)}, u32[]{:S(2)}) collective-permute-start(f32[10,64,128]{2,1,0:T(8,128)S(1)} %get-tuple-element.95), channel_id=1, source_target_pairs={{6,0},{0,1},{4,2},{2,3},{3,4},{5,5},{1,6},{7,7},{14,8},{8,9},{12,1... | collective-permute-start | bytes 983048 | tf_op jit(solution)/shard_map/ppermute | solution.py:625
  97.1 8.1 %collective-permute-start.14 = (f32[10,64,128]{2,1,0:T(8,128)S(1)}, f32[10,64,128]{2,1,0:T(8,128)S(1)}, u32[]{:S(2)}, u32[]{:S(2)}) collective-permute-start(f32[10,64,128]{2,1,0:T(8,128)S(1)} %get-tuple-element.87), channel_id=1, source_target_pairs={{0,0},{6,1},{2,2},{4,3},{5,4},{3,5},{7,6},{1,7},{8,8},{14,9},{10,1... | collective-permute-start | bytes 983048 | tf_op jit(solution)/shard_map/ppermute | solution.py:625
  97.8 12.2 %collective-permute-start.15 = (f32[10,64,128]{2,1,0:T(8,128)S(1)}, f32[10,64,128]{2,1,0:T(8,128)S(1)}, u32[]{:S(2)}, u32[]{:S(2)}) collective-permute-start(f32[10,64,128]{2,1,0:T(8,128)S(1)} %get-tuple-element.88), channel_id=1, source_target_pairs={{2,0},{4,1},{0,2},{6,3},{7,4},{1,5},{5,6},{3,7},{10,8},{12,9},{8,1... | collective-permute-start | bytes 983048 | tf_op jit(solution)/shard_map/ppermute | solution.py:625
  98.9 15.6 %collective-permute-start.16 = (f32[10,64,128]{2,1,0:T(8,128)S(1)}, f32[10,64,128]{2,1,0:T(8,128)S(1)}, u32[]{:S(2)}, u32[]{:S(2)}) collective-permute-start(f32[10,64,128]{2,1,0:T(8,128)S(1)} %get-tuple-element.89), channel_id=1, source_target_pairs={{4,0},{2,1},{6,2},{0,3},{1,4},{7,5},{3,6},{5,7},{12,8},{10,9},{14,... | collective-permute-start | bytes 983048 | tf_op jit(solution)/shard_map/ppermute | solution.py:625
  102.4 15.1 %collective-permute-start.17 = (f32[10,64,128]{2,1,0:T(8,128)S(1)}, f32[10,64,128]{2,1,0:T(8,128)S(1)}, u32[]{:S(2)}, u32[]{:S(2)}) collective-permute-start(f32[10,64,128]{2,1,0:T(8,128)S(1)} %get-tuple-element.90), channel_id=1, source_target_pairs={{6,0},{0,1},{4,2},{2,3},{3,4},{5,5},{1,6},{7,7},{14,8},{8,9},{12,1... | collective-permute-start | bytes 983048 | tf_op jit(solution)/shard_map/ppermute | solution.py:625

commit v11 on v10

--- a/solution.py
+++ b/solution.py
@@ -286,27 +286,33 @@
     def shift_down(parts):
         return parts[1:] + [pltpu.roll(parts[0], SUBLANES - 1, axis=0)]
 
+    def in_order(t):
+        return slice(t * SUBLANES, (t + 1) * SUBLANES)
+
     for r in range(min(first[0] - 1, 1), max(first[-1] + 2, n - 1)):
-        ref, i = rows[r]
-        surface = ref[tiles, i]
-        moved[0, r] = DOPPLER * jnp.tanh(jnp.broadcast_to(surface[:, 0:1], (E, LANES)))
-        moved[1, r] = DOPPLER * jnp.tanh(jnp.broadcast_to(surface[:, L : L + 1], (E, LANES)))
+        for t in range(T):
+            ref, i = rows[r]
+            current = DOPPLER * jnp.tanh(ref[tiles, i, apart(0)[t], :])
+            for c in range(2):
+                one = current[:, c * L : c * L + 1]
+                moved[c, r, in_order(t)] = jnp.broadcast_to(one, (SUBLANES, LANES))
+            ref, i = sea_rows[r]
+            moved[3, r, in_order(t)] = ref[i, apart(sea_at)[t], :]
 
     def advect(read, write, start, stop, speed_cx, speed_cy):
         plus_before, waiting = None, None
         for r in range(start - 1, stop + 1):
             energy = read(r)
-            speed_x = [speed_cx + moved[0, r, at, :] for at in apart(0)]
+            speed_x = [speed_cx + moved[0, r, in_order(t)] for t in range(T)]
             if r >= start:
                 minus = [jnp.minimum(v, 0.0) * e for v, e in zip(speed_x, energy)]
             if r > start:
-                ref, i = sea_rows[r - 1]
-                sea = [ref[i, at, :] for at in apart(sea_at)]
+                sea = [moved[3, r - 1, in_order(t)] for t in range(T)]
                 write(r - 1, [(w - m) * s for w, m, s in zip(waiting, minus, sea)])
             if r < stop:
                 plus = [jnp.maximum(v, 0.0) * e for v, e in zip(speed_x, energy)]
             if start <= r < stop:
-                speed_y = [speed_cy + moved[1, r, at, :] for at in apart(0)]
+                speed_y = [speed_cy + moved[1, r, in_order(t)] for t in range(T)]
                 plus_y = [jnp.maximum(v, 0.0) * e for v, e in zip(speed_y, energy)]
                 minus_y = [jnp.minimum(v, 0.0) * e for v, e in zip(speed_y, energy)]
                 waiting = [
@@ -322,9 +328,6 @@
         lanes = pl.ds(pl.multiple_of(j * LANES, LANES), LANES)
         speed_cx = speed[0:1, lanes]
         speed_cy = speed[1:2, lanes]
-
-        def in_order(t):
-            return slice(t * SUBLANES, (t + 1) * SUBLANES)
 
         def read_first(r):
             ref, i = rows[r]
@@ -563,7 +566,7 @@
             in_specs=[VMEM] * (len(inputs) + 3),
             out_specs=[VMEM] * len(shapes),
             scratch_shapes=[
-                pltpu.VMEM((3, deepest, width, LANES), F32),
+                pltpu.VMEM((4, deepest, width, LANES), F32),
                 pltpu.VMEM((NB // LANES, count, width + PAD, LANES), F32),
             ],
             compiler_params=params(24),

time: 120 us -> 120 us (level)
  transfers between devices with their start and end apart: 22 -> 22, of which waited for: 9 -> 9; matrix products, arithmetic and copies ran while one was open for 0% -> 0% of each run, Pallas kernels for 33% -> 32%
where the time goes in v11:
time: 120 us; the launch traced here: 119 us
  Pallas kernels  43.4 us (36%)
  starting transfers between devices  37.4 us (31%)
  waiting for transfers between devices  35.2 us (29%)
  local copies, waits for them, and re-layouts  1.92 us (2%)
    pallas_call x9, Pallas kernels, step_call(): pl.pallas_call(functools.partial(body, z, first, cut, sea_at), out_shape=...  31 us
    ppermute x4, waiting for transfers between devices, per_device(): got = [lax.ppermute(blocks[k], axes, forward[k]) for k in range(B)]  13.3 us
    ppermute x8, starting transfers between devices, per_device(): lax.ppermute(packed[i], axes, [(t, s) for s, t in forward[i % B]])  12.8 us
    ppermute x8, waiting for transfers between devices, per_device(): lax.ppermute(packed[i], axes, [(t, s) for s, t in forward[i % B]])  12.6 us
    ppermute x4, starting transfers between devices, per_device(): got = [lax.ppermute(packed[k], axes, forward[k]) for k in range(B)]  9.52 us
    ppermute x3, starting transfers between devices, per_device(): down = lax.ppermute(top, axes, to_prev_row)  9.43 us
    pallas_call x2, Pallas kernels, pack(): pl.pallas_call(functools.partial(pack_kernel, z, rows), out_shape=[jax.Sh...  6.6 us
    ppermute x4, waiting for transfers between devices, per_device(): got = [lax.ppermute(packed[k], axes, forward[k]) for k in range(B)]  5.92 us
  transfers between devices with their start and end apart: 22, of which 9 were waited for; matrix products, arithmetic and copies ran while one was open for 0% of the time, Pallas kernels for 32%

profile of v11, /device:TPU:0, one launch (start us, length us, event | category | flops | bytes accessed | tf_op | source)
XLA Modules:
  0.0 119.3 jit_solution(16516919301844507590)
XLA Ops:
  0.7 3.4 %pack.2 = (f32[768,128]{1,0:T(8,128)}, f32[768,128]{1,0:T(8,128)}, f32[768,128]{1,0:T(8,128)}, f32[768,128]{1,0:T(8,128)}) custom-call(s32[1]{0:T(128)} %bitcast.odd, s32[1]{0:T(128)} %bitcast.1.part, f32[2304,256]{1,0:T(8,128)} %bitcast.6, f32[256,256]{1,0:T(8,128)} %bitcast.8, s32[8,256]{1,0:T(8,128)} %mask_in.3), custom_call_target="tpu_custom_call" | custom-call | tf_op jit(solution)/shard_map/pack/pallas_call | solution.py:501
  4.0 1.7 %collective-permute-start = (f32[768,128]{1,0:T(8,128)}, f32[768,128]{1,0:T(8,128)S(1)}, u32[]{:S(2)}, u32[]{:S(2)}) collective-permute-start(f32[768,128]{1,0:T(8,128)} %get-tuple-element.51), channel_id=1, source_target_pairs={{0,0},{1,6},{2,2},{3,4},{4,5},{5,3},{6,7},{7,1},{8,8},{9,14},{10,1... | collective-permute-start | bytes 1179656 | tf_op jit(solution)/shard_map/ppermute | solution.py:517
  5.7 3.0 %collective-permute-start.1 = (f32[768,128]{1,0:T(8,128)}, f32[768,128]{1,0:T(8,128)S(1)}, u32[]{:S(2)}, u32[]{:S(2)}) collective-permute-start(f32[768,128]{1,0:T(8,128)} %get-tuple-element.56), channel_id=1, source_target_pairs={{0,2},{1,4},{2,0},{3,6},{4,7},{5,1},{6,5},{7,3},{8,10},{9,12},{10,... | collective-permute-start | bytes 1179656 | tf_op jit(solution)/shard_map/ppermute | solution.py:517
  9.9 3.6 %collective-permute-start.3 = (f32[768,128]{1,0:T(8,128)}, f32[768,128]{1,0:T(8,128)S(1)}, u32[]{:S(2)}, u32[]{:S(2)}) collective-permute-start(f32[768,128]{1,0:T(8,128)} %get-tuple-element.58), channel_id=1, source_target_pairs={{0,6},{1,0},{2,4},{3,2},{4,3},{5,5},{6,1},{7,7},{8,14},{9,8},{10,1... | collective-permute-start | bytes 1179656 | tf_op jit(solution)/shard_map/ppermute | solution.py:517
  13.6 3.2 %pack.3 = (f32[800,128]{1,0:T(8,128)}, f32[800,128]{1,0:T(8,128)}, f32[800,128]{1,0:T(8,128)}, f32[800,128]{1,0:T(8,128)}) custom-call(s32[1]{0:T(128)} %bitcast.odd, s32[1]{0:T(128)} %bitcast.1.part, f32[2304,256]{1,0:T(8,128)} %bitcast.7, f32[256,256]{1,0:T(8,128)} %bitcast.9, s32[8,256]{1,0:T(8,128)} %mask_in.3), custom_call_target="tpu_custom_call" | custom-call | tf_op jit(solution)/shard_map/pack/pallas_call | solution.py:501
  16.8 1.7 %collective-permute-start.5 = (f32[800,128]{1,0:T(8,128)}, f32[800,128]{1,0:T(8,128)S(1)}, u32[]{:S(2)}, u32[]{:S(2)}) collective-permute-start(f32[800,128]{1,0:T(8,128)} %get-tuple-element.68), channel_id=1, source_target_pairs={{0,0},{1,6},{2,2},{3,4},{4,5},{5,3},{6,7},{7,1},{8,8},{9,14},{10,1... | collective-permute-start | bytes 1228808 | tf_op jit(solution)/shard_map/ppermute | solution.py:556
  18.8 1.7 %copy-done.1 = bf16[1152,1152]{1,0:T(8,128)(2,1)S(1)} copy-done((bf16[1152,1152]{1,0:T(8,128)(2,1)S(1)}, bf16[1152,1152]{1,0:T(8,128)(2,1)}, u32[]{:S(2)}) %copy-start.1) | copy-done | bytes 2654232
  20.6 1.5 %weights.1 = (bf16[2304,1152]{1,0:T(8,128)(2,1)S(1)}, bf16[1152,128]{1,0:T(8,128)(2,1)S(1)}) custom-call(bf16[1152,1152]{1,0:T(8,128)(2,1)S(1)} %copy-done, bf16[1152,1152]{1,0:T(8,128)(2,1)S(1)} %copy-done.1, bf16[128,1152]{1,0:T(8,128)(2,1)S(1)} %copy-done.2), custom_call_target="tpu_custom_call" | custom-call | flops 2000000000 | bytes 10616832 | tf_op jit(solution)/shard_map/weights/pallas_call | solution.py:521
  24.2 3.9 %collective-permute-done.3.refs_3_ = f32[768,128]{1,0:T(8,128)S(1)} collective-permute-done((f32[768,128]{1,0:T(8,128)}, f32[768,128]{1,0:T(8,128)S(1)}, u32[]{:S(2)}, u32[]{:S(2)}) %collective-permute-start.3) | collective-permute-done | bytes 393248 | tf_op jit(solution)/shard_map/ppermute | solution.py:517
  28.8 5.3 %collective-permute-start.4 = (f32[10,2,80,128]{3,2,1,0:T(8,128)S(1)}, f32[10,2,80,128]{3,2,1,0:T(8,128)S(1)}, u32[]{:S(2)}, u32[]{:S(2)}) collective-permute-start(f32[10,2,80,128]{3,2,1,0:T(8,128)S(1)} %get-tuple-element.66.top), channel_id=1, source_target_pairs={{1,0},{3,2},{5,4},{7,6},{8,1},{10,3},{12,5},{14,7},{9,8},{11,10},{... | collective-permute-start | bytes 2457608 | tf_op jit(solution)/shard_map/ppermute | solution.py:583
  34.1 1.5 %collective-permute-start.6 = (f32[800,128]{1,0:T(8,128)S(1)}, f32[800,128]{1,0:T(8,128)S(1)}, u32[]{:S(2)}, u32[]{:S(2)}) collective-permute-start(f32[800,128]{1,0:T(8,128)S(1)} %copy-done.5), channel_id=1, source_target_pairs={{0,2},{1,4},{2,0},{3,6},{4,7},{5,1},{6,5},{7,3},{8,10},{9,12},{10,... | collective-permute-start | bytes 1228808 | tf_op jit(solution)/shard_map/ppermute | solution.py:556
  35.6 1.9 %collective-permute-start.8 = (f32[800,128]{1,0:T(8,128)S(1)}, f32[800,128]{1,0:T(8,128)S(1)}, u32[]{:S(2)}, u32[]{:S(2)}) collective-permute-start(f32[800,128]{1,0:T(8,128)S(1)} %copy-done.3), channel_id=1, source_target_pairs={{0,6},{1,0},{2,4},{3,2},{4,3},{5,5},{6,1},{7,7},{8,14},{9,8},{10,1... | collective-permute-start | bytes 1228808 | tf_op jit(solution)/shard_map/ppermute | solution.py:556
  37.5 12.3 %collective-permute-done.6.refs_1_ = f32[800,128]{1,0:T(8,128)S(1)} collective-permute-done((f32[800,128]{1,0:T(8,128)S(1)}, f32[800,128]{1,0:T(8,128)S(1)}, u32[]{:S(2)}, u32[]{:S(2)}) %collective-permute-start.6) | collective-permute-done | bytes 409632 | tf_op jit(solution)/shard_map/ppermute | solution.py:556
  51.3 3.2 %bottom_kernel.3 = (f32[10,2,72,128]{3,2,1,0:T(8,128)S(1)}, f32[2,80,128]{2,1,0:T(8,128)S(1)}) custom-call(f32[10,2,80,128]{3,2,1,0:T(8,128)S(1)} %collective-permute-done.4.down, f32[10,2,80,128]{3,2,1,0:T(8,128)S(1)} %get-tuple-element.67.bottom, f32[10,4,80,128]{3,2,1,0:T(8,128)S(1)} %unpack.3.inner, f32[8,80,128]{2,1,0:T(8,128)S(1)} %get-tuple-element.72.sea, ...), custom_call_target="tpu_custom_call" | custom-call | flops 200000000 | bytes 200000 | tf_op jit(solution)/shard_map/bottom_kernel/pallas_call | solution.py:563
  54.6 3.2 %top_kernel.3 = (f32[10,2,72,128]{3,2,1,0:T(8,128)S(1)}, f32[2,80,128]{2,1,0:T(8,128)S(1)}) custom-call(f32[10,2,80,128]{3,2,1,0:T(8,128)S(1)} %collective-permute-done.10.up, f32[10,2,80,128]{3,2,1,0:T(8,128)S(1)} %get-tuple-element.66.top, f32[10,4,80,128]{3,2,1,0:T(8,128)S(1)} %unpack.3.inner, f32[8,80,128]{2,1,0:T(8,128)S(1)} %get-tuple-element.72.sea, ...), custom_call_target="tpu_custom_call" | custom-call | flops 200000000 | bytes 200000 | tf_op jit(solution)/shard_map/top_kernel/pallas_call | solution.py:563
  57.9 3.8 %collective-permute-start.12 = (f32[10,2,72,128]{3,2,1,0:T(8,128)S(1)}, f32[10,2,72,128]{3,2,1,0:T(8,128)S(1)}, u32[]{:S(2)}, u32[]{:S(2)}) collective-permute-start(f32[10,2,72,128]{3,2,1,0:T(8,128)S(1)} %get-tuple-element.78.top), channel_id=1, source_target_pairs={{1,0},{3,2},{5,4},{7,6},{8,1},{10,3},{12,5},{14,7},{9,8},{11,10},{... | collective-permute-start | bytes 2211848 | tf_op jit(solution)/shard_map/ppermute | solution.py:583
  61.6 5.2 %inner_kernel.3.inner = f32[10,4,72,128]{3,2,1,0:T(8,128)S(1)} custom-call(f32[10,2,80,128]{3,2,1,0:T(8,128)S(1)} %get-tuple-element.66.top, f32[10,4,80,128]{3,2,1,0:T(8,128)S(1)} %unpack.3.inner, f32[10,2,80,128]{3,2,1,0:T(8,128)S(1)} %get-tuple-element.67.bottom, f32[8,80,128]{2,1,0:T(8,128)S(1)} %get-tuple-element.72.sea, ...), custom_call_target="tpu_custom_call" | custom-call | flops 400000000 | bytes 400000 | tf_op jit(solution)/shard_map/inner_kernel/pallas_call | solution.py:563
  66.8 4.9 %inner_kernel.4 = (f32[10,4,72,128]{3,2,1,0:T(8,128)S(1)}, f32[9,2,72,128]{3,2,1,0:T(8,128)S(1)}, f32[9,2,72,128]{3,2,1,0:T(8,128)S(1)}) custom-call(f32[10,2,72,128]{3,2,1,0:T(8,128)S(1)} %get-tuple-element.78.top, f32[10,4,72,128]{3,2,1,0:T(8,128)S(1)} %inner_kernel.3.inner, f32[10,2,72,128]{3,2,1,0:T(8,128)S(1)} %get-tuple-element.76.bottom, ...), custom_call_target="tpu_custom_call" | custom-call | flops 400000000 | bytes 400000 | tf_op jit(solution)/shard_map/inner_kernel/pallas_call | solution.py:563
  71.7 2.5 %top_kernel.4.top = f32[10,2,72,128]{3,2,1,0:T(8,128)S(1)} custom-call(f32[10,2,72,128]{3,2,1,0:T(8,128)S(1)} %collective-permute-done.9.up, f32[10,2,72,128]{3,2,1,0:T(8,128)S(1)} %get-tuple-element.78.top, f32[10,4,72,128]{3,2,1,0:T(8,128)S(1)} %inner_kernel.3.inner, f32[8,80,128]{2,1,0:T(8,128)S(1)} %get-tuple-element.72.sea, ...), custom_call_target="tpu_custom_call" | custom-call | flops 200000000 | bytes 200000 | tf_op jit(solution)/shard_map/top_kernel/pallas_call | solution.py:563
  74.6 2.6 %bottom_kernel.4.bottom = f32[10,2,72,128]{3,2,1,0:T(8,128)S(1)} custom-call(f32[10,2,72,128]{3,2,1,0:T(8,128)S(1)} %collective-permute-done.12.down, f32[10,2,72,128]{3,2,1,0:T(8,128)S(1)} %get-tuple-element.76.bottom, f32[10,4,72,128]{3,2,1,0:T(8,128)S(1)} %inner_kernel.3.inner, f32[8,80,128]{2,1,0:T(8,128)S(1)} %get-tuple-element.72.sea, ...), custom_call_target="tpu_custom_call" | custom-call | flops 200000000 | bytes 200000 | tf_op jit(solution)/shard_map/bottom_kernel/pallas_call | solution.py:563
  77.6 4.6 %inner_kernel.5 = (f32[10,4,64,128]{3,2,1,0:T(8,128)S(1)}, f32[9,2,72,128]{3,2,1,0:T(8,128)S(1)}, f32[9,2,72,128]{3,2,1,0:T(8,128)S(1)}) custom-call(f32[10,2,72,128]{3,2,1,0:T(8,128)S(1)} %top_kernel.4.top, f32[10,4,72,128]{3,2,1,0:T(8,128)S(1)} %get-tuple-element.84.inner, f32[10,2,72,128]{3,2,1,0:T(8,128)S(1)} %bottom_kernel.4.bottom, ...), custom_call_target="tpu_custom_call" | custom-call | flops 400000000 | bytes 400000 | tf_op jit(solution)/shard_map/inner_kernel/pallas_call | solution.py:563
  83.3 1.5 %collective-permute-start.19 = (f32[10,64,128]{2,1,0:T(8,128)S(1)}, f32[10,64,128]{2,1,0:T(8,128)S(1)}, u32[]{:S(2)}, u32[]{:S(2)}) collective-permute-start(f32[10,64,128]{2,1,0:T(8,128)S(1)} %get-tuple-element.93), channel_id=1, source_target_pairs={{2,0},{4,1},{0,2},{6,3},{7,4},{1,5},{5,6},{3,7},{10,8},{12,9},{8,1... | collective-permute-start | bytes 983048 | tf_op jit(solution)/shard_map/ppermute | solution.py:628
  85.7 3.3 %collective-permute-done.11.down = f32[10,2,72,128]{3,2,1,0:T(8,128)S(1)} collective-permute-done((f32[10,2,72,128]{3,2,1,0:T(8,128)S(1)}, f32[10,2,72,128]{3,2,1,0:T(8,128)S(1)}, u32[]{:S(2)}, u32[]{:S(2)}) %collective-permute-start.11) | collective-permute-done | bytes 737312 | tf_op jit(solution)/shard_map/ppermute | solution.py:583
  89.1 2.1 %collective-permute-start.21 = (f32[10,64,128]{2,1,0:T(8,128)S(1)}, f32[10,64,128]{2,1,0:T(8,128)S(1)}, u32[]{:S(2)}, u32[]{:S(2)}) collective-permute-start(f32[10,64,128]{2,1,0:T(8,128)S(1)} %get-tuple-element.95), channel_id=1, source_target_pairs={{6,0},{0,1},{4,2},{2,3},{3,4},{5,5},{1,6},{7,7},{14,8},{8,9},{12,1... | collective-permute-start | bytes 983048 | tf_op jit(solution)/shard_map/ppermute | solution.py:628
  91.2 2.4 %bottom_kernel.5.refs_0_ = f32[10,2,64,128]{3,2,1,0:T(8,128)S(1)} custom-call(f32[10,2,72,128]{3,2,1,0:T(8,128)S(1)} %collective-permute-done.11.down, f32[10,2,72,128]{3,2,1,0:T(8,128)S(1)} %bottom_kernel.4.bottom, f32[10,4,72,128]{3,2,1,0:T(8,128)S(1)} %get-tuple-element.84.inner, f32[8,80,128]{2,1,0:T(8,128)S(1)} %get-tuple-element.72.sea, ...), custom_call_target="tpu_custom_call" | custom-call | flops 200000000 | bytes 200000 | tf_op jit(solution)/shard_map/bottom_kernel/pallas_call | solution.py:563
  93.7 2.4 %top_kernel.5.refs_1_ = f32[10,2,64,128]{3,2,1,0:T(8,128)S(1)} custom-call(f32[10,2,72,128]{3,2,1,0:T(8,128)S(1)} %collective-permute-done.13.up, f32[10,2,72,128]{3,2,1,0:T(8,128)S(1)} %top_kernel.4.top, f32[10,4,72,128]{3,2,1,0:T(8,128)S(1)} %get-tuple-element.84.inner, f32[8,80,128]{2,1,0:T(8,128)S(1)} %get-tuple-element.72.sea, ...), custom_call_target="tpu_custom_call" | custom-call | flops 200000000 | bytes 200000 | tf_op jit(solution)/shard_map/top_kernel/pallas_call | solution.py:563
  98.3 3.9 %collective-permute-start.16 = (f32[10,64,128]{2,1,0:T(8,128)S(1)}, f32[10,64,128]{2,1,0:T(8,128)S(1)}, u32[]{:S(2)}, u32[]{:S(2)}) collective-permute-start(f32[10,64,128]{2,1,0:T(8,128)S(1)} %get-tuple-element.89), channel_id=1, source_target_pairs={{4,0},{2,1},{6,2},{0,3},{1,4},{7,5},{3,6},{5,7},{12,8},{10,9},{14,... | collective-permute-start | bytes 983048 | tf_op jit(solution)/shard_map/ppermute | solution.py:628
  102.1 1.9 %collective-permute-start.17 = (f32[10,64,128]{2,1,0:T(8,128)S(1)}, f32[10,64,128]{2,1,0:T(8,128)S(1)}, u32[]{:S(2)}, u32[]{:S(2)}) collective-permute-start(f32[10,64,128]{2,1,0:T(8,128)S(1)} %get-tuple-element.90), channel_id=1, source_target_pairs={{6,0},{0,1},{4,2},{2,3},{3,4},{5,5},{1,6},{7,7},{14,8},{8,9},{12,1... | collective-permute-start | bytes 983048 | tf_op jit(solution)/shard_map/ppermute | solution.py:628
  104.6 5.0 %collective-permute-done.15.refs_1_ = f32[10,64,128]{2,1,0:T(8,128)S(1)} collective-permute-done((f32[10,64,128]{2,1,0:T(8,128)S(1)}, f32[10,64,128]{2,1,0:T(8,128)S(1)}, u32[]{:S(2)}, u32[]{:S(2)}) %collective-permute-start.15) | collective-permute-done | bytes 327712 | tf_op jit(solution)/shard_map/ppermute | solution.py:628
  109.7 4.2 %collective-permute-done.16.refs_2_ = f32[10,64,128]{2,1,0:T(8,128)S(1)} collective-permute-done((f32[10,64,128]{2,1,0:T(8,128)S(1)}, f32[10,64,128]{2,1,0:T(8,128)S(1)}, u32[]{:S(2)}, u32[]{:S(2)}) %collective-permute-start.16) | collective-permute-done | bytes 327712 | tf_op jit(solution)/shard_map/ppermute | solution.py:628
  113.9 3.4 %collective-permute-done.17.refs_3_ = f32[10,64,128]{2,1,0:T(8,128)S(1)} collective-permute-done((f32[10,64,128]{2,1,0:T(8,128)S(1)}, f32[10,64,128]{2,1,0:T(8,128)S(1)}, u32[]{:S(2)}, u32[]{:S(2)}) %collective-permute-start.17) | collective-permute-done | bytes 327712 | tf_op jit(solution)/shard_map/ppermute | solution.py:628
  117.2 1.9 %restore.1 = (f32[2304,256]{1,0:T(8,128)}, f32[256,256]{1,0:T(8,128)}, f32[2,2304,128]{2,1,0:T(8,128)S(1)}, f32[2,256,128]{2,1,0:T(8,128)S(1)}) custom-call(s32[1]{0:T(128)} %bitcast.odd, s32[1]{0:T(128)} %bitcast.1.part, f32[10,64,128]{2,1,0:T(8,128)S(1)} %collective-permute-done.14.refs_0_, ...), custom_call_target="tpu_custom_call", output_to_operand_aliasing={{2}: (6, {}), {3}: (7, {})} | custom-call | tf_op jit(solution)/shard_map/restore/pallas_call | solution.py:643
  (48 shorter events, 11.4 us)
Async XLA Ops:
  0.6 18.2 %copy-start = (bf16[1152,1152]{1,0:T(8,128)(2,1)S(1)}, bf16[1152,1152]{1,0:T(8,128)(2,1)}, u32[]{:S(2)}) copy-start(bf16[1152,1152]{1,0:T(8,128)(2,1)} %linear.1) | copy-start | bytes 7962628
  0.7 18.2 %copy-start.2 = (bf16[128,1152]{1,0:T(8,128)(2,1)S(1)}, bf16[128,1152]{1,0:T(8,128)(2,1)}, u32[]{:S(2)}) copy-start(bf16[128,1152]{1,0:T(8,128)(2,1)} %drift.1) | copy-start | bytes 884740
  4.0 18.2 %collective-permute-start = (f32[768,128]{1,0:T(8,128)}, f32[768,128]{1,0:T(8,128)S(1)}, u32[]{:S(2)}, u32[]{:S(2)}) collective-permute-start(f32[768,128]{1,0:T(8,128)} %get-tuple-element.51), channel_id=1, source_target_pairs={{0,0},{1,6},{2,2},{3,4},{4,5},{5,3},{6,7},{7,1},{8,8},{9,14},{10,1... | collective-permute-start | bytes 1179656 | tf_op jit(solution)/shard_map/ppermute | solution.py:517
  5.7 17.9 %collective-permute-start.1 = (f32[768,128]{1,0:T(8,128)}, f32[768,128]{1,0:T(8,128)S(1)}, u32[]{:S(2)}, u32[]{:S(2)}) collective-permute-start(f32[768,128]{1,0:T(8,128)} %get-tuple-element.56), channel_id=1, source_target_pairs={{0,2},{1,4},{2,0},{3,6},{4,7},{5,1},{6,5},{7,3},{8,10},{9,12},{10,... | collective-permute-start | bytes 1179656 | tf_op jit(solution)/shard_map/ppermute | solution.py:517
  8.7 15.5 %collective-permute-start.2 = (f32[768,128]{1,0:T(8,128)}, f32[768,128]{1,0:T(8,128)S(1)}, u32[]{:S(2)}, u32[]{:S(2)}) collective-permute-start(f32[768,128]{1,0:T(8,128)} %get-tuple-element.57), channel_id=1, source_target_pairs={{0,4},{1,2},{2,6},{3,0},{4,1},{5,7},{6,3},{7,5},{8,12},{9,10},{10,... | collective-permute-start | bytes 1179656 | tf_op jit(solution)/shard_map/ppermute | solution.py:517
  9.9 18.2 %collective-permute-start.3 = (f32[768,128]{1,0:T(8,128)}, f32[768,128]{1,0:T(8,128)S(1)}, u32[]{:S(2)}, u32[]{:S(2)}) collective-permute-start(f32[768,128]{1,0:T(8,128)} %get-tuple-element.58), channel_id=1, source_target_pairs={{0,6},{1,0},{2,4},{3,2},{4,3},{5,5},{6,1},{7,7},{8,14},{9,8},{10,1... | collective-permute-start | bytes 1179656 | tf_op jit(solution)/shard_map/ppermute | solution.py:517
  16.8 18.8 %collective-permute-start.5 = (f32[800,128]{1,0:T(8,128)}, f32[800,128]{1,0:T(8,128)S(1)}, u32[]{:S(2)}, u32[]{:S(2)}) collective-permute-start(f32[800,128]{1,0:T(8,128)} %get-tuple-element.68), channel_id=1, source_target_pairs={{0,0},{1,6},{2,2},{3,4},{4,5},{5,3},{6,7},{7,1},{8,8},{9,14},{10,1... | collective-permute-start | bytes 1228808 | tf_op jit(solution)/shard_map/ppermute | solution.py:556
  18.8 1.8 %copy-start.1 = (bf16[1152,1152]{1,0:T(8,128)(2,1)S(1)}, bf16[1152,1152]{1,0:T(8,128)(2,1)}, u32[]{:S(2)}) copy-start(bf16[1152,1152]{1,0:T(8,128)(2,1)} %square.1) | copy-start | bytes 7962628
  20.6 13.5 %copy-start.5 = (f32[800,128]{1,0:T(8,128)S(1)}, f32[800,128]{1,0:T(8,128)}, u32[]{:S(2)}) copy-start(f32[800,128]{1,0:T(8,128)} %get-tuple-element.69) | copy-start | bytes 1228804
  20.6 15.0 %copy-start.4 = (f32[800,128]{1,0:T(8,128)S(1)}, f32[800,128]{1,0:T(8,128)}, u32[]{:S(2)}) copy-start(f32[800,128]{1,0:T(8,128)} %get-tuple-element.70) | copy-start | bytes 1228804
  20.6 15.0 %copy-start.3 = (f32[800,128]{1,0:T(8,128)S(1)}, f32[800,128]{1,0:T(8,128)}, u32[]{:S(2)}) copy-start(f32[800,128]{1,0:T(8,128)} %get-tuple-element.71) | copy-start | bytes 1228804
  28.8 22.5 %collective-permute-start.4 = (f32[10,2,80,128]{3,2,1,0:T(8,128)S(1)}, f32[10,2,80,128]{3,2,1,0:T(8,128)S(1)}, u32[]{:S(2)}, u32[]{:S(2)}) collective-permute-start(f32[10,2,80,128]{3,2,1,0:T(8,128)S(1)} %get-tuple-element.66.top), channel_id=1, source_target_pairs={{1,0},{3,2},{5,4},{7,6},{8,1},{10,3},{12,5},{14,7},{9,8},{11,10},{... | collective-permute-start | bytes 2457608 | tf_op jit(solution)/shard_map/ppermute | solution.py:583
  34.1 20.5 %collective-permute-start.10 = (f32[10,2,80,128]{3,2,1,0:T(8,128)S(1)}, f32[10,2,80,128]{3,2,1,0:T(8,128)S(1)}, u32[]{:S(2)}, u32[]{:S(2)}) collective-permute-start(f32[10,2,80,128]{3,2,1,0:T(8,128)S(1)} %get-tuple-element.67.bottom), channel_id=1, source_target_pairs={{0,1},{2,3},{4,5},{6,7},{1,8},{3,10},{5,12},{7,14},{8,9},{10,11},{... | collective-permute-start | bytes 2457608 | tf_op jit(solution)/shard_map/ppermute | solution.py:584
  34.1 15.8 %collective-permute-start.6 = (f32[800,128]{1,0:T(8,128)S(1)}, f32[800,128]{1,0:T(8,128)S(1)}, u32[]{:S(2)}, u32[]{:S(2)}) collective-permute-start(f32[800,128]{1,0:T(8,128)S(1)} %copy-done.5), channel_id=1, source_target_pairs={{0,2},{1,4},{2,0},{3,6},{4,7},{5,1},{6,5},{7,3},{8,10},{9,12},{10,... | collective-permute-start | bytes 1228808 | tf_op jit(solution)/shard_map/ppermute | solution.py:556
  35.6 15.2 %collective-permute-start.7 = (f32[800,128]{1,0:T(8,128)S(1)}, f32[800,128]{1,0:T(8,128)S(1)}, u32[]{:S(2)}, u32[]{:S(2)}) collective-permute-start(f32[800,128]{1,0:T(8,128)S(1)} %copy-done.4), channel_id=1, source_target_pairs={{0,4},{1,2},{2,6},{3,0},{4,1},{5,7},{6,3},{7,5},{8,12},{9,10},{10,... | collective-permute-start | bytes 1228808 | tf_op jit(solution)/shard_map/ppermute | solution.py:556
  35.6 15.2 %collective-permute-start.8 = (f32[800,128]{1,0:T(8,128)S(1)}, f32[800,128]{1,0:T(8,128)S(1)}, u32[]{:S(2)}, u32[]{:S(2)}) collective-permute-start(f32[800,128]{1,0:T(8,128)S(1)} %copy-done.3), channel_id=1, source_target_pairs={{0,6},{1,0},{2,4},{3,2},{4,3},{5,5},{6,1},{7,7},{8,14},{9,8},{10,1... | collective-permute-start | bytes 1228808 | tf_op jit(solution)/shard_map/ppermute | solution.py:556
  54.6 17.2 %collective-permute-start.9 = (f32[10,2,72,128]{3,2,1,0:T(8,128)S(1)}, f32[10,2,72,128]{3,2,1,0:T(8,128)S(1)}, u32[]{:S(2)}, u32[]{:S(2)}) collective-permute-start(f32[10,2,72,128]{3,2,1,0:T(8,128)S(1)} %get-tuple-element.76.bottom), channel_id=1, source_target_pairs={{0,1},{2,3},{4,5},{6,7},{1,8},{3,10},{5,12},{7,14},{8,9},{10,11},{... | collective-permute-start | bytes 2211848 | tf_op jit(solution)/shard_map/ppermute | solution.py:584
  57.9 16.7 %collective-permute-start.12 = (f32[10,2,72,128]{3,2,1,0:T(8,128)S(1)}, f32[10,2,72,128]{3,2,1,0:T(8,128)S(1)}, u32[]{:S(2)}, u32[]{:S(2)}) collective-permute-start(f32[10,2,72,128]{3,2,1,0:T(8,128)S(1)} %get-tuple-element.78.top), channel_id=1, source_target_pairs={{1,0},{3,2},{5,4},{7,6},{8,1},{10,3},{12,5},{14,7},{9,8},{11,10},{... | collective-permute-start | bytes 2211848 | tf_op jit(solution)/shard_map/ppermute | solution.py:583
  74.2 14.9 %collective-permute-start.11 = (f32[10,2,72,128]{3,2,1,0:T(8,128)S(1)}, f32[10,2,72,128]{3,2,1,0:T(8,128)S(1)}, u32[]{:S(2)}, u32[]{:S(2)}) collective-permute-start(f32[10,2,72,128]{3,2,1,0:T(8,128)S(1)} %top_kernel.4.top), channel_id=1, source_target_pairs={{1,0},{3,2},{5,4},{7,6},{8,1},{10,3},{12,5},{14,7},{9,8},{11,10},{... | collective-permute-start | bytes 2211848 | tf_op jit(solution)/shard_map/ppermute | solution.py:583
  77.2 16.5 %collective-permute-start.13 = (f32[10,2,72,128]{3,2,1,0:T(8,128)S(1)}, f32[10,2,72,128]{3,2,1,0:T(8,128)S(1)}, u32[]{:S(2)}, u32[]{:S(2)}) collective-permute-start(f32[10,2,72,128]{3,2,1,0:T(8,128)S(1)} %bottom_kernel.4.bottom), channel_id=1, source_target_pairs={{0,1},{2,3},{4,5},{6,7},{1,8},{3,10},{5,12},{7,14},{8,9},{10,11},{... | collective-permute-start | bytes 2211848 | tf_op jit(solution)/shard_map/ppermute | solution.py:584
  82.6 14.5 %collective-permute-start.18 = (f32[10,64,128]{2,1,0:T(8,128)S(1)}, f32[10,64,128]{2,1,0:T(8,128)S(1)}, u32[]{:S(2)}, u32[]{:S(2)}) collective-permute-start(f32[10,64,128]{2,1,0:T(8,128)S(1)} %get-tuple-element.92), channel_id=1, source_target_pairs={{0,0},{6,1},{2,2},{4,3},{5,4},{3,5},{7,6},{1,7},{8,8},{14,9},{10,1... | collective-permute-start | bytes 983048 | tf_op jit(solution)/shard_map/ppermute | solution.py:628
  83.3 15.0 %collective-permute-start.19 = (f32[10,64,128]{2,1,0:T(8,128)S(1)}, f32[10,64,128]{2,1,0:T(8,128)S(1)}, u32[]{:S(2)}, u32[]{:S(2)}) collective-permute-start(f32[10,64,128]{2,1,0:T(8,128)S(1)} %get-tuple-element.93), channel_id=1, source_target_pairs={{2,0},{4,1},{0,2},{6,3},{7,4},{1,5},{5,6},{3,7},{10,8},{12,9},{8,1... | collective-permute-start | bytes 983048 | tf_op jit(solution)/shard_map/ppermute | solution.py:628
  84.8 17.4 %collective-permute-start.20 = (f32[10,64,128]{2,1,0:T(8,128)S(1)}, f32[10,64,128]{2,1,0:T(8,128)S(1)}, u32[]{:S(2)}, u32[]{:S(2)}) collective-permute-start(f32[10,64,128]{2,1,0:T(8,128)S(1)} %get-tuple-element.94), channel_id=1, source_target_pairs={{4,0},{2,1},{6,2},{0,3},{1,4},{7,5},{3,6},{5,7},{12,8},{10,9},{14,... | collective-permute-start | bytes 983048 | tf_op jit(solution)/shard_map/ppermute | solution.py:628
  89.1 15.0 %collective-permute-start.21 = (f32[10,64,128]{2,1,0:T(8,128)S(1)}, f32[10,64,128]{2,1,0:T(8,128)S(1)}, u32[]{:S(2)}, u32[]{:S(2)}) collective-permute-start(f32[10,64,128]{2,1,0:T(8,128)S(1)} %get-tuple-element.95), channel_id=1, source_target_pairs={{6,0},{0,1},{4,2},{2,3},{3,4},{5,5},{1,6},{7,7},{14,8},{8,9},{12,1... | collective-permute-start | bytes 983048 | tf_op jit(solution)/shard_map/ppermute | solution.py:628
  96.4 8.2 %collective-permute-start.14 = (f32[10,64,128]{2,1,0:T(8,128)S(1)}, f32[10,64,128]{2,1,0:T(8,128)S(1)}, u32[]{:S(2)}, u32[]{:S(2)}) collective-permute-start(f32[10,64,128]{2,1,0:T(8,128)S(1)} %get-tuple-element.87), channel_id=1, source_target_pairs={{0,0},{6,1},{2,2},{4,3},{5,4},{3,5},{7,6},{1,7},{8,8},{14,9},{10,1... | collective-permute-start | bytes 983048 | tf_op jit(solution)/shard_map/ppermute | solution.py:628
  97.1 12.5 %collective-permute-start.15 = (f32[10,64,128]{2,1,0:T(8,128)S(1)}, f32[10,64,128]{2,1,0:T(8,128)S(1)}, u32[]{:S(2)}, u32[]{:S(2)}) collective-permute-start(f32[10,64,128]{2,1,0:T(8,128)S(1)} %get-tuple-element.88), channel_id=1, source_target_pairs={{2,0},{4,1},{0,2},{6,3},{7,4},{1,5},{5,6},{3,7},{10,8},{12,9},{8,1... | collective-permute-start | bytes 983048 | tf_op jit(solution)/shard_map/ppermute | solution.py:628
  98.3 15.6 %collective-permute-start.16 = (f32[10,64,128]{2,1,0:T(8,128)S(1)}, f32[10,64,128]{2,1,0:T(8,128)S(1)}, u32[]{:S(2)}, u32[]{:S(2)}) collective-permute-start(f32[10,64,128]{2,1,0:T(8,128)S(1)} %get-tuple-element.89), channel_id=1, source_target_pairs={{4,0},{2,1},{6,2},{0,3},{1,4},{7,5},{3,6},{5,7},{12,8},{10,9},{14,... | collective-permute-start | bytes 983048 | tf_op jit(solution)/shard_map/ppermute | solution.py:628
  102.1 15.1 %collective-permute-start.17 = (f32[10,64,128]{2,1,0:T(8,128)S(1)}, f32[10,64,128]{2,1,0:T(8,128)S(1)}, u32[]{:S(2)}, u32[]{:S(2)}) collective-permute-start(f32[10,64,128]{2,1,0:T(8,128)S(1)} %get-tuple-element.90), channel_id=1, source_target_pairs={{6,0},{0,1},{4,2},{2,3},{3,4},{5,5},{1,6},{7,7},{14,8},{8,9},{12,1... | collective-permute-start | bytes 983048 | tf_op jit(solution)/shard_map/ppermute | solution.py:628

commit v12 on v11

--- a/solution.py
+++ b/solution.py
@@ -363,9 +363,8 @@
         [moved_twice[j, :, own].reshape(count * N, LANES) for j in range(tiles)], axis=1
     )
     squares = energy * energy
-    interaction = jnp.dot(
-        energy.astype(BF16), weights[:NB], preferred_element_type=F32
-    ) + jnp.dot(squares.astype(BF16), weights[NB:], preferred_element_type=F32)
+    both = jnp.concatenate([energy.astype(BF16), squares.astype(BF16)], axis=1)
+    interaction = jnp.dot(both, weights[...], preferred_element_type=F32)
     total = jnp.sum(squares, axis=1, keepdims=True)
     sea_here = jnp.concatenate([sea_row(place)[keep] for place in own_sea], axis=0)
     scale = (DT_SOURCE * sea_here[:, 0:1]) / (1.0 + total / NB)

time: 120 us -> 120 us (level)
  transfers between devices with their start and end apart: 22 -> 22, of which waited for: 9 -> 9; matrix products, arithmetic and copies ran while one was open for 0% -> 0% of each run, Pallas kernels for 32% -> 31%
where the time goes in v12:
time: 120 us; the launch traced here: 119 us
  Pallas kernels  42.6 us (36%)
  starting transfers between devices  38.2 us (32%)
  waiting for transfers between devices  34.9 us (29%)
  local copies, waits for them, and re-layouts  1.92 us (2%)
    pallas_call x9, Pallas kernels, step_call(): pl.pallas_call(functools.partial(body, z, first, cut, sea_at), out_shape=...  30.2 us
    ppermute x8, starting transfers between devices, per_device(): lax.ppermute(packed[i], axes, [(t, s) for s, t in forward[i % B]])  13.4 us
    ppermute x4, waiting for transfers between devices, per_device(): got = [lax.ppermute(blocks[k], axes, forward[k]) for k in range(B)]  13.3 us
    ppermute x8, waiting for transfers between devices, per_device(): lax.ppermute(packed[i], axes, [(t, s) for s, t in forward[i % B]])  12.7 us
    ppermute x4, starting transfers between devices, per_device(): got = [lax.ppermute(packed[k], axes, forward[k]) for k in range(B)]  9.52 us
    ppermute x3, starting transfers between devices, per_device(): down = lax.ppermute(top, axes, to_prev_row)  9.41 us
    pallas_call x2, Pallas kernels, pack(): pl.pallas_call(functools.partial(pack_kernel, z, rows), out_shape=[jax.Sh...  6.6 us
    ppermute x4, waiting for transfers between devices, per_device(): got = [lax.ppermute(packed[k], axes, forward[k]) for k in range(B)]  5.92 us
  transfers between devices with their start and end apart: 22, of which 9 were waited for; matrix products, arithmetic and copies ran while one was open for 0% of the time, Pallas kernels for 31%

profile of v12, /device:TPU:0, one launch (start us, length us, event | category | flops | bytes accessed | tf_op | source)
XLA Modules:
  0.0 119.1 jit_solution(15143090187565685894)
XLA Ops:
  0.7 3.4 %pack.2 = (f32[768,128]{1,0:T(8,128)}, f32[768,128]{1,0:T(8,128)}, f32[768,128]{1,0:T(8,128)}, f32[768,128]{1,0:T(8,128)}) custom-call(s32[1]{0:T(128)} %bitcast.odd, s32[1]{0:T(128)} %bitcast.1.part, f32[2304,256]{1,0:T(8,128)} %bitcast.6, f32[256,256]{1,0:T(8,128)} %bitcast.8, s32[8,256]{1,0:T(8,128)} %mask_in.3), custom_call_target="tpu_custom_call" | custom-call | tf_op jit(solution)/shard_map/pack/pallas_call | solution.py:500
  4.0 1.7 %collective-permute-start = (f32[768,128]{1,0:T(8,128)}, f32[768,128]{1,0:T(8,128)S(1)}, u32[]{:S(2)}, u32[]{:S(2)}) collective-permute-start(f32[768,128]{1,0:T(8,128)} %get-tuple-element.51), channel_id=1, source_target_pairs={{0,0},{1,6},{2,2},{3,4},{4,5},{5,3},{6,7},{7,1},{8,8},{9,14},{10,1... | collective-permute-start | bytes 1179656 | tf_op jit(solution)/shard_map/ppermute | solution.py:516
  5.7 3.0 %collective-permute-start.1 = (f32[768,128]{1,0:T(8,128)}, f32[768,128]{1,0:T(8,128)S(1)}, u32[]{:S(2)}, u32[]{:S(2)}) collective-permute-start(f32[768,128]{1,0:T(8,128)} %get-tuple-element.56), channel_id=1, source_target_pairs={{0,2},{1,4},{2,0},{3,6},{4,7},{5,1},{6,5},{7,3},{8,10},{9,12},{10,... | collective-permute-start | bytes 1179656 | tf_op jit(solution)/shard_map/ppermute | solution.py:516
  9.9 3.6 %collective-permute-start.3 = (f32[768,128]{1,0:T(8,128)}, f32[768,128]{1,0:T(8,128)S(1)}, u32[]{:S(2)}, u32[]{:S(2)}) collective-permute-start(f32[768,128]{1,0:T(8,128)} %get-tuple-element.58), channel_id=1, source_target_pairs={{0,6},{1,0},{2,4},{3,2},{4,3},{5,5},{6,1},{7,7},{8,14},{9,8},{10,1... | collective-permute-start | bytes 1179656 | tf_op jit(solution)/shard_map/ppermute | solution.py:516
  13.6 3.2 %pack.3 = (f32[800,128]{1,0:T(8,128)}, f32[800,128]{1,0:T(8,128)}, f32[800,128]{1,0:T(8,128)}, f32[800,128]{1,0:T(8,128)}) custom-call(s32[1]{0:T(128)} %bitcast.odd, s32[1]{0:T(128)} %bitcast.1.part, f32[2304,256]{1,0:T(8,128)} %bitcast.7, f32[256,256]{1,0:T(8,128)} %bitcast.9, s32[8,256]{1,0:T(8,128)} %mask_in.3), custom_call_target="tpu_custom_call" | custom-call | tf_op jit(solution)/shard_map/pack/pallas_call | solution.py:500
  16.8 1.7 %collective-permute-start.5 = (f32[800,128]{1,0:T(8,128)}, f32[800,128]{1,0:T(8,128)S(1)}, u32[]{:S(2)}, u32[]{:S(2)}) collective-permute-start(f32[800,128]{1,0:T(8,128)} %get-tuple-element.68), channel_id=1, source_target_pairs={{0,0},{1,6},{2,2},{3,4},{4,5},{5,3},{6,7},{7,1},{8,8},{9,14},{10,1... | collective-permute-start | bytes 1228808 | tf_op jit(solution)/shard_map/ppermute | solution.py:555
  18.8 1.7 %copy-done.1 = bf16[1152,1152]{1,0:T(8,128)(2,1)S(1)} copy-done((bf16[1152,1152]{1,0:T(8,128)(2,1)S(1)}, bf16[1152,1152]{1,0:T(8,128)(2,1)}, u32[]{:S(2)}) %copy-start.1) | copy-done | bytes 2654232
  20.6 1.5 %weights.1 = (bf16[2304,1152]{1,0:T(8,128)(2,1)S(1)}, bf16[1152,128]{1,0:T(8,128)(2,1)S(1)}) custom-call(bf16[1152,1152]{1,0:T(8,128)(2,1)S(1)} %copy-done, bf16[1152,1152]{1,0:T(8,128)(2,1)S(1)} %copy-done.1, bf16[128,1152]{1,0:T(8,128)(2,1)S(1)} %copy-done.2), custom_call_target="tpu_custom_call" | custom-call | flops 2000000000 | bytes 10616832 | tf_op jit(solution)/shard_map/weights/pallas_call | solution.py:520
  24.2 3.9 %collective-permute-done.3.refs_3_ = f32[768,128]{1,0:T(8,128)S(1)} collective-permute-done((f32[768,128]{1,0:T(8,128)}, f32[768,128]{1,0:T(8,128)S(1)}, u32[]{:S(2)}, u32[]{:S(2)}) %collective-permute-start.3) | collective-permute-done | bytes 393248 | tf_op jit(solution)/shard_map/ppermute | solution.py:516
  28.8 5.3 %collective-permute-start.4 = (f32[10,2,80,128]{3,2,1,0:T(8,128)S(1)}, f32[10,2,80,128]{3,2,1,0:T(8,128)S(1)}, u32[]{:S(2)}, u32[]{:S(2)}) collective-permute-start(f32[10,2,80,128]{3,2,1,0:T(8,128)S(1)} %get-tuple-element.66.top), channel_id=1, source_target_pairs={{1,0},{3,2},{5,4},{7,6},{8,1},{10,3},{12,5},{14,7},{9,8},{11,10},{... | collective-permute-start | bytes 2457608 | tf_op jit(solution)/shard_map/ppermute | solution.py:582
  34.1 1.5 %collective-permute-start.6 = (f32[800,128]{1,0:T(8,128)S(1)}, f32[800,128]{1,0:T(8,128)S(1)}, u32[]{:S(2)}, u32[]{:S(2)}) collective-permute-start(f32[800,128]{1,0:T(8,128)S(1)} %copy-done.5), channel_id=1, source_target_pairs={{0,2},{1,4},{2,0},{3,6},{4,7},{5,1},{6,5},{7,3},{8,10},{9,12},{10,... | collective-permute-start | bytes 1228808 | tf_op jit(solution)/shard_map/ppermute | solution.py:555
  35.6 1.9 %collective-permute-start.8 = (f32[800,128]{1,0:T(8,128)S(1)}, f32[800,128]{1,0:T(8,128)S(1)}, u32[]{:S(2)}, u32[]{:S(2)}) collective-permute-start(f32[800,128]{1,0:T(8,128)S(1)} %copy-done.3), channel_id=1, source_target_pairs={{0,6},{1,0},{2,4},{3,2},{4,3},{5,5},{6,1},{7,7},{8,14},{9,8},{10,1... | collective-permute-start | bytes 1228808 | tf_op jit(solution)/shard_map/ppermute | solution.py:555
  37.5 12.3 %collective-permute-done.6.refs_1_ = f32[800,128]{1,0:T(8,128)S(1)} collective-permute-done((f32[800,128]{1,0:T(8,128)S(1)}, f32[800,128]{1,0:T(8,128)S(1)}, u32[]{:S(2)}, u32[]{:S(2)}) %collective-permute-start.6) | collective-permute-done | bytes 409632 | tf_op jit(solution)/shard_map/ppermute | solution.py:555
  51.3 3.1 %bottom_kernel.3 = (f32[10,2,72,128]{3,2,1,0:T(8,128)S(1)}, f32[2,80,128]{2,1,0:T(8,128)S(1)}) custom-call(f32[10,2,80,128]{3,2,1,0:T(8,128)S(1)} %collective-permute-done.4.down, f32[10,2,80,128]{3,2,1,0:T(8,128)S(1)} %get-tuple-element.67.bottom, f32[10,4,80,128]{3,2,1,0:T(8,128)S(1)} %unpack.3.inner, f32[8,80,128]{2,1,0:T(8,128)S(1)} %get-tuple-element.72.sea, ...), custom_call_target="tpu_custom_call" | custom-call | flops 200000000 | bytes 200000 | tf_op jit(solution)/shard_map/bottom_kernel/pallas_call | solution.py:562
  54.5 3.1 %top_kernel.3 = (f32[10,2,72,128]{3,2,1,0:T(8,128)S(1)}, f32[2,80,128]{2,1,0:T(8,128)S(1)}) custom-call(f32[10,2,80,128]{3,2,1,0:T(8,128)S(1)} %collective-permute-done.10.up, f32[10,2,80,128]{3,2,1,0:T(8,128)S(1)} %get-tuple-element.66.top, f32[10,4,80,128]{3,2,1,0:T(8,128)S(1)} %unpack.3.inner, f32[8,80,128]{2,1,0:T(8,128)S(1)} %get-tuple-element.72.sea, ...), custom_call_target="tpu_custom_call" | custom-call | flops 200000000 | bytes 200000 | tf_op jit(solution)/shard_map/top_kernel/pallas_call | solution.py:562
  57.7 3.8 %collective-permute-start.12 = (f32[10,2,72,128]{3,2,1,0:T(8,128)S(1)}, f32[10,2,72,128]{3,2,1,0:T(8,128)S(1)}, u32[]{:S(2)}, u32[]{:S(2)}) collective-permute-start(f32[10,2,72,128]{3,2,1,0:T(8,128)S(1)} %get-tuple-element.78.top), channel_id=1, source_target_pairs={{1,0},{3,2},{5,4},{7,6},{8,1},{10,3},{12,5},{14,7},{9,8},{11,10},{... | collective-permute-start | bytes 2211848 | tf_op jit(solution)/shard_map/ppermute | solution.py:582
  61.4 5.1 %inner_kernel.3.inner = f32[10,4,72,128]{3,2,1,0:T(8,128)S(1)} custom-call(f32[10,2,80,128]{3,2,1,0:T(8,128)S(1)} %get-tuple-element.66.top, f32[10,4,80,128]{3,2,1,0:T(8,128)S(1)} %unpack.3.inner, f32[10,2,80,128]{3,2,1,0:T(8,128)S(1)} %get-tuple-element.67.bottom, f32[8,80,128]{2,1,0:T(8,128)S(1)} %get-tuple-element.72.sea, ...), custom_call_target="tpu_custom_call" | custom-call | flops 400000000 | bytes 400000 | tf_op jit(solution)/shard_map/inner_kernel/pallas_call | solution.py:562
  66.6 4.8 %inner_kernel.4 = (f32[10,4,72,128]{3,2,1,0:T(8,128)S(1)}, f32[9,2,72,128]{3,2,1,0:T(8,128)S(1)}, f32[9,2,72,128]{3,2,1,0:T(8,128)S(1)}) custom-call(f32[10,2,72,128]{3,2,1,0:T(8,128)S(1)} %get-tuple-element.78.top, f32[10,4,72,128]{3,2,1,0:T(8,128)S(1)} %inner_kernel.3.inner, f32[10,2,72,128]{3,2,1,0:T(8,128)S(1)} %get-tuple-element.76.bottom, ...), custom_call_target="tpu_custom_call" | custom-call | flops 400000000 | bytes 400000 | tf_op jit(solution)/shard_map/inner_kernel/pallas_call | solution.py:562
  71.4 2.4 %top_kernel.4.top = f32[10,2,72,128]{3,2,1,0:T(8,128)S(1)} custom-call(f32[10,2,72,128]{3,2,1,0:T(8,128)S(1)} %collective-permute-done.9.up, f32[10,2,72,128]{3,2,1,0:T(8,128)S(1)} %get-tuple-element.78.top, f32[10,4,72,128]{3,2,1,0:T(8,128)S(1)} %inner_kernel.3.inner, f32[8,80,128]{2,1,0:T(8,128)S(1)} %get-tuple-element.72.sea, ...), custom_call_target="tpu_custom_call" | custom-call | flops 200000000 | bytes 200000 | tf_op jit(solution)/shard_map/top_kernel/pallas_call | solution.py:562
  74.2 2.5 %bottom_kernel.4.bottom = f32[10,2,72,128]{3,2,1,0:T(8,128)S(1)} custom-call(f32[10,2,72,128]{3,2,1,0:T(8,128)S(1)} %collective-permute-done.12.down, f32[10,2,72,128]{3,2,1,0:T(8,128)S(1)} %get-tuple-element.76.bottom, f32[10,4,72,128]{3,2,1,0:T(8,128)S(1)} %inner_kernel.3.inner, f32[8,80,128]{2,1,0:T(8,128)S(1)} %get-tuple-element.72.sea, ...), custom_call_target="tpu_custom_call" | custom-call | flops 200000000 | bytes 200000 | tf_op jit(solution)/shard_map/bottom_kernel/pallas_call | solution.py:562
  77.4 4.5 %inner_kernel.5 = (f32[10,4,64,128]{3,2,1,0:T(8,128)S(1)}, f32[9,2,72,128]{3,2,1,0:T(8,128)S(1)}, f32[9,2,72,128]{3,2,1,0:T(8,128)S(1)}) custom-call(f32[10,2,72,128]{3,2,1,0:T(8,128)S(1)} %top_kernel.4.top, f32[10,4,72,128]{3,2,1,0:T(8,128)S(1)} %get-tuple-element.84.inner, f32[10,2,72,128]{3,2,1,0:T(8,128)S(1)} %bottom_kernel.4.bottom, ...), custom_call_target="tpu_custom_call" | custom-call | flops 400000000 | bytes 400000 | tf_op jit(solution)/shard_map/inner_kernel/pallas_call | solution.py:562
  83.0 1.5 %collective-permute-start.19 = (f32[10,64,128]{2,1,0:T(8,128)S(1)}, f32[10,64,128]{2,1,0:T(8,128)S(1)}, u32[]{:S(2)}, u32[]{:S(2)}) collective-permute-start(f32[10,64,128]{2,1,0:T(8,128)S(1)} %get-tuple-element.93), channel_id=1, source_target_pairs={{2,0},{4,1},{0,2},{6,3},{7,4},{1,5},{5,6},{3,7},{10,8},{12,9},{8,1... | collective-permute-start | bytes 983048 | tf_op jit(solution)/shard_map/ppermute | solution.py:627
  85.4 3.0 %collective-permute-done.11.down = f32[10,2,72,128]{3,2,1,0:T(8,128)S(1)} collective-permute-done((f32[10,2,72,128]{3,2,1,0:T(8,128)S(1)}, f32[10,2,72,128]{3,2,1,0:T(8,128)S(1)}, u32[]{:S(2)}, u32[]{:S(2)}) %collective-permute-start.11) | collective-permute-done | bytes 737312 | tf_op jit(solution)/shard_map/ppermute | solution.py:582
  88.5 2.1 %collective-permute-start.21 = (f32[10,64,128]{2,1,0:T(8,128)S(1)}, f32[10,64,128]{2,1,0:T(8,128)S(1)}, u32[]{:S(2)}, u32[]{:S(2)}) collective-permute-start(f32[10,64,128]{2,1,0:T(8,128)S(1)} %get-tuple-element.95), channel_id=1, source_target_pairs={{6,0},{0,1},{4,2},{2,3},{3,4},{5,5},{1,6},{7,7},{14,8},{8,9},{12,1... | collective-permute-start | bytes 983048 | tf_op jit(solution)/shard_map/ppermute | solution.py:627
  90.6 2.4 %bottom_kernel.5.refs_0_ = f32[10,2,64,128]{3,2,1,0:T(8,128)S(1)} custom-call(f32[10,2,72,128]{3,2,1,0:T(8,128)S(1)} %collective-permute-done.11.down, f32[10,2,72,128]{3,2,1,0:T(8,128)S(1)} %bottom_kernel.4.bottom, f32[10,4,72,128]{3,2,1,0:T(8,128)S(1)} %get-tuple-element.84.inner, f32[8,80,128]{2,1,0:T(8,128)S(1)} %get-tuple-element.72.sea, ...), custom_call_target="tpu_custom_call" | custom-call | flops 200000000 | bytes 200000 | tf_op jit(solution)/shard_map/bottom_kernel/pallas_call | solution.py:562
  93.0 2.3 %top_kernel.5.refs_1_ = f32[10,2,64,128]{3,2,1,0:T(8,128)S(1)} custom-call(f32[10,2,72,128]{3,2,1,0:T(8,128)S(1)} %collective-permute-done.13.up, f32[10,2,72,128]{3,2,1,0:T(8,128)S(1)} %top_kernel.4.top, f32[10,4,72,128]{3,2,1,0:T(8,128)S(1)} %get-tuple-element.84.inner, f32[8,80,128]{2,1,0:T(8,128)S(1)} %get-tuple-element.72.sea, ...), custom_call_target="tpu_custom_call" | custom-call | flops 200000000 | bytes 200000 | tf_op jit(solution)/shard_map/top_kernel/pallas_call | solution.py:562
  97.5 4.4 %collective-permute-start.16 = (f32[10,64,128]{2,1,0:T(8,128)S(1)}, f32[10,64,128]{2,1,0:T(8,128)S(1)}, u32[]{:S(2)}, u32[]{:S(2)}) collective-permute-start(f32[10,64,128]{2,1,0:T(8,128)S(1)} %get-tuple-element.89), channel_id=1, source_target_pairs={{4,0},{2,1},{6,2},{0,3},{1,4},{7,5},{3,6},{5,7},{12,8},{10,9},{14,... | collective-permute-start | bytes 983048 | tf_op jit(solution)/shard_map/ppermute | solution.py:627
  101.9 1.9 %collective-permute-start.17 = (f32[10,64,128]{2,1,0:T(8,128)S(1)}, f32[10,64,128]{2,1,0:T(8,128)S(1)}, u32[]{:S(2)}, u32[]{:S(2)}) collective-permute-start(f32[10,64,128]{2,1,0:T(8,128)S(1)} %get-tuple-element.90), channel_id=1, source_target_pairs={{6,0},{0,1},{4,2},{2,3},{3,4},{5,5},{1,6},{7,7},{14,8},{8,9},{12,1... | collective-permute-start | bytes 983048 | tf_op jit(solution)/shard_map/ppermute | solution.py:627
  104.4 5.0 %collective-permute-done.15.refs_1_ = f32[10,64,128]{2,1,0:T(8,128)S(1)} collective-permute-done((f32[10,64,128]{2,1,0:T(8,128)S(1)}, f32[10,64,128]{2,1,0:T(8,128)S(1)}, u32[]{:S(2)}, u32[]{:S(2)}) %collective-permute-start.15) | collective-permute-done | bytes 327712 | tf_op jit(solution)/shard_map/ppermute | solution.py:627
  109.4 4.0 %collective-permute-done.16.refs_2_ = f32[10,64,128]{2,1,0:T(8,128)S(1)} collective-permute-done((f32[10,64,128]{2,1,0:T(8,128)S(1)}, f32[10,64,128]{2,1,0:T(8,128)S(1)}, u32[]{:S(2)}, u32[]{:S(2)}) %collective-permute-start.16) | collective-permute-done | bytes 327712 | tf_op jit(solution)/shard_map/ppermute | solution.py:627
  113.4 3.7 %collective-permute-done.17.refs_3_ = f32[10,64,128]{2,1,0:T(8,128)S(1)} collective-permute-done((f32[10,64,128]{2,1,0:T(8,128)S(1)}, f32[10,64,128]{2,1,0:T(8,128)S(1)}, u32[]{:S(2)}, u32[]{:S(2)}) %collective-permute-start.17) | collective-permute-done | bytes 327712 | tf_op jit(solution)/shard_map/ppermute | solution.py:627
  117.0 1.9 %restore.1 = (f32[2304,256]{1,0:T(8,128)}, f32[256,256]{1,0:T(8,128)}, f32[2,2304,128]{2,1,0:T(8,128)S(1)}, f32[2,256,128]{2,1,0:T(8,128)S(1)}) custom-call(s32[1]{0:T(128)} %bitcast.odd, s32[1]{0:T(128)} %bitcast.1.part, f32[10,64,128]{2,1,0:T(8,128)S(1)} %collective-permute-done.14.refs_0_, ...), custom_call_target="tpu_custom_call", output_to_operand_aliasing={{2}: (6, {}), {3}: (7, {})} | custom-call | tf_op jit(solution)/shard_map/restore/pallas_call | solution.py:642
  (48 shorter events, 11.7 us)
Async XLA Ops:
  0.6 18.2 %copy-start = (bf16[1152,1152]{1,0:T(8,128)(2,1)S(1)}, bf16[1152,1152]{1,0:T(8,128)(2,1)}, u32[]{:S(2)}) copy-start(bf16[1152,1152]{1,0:T(8,128)(2,1)} %linear.1) | copy-start | bytes 7962628
  0.7 18.2 %copy-start.2 = (bf16[128,1152]{1,0:T(8,128)(2,1)S(1)}, bf16[128,1152]{1,0:T(8,128)(2,1)}, u32[]{:S(2)}) copy-start(bf16[128,1152]{1,0:T(8,128)(2,1)} %drift.1) | copy-start | bytes 884740
  4.0 18.2 %collective-permute-start = (f32[768,128]{1,0:T(8,128)}, f32[768,128]{1,0:T(8,128)S(1)}, u32[]{:S(2)}, u32[]{:S(2)}) collective-permute-start(f32[768,128]{1,0:T(8,128)} %get-tuple-element.51), channel_id=1, source_target_pairs={{0,0},{1,6},{2,2},{3,4},{4,5},{5,3},{6,7},{7,1},{8,8},{9,14},{10,1... | collective-permute-start | bytes 1179656 | tf_op jit(solution)/shard_map/ppermute | solution.py:516
  5.7 17.9 %collective-permute-start.1 = (f32[768,128]{1,0:T(8,128)}, f32[768,128]{1,0:T(8,128)S(1)}, u32[]{:S(2)}, u32[]{:S(2)}) collective-permute-start(f32[768,128]{1,0:T(8,128)} %get-tuple-element.56), channel_id=1, source_target_pairs={{0,2},{1,4},{2,0},{3,6},{4,7},{5,1},{6,5},{7,3},{8,10},{9,12},{10,... | collective-permute-start | bytes 1179656 | tf_op jit(solution)/shard_map/ppermute | solution.py:516
  8.7 15.5 %collective-permute-start.2 = (f32[768,128]{1,0:T(8,128)}, f32[768,128]{1,0:T(8,128)S(1)}, u32[]{:S(2)}, u32[]{:S(2)}) collective-permute-start(f32[768,128]{1,0:T(8,128)} %get-tuple-element.57), channel_id=1, source_target_pairs={{0,4},{1,2},{2,6},{3,0},{4,1},{5,7},{6,3},{7,5},{8,12},{9,10},{10,... | collective-permute-start | bytes 1179656 | tf_op jit(solution)/shard_map/ppermute | solution.py:516
  9.9 18.2 %collective-permute-start.3 = (f32[768,128]{1,0:T(8,128)}, f32[768,128]{1,0:T(8,128)S(1)}, u32[]{:S(2)}, u32[]{:S(2)}) collective-permute-start(f32[768,128]{1,0:T(8,128)} %get-tuple-element.58), channel_id=1, source_target_pairs={{0,6},{1,0},{2,4},{3,2},{4,3},{5,5},{6,1},{7,7},{8,14},{9,8},{10,1... | collective-permute-start | bytes 1179656 | tf_op jit(solution)/shard_map/ppermute | solution.py:516
  16.8 18.8 %collective-permute-start.5 = (f32[800,128]{1,0:T(8,128)}, f32[800,128]{1,0:T(8,128)S(1)}, u32[]{:S(2)}, u32[]{:S(2)}) collective-permute-start(f32[800,128]{1,0:T(8,128)} %get-tuple-element.68), channel_id=1, source_target_pairs={{0,0},{1,6},{2,2},{3,4},{4,5},{5,3},{6,7},{7,1},{8,8},{9,14},{10,1... | collective-permute-start | bytes 1228808 | tf_op jit(solution)/shard_map/ppermute | solution.py:555
  18.8 1.8 %copy-start.1 = (bf16[1152,1152]{1,0:T(8,128)(2,1)S(1)}, bf16[1152,1152]{1,0:T(8,128)(2,1)}, u32[]{:S(2)}) copy-start(bf16[1152,1152]{1,0:T(8,128)(2,1)} %square.1) | copy-start | bytes 7962628
  20.6 13.5 %copy-start.5 = (f32[800,128]{1,0:T(8,128)S(1)}, f32[800,128]{1,0:T(8,128)}, u32[]{:S(2)}) copy-start(f32[800,128]{1,0:T(8,128)} %get-tuple-element.69) | copy-start | bytes 1228804
  20.6 15.0 %copy-start.4 = (f32[800,128]{1,0:T(8,128)S(1)}, f32[800,128]{1,0:T(8,128)}, u32[]{:S(2)}) copy-start(f32[800,128]{1,0:T(8,128)} %get-tuple-element.70) | copy-start | bytes 1228804
  20.6 15.0 %copy-start.3 = (f32[800,128]{1,0:T(8,128)S(1)}, f32[800,128]{1,0:T(8,128)}, u32[]{:S(2)}) copy-start(f32[800,128]{1,0:T(8,128)} %get-tuple-element.71) | copy-start | bytes 1228804
  28.8 22.5 %collective-permute-start.4 = (f32[10,2,80,128]{3,2,1,0:T(8,128)S(1)}, f32[10,2,80,128]{3,2,1,0:T(8,128)S(1)}, u32[]{:S(2)}, u32[]{:S(2)}) collective-permute-start(f32[10,2,80,128]{3,2,1,0:T(8,128)S(1)} %get-tuple-element.66.top), channel_id=1, source_target_pairs={{1,0},{3,2},{5,4},{7,6},{8,1},{10,3},{12,5},{14,7},{9,8},{11,10},{... | collective-permute-start | bytes 2457608 | tf_op jit(solution)/shard_map/ppermute | solution.py:582
  34.1 20.5 %collective-permute-start.10 = (f32[10,2,80,128]{3,2,1,0:T(8,128)S(1)}, f32[10,2,80,128]{3,2,1,0:T(8,128)S(1)}, u32[]{:S(2)}, u32[]{:S(2)}) collective-permute-start(f32[10,2,80,128]{3,2,1,0:T(8,128)S(1)} %get-tuple-element.67.bottom), channel_id=1, source_target_pairs={{0,1},{2,3},{4,5},{6,7},{1,8},{3,10},{5,12},{7,14},{8,9},{10,11},{... | collective-permute-start | bytes 2457608 | tf_op jit(solution)/shard_map/ppermute | solution.py:583
  34.1 15.8 %collective-permute-start.6 = (f32[800,128]{1,0:T(8,128)S(1)}, f32[800,128]{1,0:T(8,128)S(1)}, u32[]{:S(2)}, u32[]{:S(2)}) collective-permute-start(f32[800,128]{1,0:T(8,128)S(1)} %copy-done.5), channel_id=1, source_target_pairs={{0,2},{1,4},{2,0},{3,6},{4,7},{5,1},{6,5},{7,3},{8,10},{9,12},{10,... | collective-permute-start | bytes 1228808 | tf_op jit(solution)/shard_map/ppermute | solution.py:555
  35.6 15.2 %collective-permute-start.7 = (f32[800,128]{1,0:T(8,128)S(1)}, f32[800,128]{1,0:T(8,128)S(1)}, u32[]{:S(2)}, u32[]{:S(2)}) collective-permute-start(f32[800,128]{1,0:T(8,128)S(1)} %copy-done.4), channel_id=1, source_target_pairs={{0,4},{1,2},{2,6},{3,0},{4,1},{5,7},{6,3},{7,5},{8,12},{9,10},{10,... | collective-permute-start | bytes 1228808 | tf_op jit(solution)/shard_map/ppermute | solution.py:555
  35.6 15.2 %collective-permute-start.8 = (f32[800,128]{1,0:T(8,128)S(1)}, f32[800,128]{1,0:T(8,128)S(1)}, u32[]{:S(2)}, u32[]{:S(2)}) collective-permute-start(f32[800,128]{1,0:T(8,128)S(1)} %copy-done.3), channel_id=1, source_target_pairs={{0,6},{1,0},{2,4},{3,2},{4,3},{5,5},{6,1},{7,7},{8,14},{9,8},{10,1... | collective-permute-start | bytes 1228808 | tf_op jit(solution)/shard_map/ppermute | solution.py:555
  54.5 16.9 %collective-permute-start.9 = (f32[10,2,72,128]{3,2,1,0:T(8,128)S(1)}, f32[10,2,72,128]{3,2,1,0:T(8,128)S(1)}, u32[]{:S(2)}, u32[]{:S(2)}) collective-permute-start(f32[10,2,72,128]{3,2,1,0:T(8,128)S(1)} %get-tuple-element.76.bottom), channel_id=1, source_target_pairs={{0,1},{2,3},{4,5},{6,7},{1,8},{3,10},{5,12},{7,14},{8,9},{10,11},{... | collective-permute-start | bytes 2211848 | tf_op jit(solution)/shard_map/ppermute | solution.py:583
  57.7 16.5 %collective-permute-start.12 = (f32[10,2,72,128]{3,2,1,0:T(8,128)S(1)}, f32[10,2,72,128]{3,2,1,0:T(8,128)S(1)}, u32[]{:S(2)}, u32[]{:S(2)}) collective-permute-start(f32[10,2,72,128]{3,2,1,0:T(8,128)S(1)} %get-tuple-element.78.top), channel_id=1, source_target_pairs={{1,0},{3,2},{5,4},{7,6},{8,1},{10,3},{12,5},{14,7},{9,8},{11,10},{... | collective-permute-start | bytes 2211848 | tf_op jit(solution)/shard_map/ppermute | solution.py:582
  73.8 14.6 %collective-permute-start.11 = (f32[10,2,72,128]{3,2,1,0:T(8,128)S(1)}, f32[10,2,72,128]{3,2,1,0:T(8,128)S(1)}, u32[]{:S(2)}, u32[]{:S(2)}) collective-permute-start(f32[10,2,72,128]{3,2,1,0:T(8,128)S(1)} %top_kernel.4.top), channel_id=1, source_target_pairs={{1,0},{3,2},{5,4},{7,6},{8,1},{10,3},{12,5},{14,7},{9,8},{11,10},{... | collective-permute-start | bytes 2211848 | tf_op jit(solution)/shard_map/ppermute | solution.py:582
  76.7 16.3 %collective-permute-start.13 = (f32[10,2,72,128]{3,2,1,0:T(8,128)S(1)}, f32[10,2,72,128]{3,2,1,0:T(8,128)S(1)}, u32[]{:S(2)}, u32[]{:S(2)}) collective-permute-start(f32[10,2,72,128]{3,2,1,0:T(8,128)S(1)} %bottom_kernel.4.bottom), channel_id=1, source_target_pairs={{0,1},{2,3},{4,5},{6,7},{1,8},{3,10},{5,12},{7,14},{8,9},{10,11},{... | collective-permute-start | bytes 2211848 | tf_op jit(solution)/shard_map/ppermute | solution.py:583
  82.3 14.1 %collective-permute-start.18 = (f32[10,64,128]{2,1,0:T(8,128)S(1)}, f32[10,64,128]{2,1,0:T(8,128)S(1)}, u32[]{:S(2)}, u32[]{:S(2)}) collective-permute-start(f32[10,64,128]{2,1,0:T(8,128)S(1)} %get-tuple-element.92), channel_id=1, source_target_pairs={{0,0},{6,1},{2,2},{4,3},{5,4},{3,5},{7,6},{1,7},{8,8},{14,9},{10,1... | collective-permute-start | bytes 983048 | tf_op jit(solution)/shard_map/ppermute | solution.py:627
  83.0 14.6 %collective-permute-start.19 = (f32[10,64,128]{2,1,0:T(8,128)S(1)}, f32[10,64,128]{2,1,0:T(8,128)S(1)}, u32[]{:S(2)}, u32[]{:S(2)}) collective-permute-start(f32[10,64,128]{2,1,0:T(8,128)S(1)} %get-tuple-element.93), channel_id=1, source_target_pairs={{2,0},{4,1},{0,2},{6,3},{7,4},{1,5},{5,6},{3,7},{10,8},{12,9},{8,1... | collective-permute-start | bytes 983048 | tf_op jit(solution)/shard_map/ppermute | solution.py:627
  84.5 17.4 %collective-permute-start.20 = (f32[10,64,128]{2,1,0:T(8,128)S(1)}, f32[10,64,128]{2,1,0:T(8,128)S(1)}, u32[]{:S(2)}, u32[]{:S(2)}) collective-permute-start(f32[10,64,128]{2,1,0:T(8,128)S(1)} %get-tuple-element.94), channel_id=1, source_target_pairs={{4,0},{2,1},{6,2},{0,3},{1,4},{7,5},{3,6},{5,7},{12,8},{10,9},{14,... | collective-permute-start | bytes 983048 | tf_op jit(solution)/shard_map/ppermute | solution.py:627
  88.5 15.4 %collective-permute-start.21 = (f32[10,64,128]{2,1,0:T(8,128)S(1)}, f32[10,64,128]{2,1,0:T(8,128)S(1)}, u32[]{:S(2)}, u32[]{:S(2)}) collective-permute-start(f32[10,64,128]{2,1,0:T(8,128)S(1)} %get-tuple-element.95), channel_id=1, source_target_pairs={{6,0},{0,1},{4,2},{2,3},{3,4},{5,5},{1,6},{7,7},{14,8},{8,9},{12,1... | collective-permute-start | bytes 983048 | tf_op jit(solution)/shard_map/ppermute | solution.py:627
  95.7 8.7 %collective-permute-start.14 = (f32[10,64,128]{2,1,0:T(8,128)S(1)}, f32[10,64,128]{2,1,0:T(8,128)S(1)}, u32[]{:S(2)}, u32[]{:S(2)}) collective-permute-start(f32[10,64,128]{2,1,0:T(8,128)S(1)} %get-tuple-element.87), channel_id=1, source_target_pairs={{0,0},{6,1},{2,2},{4,3},{5,4},{3,5},{7,6},{1,7},{8,8},{14,9},{10,1... | collective-permute-start | bytes 983048 | tf_op jit(solution)/shard_map/ppermute | solution.py:627
  96.4 13.0 %collective-permute-start.15 = (f32[10,64,128]{2,1,0:T(8,128)S(1)}, f32[10,64,128]{2,1,0:T(8,128)S(1)}, u32[]{:S(2)}, u32[]{:S(2)}) collective-permute-start(f32[10,64,128]{2,1,0:T(8,128)S(1)} %get-tuple-element.88), channel_id=1, source_target_pairs={{2,0},{4,1},{0,2},{6,3},{7,4},{1,5},{5,6},{3,7},{10,8},{12,9},{8,1... | collective-permute-start | bytes 983048 | tf_op jit(solution)/shard_map/ppermute | solution.py:627
  97.5 15.8 %collective-permute-start.16 = (f32[10,64,128]{2,1,0:T(8,128)S(1)}, f32[10,64,128]{2,1,0:T(8,128)S(1)}, u32[]{:S(2)}, u32[]{:S(2)}) collective-permute-start(f32[10,64,128]{2,1,0:T(8,128)S(1)} %get-tuple-element.89), channel_id=1, source_target_pairs={{4,0},{2,1},{6,2},{0,3},{1,4},{7,5},{3,6},{5,7},{12,8},{10,9},{14,... | collective-permute-start | bytes 983048 | tf_op jit(solution)/shard_map/ppermute | solution.py:627
  101.9 15.1 %collective-permute-start.17 = (f32[10,64,128]{2,1,0:T(8,128)S(1)}, f32[10,64,128]{2,1,0:T(8,128)S(1)}, u32[]{:S(2)}, u32[]{:S(2)}) collective-permute-start(f32[10,64,128]{2,1,0:T(8,128)S(1)} %get-tuple-element.90), channel_id=1, source_target_pairs={{6,0},{0,1},{4,2},{2,3},{3,4},{5,5},{1,6},{7,7},{14,8},{8,9},{12,1... | collective-permute-start | bytes 983048 | tf_op jit(solution)/shard_map/ppermute | solution.py:627
